TPU v7x, 32 devices: a whole 2x2x4 slice. The times are simulated.
32 devices in a mesh: dp: 16 (over z, y, x), cent: 2 (over core).
Axes of the slice: x: 2, y: 2, z: 4, core: 2. Of those that a mesh axis runs over, the one named last changes fastest.
Arguments:
- embeddings: float32 [6144, 1024], P(('dp', 'cent')), may hold values from -128 to 128
- centroids: float32 [4096, 1024], P(('dp', 'cent')), may hold values from -6 to 6
Outputs:
- updated: float32 [4096, 1024], P(('dp', 'cent'))
- entropy: float32 [6144], P(('dp', 'cent'))
All inputs are finite; a program needn't handle non-finite values.
Results may differ from a plain program's by a relative error of at most 0.024.
Values may be sent and summed in bfloat16 or wider, within the bound.
No kernel may reach another device: no remote copies, remote signals or barrier semaphores. Data moves between devices by JAX's collectives and lax.ppermute only.
A program may use at most 64 MiB of HBM per device.

v0:
```python
import jax
import jax.numpy as jnp
from jax import lax
from jax.sharding import PartitionSpec as P

softness_level = 32.0
prior_mass = 4.0


def row_stats(score):
    top = lax.pmax(jnp.max(score, axis=1), "cent")
    shifted = score - top[:, None]
    weight = jnp.exp(shifted)
    total, spread = lax.psum((jnp.sum(weight, axis=1), jnp.sum(weight * shifted, axis=1)), "cent")
    return (weight, total, spread)


def on_device(embeddings, centroids):
    shard_rows = embeddings.shape[0]
    per_device = centroids.shape[0]
    rows_b = lax.all_gather(embeddings.astype(jnp.bfloat16), "cent", axis=0, tiled=True)
    row_squared_norm = jnp.einsum("rd,rd->r", rows_b, rows_b, preferred_element_type=jnp.float32)

    def score_piece(piece):
        inner_products = jnp.einsum("rd,kd->rk", rows_b, piece, preferred_element_type=jnp.float32)
        centroid_squared_norm = jnp.einsum(
            "kd,kd->k", piece, piece, preferred_element_type=jnp.float32
        )
        return -(
            row_squared_norm[:, None] - 2.0 * inner_products + centroid_squared_norm[None, :]
        ) / (2.0 * softness_level)

    previous = lax.all_gather(centroids, "dp", axis=0, tiled=True)
    first_score = score_piece(previous.astype(jnp.bfloat16))
    weight, total, unused = row_stats(first_score)
    resp = (weight / total[:, None]).astype(jnp.bfloat16)
    sums = jnp.einsum("rk,rd->kd", resp, rows_b, preferred_element_type=jnp.float32)
    counts = jnp.sum(resp, axis=0, dtype=jnp.float32)
    sums, counts = lax.psum((sums, counts), "dp")
    renewed = (sums + prior_mass * previous) / (counts + prior_mass)[:, None]
    second_score = score_piece(renewed.astype(jnp.bfloat16))
    updated = lax.dynamic_slice_in_dim(renewed, lax.axis_index("dp") * per_device, per_device, 0)
    unused_weight, total_two, spread_two = row_stats(second_score)
    entropy_group = jnp.log(total_two) - spread_two / total_two
    entropy = lax.dynamic_slice_in_dim(
        entropy_group, lax.axis_index("cent") * shard_rows, shard_rows, 0
    )
    return (updated, entropy)


def solution(mesh):
    in_specs = (P(("dp", "cent"), None), P(("dp", "cent"), None))
    out_specs = (P(("dp", "cent"), None), P(("dp", "cent")))
    return jax.shard_map(
        on_device, mesh=mesh, in_specs=in_specs, out_specs=out_specs, check_vma=False
    )
```

profile of v0, /device:TPU:0, one launch (start us, length us, event | category | flops | bytes accessed | tf_op | source)
XLA Modules:
  0.0 431.2 jit_solution(11547274734267204340)
XLA Ops:
  7.2 0.0 all-gather.2.cloned.1.call-start
  7.2 0.7 all-gather.2.cloned.1.call-update
  7.9 0.0 all-reduce.3.cloned.1.call-start
  7.9 1.2 convert_element_type.15
  9.1 2.4 all_gather.6
  11.6 0.0 copy-start.2
  11.6 0.9 copy-done.2
  12.5 0.2 fusion.6
  12.7 113.6 %all-gather.2.cloned.1.call-done = f32[2048,1024]{1,0:T(8,128)} async-done(((f32[128,1024]{1,0:T(8,128)}), f32[2048,1024]{1,0:T(8,128)}) %all-gather.2.cloned.1.call-update) | async-done | bytes 8388624 | tf_op jit(solution)/shard_map/all_gather | solution.py:33
  126.3 0.0 copy-start
  126.3 4.1 fusion.1
  130.5 1.6 copy-done
  132.1 3.3 fusion.7
  135.4 2.5 pmax.14
  137.8 0.6 fusion.3
  138.4 2.5 psum.35
  140.9 0.0 copy-start.3
  140.9 1.1 convert_reduce_fusion
  142.0 0.0 copy-done.3
  142.0 5.6 %fusion.9 = f32[2048,1024]{1,0:T(8,128)} fusion(bf16[384,2048]{1,0:T(8,128)(2,1)S(1)} %get-tuple-element.9, bf16[384,1024]{1,0:T(8,128)(2,1)S(1)} %copy-done.3), kind=kOutput, calls=%fused_computation.23 | convolution fusion | flops 1610612736 | bytes 10747904 | tf_op jit(solution)/shard_map/rk,rd->kd/dot_general | solution.py:37
  147.6 0.0 all-reduce.3.cloned.1.call-update
  147.6 42.2 %psum.37 = f32[2048]{0:T(1024)S(1)} all-reduce(f32[2048]{0:T(1024)S(1)} %get-tuple-element.8), channel_id=1, replica_groups=mesh['dp'=16,'cent'=2] {'dp'}, use_global_device_ids=true, to_apply=%region_6.0 | all-reduce | flops 2048 | bytes 16384 | tf_op jit(solution)/shard_map/psum | solution.py:39
  189.8 0.0 copy-start.4
  189.8 213.5 %all-reduce.3.cloned.1.call-done = f32[2048,1024]{1,0:T(8,128)} async-done(((f32[2048,1024]{1,0:T(8,128)}), f32[2048,1024]{1,0:T(8,128)}) %all-reduce.3.cloned.1.call-update) | async-done | bytes 8388624 | tf_op jit(solution)/shard_map/psum | solution.py:39
  403.3 6.7 %fusion = (f32[2048]{0:T(1024)S(1)}, f32[2048,1024]{1,0:T(8,128)S(1)}) fusion(f32[2048]{0:T(1024)S(1)} %broadcast_add_fusion, f32[2048,1024]{1,0:T(8,128)} %all-reduce.3.cloned.1.call-done, f32[2048,1024]{1,0:T(8,128)} %all-gather.2.cloned.1.call-done), kind=kLoop, calls=%fused_computation.1 | loop fusion | flops 14678016 | bytes 25182208 | tf_op jit(solution)/shard_map/kd,kd->k/dot_general | solution.py:26
  410.0 0.0 copy-start.1
  410.0 0.0 copy-done.4
  410.0 4.3 %fusion.8 = (f32[384]{0:T(512)S(1)}, f32[2048,384]{1,0:T(8,128)}) fusion(f32[2048]{0:T(1024)S(1)} %get-tuple-element.6, bf16[384,1024]{1,0:T(8,128)(2,1)S(1)} %copy-done.4, f32[2048,1024]{1,0:T(8,128)S(1)} %get-tuple-element.7, f32[384]{0:T(512)S(1)} %fusion.6), kind=kOutput, calls=%fused_computation.22 | convolution fusion | flops 1617428096 | bytes 12332032 | tf_op jit(solution)/shard_map/rd,kd->rk/dot_general | solution.py:25
  414.4 0.0 copy-done.1
  414.4 2.4 pmax.15
  416.8 1.9 constant_dynamic-slice_fusion
  418.7 2.6 exponential_reduce_fusion
  421.3 2.5 all-reduce
  423.7 0.6 dynamic_slice.7
  (2 shorter events, 0.0 us)
Async XLA Ops:
  7.2 119.2 %all-gather.2.cloned.1.call-start = ((), (), s32[]{:S(2)}) async-start(), calls=%async_computation | async-start | bytes 8912896 | tf_op jit(solution)/shard_map/all_gather | solution.py:33
  7.9 395.4 %all-reduce.3.cloned.1.call-start = ((), (), s32[]{:S(2)}) async-start(), calls=%async_computation.1 | async-start | bytes 16777216 | tf_op jit(solution)/shard_map/psum | solution.py:39
  11.6 0.9 copy-start.2
  126.3 5.8 %copy-start = (f32[2048,1024]{1,0:T(8,128)S(1)}, f32[2048,1024]{1,0:T(8,128)}, u32[]{:S(2)}) copy-start(f32[2048,1024]{1,0:T(8,128)} %all-gather.2.cloned.1.call-done) | copy-start | bytes 25165828
  140.9 1.1 copy-start.3
  189.8 220.2 %copy-start.4 = (bf16[384,1024]{1,0:T(8,128)(2,1)S(1)}, bf16[384,1024]{1,0:T(8,128)(2,1)}, u32[]{:S(2)}) copy-start(bf16[384,1024]{1,0:T(8,128)(2,1)} %copy-done.2) | copy-start | bytes 2359300
  410.0 4.4 %copy-start.1 = (f32[2048,1024]{1,0:T(8,128)}, f32[2048,1024]{1,0:T(8,128)S(1)}, u32[]{:S(2)}) copy-start(f32[2048,1024]{1,0:T(8,128)S(1)} %get-tuple-element.7) | copy-start | bytes 25165828
Sparse Core Ops, SparseCore 0:
  10.8 115.5 all-gather.1
  147.8 255.5 all-reduce.2
where the time goes:
time: 432 us; the launch traced here: 431 us
  waiting for transfers between devices  328 us (76%)
  blocking collectives  54.4 us (13%)
  other arithmetic  16.5 us (4%)
  between operations  14.1 us (3%)
  matrix products  13.2 us (3%)
  local copies, waits for them, and re-layouts  5.12 us (1%)
    psum x1, waiting for transfers between devices, on_device(): sums, counts = lax.psum((sums, counts), 'dp')  214 us
    all_gather x1, waiting for transfers between devices, on_device(): previous = lax.all_gather(centroids, 'dp', axis=0, tiled=True)  114 us
    psum x1, blocking collectives, on_device(): sums, counts = lax.psum((sums, counts), 'dp')  42.2 us
    dot_general x2, other arithmetic, score_piece(): jnp.einsum('kd,kd->k', piece, piece, preferred_element_type=jnp.float32)  10.8 us
  transfers between devices with their start and end apart: 2, of which 2 were waited for; matrix products, arithmetic and copies ran while one was open for 0% of the time, Pallas kernels for 0%

commit v1 on v0

v1 whole, which is shorter than its diff:
```python
import functools

import jax
import jax.numpy as jnp
from jax import lax
from jax.experimental import pallas as pl
from jax.experimental.pallas import tpu as pltpu
from jax.sharding import PartitionSpec as P

softness_level = 32.0
prior_mass = 4.0
PLANE = 4


def vmem_limit(*arrays):
    held = sum(2 * v.size * v.dtype.itemsize for v in arrays)
    return min(56 << 20, held + (16 << 20))


def load_chunks(chunks, rows_v, sems, shard):
    copies = []
    for i, chunk in enumerate(chunks):
        copy = pltpu.make_async_copy(chunk, rows_v.at[pl.ds(i * shard, shard)], sems.at[i])
        copy.start()
        copies.append(copy)
    return copies


def row_squares(rows):
    wide = rows.astype(jnp.float32)
    square = wide * wide
    part = square[:, :128]
    for j in range(128, square.shape[1], 128):
        part = part + square[:, j : j + 128]
    return jnp.sum(part.T, axis=0, keepdims=True)


def centroid_squares(piece):
    wide = piece.astype(jnp.float32)
    return jnp.sum(wide * wide, axis=1, keepdims=True)


def scores(piece, cent_sq, rows, row_sq):
    inner = lax.dot_general(piece, rows, (((1,), (1,)), ((), ())), preferred_element_type=jnp.float32)
    return -(row_sq - 2.0 * inner + cent_sq) / (2.0 * softness_level)


def first_kernel(shard, cents, *refs):
    chunks = refs[:PLANE]
    weight_ref, stats_ref, row_sq_ref, rows_v, sems = refs[PLANE:]
    copies = load_chunks(chunks, rows_v, sems, shard)
    piece = cents[...]
    cent_sq = centroid_squares(piece)
    tile = 2 * shard
    for j in range(PLANE // 2):
        copies[2 * j].wait()
        copies[2 * j + 1].wait()
        rows = rows_v[j * tile : (j + 1) * tile, :]
        row_sq = row_squares(rows)
        score = scores(piece, cent_sq, rows, row_sq)
        top = jnp.max(score, axis=0, keepdims=True)
        weight = jnp.exp(score - top)
        total = jnp.sum(weight, axis=0, keepdims=True)
        weight_ref[:, j * tile : (j + 1) * tile] = weight
        row_sq_ref[:, j * tile : (j + 1) * tile] = row_sq
        for i in range(2):
            stats_ref[0, 2 * j + i : 2 * j + i + 1, :] = top[:, i * shard : (i + 1) * shard]
            stats_ref[1, 2 * j + i : 2 * j + i + 1, :] = total[:, i * shard : (i + 1) * shard]


def first_pass(cents, chunks):
    shard, width = chunks[0].shape
    n_k = cents.shape[0]
    n_rows = PLANE * shard
    vmem = pl.BlockSpec(memory_space=pltpu.VMEM)
    hbm = pl.BlockSpec(memory_space=pl.ANY)
    return pl.pallas_call(
        functools.partial(first_kernel, shard),
        out_shape=(
            jax.ShapeDtypeStruct((n_k, n_rows), jnp.float32),
            jax.ShapeDtypeStruct((2, PLANE, shard), jnp.float32),
            jax.ShapeDtypeStruct((1, n_rows), jnp.float32),
        ),
        in_specs=[vmem] + [hbm] * PLANE,
        out_specs=(vmem, vmem, vmem),
        scratch_shapes=[pltpu.VMEM((n_rows, width), jnp.bfloat16), pltpu.SemaphoreType.DMA((PLANE,))],
        compiler_params=pltpu.CompilerParams(vmem_limit_bytes=vmem_limit(cents, *chunks)),
        cost_estimate=pl.CostEstimate(
            flops=2 * n_k * n_rows * width, bytes_accessed=2 * n_rows * width, transcendentals=n_k * n_rows
        ),
        name="first_pass",
    )(cents, *chunks)


def sums_kernel(shard, n_slots, scale, *refs):
    weights = refs[:n_slots]
    n_chunks = PLANE * n_slots
    chunks = refs[n_slots : n_slots + n_chunks]
    out_ref, rows_v, sems = refs[n_slots + n_chunks :]
    copies = load_chunks(chunks, rows_v, sems, shard)
    width = rows_v.shape[1]
    n_rows = PLANE * shard
    counts = jnp.zeros((out_ref.shape[0], 1), jnp.float32)
    for s in range(n_slots):
        resp = (weights[s][...] * scale[s : s + 1, :]).astype(jnp.bfloat16)
        counts = counts + jnp.sum(resp.astype(jnp.float32), axis=1, keepdims=True)
        for i in range(PLANE):
            copies[PLANE * s + i].wait()
        part = jnp.dot(resp, rows_v[s * n_rows : (s + 1) * n_rows, :], preferred_element_type=jnp.float32)
        if s:
            part = part + out_ref[:, :width]
        out_ref[:, :width] = part
    out_ref[:, width:] = jnp.broadcast_to(counts, (out_ref.shape[0], 128))


def sums_pass(scale, weights, chunks):
    shard, width = chunks[0].shape
    n_slots = len(weights)
    n_k = weights[0].shape[0]
    n_rows = len(chunks) * shard
    vmem = pl.BlockSpec(memory_space=pltpu.VMEM)
    hbm = pl.BlockSpec(memory_space=pl.ANY)
    return pl.pallas_call(
        functools.partial(sums_kernel, shard, n_slots),
        out_shape=jax.ShapeDtypeStruct((n_k, width + 128), jnp.float32),
        in_specs=[vmem] * (1 + n_slots) + [hbm] * len(chunks),
        out_specs=vmem,
        scratch_shapes=[pltpu.VMEM((n_rows, width), jnp.bfloat16), pltpu.SemaphoreType.DMA((len(chunks),))],
        compiler_params=pltpu.CompilerParams(vmem_limit_bytes=vmem_limit(*weights, *chunks)),
        cost_estimate=pl.CostEstimate(
            flops=2 * n_k * n_rows * width, bytes_accessed=2 * n_rows * width, transcendentals=0
        ),
        name="sums_pass",
    )(scale, *weights, *chunks)


def second_kernel(shard, n_slots, per_device, sums, previous, *refs):
    n_chunks = PLANE * n_slots
    row_sqs = refs[:n_slots]
    chunks = refs[n_slots : n_slots + n_chunks]
    updated_ref, stats_ref, rows_v, sems = refs[n_slots + n_chunks :]
    copies = load_chunks(chunks, rows_v, sems, shard)
    width = rows_v.shape[1]
    counts = sums[:, width : width + 1]
    renewed = (sums[:, :width] + prior_mass * previous[...]) / (counts + prior_mass)
    updated_ref[...] = renewed[:per_device, :]
    piece = renewed.astype(jnp.bfloat16)
    cent_sq = centroid_squares(piece)
    tile = 2 * shard
    for s in range(n_slots):
        for j in range(PLANE // 2):
            first = PLANE * s + 2 * j
            copies[first].wait()
            copies[first + 1].wait()
            rows = rows_v[first * shard : (first + 2) * shard, :]
            score = scores(piece, cent_sq, rows, row_sqs[s][:, j * tile : (j + 1) * tile])
            top = jnp.max(score, axis=0, keepdims=True)
            shifted = score - top
            weight = jnp.exp(shifted)
            total = jnp.sum(weight, axis=0, keepdims=True)
            spread = jnp.sum(weight * shifted, axis=0, keepdims=True)
            for i in range(2):
                span = slice(i * shard, (i + 1) * shard)
                row = slice(2 * j + i, 2 * j + i + 1)
                stats_ref[s, 0, row, :] = top[:, span]
                stats_ref[s, 1, row, :] = total[:, span]
                stats_ref[s, 2, row, :] = spread[:, span]


def second_pass(sums, previous, row_sqs, chunks, per_device):
    shard, width = chunks[0].shape
    n_slots = len(row_sqs)
    n_k = previous.shape[0]
    n_rows = len(chunks) * shard
    vmem = pl.BlockSpec(memory_space=pltpu.VMEM)
    hbm = pl.BlockSpec(memory_space=pl.ANY)
    return pl.pallas_call(
        functools.partial(second_kernel, shard, n_slots, per_device),
        out_shape=(
            jax.ShapeDtypeStruct((per_device, width), jnp.float32),
            jax.ShapeDtypeStruct((n_slots, 3, PLANE, shard), jnp.float32),
        ),
        in_specs=[vmem] * (2 + n_slots) + [hbm] * len(chunks),
        out_specs=(vmem, vmem),
        scratch_shapes=[pltpu.VMEM((n_rows, width), jnp.bfloat16), pltpu.SemaphoreType.DMA((len(chunks),))],
        compiler_params=pltpu.CompilerParams(vmem_limit_bytes=vmem_limit(sums, previous, *chunks)),
        cost_estimate=pl.CostEstimate(
            flops=2 * n_k * n_rows * width, bytes_accessed=2 * n_rows * width, transcendentals=n_k * n_rows
        ),
        name="second_pass",
    )(sums, previous, *row_sqs, *chunks)


def merge(parts, axis):
    tops = [jnp.take(p, 0, axis=axis) for p in parts]
    top = functools.reduce(jnp.maximum, tops)
    total = 0.0
    spread = 0.0
    for p, own in zip(parts, tops):
        drop = own - top
        factor = jnp.exp(drop)
        part_total = jnp.take(p, 1, axis=axis)
        total = total + factor * part_total
        if p.shape[axis] == 3:
            spread = spread + factor * (jnp.take(p, 2, axis=axis) + drop * part_total)
    return top, total, spread


def solution(mesh):
    n_dp = mesh.shape["dp"]
    n_cent = mesh.shape["cent"]
    n_slots = n_dp // PLANE

    def along_z(value, shift):
        return lax.ppermute(value, "dp", [(i, (i + PLANE * shift) % n_dp) for i in range(n_dp)])

    def in_plane(value, bits):
        return lax.ppermute(value, "dp", [(i, i ^ bits) for i in range(n_dp)])

    def across(value, bits):
        return lax.ppermute(value, "cent", [(i, i ^ bits) for i in range(n_cent)])

    def blocks_swapped(value, bits):
        blocks = jnp.split(value, n_cent, axis=0)
        return jnp.concatenate([blocks[i ^ bits] for i in range(n_cent)], axis=0)

    def on_device(embeddings, centroids):
        per_device = centroids.shape[0]
        own = embeddings.astype(jnp.bfloat16)
        order = [0] + sorted(range(1, n_slots), key=lambda s: (min(s, n_slots - s), s))
        slots = {0: own}
        for s in order[1:]:
            slots[s] = along_z(own, s)
        planes = {}
        for s in order:
            chunk = slots[s]
            early, late = (1, 2) if s % 2 == 0 else (2, 1)
            pieces = {0: chunk, early: in_plane(chunk, early), late: in_plane(chunk, late)}
            pieces[3] = in_plane(pieces[early], late)
            planes[s] = [pieces[b] for b in range(PLANE)]
        chunks = [c for s in range(n_slots) for c in planes[s]]

        previous = jnp.concatenate([centroids] + [across(centroids, b) for b in range(1, n_cent)], axis=0)
        piece = previous.astype(jnp.bfloat16)

        weights, local, row_sqs, plane_stats = [], [], [], []
        for s in range(n_slots):
            weight, stats, row_sq = first_pass(piece, planes[s])
            weights.append(weight)
            local.append(stats)
            row_sqs.append(row_sq)
            parts = [stats]
            for bits in range(1, PLANE):
                other = in_plane(stats, bits)
                parts.append(jnp.stack([other[:, b ^ bits] for b in range(PLANE)], axis=1))
            top, total, unused = merge(parts, 0)
            plane_stats.append(jnp.stack([top, total]))
        plane_stats = jnp.stack(plane_stats)
        parts = [plane_stats]
        for shift in range(1, n_slots):
            other = along_z(plane_stats, shift)
            parts.append(jnp.concatenate([other[n_slots - shift :], other[: n_slots - shift]], axis=0))
        top, total, unused = merge(parts, 1)
        scale = jnp.exp(jnp.stack([stats[0] for stats in local]) - top) / total
        scale = scale.reshape(n_slots, PLANE * own.shape[0])

        sums = sums_pass(scale, weights, chunks)
        bits = 1
        while bits < n_cent:
            sums = sums + blocks_swapped(across(sums, bits), bits)
            bits *= 2

        updated, stats = second_pass(sums, previous, row_sqs, chunks, per_device)
        parts = [stats[0]]
        for shift in range(1, n_slots):
            parts.append(along_z(stats[shift], -shift))
        stats = jnp.stack(merge(parts, 0))
        parts = [stats[:, 0]]
        for bits in range(1, PLANE):
            parts.append(in_plane(stats[:, bits], bits))
        top, total, spread = merge(parts, 0)
        entropy = jnp.log(total) - spread / total
        return (updated, entropy)

    in_specs = (P(("dp", "cent"), None), P(("dp", "cent"), None))
    out_specs = (P(("dp", "cent"), None), P(("dp", "cent")))
    return jax.shard_map(
        on_device, mesh=mesh, in_specs=in_specs, out_specs=out_specs, check_vma=False
    )
```

time: 432 us -> 159 us (0.37)
  waiting for transfers between devices: 328 us -> 60.7 us
  blocking collectives: 54.4 us -> 0 us
  starting transfers between devices: 0.08 us -> 51.6 us
  Pallas kernels: 0 us -> 23.1 us
  local copies, waits for them, and re-layouts: 5.12 us -> 19.4 us
  other arithmetic: 16.5 us -> 2.31 us
  matrix products: 13.2 us -> 0 us
  between operations: 14.1 us -> 1.24 us
    psum x1 -> x0, waiting for transfers between devices: 214 us -> none  [on_device(): sums, counts = lax.psum((sums, counts), 'dp')]
    all_gather x1 -> x0, waiting for transfers between devices: 114 us -> none  [on_device(): previous = lax.all_gather(centroids, 'dp', axis=0, tiled=True)]
    ppermute x0 -> x38, waiting for transfers between devices: none -> 60.7 us  [the longest x27 33.3 us: in_plane(): return lax.ppermute(value, 'dp', [(i, i ^ bits) for i in range(n_dp)])]
    ppermute x0 -> x38, starting transfers between devices: none -> 51.6 us  [the longest x27 34.5 us: in_plane(): return lax.ppermute(value, 'dp', [(i, i ^ bits) for i in range(n_dp)])]
    psum x3 -> x0, blocking collectives: 47.1 us -> none  [the longest x1 42.2 us: on_device(): sums, counts = lax.psum((sums, counts), 'dp')]
    pallas_call x0 -> x6, Pallas kernels: none -> 23.1 us  [the longest x4 9 us: first_pass(): pl.pallas_call(functools.partial(first_kernel, shard), out_shape=(jax.Sha...]
    unnamed x10 -> x83, local copies, waits for them, and re-layouts: 2.6 us -> 19 us
    dot_general x3 -> x0, matrix products: 13.2 us -> none  [the longest x2 7.6 us: score_piece(): jnp.einsum('rd,kd->rk', rows_b, piece, preferred_element_type=jnp.float32)]
  transfers between devices with their start and end apart: 2 -> 38, of which waited for: 2 -> 16; matrix products, arithmetic and copies ran while one was open for 0% -> 1% of each run, Pallas kernels for 0% -> 6%
where the time goes in v1:
time: 159 us; the launch traced here: 158 us
  waiting for transfers between devices  60.7 us (38%)
  starting transfers between devices  51.6 us (32%)
  Pallas kernels  23.1 us (15%)
  local copies, waits for them, and re-layouts  19.4 us (12%)
  other arithmetic  2.31 us (1%)
    ppermute x27, starting transfers between devices, in_plane(): return lax.ppermute(value, 'dp', [(i, i ^ bits) for i in range(n_dp)])  34.5 us
    ppermute x27, waiting for transfers between devices, in_plane(): return lax.ppermute(value, 'dp', [(i, i ^ bits) for i in range(n_dp)])  33.3 us
    ppermute x9, waiting for transfers between devices, along_z(): lax.ppermute(value, 'dp', [(i, (i + PLANE * shift) % n_dp) for i in range...  24.6 us
    unnamed x83, local copies, waits for them, and re-layouts  19 us
    ppermute x9, starting transfers between devices, along_z(): lax.ppermute(value, 'dp', [(i, (i + PLANE * shift) % n_dp) for i in range...  16.5 us
    pallas_call x4, Pallas kernels, first_pass(): pl.pallas_call(functools.partial(first_kernel, shard), out_shape=(jax.Sha...  9 us
    pallas_call x1, Pallas kernels, second_pass(): pl.pallas_call(functools.partial(second_kernel, shard, n_slots, per_devic...  8.76 us
    pallas_call x1, Pallas kernels, sums_pass(): pl.pallas_call(functools.partial(sums_kernel, shard, n_slots), out_shape=...  5.32 us
  transfers between devices with their start and end apart: 38, of which 16 were waited for; matrix products, arithmetic and copies ran while one was open for 1% of the time, Pallas kernels for 6%

profile of v1, /device:TPU:0, one launch (start us, length us, event | category | flops | bytes accessed | tf_op | source)
XLA Modules:
  0.0 158.3 jit_solution(10357420145176902034)
XLA Ops:
  1.2 1.2 convert_element_type.7.refs_0_.refs_4_
  2.3 2.6 %collective-permute-start.1 = (bf16[192,1024]{1,0:T(8,128)(2,1)S(1)}, bf16[192,1024]{1,0:T(8,128)(2,1)S(1)}, u32[]{:S(2)}, u32[]{:S(2)}) collective-permute-start(bf16[192,1024]{1,0:T(8,128)(2,1)S(1)} %convert_element_type.7.refs_0_.refs_4_), channel_id=1, source_target_pairs={{0,2},{2,0},{4,6},{6,4},{8,10},{10,8},{12,14},{14,12},{16,18},{18,... | collective-permute-start | bytes 1179656 | tf_op jit(solution)/shard_map/ppermute | solution.py:218
  5.0 1.5 collective-permute-start.2
  6.5 8.2 %collective-permute-done.1.refs_1_.refs_5_ = bf16[192,1024]{1,0:T(8,128)(2,1)S(1)} collective-permute-done((bf16[192,1024]{1,0:T(8,128)(2,1)S(1)}, bf16[192,1024]{1,0:T(8,128)(2,1)S(1)}, u32[]{:S(2)}, u32[]{:S(2)}) %collective-permute-start.1) | collective-permute-done | bytes 393248 | tf_op jit(solution)/shard_map/ppermute | solution.py:218
  14.7 1.8 %collective-permute-start.3 = (bf16[192,1024]{1,0:T(8,128)(2,1)S(1)}, bf16[192,1024]{1,0:T(8,128)(2,1)S(1)}, u32[]{:S(2)}, u32[]{:S(2)}) collective-permute-start(bf16[192,1024]{1,0:T(8,128)(2,1)S(1)} %collective-permute-done.1.refs_1_.refs_5_), channel_id=1, source_target_pairs={{0,4},{2,6},{4,0},{6,2},{8,12},{10,14},{12,8},{14,10},{16,20},{18,... | collective-permute-start | bytes 1179656 | tf_op jit(solution)/shard_map/ppermute | solution.py:218
  16.5 3.6 %collective-permute-start.12 = (bf16[192,1024]{1,0:T(8,128)(2,1)S(1)}, bf16[192,1024]{1,0:T(8,128)(2,1)S(1)}, u32[]{:S(2)}, u32[]{:S(2)}) collective-permute-start(bf16[192,1024]{1,0:T(8,128)(2,1)S(1)} %convert_element_type.7.refs_0_.refs_4_), channel_id=1, source_target_pairs={{0,24},{2,26},{4,28},{6,30},{8,0},{10,2},{12,4},{14,6},{16,8},{18,... | collective-permute-start | bytes 1179656 | tf_op jit(solution)/shard_map/ppermute | solution.py:215
  20.1 1.0 collective-permute-start.4
  21.3 4.3 %collective-permute-done.3.refs_3_.refs_7_ = bf16[192,1024]{1,0:T(8,128)(2,1)S(1)} collective-permute-done((bf16[192,1024]{1,0:T(8,128)(2,1)S(1)}, bf16[192,1024]{1,0:T(8,128)(2,1)S(1)}, u32[]{:S(2)}, u32[]{:S(2)}) %collective-permute-start.3) | collective-permute-done | bytes 393248 | tf_op jit(solution)/shard_map/ppermute | solution.py:218
  25.6 2.2 %first_pass.4 = (f32[256,768]{1,0:T(8,128)S(1)}, f32[2,4,192]{2,1,0:T(4,128)S(1)}, f32[1,768]{1,0:T(1,128)S(1)}) custom-call(bf16[256,1024]{1,0:T(8,128)(2,1)S(1)} %convert_element_type.6.cents, bf16[192,1024]{1,0:T(8,128)(2,1)S(1)} %convert_element_type.7.refs_0_.refs_4_, bf16[192,1024]{1,0:T(8,128)(2,1)S(1)} %collective-permute-done.1.refs_1_.refs_5_, ...), custom_call_target="tpu_custom_call" | custom-call | flops 402653184 | bytes 1572864 | tf_op jit(solution)/shard_map/first_pass/pallas_call | solution.py:77
  27.8 0.9 copy-done.30
  28.7 2.5 %collective-permute-start.18 = (f32[2,4,192]{2,1,0:T(4,128)S(1)}, f32[2,4,192]{2,1,0:T(4,128)S(1)}, u32[]{:S(2)}, u32[]{:S(2)}) collective-permute-start(f32[2,4,192]{2,1,0:T(4,128)S(1)} %get-tuple-element.26), channel_id=1, source_target_pairs={{0,6},{2,4},{4,2},{6,0},{8,14},{10,12},{12,10},{14,8},{16,22},{18,... | collective-permute-start | bytes 18440 | tf_op jit(solution)/shard_map/ppermute | solution.py:218
  32.2 20.9 %collective-permute-done.8.refs_0_.refs_12_ = bf16[192,1024]{1,0:T(8,128)(2,1)S(1)} collective-permute-done((bf16[192,1024]{1,0:T(8,128)(2,1)S(1)}, bf16[192,1024]{1,0:T(8,128)(2,1)S(1)}, u32[]{:S(2)}, u32[]{:S(2)}) %collective-permute-start.8) | collective-permute-done | bytes 393248 | tf_op jit(solution)/shard_map/ppermute | solution.py:215
  53.2 1.5 collective-permute-start.9
  55.2 1.5 collective-permute-start.17
  56.7 7.3 %collective-permute-done.17 = f32[2,4,192]{2,1,0:T(4,128)S(1)} collective-permute-done((f32[2,4,192]{2,1,0:T(4,128)S(1)}, f32[2,4,192]{2,1,0:T(4,128)S(1)}, u32[]{:S(2)}, u32[]{:S(2)}) %collective-permute-start.17) | collective-permute-done | bytes 6176 | tf_op jit(solution)/shard_map/ppermute | solution.py:218
  65.2 1.5 collective-permute-start.15
  66.7 1.2 collective-permute-done.16
  69.0 1.5 collective-permute-start.7
  70.5 6.7 %collective-permute-done.15.refs_3_.refs_19_ = bf16[192,1024]{1,0:T(8,128)(2,1)S(1)} collective-permute-done((bf16[192,1024]{1,0:T(8,128)(2,1)S(1)}, bf16[192,1024]{1,0:T(8,128)(2,1)S(1)}, u32[]{:S(2)}, u32[]{:S(2)}) %collective-permute-start.15) | collective-permute-done | bytes 393248 | tf_op jit(solution)/shard_map/ppermute | solution.py:218
  77.2 2.2 %first_pass.7 = (f32[256,768]{1,0:T(8,128)S(1)}, f32[2,4,192]{2,1,0:T(4,128)S(1)}, f32[1,768]{1,0:T(1,128)S(1)}) custom-call(bf16[256,1024]{1,0:T(8,128)(2,1)S(1)} %convert_element_type.6.cents, bf16[192,1024]{1,0:T(8,128)(2,1)S(1)} %collective-permute-done.12.refs_0_.refs_16_, bf16[192,1024]{1,0:T(8,128)(2,1)S(1)} %collective-permute-done.13.refs_1_.refs_17_, ...), custom_call_target="tpu_custom_call" | custom-call | flops 402653184 | bytes 1572864 | tf_op jit(solution)/shard_map/first_pass/pallas_call | solution.py:77
  79.5 0.9 copy-done.32
  80.4 2.5 %collective-permute-start.27 = (f32[2,4,192]{2,1,0:T(4,128)S(1)}, f32[2,4,192]{2,1,0:T(4,128)S(1)}, u32[]{:S(2)}, u32[]{:S(2)}) collective-permute-start(f32[2,4,192]{2,1,0:T(4,128)S(1)} %get-tuple-element.29), channel_id=1, source_target_pairs={{0,6},{2,4},{4,2},{6,0},{8,14},{10,12},{12,10},{14,8},{16,22},{18,... | collective-permute-start | bytes 18440 | tf_op jit(solution)/shard_map/ppermute | solution.py:218
  83.9 2.3 %first_pass.6 = (f32[256,768]{1,0:T(8,128)S(1)}, f32[2,4,192]{2,1,0:T(4,128)S(1)}, f32[1,768]{1,0:T(1,128)S(1)}) custom-call(bf16[256,1024]{1,0:T(8,128)(2,1)S(1)} %convert_element_type.6.cents, bf16[192,1024]{1,0:T(8,128)(2,1)S(1)} %collective-permute-done.8.refs_0_.refs_12_, bf16[192,1024]{1,0:T(8,128)(2,1)S(1)} %collective-permute-done.9.refs_1_.refs_13_, ...), custom_call_target="tpu_custom_call" | custom-call | flops 402653184 | bytes 1572864 | tf_op jit(solution)/shard_map/first_pass/pallas_call | solution.py:77
  86.3 2.5 %collective-permute-start.24 = (f32[2,4,192]{2,1,0:T(4,128)S(1)}, f32[2,4,192]{2,1,0:T(4,128)S(1)}, u32[]{:S(2)}, u32[]{:S(2)}) collective-permute-start(f32[2,4,192]{2,1,0:T(4,128)S(1)} %get-tuple-element.28), channel_id=1, source_target_pairs={{0,6},{2,4},{4,2},{6,0},{8,14},{10,12},{12,10},{14,8},{16,22},{18,... | collective-permute-start | bytes 18440 | tf_op jit(solution)/shard_map/ppermute | solution.py:218
  88.8 1.3 collective-permute-done.7.refs_3_.refs_11_
  90.1 1.5 collective-permute-start.23
  91.6 2.3 %first_pass.5 = (f32[256,768]{1,0:T(8,128)S(1)}, f32[2,4,192]{2,1,0:T(4,128)S(1)}, f32[1,768]{1,0:T(1,128)S(1)}) custom-call(bf16[256,1024]{1,0:T(8,128)(2,1)S(1)} %convert_element_type.6.cents, bf16[192,1024]{1,0:T(8,128)(2,1)S(1)} %collective-permute-done.4.refs_0_.refs_8_, bf16[192,1024]{1,0:T(8,128)(2,1)S(1)} %collective-permute-done.5.refs_1_.refs_9_, ...), custom_call_target="tpu_custom_call" | custom-call | flops 402653184 | bytes 1572864 | tf_op jit(solution)/shard_map/first_pass/pallas_call | solution.py:77
  93.9 0.9 copy-done.36
  94.8 1.5 collective-permute-start.22
  96.9 1.6 collective-permute-start.20
  98.5 1.6 collective-permute-start.19
  100.2 0.7 collective-permute-done.21
  100.9 1.3 collective-permute-done.19
  102.4 2.5 %collective-permute-start.28 = (f32[4,2,4,192]{3,2,0,1:T(4,128)S(1)}, f32[4,2,4,192]{3,2,0,1:T(4,128)S(1)}, u32[]{:S(2)}, u32[]{:S(2)}) collective-permute-start(f32[4,2,4,192]{3,2,0,1:T(4,128)S(1)} %copy.4), channel_id=1, source_target_pairs={{0,8},{2,10},{4,12},{6,14},{8,16},{10,18},{12,20},{14,22},{16,24},... | collective-permute-start | bytes 73736 | tf_op jit(solution)/shard_map/ppermute | solution.py:215
  104.9 1.4 collective-permute-start.30
  106.3 2.5 %collective-permute-start.29 = (f32[4,2,4,192]{3,2,0,1:T(4,128)S(1)}, f32[4,2,4,192]{3,2,0,1:T(4,128)S(1)}, u32[]{:S(2)}, u32[]{:S(2)}) collective-permute-start(f32[4,2,4,192]{3,2,0,1:T(4,128)S(1)} %copy.4), channel_id=1, source_target_pairs={{0,16},{2,18},{4,20},{6,22},{8,24},{10,26},{12,28},{14,30},{16,0},... | collective-permute-start | bytes 73736 | tf_op jit(solution)/shard_map/ppermute | solution.py:215
  109.2 1.8 %collective-permute-done.29 = f32[4,2,4,192]{3,2,0,1:T(4,128)S(1)} collective-permute-done((f32[4,2,4,192]{3,2,0,1:T(4,128)S(1)}, f32[4,2,4,192]{3,2,0,1:T(4,128)S(1)}, u32[]{:S(2)}, u32[]{:S(2)}) %collective-permute-start.29) | collective-permute-done | bytes 24608 | tf_op jit(solution)/shard_map/ppermute | solution.py:215
  111.2 1.0 copy-done.1
  112.2 1.0 copy-done.4
  113.2 1.0 copy-done.7
  114.2 1.0 copy-done.10
  115.2 1.0 copy-done.13
  116.2 1.0 copy-done.16
  117.2 1.0 copy-done.19
  118.2 1.0 copy-done.22
  119.2 1.0 copy-done.25
  120.2 1.0 copy-done.28
  121.2 1.1 copy-done.31
  122.3 1.1 copy-done.33
  123.5 1.1 copy-done.35
  124.6 1.1 copy-done.37
  125.7 5.3 %sums_pass.1 = f32[256,1152]{1,0:T(8,128)S(1)} custom-call(f32[4,768]{1,0:T(4,128)S(1)} %reshape.17.scale, f32[256,768]{1,0:T(8,128)S(1)} %copy-done.31, f32[256,768]{1,0:T(8,128)S(1)} %copy-done.37, f32[256,768]{1,0:T(8,128)S(1)} %copy-done.35, f32[256,768]{1,0:T(8,128)S(1)} %copy-done.33, bf16[192,1024]{1,0:T(8,128)(2,1)S(1)} %convert_element_type.7.refs_0_.refs_4_, ...), custom_call_target="tpu_custom_call" | custom-call | flops 1610612736 | bytes 6291456 | tf_op jit(solution)/shard_map/sums_pass/pallas_call | solution.py:123
  131.1 2.8 %collective-permute-done.31 = f32[256,1152]{1,0:T(8,128)S(1)} collective-permute-done((f32[256,1152]{1,0:T(8,128)S(1)}, f32[256,1152]{1,0:T(8,128)S(1)}, u32[]{:S(2)}, u32[]{:S(2)}) %collective-permute-start.31) | collective-permute-done | bytes 1179680 | tf_op jit(solution)/shard_map/ppermute | solution.py:221
  134.3 0.7 copy-done.29
  136.1 8.8 %second_pass.1 = (f32[128,1024]{1,0:T(8,128)}, f32[4,3,4,192]{3,2,1,0:T(4,128)S(1)}) custom-call(f32[256,1152]{1,0:T(8,128)S(1)} %maximum_add_fusion.sums, f32[256,1024]{1,0:T(8,128)S(1)} %constant_dynamic-update-slice_fusion.previous, f32[1,768]{1,0:T(1,128)S(1)} %get-tuple-element.34.refs_0_, f32[1,768]{1,0:T(1,128)S(1)} %get-tuple-element.35.refs_1_, ...), custom_call_target="tpu_custom_call" | custom-call | flops 1610612736 | bytes 6291456 | tf_op jit(solution)/shard_map/second_pass/pallas_call | solution.py:177
  144.8 1.1 collective-permute-start.34
  146.0 1.7 %collective-permute-start.33 = (f32[3,4,192]{2,1,0:T(4,128)S(1)}, f32[3,4,192]{2,1,0:T(4,128)S(1)}, u32[]{:S(2)}, u32[]{:S(2)}) collective-permute-start(f32[3,4,192]{2,1,0:T(4,128)S(1)} %get-tuple-element.156), channel_id=1, source_target_pairs={{0,16},{2,18},{4,20},{6,22},{8,24},{10,26},{12,28},{14,30},{16,0},... | collective-permute-start | bytes 27656 | tf_op jit(solution)/shard_map/ppermute | solution.py:215
  147.7 2.7 %collective-permute-start.32 = (f32[3,4,192]{2,1,0:T(4,128)S(1)}, f32[3,4,192]{2,1,0:T(4,128)S(1)}, u32[]{:S(2)}, u32[]{:S(2)}) collective-permute-start(f32[3,4,192]{2,1,0:T(4,128)S(1)} %get-tuple-element.157), channel_id=1, source_target_pairs={{0,24},{2,26},{4,28},{6,30},{8,0},{10,2},{12,4},{14,6},{16,8},{18,... | collective-permute-start | bytes 27656 | tf_op jit(solution)/shard_map/ppermute | solution.py:215
  150.6 1.2 collective-permute-done.32
  151.9 0.8 collective-permute-start.35
  153.2 2.3 %collective-permute-start.37 = (f32[3,192]{1,0:T(4,128)S(1)}, f32[3,192]{1,0:T(4,128)S(1)}, u32[]{:S(2)}, u32[]{:S(2)}) collective-permute-start(f32[3,192]{1,0:T(4,128)S(1)} %bitcast.459), channel_id=1, source_target_pairs={{0,6},{2,4},{4,2},{6,0},{8,14},{10,12},{12,10},{14,8},{16,22},{18,... | collective-permute-start | bytes 6920 | tf_op jit(solution)/shard_map/ppermute | solution.py:218
  155.5 0.8 collective-permute-done.36
  156.3 1.4 collective-permute-done.37
  157.7 0.6 divide_subtract_fusion
  (153 shorter events, 9.3 us)
Async XLA Ops:
  0.6 20.4 %copy-start.38 = (f32[128,1024]{1,0:T(8,128)S(1)}, f32[128,1024]{1,0:T(8,128)}, u32[]{:S(2)}) copy-start(f32[128,1024]{1,0:T(8,128)} %param.23) | copy-start | bytes 1572868
  0.6 19.4 %collective-permute-start = (f32[128,1024]{1,0:T(8,128)}, f32[128,1024]{1,0:T(8,128)S(1)}, u32[]{:S(2)}, u32[]{:S(2)}) collective-permute-start(f32[128,1024]{1,0:T(8,128)} %param.23), channel_id=1, source_target_pairs={{0,1},{1,0},{2,3},{3,2},{4,5},{5,4},{6,7},{7,6},{8,9},{9,8},{10,11... | collective-permute-start | bytes 1572872 | tf_op jit(solution)/shard_map/ppermute | solution.py:221
  2.3 12.3 %collective-permute-start.1 = (bf16[192,1024]{1,0:T(8,128)(2,1)S(1)}, bf16[192,1024]{1,0:T(8,128)(2,1)S(1)}, u32[]{:S(2)}, u32[]{:S(2)}) collective-permute-start(bf16[192,1024]{1,0:T(8,128)(2,1)S(1)} %convert_element_type.7.refs_0_.refs_4_), channel_id=1, source_target_pairs={{0,2},{2,0},{4,6},{6,4},{8,10},{10,8},{12,14},{14,12},{16,18},{18,... | collective-permute-start | bytes 1179656 | tf_op jit(solution)/shard_map/ppermute | solution.py:218
  5.0 16.3 %collective-permute-start.2 = (bf16[192,1024]{1,0:T(8,128)(2,1)S(1)}, bf16[192,1024]{1,0:T(8,128)(2,1)S(1)}, u32[]{:S(2)}, u32[]{:S(2)}) collective-permute-start(bf16[192,1024]{1,0:T(8,128)(2,1)S(1)} %convert_element_type.7.refs_0_.refs_4_), channel_id=1, source_target_pairs={{0,4},{2,6},{4,0},{6,2},{8,12},{10,14},{12,8},{14,10},{16,20},{18,... | collective-permute-start | bytes 1179656 | tf_op jit(solution)/shard_map/ppermute | solution.py:218
  14.7 10.9 %collective-permute-start.3 = (bf16[192,1024]{1,0:T(8,128)(2,1)S(1)}, bf16[192,1024]{1,0:T(8,128)(2,1)S(1)}, u32[]{:S(2)}, u32[]{:S(2)}) collective-permute-start(bf16[192,1024]{1,0:T(8,128)(2,1)S(1)} %collective-permute-done.1.refs_1_.refs_5_), channel_id=1, source_target_pairs={{0,4},{2,6},{4,0},{6,2},{8,12},{10,14},{12,8},{14,10},{16,20},{18,... | collective-permute-start | bytes 1179656 | tf_op jit(solution)/shard_map/ppermute | solution.py:218
  16.5 14.8 %collective-permute-start.12 = (bf16[192,1024]{1,0:T(8,128)(2,1)S(1)}, bf16[192,1024]{1,0:T(8,128)(2,1)S(1)}, u32[]{:S(2)}, u32[]{:S(2)}) collective-permute-start(bf16[192,1024]{1,0:T(8,128)(2,1)S(1)} %convert_element_type.7.refs_0_.refs_4_), channel_id=1, source_target_pairs={{0,24},{2,26},{4,28},{6,30},{8,0},{10,2},{12,4},{14,6},{16,8},{18,... | collective-permute-start | bytes 1179656 | tf_op jit(solution)/shard_map/ppermute | solution.py:215
  20.1 33.1 %collective-permute-start.8 = (bf16[192,1024]{1,0:T(8,128)(2,1)S(1)}, bf16[192,1024]{1,0:T(8,128)(2,1)S(1)}, u32[]{:S(2)}, u32[]{:S(2)}) collective-permute-start(bf16[192,1024]{1,0:T(8,128)(2,1)S(1)} %convert_element_type.7.refs_0_.refs_4_), channel_id=1, source_target_pairs={{0,16},{2,18},{4,20},{6,22},{8,24},{10,26},{12,28},{14,30},{16,0},... | collective-permute-start | bytes 1179656 | tf_op jit(solution)/shard_map/ppermute | solution.py:215
  20.1 34.6 %collective-permute-start.4 = (bf16[192,1024]{1,0:T(8,128)(2,1)S(1)}, bf16[192,1024]{1,0:T(8,128)(2,1)S(1)}, u32[]{:S(2)}, u32[]{:S(2)}) collective-permute-start(bf16[192,1024]{1,0:T(8,128)(2,1)S(1)} %convert_element_type.7.refs_0_.refs_4_), channel_id=1, source_target_pairs={{0,8},{2,10},{4,12},{6,14},{8,16},{10,18},{12,20},{14,22},{16,24},... | collective-permute-start | bytes 1179656 | tf_op jit(solution)/shard_map/ppermute | solution.py:215
  28.7 26.4 %collective-permute-start.18 = (f32[2,4,192]{2,1,0:T(4,128)S(1)}, f32[2,4,192]{2,1,0:T(4,128)S(1)}, u32[]{:S(2)}, u32[]{:S(2)}) collective-permute-start(f32[2,4,192]{2,1,0:T(4,128)S(1)} %get-tuple-element.26), channel_id=1, source_target_pairs={{0,6},{2,4},{4,2},{6,0},{8,14},{10,12},{12,10},{14,8},{16,22},{18,... | collective-permute-start | bytes 18440 | tf_op jit(solution)/shard_map/ppermute | solution.py:218
  31.2 33.4 %collective-permute-start.14 = (bf16[192,1024]{1,0:T(8,128)(2,1)S(1)}, bf16[192,1024]{1,0:T(8,128)(2,1)S(1)}, u32[]{:S(2)}, u32[]{:S(2)}) collective-permute-start(bf16[192,1024]{1,0:T(8,128)(2,1)S(1)} %collective-permute-done.12.refs_0_.refs_16_), channel_id=1, source_target_pairs={{0,4},{2,6},{4,0},{6,2},{8,12},{10,14},{12,8},{14,10},{16,20},{18,... | collective-permute-start | bytes 1179656 | tf_op jit(solution)/shard_map/ppermute | solution.py:218
  31.7 36.7 %collective-permute-start.13 = (bf16[192,1024]{1,0:T(8,128)(2,1)S(1)}, bf16[192,1024]{1,0:T(8,128)(2,1)S(1)}, u32[]{:S(2)}, u32[]{:S(2)}) collective-permute-start(bf16[192,1024]{1,0:T(8,128)(2,1)S(1)} %collective-permute-done.12.refs_0_.refs_16_), channel_id=1, source_target_pairs={{0,2},{2,0},{4,6},{6,4},{8,10},{10,8},{12,14},{14,12},{16,18},{18,... | collective-permute-start | bytes 1179656 | tf_op jit(solution)/shard_map/ppermute | solution.py:218
  53.2 12.0 %collective-permute-start.9 = (bf16[192,1024]{1,0:T(8,128)(2,1)S(1)}, bf16[192,1024]{1,0:T(8,128)(2,1)S(1)}, u32[]{:S(2)}, u32[]{:S(2)}) collective-permute-start(bf16[192,1024]{1,0:T(8,128)(2,1)S(1)} %collective-permute-done.8.refs_0_.refs_12_), channel_id=1, source_target_pairs={{0,2},{2,0},{4,6},{6,4},{8,10},{10,8},{12,14},{14,12},{16,18},{18,... | collective-permute-start | bytes 1179656 | tf_op jit(solution)/shard_map/ppermute | solution.py:218
  54.6 37.0 %copy-start = (bf16[192,1024]{1,0:T(8,128)(2,1)}, bf16[192,1024]{1,0:T(8,128)(2,1)S(1)}, u32[]{:S(2)}) copy-start(bf16[192,1024]{1,0:T(8,128)(2,1)S(1)} %collective-permute-done.4.refs_0_.refs_8_) | copy-start | bytes 1179652
  54.7 14.3 %collective-permute-start.6 = (bf16[192,1024]{1,0:T(8,128)(2,1)S(1)}, bf16[192,1024]{1,0:T(8,128)(2,1)S(1)}, u32[]{:S(2)}, u32[]{:S(2)}) collective-permute-start(bf16[192,1024]{1,0:T(8,128)(2,1)S(1)} %collective-permute-done.4.refs_0_.refs_8_), channel_id=1, source_target_pairs={{0,4},{2,6},{4,0},{6,2},{8,12},{10,14},{12,8},{14,10},{16,20},{18,... | collective-permute-start | bytes 1179656 | tf_op jit(solution)/shard_map/ppermute | solution.py:218
  55.2 8.9 %collective-permute-start.17 = (f32[2,4,192]{2,1,0:T(4,128)S(1)}, f32[2,4,192]{2,1,0:T(4,128)S(1)}, u32[]{:S(2)}, u32[]{:S(2)}) collective-permute-start(f32[2,4,192]{2,1,0:T(4,128)S(1)} %get-tuple-element.26), channel_id=1, source_target_pairs={{0,4},{2,6},{4,0},{6,2},{8,12},{10,14},{12,8},{14,10},{16,20},{18,... | collective-permute-start | bytes 18440 | tf_op jit(solution)/shard_map/ppermute | solution.py:218
  64.0 3.8 %collective-permute-start.16 = (f32[2,4,192]{2,1,0:T(4,128)S(1)}, f32[2,4,192]{2,1,0:T(4,128)S(1)}, u32[]{:S(2)}, u32[]{:S(2)}) collective-permute-start(f32[2,4,192]{2,1,0:T(4,128)S(1)} %get-tuple-element.26), channel_id=1, source_target_pairs={{0,2},{2,0},{4,6},{6,4},{8,10},{10,8},{12,14},{14,12},{16,18},{18,... | collective-permute-start | bytes 18440 | tf_op jit(solution)/shard_map/ppermute | solution.py:218
  64.6 21.6 %copy-start.3 = (bf16[192,1024]{1,0:T(8,128)(2,1)}, bf16[192,1024]{1,0:T(8,128)(2,1)S(1)}, u32[]{:S(2)}) copy-start(bf16[192,1024]{1,0:T(8,128)(2,1)S(1)} %collective-permute-done.14.refs_2_.refs_18_) | copy-start | bytes 1179652
  64.6 18.2 %collective-permute-start.10 = (bf16[192,1024]{1,0:T(8,128)(2,1)S(1)}, bf16[192,1024]{1,0:T(8,128)(2,1)S(1)}, u32[]{:S(2)}, u32[]{:S(2)}) collective-permute-start(bf16[192,1024]{1,0:T(8,128)(2,1)S(1)} %collective-permute-done.8.refs_0_.refs_12_), channel_id=1, source_target_pairs={{0,4},{2,6},{4,0},{6,2},{8,12},{10,14},{12,8},{14,10},{16,20},{18,... | collective-permute-start | bytes 1179656 | tf_op jit(solution)/shard_map/ppermute | solution.py:218
  65.2 21.1 %copy-start.9 = (bf16[192,1024]{1,0:T(8,128)(2,1)}, bf16[192,1024]{1,0:T(8,128)(2,1)S(1)}, u32[]{:S(2)}) copy-start(bf16[192,1024]{1,0:T(8,128)(2,1)S(1)} %collective-permute-done.9.refs_1_.refs_13_) | copy-start | bytes 1179652
  65.2 12.1 %collective-permute-start.15 = (bf16[192,1024]{1,0:T(8,128)(2,1)S(1)}, bf16[192,1024]{1,0:T(8,128)(2,1)S(1)}, u32[]{:S(2)}, u32[]{:S(2)}) collective-permute-start(bf16[192,1024]{1,0:T(8,128)(2,1)S(1)} %collective-permute-done.14.refs_2_.refs_18_), channel_id=1, source_target_pairs={{0,2},{2,0},{4,6},{6,4},{8,10},{10,8},{12,14},{14,12},{16,18},{18,... | collective-permute-start | bytes 1179656 | tf_op jit(solution)/shard_map/ppermute | solution.py:218
  67.8 15.6 %collective-permute-start.11 = (bf16[192,1024]{1,0:T(8,128)(2,1)S(1)}, bf16[192,1024]{1,0:T(8,128)(2,1)S(1)}, u32[]{:S(2)}, u32[]{:S(2)}) collective-permute-start(bf16[192,1024]{1,0:T(8,128)(2,1)S(1)} %collective-permute-done.9.refs_1_.refs_13_), channel_id=1, source_target_pairs={{0,4},{2,6},{4,0},{6,2},{8,12},{10,14},{12,8},{14,10},{16,20},{18,... | collective-permute-start | bytes 1179656 | tf_op jit(solution)/shard_map/ppermute | solution.py:218
  68.4 14.4 %copy-start.6 = (bf16[192,1024]{1,0:T(8,128)(2,1)}, bf16[192,1024]{1,0:T(8,128)(2,1)S(1)}, u32[]{:S(2)}) copy-start(bf16[192,1024]{1,0:T(8,128)(2,1)S(1)} %collective-permute-done.13.refs_1_.refs_17_) | copy-start | bytes 1179652
  68.4 17.8 %collective-permute-start.5 = (bf16[192,1024]{1,0:T(8,128)(2,1)S(1)}, bf16[192,1024]{1,0:T(8,128)(2,1)S(1)}, u32[]{:S(2)}, u32[]{:S(2)}) collective-permute-start(bf16[192,1024]{1,0:T(8,128)(2,1)S(1)} %collective-permute-done.4.refs_0_.refs_8_), channel_id=1, source_target_pairs={{0,2},{2,0},{4,6},{6,4},{8,10},{10,8},{12,14},{14,12},{16,18},{18,... | collective-permute-start | bytes 1179656 | tf_op jit(solution)/shard_map/ppermute | solution.py:218
  69.0 22.7 %copy-start.12 = (bf16[192,1024]{1,0:T(8,128)(2,1)}, bf16[192,1024]{1,0:T(8,128)(2,1)S(1)}, u32[]{:S(2)}) copy-start(bf16[192,1024]{1,0:T(8,128)(2,1)S(1)} %collective-permute-done.6.refs_2_.refs_10_) | copy-start | bytes 1179652
  69.0 21.1 %collective-permute-start.7 = (bf16[192,1024]{1,0:T(8,128)(2,1)S(1)}, bf16[192,1024]{1,0:T(8,128)(2,1)S(1)}, u32[]{:S(2)}, u32[]{:S(2)}) collective-permute-start(bf16[192,1024]{1,0:T(8,128)(2,1)S(1)} %collective-permute-done.6.refs_2_.refs_10_), channel_id=1, source_target_pairs={{0,2},{2,0},{4,6},{6,4},{8,10},{10,8},{12,14},{14,12},{16,18},{18,... | collective-permute-start | bytes 1179656 | tf_op jit(solution)/shard_map/ppermute | solution.py:218
  77.2 9.0 %copy-start.18 = (bf16[192,1024]{1,0:T(8,128)(2,1)}, bf16[192,1024]{1,0:T(8,128)(2,1)S(1)}, u32[]{:S(2)}) copy-start(bf16[192,1024]{1,0:T(8,128)(2,1)S(1)} %collective-permute-done.15.refs_3_.refs_19_) | copy-start | bytes 1179652
  80.4 14.4 %collective-permute-start.27 = (f32[2,4,192]{2,1,0:T(4,128)S(1)}, f32[2,4,192]{2,1,0:T(4,128)S(1)}, u32[]{:S(2)}, u32[]{:S(2)}) collective-permute-start(f32[2,4,192]{2,1,0:T(4,128)S(1)} %get-tuple-element.29), channel_id=1, source_target_pairs={{0,6},{2,4},{4,2},{6,0},{8,14},{10,12},{12,10},{14,8},{16,22},{18,... | collective-permute-start | bytes 18440 | tf_op jit(solution)/shard_map/ppermute | solution.py:218
  82.8 7.3 %copy-start.15 = (bf16[192,1024]{1,0:T(8,128)(2,1)}, bf16[192,1024]{1,0:T(8,128)(2,1)S(1)}, u32[]{:S(2)}) copy-start(bf16[192,1024]{1,0:T(8,128)(2,1)S(1)} %collective-permute-done.10.refs_2_.refs_14_) | copy-start | bytes 1179652
  82.8 14.0 %collective-permute-start.26 = (f32[2,4,192]{2,1,0:T(4,128)S(1)}, f32[2,4,192]{2,1,0:T(4,128)S(1)}, u32[]{:S(2)}, u32[]{:S(2)}) collective-permute-start(f32[2,4,192]{2,1,0:T(4,128)S(1)} %get-tuple-element.29), channel_id=1, source_target_pairs={{0,4},{2,6},{4,0},{6,2},{8,12},{10,14},{12,8},{14,10},{16,20},{18,... | collective-permute-start | bytes 18440 | tf_op jit(solution)/shard_map/ppermute | solution.py:218
  83.4 10.5 %copy-start.21 = (bf16[192,1024]{1,0:T(8,128)(2,1)}, bf16[192,1024]{1,0:T(8,128)(2,1)S(1)}, u32[]{:S(2)}) copy-start(bf16[192,1024]{1,0:T(8,128)(2,1)S(1)} %collective-permute-done.11.refs_3_.refs_15_) | copy-start | bytes 1179652
  83.4 12.9 %collective-permute-start.25 = (f32[2,4,192]{2,1,0:T(4,128)S(1)}, f32[2,4,192]{2,1,0:T(4,128)S(1)}, u32[]{:S(2)}, u32[]{:S(2)}) collective-permute-start(f32[2,4,192]{2,1,0:T(4,128)S(1)} %get-tuple-element.29), channel_id=1, source_target_pairs={{0,2},{2,0},{4,6},{6,4},{8,10},{10,8},{12,14},{14,12},{16,18},{18,... | collective-permute-start | bytes 18440 | tf_op jit(solution)/shard_map/ppermute | solution.py:218
  86.2 14.0 %copy-start.34 = (f32[256,768]{1,0:T(8,128)}, f32[256,768]{1,0:T(8,128)S(1)}, u32[]{:S(2)}) copy-start(f32[256,768]{1,0:T(8,128)S(1)} %get-tuple-element.32.refs_2_) | copy-start | bytes 2359300
  86.3 13.9 %copy-start.24 = (bf16[192,1024]{1,0:T(8,128)(2,1)}, bf16[192,1024]{1,0:T(8,128)(2,1)S(1)}, u32[]{:S(2)}) copy-start(bf16[192,1024]{1,0:T(8,128)(2,1)S(1)} %collective-permute-done.5.refs_1_.refs_9_) | copy-start | bytes 1179652
  86.3 12.2 %collective-permute-start.24 = (f32[2,4,192]{2,1,0:T(4,128)S(1)}, f32[2,4,192]{2,1,0:T(4,128)S(1)}, u32[]{:S(2)}, u32[]{:S(2)}) collective-permute-start(f32[2,4,192]{2,1,0:T(4,128)S(1)} %get-tuple-element.28), channel_id=1, source_target_pairs={{0,6},{2,4},{4,2},{6,0},{8,14},{10,12},{12,10},{14,8},{16,22},{18,... | collective-permute-start | bytes 18440 | tf_op jit(solution)/shard_map/ppermute | solution.py:218
  90.1 10.1 %copy-start.27 = (bf16[192,1024]{1,0:T(8,128)(2,1)}, bf16[192,1024]{1,0:T(8,128)(2,1)S(1)}, u32[]{:S(2)}) copy-start(bf16[192,1024]{1,0:T(8,128)(2,1)S(1)} %collective-permute-done.7.refs_3_.refs_11_) | copy-start | bytes 1179652
  90.1 10.0 %collective-permute-start.23 = (f32[2,4,192]{2,1,0:T(4,128)S(1)}, f32[2,4,192]{2,1,0:T(4,128)S(1)}, u32[]{:S(2)}, u32[]{:S(2)}) collective-permute-start(f32[2,4,192]{2,1,0:T(4,128)S(1)} %get-tuple-element.28), channel_id=1, source_target_pairs={{0,4},{2,6},{4,0},{6,2},{8,12},{10,14},{12,8},{14,10},{16,20},{18,... | collective-permute-start | bytes 18440 | tf_op jit(solution)/shard_map/ppermute | solution.py:218
  94.8 5.3 %collective-permute-start.22 = (f32[2,4,192]{2,1,0:T(4,128)S(1)}, f32[2,4,192]{2,1,0:T(4,128)S(1)}, u32[]{:S(2)}, u32[]{:S(2)}) collective-permute-start(f32[2,4,192]{2,1,0:T(4,128)S(1)} %get-tuple-element.28), channel_id=1, source_target_pairs={{0,2},{2,0},{4,6},{6,4},{8,10},{10,8},{12,14},{14,12},{16,18},{18,... | collective-permute-start | bytes 18440 | tf_op jit(solution)/shard_map/ppermute | solution.py:218
  96.3 4.6 %collective-permute-start.21 = (f32[2,4,192]{2,1,0:T(4,128)S(1)}, f32[2,4,192]{2,1,0:T(4,128)S(1)}, u32[]{:S(2)}, u32[]{:S(2)}) collective-permute-start(f32[2,4,192]{2,1,0:T(4,128)S(1)} %get-tuple-element.27), channel_id=1, source_target_pairs={{0,6},{2,4},{4,2},{6,0},{8,14},{10,12},{12,10},{14,8},{16,22},{18,... | collective-permute-start | bytes 18440 | tf_op jit(solution)/shard_map/ppermute | solution.py:218
  96.9 5.4 %collective-permute-start.20 = (f32[2,4,192]{2,1,0:T(4,128)S(1)}, f32[2,4,192]{2,1,0:T(4,128)S(1)}, u32[]{:S(2)}, u32[]{:S(2)}) collective-permute-start(f32[2,4,192]{2,1,0:T(4,128)S(1)} %get-tuple-element.27), channel_id=1, source_target_pairs={{0,4},{2,6},{4,0},{6,2},{8,12},{10,14},{12,8},{14,10},{16,20},{18,... | collective-permute-start | bytes 18440 | tf_op jit(solution)/shard_map/ppermute | solution.py:218
  98.5 3.7 %collective-permute-start.19 = (f32[2,4,192]{2,1,0:T(4,128)S(1)}, f32[2,4,192]{2,1,0:T(4,128)S(1)}, u32[]{:S(2)}, u32[]{:S(2)}) collective-permute-start(f32[2,4,192]{2,1,0:T(4,128)S(1)} %get-tuple-element.27), channel_id=1, source_target_pairs={{0,2},{2,0},{4,6},{6,4},{8,10},{10,8},{12,14},{14,12},{16,18},{18,... | collective-permute-start | bytes 18440 | tf_op jit(solution)/shard_map/ppermute | solution.py:218
  102.4 6.4 %collective-permute-start.28 = (f32[4,2,4,192]{3,2,0,1:T(4,128)S(1)}, f32[4,2,4,192]{3,2,0,1:T(4,128)S(1)}, u32[]{:S(2)}, u32[]{:S(2)}) collective-permute-start(f32[4,2,4,192]{3,2,0,1:T(4,128)S(1)} %copy.4), channel_id=1, source_target_pairs={{0,8},{2,10},{4,12},{6,14},{8,16},{10,18},{12,20},{14,22},{16,24},... | collective-permute-start | bytes 73736 | tf_op jit(solution)/shard_map/ppermute | solution.py:215
  104.9 4.4 %collective-permute-start.30 = (f32[4,2,4,192]{3,2,0,1:T(4,128)S(1)}, f32[4,2,4,192]{3,2,0,1:T(4,128)S(1)}, u32[]{:S(2)}, u32[]{:S(2)}) collective-permute-start(f32[4,2,4,192]{3,2,0,1:T(4,128)S(1)} %copy.4), channel_id=1, source_target_pairs={{0,24},{2,26},{4,28},{6,30},{8,0},{10,2},{12,4},{14,6},{16,8},{18,... | collective-permute-start | bytes 73736 | tf_op jit(solution)/shard_map/ppermute | solution.py:215
  106.3 4.8 %collective-permute-start.29 = (f32[4,2,4,192]{3,2,0,1:T(4,128)S(1)}, f32[4,2,4,192]{3,2,0,1:T(4,128)S(1)}, u32[]{:S(2)}, u32[]{:S(2)}) collective-permute-start(f32[4,2,4,192]{3,2,0,1:T(4,128)S(1)} %copy.4), channel_id=1, source_target_pairs={{0,16},{2,18},{4,20},{6,22},{8,24},{10,26},{12,28},{14,30},{16,0},... | collective-permute-start | bytes 73736 | tf_op jit(solution)/shard_map/ppermute | solution.py:215
  111.2 1.0 copy-start.1
  121.2 1.1 copy-start.31
  122.3 1.1 copy-start.33
  123.5 1.1 copy-start.35
  124.6 1.1 copy-start.37
  131.1 2.9 %collective-permute-start.31 = (f32[256,1152]{1,0:T(8,128)S(1)}, f32[256,1152]{1,0:T(8,128)S(1)}, u32[]{:S(2)}, u32[]{:S(2)}) collective-permute-start(f32[256,1152]{1,0:T(8,128)S(1)} %sums_pass.1), channel_id=1, source_target_pairs={{0,1},{1,0},{2,3},{3,2},{4,5},{5,4},{6,7},{7,6},{8,9},{9,8},{10,11... | collective-permute-start | bytes 3538952 | tf_op jit(solution)/shard_map/ppermute | solution.py:221
  134.1 1.1 copy-start.2
  134.1 1.2 copy-start.5
  134.1 1.3 copy-start.8
  134.1 1.4 copy-start.11
  134.1 1.5 copy-start.14
  134.1 1.6 %copy-start.17 = (bf16[192,1024]{1,0:T(8,128)(2,1)S(1)}, bf16[192,1024]{1,0:T(8,128)(2,1)}, u32[]{:S(2)}) copy-start(bf16[192,1024]{1,0:T(8,128)(2,1)} %copy-done.15) | copy-start | bytes 1179652
  134.1 1.7 %copy-start.20 = (bf16[192,1024]{1,0:T(8,128)(2,1)S(1)}, bf16[192,1024]{1,0:T(8,128)(2,1)}, u32[]{:S(2)}) copy-start(bf16[192,1024]{1,0:T(8,128)(2,1)} %copy-done.18) | copy-start | bytes 1179652
  134.1 1.8 %copy-start.23 = (bf16[192,1024]{1,0:T(8,128)(2,1)S(1)}, bf16[192,1024]{1,0:T(8,128)(2,1)}, u32[]{:S(2)}) copy-start(bf16[192,1024]{1,0:T(8,128)(2,1)} %copy-done.21) | copy-start | bytes 1179652
  134.1 1.9 %copy-start.26 = (bf16[192,1024]{1,0:T(8,128)(2,1)S(1)}, bf16[192,1024]{1,0:T(8,128)(2,1)}, u32[]{:S(2)}) copy-start(bf16[192,1024]{1,0:T(8,128)(2,1)} %copy-done.24) | copy-start | bytes 1179652
  144.8 5.5 %collective-permute-start.34 = (f32[3,4,192]{2,1,0:T(4,128)S(1)}, f32[3,4,192]{2,1,0:T(4,128)S(1)}, u32[]{:S(2)}, u32[]{:S(2)}) collective-permute-start(f32[3,4,192]{2,1,0:T(4,128)S(1)} %get-tuple-element.155), channel_id=1, source_target_pairs={{0,8},{2,10},{4,12},{6,14},{8,16},{10,18},{12,20},{14,22},{16,24},... | collective-permute-start | bytes 27656 | tf_op jit(solution)/shard_map/ppermute | solution.py:215
  146.0 4.6 %collective-permute-start.33 = (f32[3,4,192]{2,1,0:T(4,128)S(1)}, f32[3,4,192]{2,1,0:T(4,128)S(1)}, u32[]{:S(2)}, u32[]{:S(2)}) collective-permute-start(f32[3,4,192]{2,1,0:T(4,128)S(1)} %get-tuple-element.156), channel_id=1, source_target_pairs={{0,16},{2,18},{4,20},{6,22},{8,24},{10,26},{12,28},{14,30},{16,0},... | collective-permute-start | bytes 27656 | tf_op jit(solution)/shard_map/ppermute | solution.py:215
  147.7 4.1 %collective-permute-start.32 = (f32[3,4,192]{2,1,0:T(4,128)S(1)}, f32[3,4,192]{2,1,0:T(4,128)S(1)}, u32[]{:S(2)}, u32[]{:S(2)}) collective-permute-start(f32[3,4,192]{2,1,0:T(4,128)S(1)} %get-tuple-element.157), channel_id=1, source_target_pairs={{0,24},{2,26},{4,28},{6,30},{8,0},{10,2},{12,4},{14,6},{16,8},{18,... | collective-permute-start | bytes 27656 | tf_op jit(solution)/shard_map/ppermute | solution.py:215
  151.9 3.7 %collective-permute-start.35 = (f32[3,192]{1,0:T(4,128)S(1)}, f32[3,192]{1,0:T(4,128)S(1)}, u32[]{:S(2)}, u32[]{:S(2)}) collective-permute-start(f32[3,192]{1,0:T(4,128)S(1)} %bitcast.460), channel_id=1, source_target_pairs={{0,2},{2,0},{4,6},{6,4},{8,10},{10,8},{12,14},{14,12},{16,18},{18,... | collective-permute-start | bytes 6920 | tf_op jit(solution)/shard_map/ppermute | solution.py:218
  152.6 3.7 %collective-permute-start.36 = (f32[3,192]{1,0:T(4,128)S(1)}, f32[3,192]{1,0:T(4,128)S(1)}, u32[]{:S(2)}, u32[]{:S(2)}) collective-permute-start(f32[3,192]{1,0:T(4,128)S(1)} %bitcast.461), channel_id=1, source_target_pairs={{0,4},{2,6},{4,0},{6,2},{8,12},{10,14},{12,8},{14,10},{16,20},{18,... | collective-permute-start | bytes 6920 | tf_op jit(solution)/shard_map/ppermute | solution.py:218
  153.2 4.5 %collective-permute-start.37 = (f32[3,192]{1,0:T(4,128)S(1)}, f32[3,192]{1,0:T(4,128)S(1)}, u32[]{:S(2)}, u32[]{:S(2)}) collective-permute-start(f32[3,192]{1,0:T(4,128)S(1)} %bitcast.459), channel_id=1, source_target_pairs={{0,6},{2,4},{4,2},{6,0},{8,14},{10,12},{12,10},{14,8},{16,22},{18,... | collective-permute-start | bytes 6920 | tf_op jit(solution)/shard_map/ppermute | solution.py:218
  (13 other events, 12.6 us)

commit v2 on v0

v2 whole, which is shorter than its diff:
```python
import functools

import jax
import jax.numpy as jnp
from jax import lax
from jax.experimental import pallas as pl
from jax.experimental.pallas import tpu as pltpu
from jax.sharding import PartitionSpec as P

softness_level = 32.0
prior_mass = 4.0
CUBE = 8
GROUPS = ((0, 1, 2, 4), (3, 5), (6, 7))
VMEM = pl.BlockSpec(memory_space=pltpu.VMEM)
GRANT = 20 << 20


def params():
    return pltpu.CompilerParams(vmem_limit_bytes=GRANT)


def row_squares(rows):
    wide = rows.astype(jnp.float32)
    square = wide * wide
    part = square[:, :128]
    for j in range(128, square.shape[1], 128):
        part = part + square[:, j : j + 128]
    return jnp.sum(part.T, axis=0, keepdims=True)


def centroid_squares(piece):
    wide = piece.astype(jnp.float32)
    return jnp.sum(wide * wide, axis=1, keepdims=True)


def scores(piece, cent_sq, rows, row_sq):
    inner = lax.dot_general(piece, rows, (((1,), (1,)), ((), ())), preferred_element_type=jnp.float32)
    return -(row_sq - 2.0 * inner + cent_sq) * (0.5 / softness_level)


def first_kernel(n, shard, cents, *refs):
    chunks = refs[:n]
    weight_ref, stats_ref, row_sq_ref, rows_ref = refs[n:]
    for i in range(n):
        rows_ref[i * shard : (i + 1) * shard, :] = chunks[i][...]
    piece = cents[...]
    cent_sq = centroid_squares(piece)
    tile = 2 * shard
    for j in range(n // 2):
        span = slice(j * tile, (j + 1) * tile)
        rows = rows_ref[span, :]
        row_sq = row_squares(rows)
        score = scores(piece, cent_sq, rows, row_sq)
        top = jnp.max(score, axis=0, keepdims=True)
        weight = jnp.exp(score - top)
        total = jnp.sum(weight, axis=0, keepdims=True)
        weight_ref[:, span] = weight
        row_sq_ref[:, span] = row_sq
        for i in range(2):
            stats_ref[0, 2 * j + i : 2 * j + i + 1, :] = top[:, i * shard : (i + 1) * shard]
            stats_ref[1, 2 * j + i : 2 * j + i + 1, :] = total[:, i * shard : (i + 1) * shard]


def first_pass(cents, chunks):
    n = len(chunks)
    shard, width = chunks[0].shape
    n_k = cents.shape[0]
    n_rows = n * shard
    return pl.pallas_call(
        functools.partial(first_kernel, n, shard),
        out_shape=(
            jax.ShapeDtypeStruct((n_k, n_rows), jnp.float32),
            jax.ShapeDtypeStruct((2, n, shard), jnp.float32),
            jax.ShapeDtypeStruct((1, n_rows), jnp.float32),
            jax.ShapeDtypeStruct((n_rows, width), jnp.bfloat16),
        ),
        in_specs=[VMEM] * (1 + n),
        out_specs=(VMEM,) * 4,
        compiler_params=params(),
        cost_estimate=pl.CostEstimate(
            flops=2 * n_k * n_rows * width, bytes_accessed=2 * n_rows * width, transcendentals=n_k * n_rows
        ),
        name="first_pass",
    )(cents, *chunks)


def sums_kernel(first, last, n, *refs):
    scales, weights, rows = refs[:n], refs[n : 2 * n], refs[2 * n : 3 * n]
    out_ref = refs[3 * n]
    width = rows[0].shape[1]
    counts = 0.0
    for s in range(n):
        resp = (weights[s][first:last, :] * scales[s][...]).astype(jnp.bfloat16)
        counts = counts + jnp.sum(resp.astype(jnp.float32), axis=1, keepdims=True)
        part = jnp.dot(resp, rows[s][...], preferred_element_type=jnp.float32)
        if s:
            part = part + out_ref[:, :width]
        out_ref[:, :width] = part
    out_ref[:, width:] = jnp.broadcast_to(counts, (last - first, 128))


def sums_pass(scales, weights, rows, first, last):
    n = len(rows)
    width = rows[0].shape[1]
    n_rows = sum(r.shape[0] for r in rows)
    return pl.pallas_call(
        functools.partial(sums_kernel, first, last, n),
        out_shape=jax.ShapeDtypeStruct((last - first, width + 128), jnp.float32),
        in_specs=[VMEM] * (3 * n),
        out_specs=VMEM,
        compiler_params=params(),
        cost_estimate=pl.CostEstimate(
            flops=2 * (last - first) * n_rows * width, bytes_accessed=2 * n_rows * width, transcendentals=0
        ),
        name="sums_pass",
    )(*scales, *weights, *rows)


def second_kernel(shard, n, cents, *refs):
    row_sqs, rows, stats = refs[:n], refs[n : 2 * n], refs[2 * n :]
    piece = cents[...]
    cent_sq = centroid_squares(piece)
    tile = 2 * shard
    for s in range(n):
        for j in range(rows[s].shape[0] // tile):
            span = slice(j * tile, (j + 1) * tile)
            score = scores(piece, cent_sq, rows[s][span, :], row_sqs[s][:, span])
            top = jnp.max(score, axis=0, keepdims=True)
            shifted = score - top
            weight = jnp.exp(shifted)
            total = jnp.sum(weight, axis=0, keepdims=True)
            spread = jnp.sum(weight * shifted, axis=0, keepdims=True)
            for i in range(2):
                part = slice(i * shard, (i + 1) * shard)
                at = slice(2 * j + i, 2 * j + i + 1)
                stats[s][0, at, :] = top[:, part]
                stats[s][1, at, :] = total[:, part]
                stats[s][2, at, :] = spread[:, part]


def second_pass(cents, row_sqs, rows, shard):
    n = len(rows)
    n_k, width = cents.shape
    n_rows = sum(r.shape[0] for r in rows)
    return pl.pallas_call(
        functools.partial(second_kernel, shard, n),
        out_shape=tuple(jax.ShapeDtypeStruct((3, r.shape[0] // shard, shard), jnp.float32) for r in rows),
        in_specs=[VMEM] * (1 + 2 * n),
        out_specs=(VMEM,) * n,
        compiler_params=params(),
        cost_estimate=pl.CostEstimate(
            flops=2 * n_k * n_rows * width, bytes_accessed=2 * n_rows * width, transcendentals=n_k * n_rows
        ),
        name="second_pass",
    )(cents, *row_sqs, *rows)


def merge(a, b):
    top = jnp.maximum(a[0], b[0])
    drops = (a[0] - top, b[0] - top)
    factors = (jnp.exp(drops[0]), jnp.exp(drops[1]))
    out = [top, factors[0] * a[1] + factors[1] * b[1]]
    if a.shape[0] == 3:
        out.append(factors[0] * (a[2] + drops[0] * a[1]) + factors[1] * (b[2] + drops[1] * b[1]))
    return jnp.stack(out)


def by_chunk(groups):
    place = {b: (g, i) for g, bits in enumerate(GROUPS) for i, b in enumerate(bits)}
    return jnp.stack([groups[place[b][0]][:, place[b][1]] for b in range(CUBE)], axis=1)


def solution(mesh):
    n_dp = mesh.shape["dp"]
    n_cent = mesh.shape["cent"]
    top_bit = n_dp // 2

    def flip(value, bits):
        return lax.ppermute(value, "dp", [(i, i ^ bits) for i in range(n_dp)])

    def across(value, bits):
        return lax.ppermute(value, "cent", [(i, i ^ bits) for i in range(n_cent)])

    def gather_cent(value):
        bits = 1
        while bits < n_cent:
            value = jnp.concatenate([value, across(value, bits)], axis=0)
            bits *= 2
        return value

    def scatter_cent(value):
        bits = n_cent // 2
        while bits:
            half = value.shape[0] // 2
            value = value[:half] + across(value[half:], bits)
            bits //= 2
        return value

    def gather_near(value):
        bits = CUBE
        while bits < top_bit:
            value = jnp.concatenate([value, flip(value, bits)], axis=0)
            bits *= 2
        return value

    def scatter_near(value):
        bits = top_bit // 2
        while bits >= CUBE:
            half = value.shape[0] // 2
            value = value[:half] + flip(value[half:], bits)
            bits //= 2
        return value

    def on_device(embeddings, centroids):
        shard, width = embeddings.shape
        half = shard // 2
        chunk = {0: embeddings.astype(jnp.bfloat16)}
        for bit in (1, 2, 4):
            chunk[bit] = flip(chunk[0], bit)
        chunk[3] = flip(chunk[1], 2)
        chunk[6] = flip(chunk[2], 4)
        chunk[5] = flip(chunk[4], 1)
        chunk[7] = jnp.concatenate([flip(chunk[6][:half], 1), flip(chunk[5][half:], 2)], axis=0)

        near_own = gather_near(centroids.astype(jnp.bfloat16))
        far_own = flip(near_own, top_bit)
        piece = jnp.concatenate([gather_cent(near_own), gather_cent(far_own)], axis=0)
        n_near = piece.shape[0] // 2

        weights, local, row_sqs, rows = [], [], [], []
        for bits in GROUPS:
            weight, stats, row_sq, held = first_pass(piece, [chunk[b] for b in bits])
            weights.append(weight)
            local.append(stats)
            row_sqs.append(row_sq)
            rows.append(held)

        stats = by_chunk(local)
        for bit in (1, 2, 4):
            other = flip(stats, bit)
            stats = merge(stats, jnp.stack([other[:, b ^ bit] for b in range(CUBE)], axis=1))
        scales = []
        for g, bits in enumerate(GROUPS):
            scale = [jnp.exp(local[g][0, i] - stats[0, b]) / stats[1, b] for i, b in enumerate(bits)]
            scales.append(jnp.concatenate(scale)[None, :])

        far = scatter_cent(sums_pass(scales, weights, rows, n_near, 2 * n_near))
        count = far[:, width:]
        coarse = lax.reduce_precision(count, 8, 7)
        lane = lax.broadcasted_iota(jnp.int32, count.shape, 1)
        far = jnp.concatenate([far[:, :width], jnp.where(lane < 64, coarse, count - coarse)], axis=1)
        far = flip(far.astype(jnp.bfloat16), top_bit).astype(jnp.float32)
        near = scatter_cent(sums_pass(scales, weights, rows, 0, n_near))
        counts = near[:, width : width + 1] + (far[:, width : width + 1] + far[:, width + 64 : width + 65])
        sums = scatter_near(jnp.concatenate([near[:, :width] + far[:, :width], jnp.broadcast_to(counts, count.shape)], axis=1))
        updated = (sums[:, :width] + prior_mass * centroids) / (sums[:, width : width + 1] + prior_mass)

        near_own = gather_near(updated.astype(jnp.bfloat16))
        far_own = flip(near_own, top_bit)
        near = second_pass(gather_cent(near_own), row_sqs, rows, shard)
        far = second_pass(gather_cent(far_own), row_sqs, rows, shard)
        stats = merge(by_chunk(near), by_chunk(far))
        for bit in (4, 2, 1):
            stats = merge(stats[:, :bit], flip(stats[:, bit:], bit))
        entropy = (jnp.log(stats[1]) - stats[2] / stats[1]).reshape(shard)
        return (updated, entropy)

    in_specs = (P(("dp", "cent"), None), P(("dp", "cent"), None))
    out_specs = (P(("dp", "cent"), None), P(("dp", "cent")))
    return jax.shard_map(
        on_device, mesh=mesh, in_specs=in_specs, out_specs=out_specs, check_vma=False
    )
```

time: 432 us -> 112 us (0.26)
  waiting for transfers between devices: 328 us -> 65.7 us
  blocking collectives: 54.4 us -> 0 us
  starting transfers between devices: 0.08 us -> 21.8 us
  matrix products: 13.2 us -> 0 us
  between operations: 14.1 us -> 1 us
  other arithmetic: 16.5 us -> 5.74 us
  Pallas kernels: 0 us -> 9.19 us
    psum x1 -> x0, waiting for transfers between devices: 214 us -> none  [on_device(): sums, counts = lax.psum((sums, counts), 'dp')]
    all_gather x1 -> x0, waiting for transfers between devices: 114 us -> none  [on_device(): previous = lax.all_gather(centroids, 'dp', axis=0, tiled=True)]
    ppermute x0 -> x23, waiting for transfers between devices: none -> 65.7 us  [the longest x17 63.8 us: flip(): return lax.ppermute(value, 'dp', [(i, i ^ bits) for i in range(n_dp)])]
    psum x3 -> x0, blocking collectives: 47.1 us -> none  [the longest x1 42.2 us: on_device(): sums, counts = lax.psum((sums, counts), 'dp')]
    ppermute x0 -> x23, starting transfers between devices: none -> 21.8 us  [the longest x17 21.5 us: flip(): return lax.ppermute(value, 'dp', [(i, i ^ bits) for i in range(n_dp)])]
    dot_general x3 -> x0, matrix products: 13.2 us -> none  [the longest x2 7.6 us: score_piece(): jnp.einsum('rd,kd->rk', rows_b, piece, preferred_element_type=jnp.float32)]
    dot_general x3 -> x0, other arithmetic: 11.1 us -> none  [the longest x2 10.8 us: score_piece(): jnp.einsum('kd,kd->k', piece, piece, preferred_element_type=jnp.float32)]
    pallas_call x0 -> x7, Pallas kernels: none -> 9.19 us  [the longest x3 3.77 us: first_pass(): pl.pallas_call(functools.partial(first_kernel, n, shard), out_shape=(jax....]
  transfers between devices with their start and end apart: 2 -> 23, of which waited for: 2 -> 14; matrix products, arithmetic and copies ran while one was open for 0% -> 1% of each run, Pallas kernels for 0% -> 5%
where the time goes in v2:
time: 112 us; the launch traced here: 111 us
  waiting for transfers between devices  65.7 us (59%)
  starting transfers between devices  21.8 us (19%)
  Pallas kernels  9.19 us (8%)
  local copies, waits for them, and re-layouts  7.99 us (7%)
  other arithmetic  5.74 us (5%)
    ppermute x17, waiting for transfers between devices, flip(): return lax.ppermute(value, 'dp', [(i, i ^ bits) for i in range(n_dp)])  63.8 us
    ppermute x17, starting transfers between devices, flip(): return lax.ppermute(value, 'dp', [(i, i ^ bits) for i in range(n_dp)])  21.5 us
    unnamed x16, local copies, waits for them, and re-layouts  7.62 us
    pallas_call x3, Pallas kernels, first_pass(): pl.pallas_call(functools.partial(first_kernel, n, shard), out_shape=(jax....  3.77 us
    pallas_call x2, Pallas kernels, second_pass(): pl.pallas_call(functools.partial(second_kernel, shard, n), out_shape=tupl...  3.18 us
  transfers between devices with their start and end apart: 23, of which 14 were waited for; matrix products, arithmetic and copies ran while one was open for 1% of the time, Pallas kernels for 5%

profile of v2, /device:TPU:0, one launch (start us, length us, event | category | flops | bytes accessed | tf_op | source)
XLA Modules:
  0.0 111.4 jit_solution(11977272222523120211)
XLA Ops:
  0.6 1.2 %convert_element_type.14.refs_0_ = bf16[192,1024]{1,0:T(8,128)(2,1)S(1)} convert(f32[192,1024]{1,0:T(8,128)} %param.2) | non-fusion elementwise | flops 196608 | bytes 1179648 | tf_op jit(solution)/shard_map/convert_element_type | solution.py:217
  1.8 3.1 %collective-permute-start.5 = (bf16[192,1024]{1,0:T(8,128)(2,1)S(1)}, bf16[192,1024]{1,0:T(8,128)(2,1)S(1)}, u32[]{:S(2)}, u32[]{:S(2)}) collective-permute-start(bf16[192,1024]{1,0:T(8,128)(2,1)S(1)} %convert_element_type.14.refs_0_), channel_id=1, source_target_pairs={{0,8},{2,10},{4,12},{6,14},{8,0},{10,2},{12,4},{14,6},{16,24},{18,... | collective-permute-start | bytes 1179656 | tf_op jit(solution)/shard_map/ppermute | solution.py:179
  4.9 1.5 %collective-permute-start.4 = (bf16[192,1024]{1,0:T(8,128)(2,1)S(1)}, bf16[192,1024]{1,0:T(8,128)(2,1)S(1)}, u32[]{:S(2)}, u32[]{:S(2)}) collective-permute-start(bf16[192,1024]{1,0:T(8,128)(2,1)S(1)} %convert_element_type.14.refs_0_), channel_id=1, source_target_pairs={{0,4},{2,6},{4,0},{6,2},{8,12},{10,14},{12,8},{14,10},{16,20},{18,... | collective-permute-start | bytes 1179656 | tf_op jit(solution)/shard_map/ppermute | solution.py:179
  6.4 1.5 %collective-permute-start.3 = (bf16[192,1024]{1,0:T(8,128)(2,1)S(1)}, bf16[192,1024]{1,0:T(8,128)(2,1)S(1)}, u32[]{:S(2)}, u32[]{:S(2)}) collective-permute-start(bf16[192,1024]{1,0:T(8,128)(2,1)S(1)} %convert_element_type.14.refs_0_), channel_id=1, source_target_pairs={{0,2},{2,0},{4,6},{6,4},{8,10},{10,8},{12,14},{14,12},{16,18},{18,... | collective-permute-start | bytes 1179656 | tf_op jit(solution)/shard_map/ppermute | solution.py:179
  7.9 1.1 convert_element_type.13
  9.0 2.7 %collective-permute-start.1 = (bf16[128,1024]{1,0:T(8,128)(2,1)S(1)}, bf16[128,1024]{1,0:T(8,128)(2,1)S(1)}, u32[]{:S(2)}, u32[]{:S(2)}) collective-permute-start(bf16[128,1024]{1,0:T(8,128)(2,1)S(1)} %convert_element_type.13), channel_id=1, source_target_pairs={{0,16},{2,18},{4,20},{6,22},{8,24},{10,26},{12,28},{14,30},{16,0},... | collective-permute-start | bytes 786440 | tf_op jit(solution)/shard_map/ppermute | solution.py:179
  11.6 0.0 collective-permute-start
  11.7 11.2 %collective-permute-done.1 = bf16[128,1024]{1,0:T(8,128)(2,1)S(1)} collective-permute-done((bf16[128,1024]{1,0:T(8,128)(2,1)S(1)}, bf16[128,1024]{1,0:T(8,128)(2,1)S(1)}, u32[]{:S(2)}, u32[]{:S(2)}) %collective-permute-start.1) | collective-permute-done | bytes 262176 | tf_op jit(solution)/shard_map/ppermute | solution.py:179
  22.8 0.0 collective-permute-start.2
  22.8 0.0 collective-permute-done.4.refs_2_
  22.9 1.1 collective-permute-start.8
  23.9 1.5 %collective-permute-start.6 = (bf16[192,1024]{1,0:T(8,128)(2,1)S(1)}, bf16[192,1024]{1,0:T(8,128)(2,1)S(1)}, u32[]{:S(2)}, u32[]{:S(2)}) collective-permute-start(bf16[192,1024]{1,0:T(8,128)(2,1)S(1)} %collective-permute-done.3.refs_1_), channel_id=1, source_target_pairs={{0,4},{2,6},{4,0},{6,2},{8,12},{10,14},{12,8},{14,10},{16,20},{18,... | collective-permute-start | bytes 1179656 | tf_op jit(solution)/shard_map/ppermute | solution.py:179
  25.4 0.1 pad_maximum_fusion.cents
  25.5 1.7 %first_pass.3 = (f32[512,768]{1,0:T(8,128)S(1)}, f32[2,4,192]{2,1,0:T(4,128)S(1)}, f32[1,768]{1,0:T(1,128)S(1)}, bf16[768,1024]{1,0:T(8,128)(2,1)S(1)}) custom-call(bf16[512,1024]{1,0:T(8,128)(2,1)S(1)} %pad_maximum_fusion.cents, bf16[192,1024]{1,0:T(8,128)(2,1)S(1)} %convert_element_type.14.refs_0_, bf16[192,1024]{1,0:T(8,128)(2,1)S(1)} %collective-permute-done.3.refs_1_, ...), custom_call_target="tpu_custom_call" | custom-call | flops 805306368 | bytes 1572864 | tf_op jit(solution)/shard_map/first_pass/pallas_call | solution.py:69
  27.2 1.2 %copy-done = f32[512,768]{1,0:T(8,128)} copy-done((f32[512,768]{1,0:T(8,128)}, f32[512,768]{1,0:T(8,128)S(1)}, u32[]{:S(2)}) %copy-start) | copy-done | bytes 1572888
  28.4 5.9 %collective-permute-done.7.refs_1_ = bf16[192,1024]{1,0:T(8,128)(2,1)S(1)} collective-permute-done((bf16[192,1024]{1,0:T(8,128)(2,1)S(1)}, bf16[192,1024]{1,0:T(8,128)(2,1)S(1)}, u32[]{:S(2)}, u32[]{:S(2)}) %collective-permute-start.7) | collective-permute-done | bytes 393248 | tf_op jit(solution)/shard_map/ppermute | solution.py:179
  34.4 0.1 collective-permute-start.10
  34.5 1.7 %collective-permute-start.9 = (bf16[96,1024]{1,0:T(8,128)(2,1)S(1)}, bf16[96,1024]{1,0:T(8,128)(2,1)S(1)}, u32[]{:S(2)}, u32[]{:S(2)}) collective-permute-start(bf16[96,1024]{1,0:T(8,128)(2,1)S(1)} %slice.469), channel_id=1, source_target_pairs={{0,2},{2,0},{4,6},{6,4},{8,10},{10,8},{12,14},{14,12},{16,18},{18,... | collective-permute-start | bytes 589832 | tf_op jit(solution)/shard_map/ppermute | solution.py:179
  36.2 1.0 first_pass.4
  37.2 0.9 copy-done.2
  38.1 2.9 %collective-permute-done.10 = bf16[96,1024]{1,0:T(8,128)(2,1)S(1)} collective-permute-done((bf16[96,1024]{1,0:T(8,128)(2,1)S(1)}, bf16[96,1024]{1,0:T(8,128)(2,1)S(1)}, u32[]{:S(2)}, u32[]{:S(2)}) %collective-permute-start.10) | collective-permute-done | bytes 196640 | tf_op jit(solution)/shard_map/ppermute | solution.py:179
  41.0 0.1 collective-permute-done.9
  41.1 1.0 first_pass.5
  42.1 0.9 copy-done.4
  43.0 1.4 %collective-permute-start.11 = (f32[2,8,192]{2,1,0:T(8,128)S(1)}, f32[2,8,192]{2,1,0:T(8,128)S(1)}, u32[]{:S(2)}, u32[]{:S(2)}) collective-permute-start(f32[2,8,192]{2,1,0:T(8,128)S(1)} %stack.53), channel_id=1, source_target_pairs={{0,2},{2,0},{4,6},{6,4},{8,10},{10,8},{12,14},{14,12},{16,18},{18,... | collective-permute-start | bytes 36872 | tf_op jit(solution)/shard_map/ppermute | solution.py:179
  44.4 2.4 %collective-permute-done.11 = f32[2,8,192]{2,1,0:T(8,128)S(1)} collective-permute-done((f32[2,8,192]{2,1,0:T(8,128)S(1)}, f32[2,8,192]{2,1,0:T(8,128)S(1)}, u32[]{:S(2)}, u32[]{:S(2)}) %collective-permute-start.11) | collective-permute-done | bytes 12320 | tf_op jit(solution)/shard_map/ppermute | solution.py:179
  46.9 1.8 %collective-permute-start.12 = (f32[2,8,192]{2,1,0:T(8,128)S(1)}, f32[2,8,192]{2,1,0:T(8,128)S(1)}, u32[]{:S(2)}, u32[]{:S(2)}) collective-permute-start(f32[2,8,192]{2,1,0:T(8,128)S(1)} %pad_maximum_fusion.5), channel_id=1, source_target_pairs={{0,4},{2,6},{4,0},{6,2},{8,12},{10,14},{12,8},{14,10},{16,20},{18,... | collective-permute-start | bytes 36872 | tf_op jit(solution)/shard_map/ppermute | solution.py:179
  48.7 2.0 %collective-permute-done.12 = f32[2,8,192]{2,1,0:T(8,128)S(1)} collective-permute-done((f32[2,8,192]{2,1,0:T(8,128)S(1)}, f32[2,8,192]{2,1,0:T(8,128)S(1)}, u32[]{:S(2)}, u32[]{:S(2)}) %collective-permute-start.12) | collective-permute-done | bytes 12320 | tf_op jit(solution)/shard_map/ppermute | solution.py:179
  50.8 0.8 collective-permute-start.13
  51.6 3.0 %collective-permute-done.13 = f32[2,8,192]{2,1,0:T(8,128)S(1)} collective-permute-done((f32[2,8,192]{2,1,0:T(8,128)S(1)}, f32[2,8,192]{2,1,0:T(8,128)S(1)}, u32[]{:S(2)}, u32[]{:S(2)}) %collective-permute-start.13) | collective-permute-done | bytes 12320 | tf_op jit(solution)/shard_map/ppermute | solution.py:179
  54.7 0.1 pad_maximum_fusion.17
  54.8 0.1 pad_maximum_fusion.16
  54.9 0.1 pad_maximum_fusion.13
  54.9 1.4 %copy-done.1 = f32[512,768]{1,0:T(8,128)S(1)} copy-done((f32[512,768]{1,0:T(8,128)S(1)}, f32[512,768]{1,0:T(8,128)}, u32[]{:S(2)}) %copy-start.1) | copy-done | bytes 1572888
  56.4 1.1 %copy-done.3 = f32[512,384]{1,0:T(8,128)S(1)} copy-done((f32[512,384]{1,0:T(8,128)S(1)}, f32[512,384]{1,0:T(8,128)}, u32[]{:S(2)}) %copy-start.3) | copy-done | bytes 786456
  57.5 1.1 %copy-done.5 = f32[512,384]{1,0:T(8,128)S(1)} copy-done((f32[512,384]{1,0:T(8,128)S(1)}, f32[512,384]{1,0:T(8,128)}, u32[]{:S(2)}) %copy-start.5) | copy-done | bytes 786456
  58.6 1.1 sums_pass.3
  59.8 0.1 collective-permute-start.15
  59.9 1.0 copy-done.6
  60.9 1.1 %sums_pass.2 = f32[256,1152]{1,0:T(8,128)S(1)} custom-call(f32[1,768]{1,0:T(1,128)S(1)} %broadcast_in_dim.12.refs_0_, f32[1,384]{1,0:T(1,128)S(1)} %broadcast_in_dim.13.refs_1_, f32[1,384]{1,0:T(1,128)S(1)} %broadcast_in_dim.14.refs_2_, f32[512,768]{1,0:T(8,128)S(1)} %copy-done.1, f32[512,384]{1,0:T(8,128)S(1)} %copy-done.3, f32[512,384]{1,0:T(8,128)S(1)} %copy-done.6, ...), custom_call_target="tpu_custom_call" | custom-call | flops 805306368 | bytes 3145728 | tf_op jit(solution)/shard_map/sums_pass/pallas_call | solution.py:106
  62.0 0.1 collective-permute-start.14
  62.1 0.0 collective-permute-done.15
  62.1 0.1 slice_add_fusion
  62.3 0.0 copy-start.7
  62.3 1.5 %collective-permute-start.16 = (bf16[128,1152]{1,0:T(8,128)(2,1)S(1)}, bf16[128,1152]{1,0:T(8,128)(2,1)S(1)}, u32[]{:S(2)}, u32[]{:S(2)}) collective-permute-start(bf16[128,1152]{1,0:T(8,128)(2,1)S(1)} %pad_maximum_fusion.4), channel_id=1, source_target_pairs={{0,16},{2,18},{4,20},{6,22},{8,24},{10,26},{12,28},{14,30},{16,0},... | collective-permute-start | bytes 884744 | tf_op jit(solution)/shard_map/ppermute | solution.py:179
  63.8 0.3 collective-permute-done.14
  64.1 0.1 slice_add_fusion.1
  64.2 14.8 %collective-permute-done.16 = bf16[128,1152]{1,0:T(8,128)(2,1)S(1)} collective-permute-done((bf16[128,1152]{1,0:T(8,128)(2,1)S(1)}, bf16[128,1152]{1,0:T(8,128)(2,1)S(1)}, u32[]{:S(2)}, u32[]{:S(2)}) %collective-permute-start.16) | collective-permute-done | bytes 294944 | tf_op jit(solution)/shard_map/ppermute | solution.py:179
  79.0 0.2 fusion.5
  79.2 0.9 fusion.29
  80.2 1.5 %collective-permute-done.17 = bf16[128,1024]{1,0:T(8,128)(2,1)S(1)} collective-permute-done((bf16[128,1024]{1,0:T(8,128)(2,1)S(1)}, bf16[128,1024]{1,0:T(8,128)(2,1)S(1)}, u32[]{:S(2)}, u32[]{:S(2)}) %collective-permute-start.17) | collective-permute-done | bytes 262176 | tf_op jit(solution)/shard_map/ppermute | solution.py:182
  81.7 13.4 %collective-permute-done.18 = bf16[128,1024]{1,0:T(8,128)(2,1)S(1)} collective-permute-done((bf16[128,1024]{1,0:T(8,128)(2,1)S(1)}, bf16[128,1024]{1,0:T(8,128)(2,1)S(1)}, u32[]{:S(2)}, u32[]{:S(2)}) %collective-permute-start.18) | collective-permute-done | bytes 262176 | tf_op jit(solution)/shard_map/ppermute | solution.py:179
  95.1 0.1 collective-permute-start.19
  95.2 1.6 %second_pass.2 = (f32[3,4,192]{2,1,0:T(4,128)S(1)}, f32[3,2,192]{2,1,0:T(2,128)S(1)}, f32[3,2,192]{2,1,0:T(2,128)S(1)}) custom-call(bf16[256,1024]{1,0:T(8,128)(2,1)S(1)} %pad_maximum_fusion.1.cents, f32[1,768]{1,0:T(1,128)S(1)} %get-tuple-element.29.refs_0_, f32[1,384]{1,0:T(1,128)S(1)} %get-tuple-element.30.refs_1_, ...), custom_call_target="tpu_custom_call" | custom-call | flops 805306368 | bytes 3145728 | tf_op jit(solution)/shard_map/second_pass/pallas_call | solution.py:145
  96.8 0.0 collective-permute-done.19
  96.8 1.0 pad_maximum_fusion.2.cents
  97.8 1.6 %second_pass.3 = (f32[3,4,192]{2,1,0:T(4,128)S(1)}, f32[3,2,192]{2,1,0:T(2,128)S(1)}, f32[3,2,192]{2,1,0:T(2,128)S(1)}) custom-call(bf16[256,1024]{1,0:T(8,128)(2,1)S(1)} %pad_maximum_fusion.2.cents, f32[1,768]{1,0:T(1,128)S(1)} %get-tuple-element.29.refs_0_, f32[1,384]{1,0:T(1,128)S(1)} %get-tuple-element.30.refs_1_, ...), custom_call_target="tpu_custom_call" | custom-call | flops 805306368 | bytes 3145728 | tf_op jit(solution)/shard_map/second_pass/pallas_call | solution.py:145
  99.5 0.1 collective-permute-start.20
  99.6 3.7 %collective-permute-done.20 = f32[3,4,192]{2,1,0:T(4,128)S(1)} collective-permute-done((f32[3,4,192]{2,1,0:T(4,128)S(1)}, f32[3,4,192]{2,1,0:T(4,128)S(1)}, u32[]{:S(2)}, u32[]{:S(2)}) %collective-permute-start.20) | collective-permute-done | bytes 9248 | tf_op jit(solution)/shard_map/ppermute | solution.py:179
  103.4 1.4 %collective-permute-start.21 = (f32[3,2,192]{2,1,0:T(2,128)S(1)}, f32[3,2,192]{2,1,0:T(2,128)S(1)}, u32[]{:S(2)}, u32[]{:S(2)}) collective-permute-start(f32[3,2,192]{2,1,0:T(2,128)S(1)} %pad_maximum_fusion.11), channel_id=1, source_target_pairs={{0,4},{2,6},{4,0},{6,2},{8,12},{10,14},{12,8},{14,10},{16,20},{18,... | collective-permute-start | bytes 13832 | tf_op jit(solution)/shard_map/ppermute | solution.py:179
  104.7 2.3 %collective-permute-done.21 = f32[3,2,192]{2,1,0:T(2,128)S(1)} collective-permute-done((f32[3,2,192]{2,1,0:T(2,128)S(1)}, f32[3,2,192]{2,1,0:T(2,128)S(1)}, u32[]{:S(2)}, u32[]{:S(2)}) %collective-permute-start.21) | collective-permute-done | bytes 4640 | tf_op jit(solution)/shard_map/ppermute | solution.py:179
  107.1 1.5 %collective-permute-start.22 = (f32[3,1,192]{2,1,0:T(1,128)S(1)}, f32[3,1,192]{2,1,0:T(1,128)S(1)}, u32[]{:S(2)}, u32[]{:S(2)}) collective-permute-start(f32[3,1,192]{2,1,0:T(1,128)S(1)} %pad_maximum_fusion.14), channel_id=1, source_target_pairs={{0,2},{2,0},{4,6},{6,4},{8,10},{10,8},{12,14},{14,12},{16,18},{18,... | collective-permute-start | bytes 6920 | tf_op jit(solution)/shard_map/ppermute | solution.py:179
  108.6 2.1 %collective-permute-done.22 = f32[3,1,192]{2,1,0:T(1,128)S(1)} collective-permute-done((f32[3,1,192]{2,1,0:T(1,128)S(1)}, f32[3,1,192]{2,1,0:T(1,128)S(1)}, u32[]{:S(2)}, u32[]{:S(2)}) %collective-permute-start.22) | collective-permute-done | bytes 2336 | tf_op jit(solution)/shard_map/ppermute | solution.py:179
  110.8 0.6 divide_subtract_fusion
  (65 shorter events, 0.8 us)
Async XLA Ops:
  1.8 21.0 %collective-permute-start.5 = (bf16[192,1024]{1,0:T(8,128)(2,1)S(1)}, bf16[192,1024]{1,0:T(8,128)(2,1)S(1)}, u32[]{:S(2)}, u32[]{:S(2)}) collective-permute-start(bf16[192,1024]{1,0:T(8,128)(2,1)S(1)} %convert_element_type.14.refs_0_), channel_id=1, source_target_pairs={{0,8},{2,10},{4,12},{6,14},{8,0},{10,2},{12,4},{14,6},{16,24},{18,... | collective-permute-start | bytes 1179656 | tf_op jit(solution)/shard_map/ppermute | solution.py:179
  4.9 17.9 %collective-permute-start.4 = (bf16[192,1024]{1,0:T(8,128)(2,1)S(1)}, bf16[192,1024]{1,0:T(8,128)(2,1)S(1)}, u32[]{:S(2)}, u32[]{:S(2)}) collective-permute-start(bf16[192,1024]{1,0:T(8,128)(2,1)S(1)} %convert_element_type.14.refs_0_), channel_id=1, source_target_pairs={{0,4},{2,6},{4,0},{6,2},{8,12},{10,14},{12,8},{14,10},{16,20},{18,... | collective-permute-start | bytes 1179656 | tf_op jit(solution)/shard_map/ppermute | solution.py:179
  6.4 17.5 %collective-permute-start.3 = (bf16[192,1024]{1,0:T(8,128)(2,1)S(1)}, bf16[192,1024]{1,0:T(8,128)(2,1)S(1)}, u32[]{:S(2)}, u32[]{:S(2)}) collective-permute-start(bf16[192,1024]{1,0:T(8,128)(2,1)S(1)} %convert_element_type.14.refs_0_), channel_id=1, source_target_pairs={{0,2},{2,0},{4,6},{6,4},{8,10},{10,8},{12,14},{14,12},{16,18},{18,... | collective-permute-start | bytes 1179656 | tf_op jit(solution)/shard_map/ppermute | solution.py:179
  9.0 13.8 %collective-permute-start.1 = (bf16[128,1024]{1,0:T(8,128)(2,1)S(1)}, bf16[128,1024]{1,0:T(8,128)(2,1)S(1)}, u32[]{:S(2)}, u32[]{:S(2)}) collective-permute-start(bf16[128,1024]{1,0:T(8,128)(2,1)S(1)} %convert_element_type.13), channel_id=1, source_target_pairs={{0,16},{2,18},{4,20},{6,22},{8,24},{10,26},{12,28},{14,30},{16,0},... | collective-permute-start | bytes 786440 | tf_op jit(solution)/shard_map/ppermute | solution.py:179
  11.6 13.8 %collective-permute-start = (bf16[128,1024]{1,0:T(8,128)(2,1)S(1)}, bf16[128,1024]{1,0:T(8,128)(2,1)S(1)}, u32[]{:S(2)}, u32[]{:S(2)}) collective-permute-start(bf16[128,1024]{1,0:T(8,128)(2,1)S(1)} %convert_element_type.13), channel_id=1, source_target_pairs={{0,1},{1,0},{2,3},{3,2},{4,5},{5,4},{6,7},{7,6},{8,9},{9,8},{10,11... | collective-permute-start | bytes 786440 | tf_op jit(solution)/shard_map/ppermute | solution.py:182
  22.8 2.6 %collective-permute-start.2 = (bf16[128,1024]{1,0:T(8,128)(2,1)S(1)}, bf16[128,1024]{1,0:T(8,128)(2,1)S(1)}, u32[]{:S(2)}, u32[]{:S(2)}) collective-permute-start(bf16[128,1024]{1,0:T(8,128)(2,1)S(1)} %collective-permute-done.1), channel_id=1, source_target_pairs={{0,1},{1,0},{2,3},{3,2},{4,5},{5,4},{6,7},{7,6},{8,9},{9,8},{10,11... | collective-permute-start | bytes 786440 | tf_op jit(solution)/shard_map/ppermute | solution.py:182
  22.8 11.5 %collective-permute-start.7 = (bf16[192,1024]{1,0:T(8,128)(2,1)S(1)}, bf16[192,1024]{1,0:T(8,128)(2,1)S(1)}, u32[]{:S(2)}, u32[]{:S(2)}) collective-permute-start(bf16[192,1024]{1,0:T(8,128)(2,1)S(1)} %collective-permute-done.5.refs_3_), channel_id=1, source_target_pairs={{0,2},{2,0},{4,6},{6,4},{8,10},{10,8},{12,14},{14,12},{16,18},{18,... | collective-permute-start | bytes 1179656 | tf_op jit(solution)/shard_map/ppermute | solution.py:179
  22.9 11.6 %collective-permute-start.8 = (bf16[192,1024]{1,0:T(8,128)(2,1)S(1)}, bf16[192,1024]{1,0:T(8,128)(2,1)S(1)}, u32[]{:S(2)}, u32[]{:S(2)}) collective-permute-start(bf16[192,1024]{1,0:T(8,128)(2,1)S(1)} %collective-permute-done.4.refs_2_), channel_id=1, source_target_pairs={{0,8},{2,10},{4,12},{6,14},{8,0},{10,2},{12,4},{14,6},{16,24},{18,... | collective-permute-start | bytes 1179656 | tf_op jit(solution)/shard_map/ppermute | solution.py:179
  23.9 12.3 %collective-permute-start.6 = (bf16[192,1024]{1,0:T(8,128)(2,1)S(1)}, bf16[192,1024]{1,0:T(8,128)(2,1)S(1)}, u32[]{:S(2)}, u32[]{:S(2)}) collective-permute-start(bf16[192,1024]{1,0:T(8,128)(2,1)S(1)} %collective-permute-done.3.refs_1_), channel_id=1, source_target_pairs={{0,4},{2,6},{4,0},{6,2},{8,12},{10,14},{12,8},{14,10},{16,20},{18,... | collective-permute-start | bytes 1179656 | tf_op jit(solution)/shard_map/ppermute | solution.py:179
  27.2 1.2 %copy-start = (f32[512,768]{1,0:T(8,128)}, f32[512,768]{1,0:T(8,128)S(1)}, u32[]{:S(2)}) copy-start(f32[512,768]{1,0:T(8,128)S(1)} %get-tuple-element.23.refs_3_) | copy-start | bytes 4718596
  34.4 6.6 %collective-permute-start.10 = (bf16[96,1024]{1,0:T(8,128)(2,1)S(1)}, bf16[96,1024]{1,0:T(8,128)(2,1)S(1)}, u32[]{:S(2)}, u32[]{:S(2)}) collective-permute-start(bf16[96,1024]{1,0:T(8,128)(2,1)S(1)} %slice.470), channel_id=1, source_target_pairs={{0,4},{2,6},{4,0},{6,2},{8,12},{10,14},{12,8},{14,10},{16,20},{18,... | collective-permute-start | bytes 589832 | tf_op jit(solution)/shard_map/ppermute | solution.py:179
  34.5 6.6 %collective-permute-start.9 = (bf16[96,1024]{1,0:T(8,128)(2,1)S(1)}, bf16[96,1024]{1,0:T(8,128)(2,1)S(1)}, u32[]{:S(2)}, u32[]{:S(2)}) collective-permute-start(bf16[96,1024]{1,0:T(8,128)(2,1)S(1)} %slice.469), channel_id=1, source_target_pairs={{0,2},{2,0},{4,6},{6,4},{8,10},{10,8},{12,14},{14,12},{16,18},{18,... | collective-permute-start | bytes 589832 | tf_op jit(solution)/shard_map/ppermute | solution.py:179
  37.2 0.9 copy-start.2
  42.1 0.9 copy-start.4
  43.0 3.8 %collective-permute-start.11 = (f32[2,8,192]{2,1,0:T(8,128)S(1)}, f32[2,8,192]{2,1,0:T(8,128)S(1)}, u32[]{:S(2)}, u32[]{:S(2)}) collective-permute-start(f32[2,8,192]{2,1,0:T(8,128)S(1)} %stack.53), channel_id=1, source_target_pairs={{0,2},{2,0},{4,6},{6,4},{8,10},{10,8},{12,14},{14,12},{16,18},{18,... | collective-permute-start | bytes 36872 | tf_op jit(solution)/shard_map/ppermute | solution.py:179
  46.9 3.8 %collective-permute-start.12 = (f32[2,8,192]{2,1,0:T(8,128)S(1)}, f32[2,8,192]{2,1,0:T(8,128)S(1)}, u32[]{:S(2)}, u32[]{:S(2)}) collective-permute-start(f32[2,8,192]{2,1,0:T(8,128)S(1)} %pad_maximum_fusion.5), channel_id=1, source_target_pairs={{0,4},{2,6},{4,0},{6,2},{8,12},{10,14},{12,8},{14,10},{16,20},{18,... | collective-permute-start | bytes 36872 | tf_op jit(solution)/shard_map/ppermute | solution.py:179
  50.8 3.8 %collective-permute-start.13 = (f32[2,8,192]{2,1,0:T(8,128)S(1)}, f32[2,8,192]{2,1,0:T(8,128)S(1)}, u32[]{:S(2)}, u32[]{:S(2)}) collective-permute-start(f32[2,8,192]{2,1,0:T(8,128)S(1)} %pad_maximum_fusion.7), channel_id=1, source_target_pairs={{0,8},{2,10},{4,12},{6,14},{8,0},{10,2},{12,4},{14,6},{16,24},{18,... | collective-permute-start | bytes 36872 | tf_op jit(solution)/shard_map/ppermute | solution.py:179
  54.9 1.4 %copy-start.1 = (f32[512,768]{1,0:T(8,128)S(1)}, f32[512,768]{1,0:T(8,128)}, u32[]{:S(2)}) copy-start(f32[512,768]{1,0:T(8,128)} %copy-done) | copy-start | bytes 4718596
  56.3 1.1 %copy-start.3 = (f32[512,384]{1,0:T(8,128)S(1)}, f32[512,384]{1,0:T(8,128)}, u32[]{:S(2)}) copy-start(f32[512,384]{1,0:T(8,128)} %copy-done.2) | copy-start | bytes 2359300
  57.5 1.1 %copy-start.5 = (f32[512,384]{1,0:T(8,128)S(1)}, f32[512,384]{1,0:T(8,128)}, u32[]{:S(2)}) copy-start(f32[512,384]{1,0:T(8,128)} %copy-done.4) | copy-start | bytes 2359300
  59.7 1.1 %copy-start.6 = (f32[512,384]{1,0:T(8,128)S(1)}, f32[512,384]{1,0:T(8,128)}, u32[]{:S(2)}) copy-start(f32[512,384]{1,0:T(8,128)} %copy-done.4) | copy-start | bytes 2359300
  59.8 2.3 %collective-permute-start.15 = (f32[128,1152]{1,0:T(8,128)S(1)}, f32[128,1152]{1,0:T(8,128)S(1)}, u32[]{:S(2)}, u32[]{:S(2)}) collective-permute-start(f32[128,1152]{1,0:T(8,128)S(1)} %slice.513), channel_id=1, source_target_pairs={{0,1},{1,0},{2,3},{3,2},{4,5},{5,4},{6,7},{7,6},{8,9},{9,8},{10,11... | collective-permute-start | bytes 1769480 | tf_op jit(solution)/shard_map/ppermute | solution.py:182
  62.0 2.1 %collective-permute-start.14 = (f32[128,1152]{1,0:T(8,128)S(1)}, f32[128,1152]{1,0:T(8,128)S(1)}, u32[]{:S(2)}, u32[]{:S(2)}) collective-permute-start(f32[128,1152]{1,0:T(8,128)S(1)} %slice.510), channel_id=1, source_target_pairs={{0,1},{1,0},{2,3},{3,2},{4,5},{5,4},{6,7},{7,6},{8,9},{9,8},{10,11... | collective-permute-start | bytes 1769480 | tf_op jit(solution)/shard_map/ppermute | solution.py:182
  62.3 16.9 %copy-start.7 = (f32[128,1024]{1,0:T(8,128)S(1)}, f32[128,1024]{1,0:T(8,128)}, u32[]{:S(2)}) copy-start(f32[128,1024]{1,0:T(8,128)} %param.3) | copy-start | bytes 1572868
  62.3 16.7 %collective-permute-start.16 = (bf16[128,1152]{1,0:T(8,128)(2,1)S(1)}, bf16[128,1152]{1,0:T(8,128)(2,1)S(1)}, u32[]{:S(2)}, u32[]{:S(2)}) collective-permute-start(bf16[128,1152]{1,0:T(8,128)(2,1)S(1)} %pad_maximum_fusion.4), channel_id=1, source_target_pairs={{0,16},{2,18},{4,20},{6,22},{8,24},{10,26},{12,28},{14,30},{16,0},... | collective-permute-start | bytes 884744 | tf_op jit(solution)/shard_map/ppermute | solution.py:179
  80.2 1.5 %collective-permute-start.17 = (bf16[128,1024]{1,0:T(8,128)(2,1)S(1)}, bf16[128,1024]{1,0:T(8,128)(2,1)S(1)}, u32[]{:S(2)}, u32[]{:S(2)}) collective-permute-start(bf16[128,1024]{1,0:T(8,128)(2,1)S(1)} %get-tuple-element.44), channel_id=1, source_target_pairs={{0,1},{1,0},{2,3},{3,2},{4,5},{5,4},{6,7},{7,6},{8,9},{9,8},{10,11... | collective-permute-start | bytes 786440 | tf_op jit(solution)/shard_map/ppermute | solution.py:182
  80.2 14.9 %collective-permute-start.18 = (bf16[128,1024]{1,0:T(8,128)(2,1)S(1)}, bf16[128,1024]{1,0:T(8,128)(2,1)S(1)}, u32[]{:S(2)}, u32[]{:S(2)}) collective-permute-start(bf16[128,1024]{1,0:T(8,128)(2,1)S(1)} %get-tuple-element.44), channel_id=1, source_target_pairs={{0,16},{2,18},{4,20},{6,22},{8,24},{10,26},{12,28},{14,30},{16,0},... | collective-permute-start | bytes 786440 | tf_op jit(solution)/shard_map/ppermute | solution.py:179
  95.1 1.7 %collective-permute-start.19 = (bf16[128,1024]{1,0:T(8,128)(2,1)S(1)}, bf16[128,1024]{1,0:T(8,128)(2,1)}, u32[]{:S(2)}, u32[]{:S(2)}) collective-permute-start(bf16[128,1024]{1,0:T(8,128)(2,1)S(1)} %collective-permute-done.18), channel_id=1, source_target_pairs={{0,1},{1,0},{2,3},{3,2},{4,5},{5,4},{6,7},{7,6},{8,9},{9,8},{10,11... | collective-permute-start | bytes 786440 | tf_op jit(solution)/shard_map/ppermute | solution.py:182
  99.5 3.8 %collective-permute-start.20 = (f32[3,4,192]{2,1,0:T(4,128)S(1)}, f32[3,4,192]{2,1,0:T(4,128)S(1)}, u32[]{:S(2)}, u32[]{:S(2)}) collective-permute-start(f32[3,4,192]{2,1,0:T(4,128)S(1)} %pad_maximum_fusion.8), channel_id=1, source_target_pairs={{0,8},{2,10},{4,12},{6,14},{8,0},{10,2},{12,4},{14,6},{16,24},{18,... | collective-permute-start | bytes 27656 | tf_op jit(solution)/shard_map/ppermute | solution.py:179
  103.4 3.7 %collective-permute-start.21 = (f32[3,2,192]{2,1,0:T(2,128)S(1)}, f32[3,2,192]{2,1,0:T(2,128)S(1)}, u32[]{:S(2)}, u32[]{:S(2)}) collective-permute-start(f32[3,2,192]{2,1,0:T(2,128)S(1)} %pad_maximum_fusion.11), channel_id=1, source_target_pairs={{0,4},{2,6},{4,0},{6,2},{8,12},{10,14},{12,8},{14,10},{16,20},{18,... | collective-permute-start | bytes 13832 | tf_op jit(solution)/shard_map/ppermute | solution.py:179
  107.1 3.7 %collective-permute-start.22 = (f32[3,1,192]{2,1,0:T(1,128)S(1)}, f32[3,1,192]{2,1,0:T(1,128)S(1)}, u32[]{:S(2)}, u32[]{:S(2)}) collective-permute-start(f32[3,1,192]{2,1,0:T(1,128)S(1)} %pad_maximum_fusion.14), channel_id=1, source_target_pairs={{0,2},{2,0},{4,6},{6,4},{8,10},{10,8},{12,14},{14,12},{16,18},{18,... | collective-permute-start | bytes 6920 | tf_op jit(solution)/shard_map/ppermute | solution.py:179

commit v3 on v2

--- a/solution.py
+++ b/solution.py
@@ -40,7 +40,7 @@
 
 def first_kernel(n, shard, cents, *refs):
     chunks = refs[:n]
-    weight_ref, stats_ref, row_sq_ref, rows_ref = refs[n:]
+    stats_ref, row_sq_ref, rows_ref = refs[n:]
     for i in range(n):
         rows_ref[i * shard : (i + 1) * shard, :] = chunks[i][...]
     piece = cents[...]
@@ -52,9 +52,7 @@
         row_sq = row_squares(rows)
         score = scores(piece, cent_sq, rows, row_sq)
         top = jnp.max(score, axis=0, keepdims=True)
-        weight = jnp.exp(score - top)
-        total = jnp.sum(weight, axis=0, keepdims=True)
-        weight_ref[:, span] = weight
+        total = jnp.sum(jnp.exp(score - top), axis=0, keepdims=True)
         row_sq_ref[:, span] = row_sq
         for i in range(2):
             stats_ref[0, 2 * j + i : 2 * j + i + 1, :] = top[:, i * shard : (i + 1) * shard]
@@ -69,13 +67,12 @@
     return pl.pallas_call(
         functools.partial(first_kernel, n, shard),
         out_shape=(
-            jax.ShapeDtypeStruct((n_k, n_rows), jnp.float32),
             jax.ShapeDtypeStruct((2, n, shard), jnp.float32),
             jax.ShapeDtypeStruct((1, n_rows), jnp.float32),
             jax.ShapeDtypeStruct((n_rows, width), jnp.bfloat16),
         ),
         in_specs=[VMEM] * (1 + n),
-        out_specs=(VMEM,) * 4,
+        out_specs=(VMEM,) * 3,
         compiler_params=params(),
         cost_estimate=pl.CostEstimate(
             flops=2 * n_k * n_rows * width, bytes_accessed=2 * n_rows * width, transcendentals=n_k * n_rows
@@ -84,13 +81,16 @@
     )(cents, *chunks)
 
 
-def sums_kernel(first, last, n, *refs):
-    scales, weights, rows = refs[:n], refs[n : 2 * n], refs[2 * n : 3 * n]
+def sums_kernel(first, last, n, cents, *refs):
+    stats, row_sqs, rows = refs[:n], refs[n : 2 * n], refs[2 * n : 3 * n]
     out_ref = refs[3 * n]
-    width = rows[0].shape[1]
+    width = cents.shape[1]
+    piece = cents[first:last, :]
+    cent_sq = centroid_squares(piece)
     counts = 0.0
     for s in range(n):
-        resp = (weights[s][first:last, :] * scales[s][...]).astype(jnp.bfloat16)
+        score = scores(piece, cent_sq, rows[s][...], row_sqs[s][...])
+        resp = (jnp.exp(score - stats[s][0:1, :]) / stats[s][1:2, :]).astype(jnp.bfloat16)
         counts = counts + jnp.sum(resp.astype(jnp.float32), axis=1, keepdims=True)
         part = jnp.dot(resp, rows[s][...], preferred_element_type=jnp.float32)
         if s:
@@ -99,21 +99,23 @@
     out_ref[:, width:] = jnp.broadcast_to(counts, (last - first, 128))
 
 
-def sums_pass(scales, weights, rows, first, last):
+def sums_pass(cents, stats, row_sqs, rows, first, last):
     n = len(rows)
     width = rows[0].shape[1]
     n_rows = sum(r.shape[0] for r in rows)
     return pl.pallas_call(
         functools.partial(sums_kernel, first, last, n),
         out_shape=jax.ShapeDtypeStruct((last - first, width + 128), jnp.float32),
-        in_specs=[VMEM] * (3 * n),
+        in_specs=[VMEM] * (1 + 3 * n),
         out_specs=VMEM,
         compiler_params=params(),
         cost_estimate=pl.CostEstimate(
-            flops=2 * (last - first) * n_rows * width, bytes_accessed=2 * n_rows * width, transcendentals=0
+            flops=4 * (last - first) * n_rows * width,
+            bytes_accessed=2 * n_rows * width,
+            transcendentals=(last - first) * n_rows,
         ),
         name="sums_pass",
-    )(*scales, *weights, *rows)
+    )(cents, *stats, *row_sqs, *rows)
 
 
 def second_kernel(shard, n, cents, *refs):
@@ -155,6 +157,10 @@
     )(cents, *row_sqs, *rows)
 
 
+def hold(*values):
+    return lax.optimization_barrier(values)
+
+
 def merge(a, b):
     top = jnp.maximum(a[0], b[0])
     drops = (a[0] - top, b[0] - top)
@@ -211,46 +217,59 @@
             bits //= 2
         return value
 
+    def by_position(stats):
+        place = lax.axis_index("dp") % CUBE
+        for bit in (1, 2, 4):
+            swapped = jnp.stack([stats[:, b ^ bit] for b in range(CUBE)], axis=1)
+            stats = jnp.where((place & bit) != 0, swapped, stats)
+        return stats
+
+    def exchange(value):
+        groups = [list(range(i, i + CUBE)) for i in range(0, n_dp, CUBE)]
+        return lax.all_to_all(value, "dp", 0, 0, axis_index_groups=groups)
+
+    def everywhere(stats):
+        return exchange(jnp.broadcast_to(stats[None], (CUBE,) + stats.shape))
+
+    def to_owner(stats):
+        return exchange(stats.transpose(1, 0, 2))
+
     def on_device(embeddings, centroids):
         shard, width = embeddings.shape
         half = shard // 2
         chunk = {0: embeddings.astype(jnp.bfloat16)}
         for bit in (1, 2, 4):
             chunk[bit] = flip(chunk[0], bit)
+        near_own = gather_near(centroids.astype(jnp.bfloat16))
+        far_own = flip(near_own, top_bit)
         chunk[3] = flip(chunk[1], 2)
         chunk[6] = flip(chunk[2], 4)
         chunk[5] = flip(chunk[4], 1)
-        chunk[7] = jnp.concatenate([flip(chunk[6][:half], 1), flip(chunk[5][half:], 2)], axis=0)
-
-        near_own = gather_near(centroids.astype(jnp.bfloat16))
-        far_own = flip(near_own, top_bit)
-        piece = jnp.concatenate([gather_cent(near_own), gather_cent(far_own)], axis=0)
-        n_near = piece.shape[0] // 2
-
-        weights, local, row_sqs, rows = [], [], [], []
-        for bits in GROUPS:
-            weight, stats, row_sq, held = first_pass(piece, [chunk[b] for b in bits])
-            weights.append(weight)
-            local.append(stats)
-            row_sqs.append(row_sq)
-            rows.append(held)
-
-        stats = by_chunk(local)
-        for bit in (1, 2, 4):
-            other = flip(stats, bit)
-            stats = merge(stats, jnp.stack([other[:, b ^ bit] for b in range(CUBE)], axis=1))
-        scales = []
-        for g, bits in enumerate(GROUPS):
-            scale = [jnp.exp(local[g][0, i] - stats[0, b]) / stats[1, b] for i, b in enumerate(bits)]
-            scales.append(jnp.concatenate(scale)[None, :])
-
-        far = scatter_cent(sums_pass(scales, weights, rows, n_near, 2 * n_near))
+        parts = (flip(chunk[6][:half], 1), flip(chunk[5][half:], 2))
+        near = gather_cent(near_own)
+        n_near = near.shape[0]
+        far_own = hold(far_own, chunk[3], chunk[5], chunk[6])[0]
+        piece = jnp.concatenate([near, gather_cent(far_own)], axis=0)
+        passes = [first_pass(piece, [chunk[b] for b in bits]) for bits in GROUPS[:2]]
+        parts, passes = hold(parts, passes)
+        chunk[7] = jnp.concatenate(parts, axis=0)
+        passes.append(first_pass(piece, [chunk[b] for b in GROUPS[2]]))
+        local, row_sqs, rows = zip(*passes)
+
+        stats = by_position(by_chunk(local))
+        stats = everywhere(stats)
+        top = jnp.max(stats[:, 0], axis=0)
+        total = jnp.sum(stats[:, 1] * jnp.exp(stats[:, 0] - top), axis=0)
+        stats = by_position(jnp.stack([top, total]))
+        final = [jnp.concatenate([stats[:, b] for b in bits], axis=1) for bits in GROUPS]
+
+        far = scatter_cent(sums_pass(piece, final, row_sqs, rows, n_near, 2 * n_near))
         count = far[:, width:]
         coarse = lax.reduce_precision(count, 8, 7)
         lane = lax.broadcasted_iota(jnp.int32, count.shape, 1)
         far = jnp.concatenate([far[:, :width], jnp.where(lane < 64, coarse, count - coarse)], axis=1)
         far = flip(far.astype(jnp.bfloat16), top_bit).astype(jnp.float32)
-        near = scatter_cent(sums_pass(scales, weights, rows, 0, n_near))
+        near = scatter_cent(sums_pass(piece, final, row_sqs, rows, 0, n_near))
         counts = near[:, width : width + 1] + (far[:, width : width + 1] + far[:, width + 64 : width + 65])
         sums = scatter_near(jnp.concatenate([near[:, :width] + far[:, :width], jnp.broadcast_to(counts, count.shape)], axis=1))
         updated = (sums[:, :width] + prior_mass * centroids) / (sums[:, width : width + 1] + prior_mass)
@@ -258,11 +277,15 @@
         near_own = gather_near(updated.astype(jnp.bfloat16))
         far_own = flip(near_own, top_bit)
         near = second_pass(gather_cent(near_own), row_sqs, rows, shard)
+        far_own, near = hold(far_own, near)
         far = second_pass(gather_cent(far_own), row_sqs, rows, shard)
         stats = merge(by_chunk(near), by_chunk(far))
-        for bit in (4, 2, 1):
-            stats = merge(stats[:, :bit], flip(stats[:, bit:], bit))
-        entropy = (jnp.log(stats[1]) - stats[2] / stats[1]).reshape(shard)
+        stats = to_owner(by_position(stats))
+        drop = stats[:, 0] - jnp.max(stats[:, 0], axis=0)
+        factor = jnp.exp(drop)
+        total = jnp.sum(factor * stats[:, 1], axis=0)
+        spread = jnp.sum(factor * (stats[:, 2] + drop * stats[:, 1]), axis=0)
+        entropy = jnp.log(total) - spread / total
         return (updated, entropy)
 
     in_specs = (P(("dp", "cent"), None), P(("dp", "cent"), None))

time: 112 us -> 105 us (0.938)
  waiting for transfers between devices: 65.7 us -> 47.1 us
  blocking collectives: 0 us -> 17 us
  local copies, waits for them, and re-layouts: 7.99 us -> 2.03 us
  Pallas kernels: 9.19 us -> 12.5 us
  starting transfers between devices: 21.8 us -> 19.3 us
    ppermute x17 -> x11, waiting for transfers between devices: 63.8 us -> 43.9 us  [flip(): return lax.ppermute(value, 'dp', [(i, i ^ bits) for i in range(n_dp)])]
    all_to_all x0 -> x2, blocking collectives: none -> 17 us  [exchange(): return lax.all_to_all(value, 'dp', 0, 0, axis_index_groups=groups)]
    unnamed x16 -> x27, local copies, waits for them, and re-layouts: 7.62 us -> 1.6 us
    pallas_call x2, Pallas kernels: 2.23 us -> 5.57 us  [sums_pass(): pl.pallas_call(functools.partial(sums_kernel, first, last, n), out_shape=...]
    ppermute x17 -> x11, starting transfers between devices: 21.5 us -> 18.6 us  [flip(): return lax.ppermute(value, 'dp', [(i, i ^ bits) for i in range(n_dp)])]
    ppermute x6, waiting for transfers between devices: 1.83 us -> 3.22 us  [across(): return lax.ppermute(value, 'cent', [(i, i ^ bits) for i in range(n_cent)])]
  transfers between devices with their start and end apart: 23 -> 17, of which waited for: 14 -> 9; matrix products, arithmetic and copies ran while one was open for 1% -> 1% of each run, Pallas kernels for 5% -> 7%
where the time goes in v3:
time: 105 us
  waiting for transfers between devices  47.1 us (45%)
  starting transfers between devices  19.3 us (18%)
  blocking collectives  17 us (16%)
  Pallas kernels  12.5 us (12%)
  other arithmetic  5.84 us (6%)
  local copies, waits for them, and re-layouts  2.03 us (2%)
  between operations  1.19 us (1%)
    ppermute x11, waiting for transfers between devices, flip(): return lax.ppermute(value, 'dp', [(i, i ^ bits) for i in range(n_dp)])  43.9 us
    ppermute x11, starting transfers between devices, flip(): return lax.ppermute(value, 'dp', [(i, i ^ bits) for i in range(n_dp)])  18.6 us
    all_to_all x2, blocking collectives, exchange(): return lax.all_to_all(value, 'dp', 0, 0, axis_index_groups=groups)  17 us
    pallas_call x2, Pallas kernels, sums_pass(): pl.pallas_call(functools.partial(sums_kernel, first, last, n), out_shape=...  5.57 us
    pallas_call x3, Pallas kernels, first_pass(): pl.pallas_call(functools.partial(first_kernel, n, shard), out_shape=(jax....  3.77 us
    ppermute x6, waiting for transfers between devices, across(): return lax.ppermute(value, 'cent', [(i, i ^ bits) for i in range(n_cent)])  3.22 us
    pallas_call x2, Pallas kernels, second_pass(): pl.pallas_call(functools.partial(second_kernel, shard, n), out_shape=tupl...  3.18 us
  transfers between devices with their start and end apart: 17, of which 9 were waited for; matrix products, arithmetic and copies ran while one was open for 1% of the time, Pallas kernels for 7%

profile of v3, /device:TPU:0, one launch (start us, length us, event | category | flops | bytes accessed | tf_op | source)
XLA Modules:
  0.0 105.0 jit_solution(2892092281521133439)
XLA Ops:
  0.6 1.2 %convert_element_type.14.refs_0_ = bf16[192,1024]{1,0:T(8,128)(2,1)S(1)} convert(f32[192,1024]{1,0:T(8,128)} %param.2) | non-fusion elementwise | flops 196608 | bytes 1179648 | tf_op jit(solution)/shard_map/convert_element_type | solution.py:240
  1.8 3.1 %collective-permute-start.4 = (bf16[192,1024]{1,0:T(8,128)(2,1)S(1)}, bf16[192,1024]{1,0:T(8,128)(2,1)S(1)}, u32[]{:S(2)}, u32[]{:S(2)}) collective-permute-start(bf16[192,1024]{1,0:T(8,128)(2,1)S(1)} %convert_element_type.14.refs_0_), channel_id=1, source_target_pairs={{0,8},{2,10},{4,12},{6,14},{8,0},{10,2},{12,4},{14,6},{16,24},{18,... | collective-permute-start | bytes 1179656 | tf_op jit(solution)/shard_map/ppermute | solution.py:185
  4.9 1.5 %collective-permute-start.6 = (bf16[192,1024]{1,0:T(8,128)(2,1)S(1)}, bf16[192,1024]{1,0:T(8,128)(2,1)S(1)}, u32[]{:S(2)}, u32[]{:S(2)}) collective-permute-start(bf16[192,1024]{1,0:T(8,128)(2,1)S(1)} %convert_element_type.14.refs_0_), channel_id=1, source_target_pairs={{0,4},{2,6},{4,0},{6,2},{8,12},{10,14},{12,8},{14,10},{16,20},{18,... | collective-permute-start | bytes 1179656 | tf_op jit(solution)/shard_map/ppermute | solution.py:185
  6.4 1.5 %collective-permute-start.2 = (bf16[192,1024]{1,0:T(8,128)(2,1)S(1)}, bf16[192,1024]{1,0:T(8,128)(2,1)S(1)}, u32[]{:S(2)}, u32[]{:S(2)}) collective-permute-start(bf16[192,1024]{1,0:T(8,128)(2,1)S(1)} %convert_element_type.14.refs_0_), channel_id=1, source_target_pairs={{0,2},{2,0},{4,6},{6,4},{8,10},{10,8},{12,14},{14,12},{16,18},{18,... | collective-permute-start | bytes 1179656 | tf_op jit(solution)/shard_map/ppermute | solution.py:185
  7.9 0.7 copy-done
  8.7 5.4 %collective-permute-done.4.refs_3_ = bf16[192,1024]{1,0:T(8,128)(2,1)S(1)} collective-permute-done((bf16[192,1024]{1,0:T(8,128)(2,1)S(1)}, bf16[192,1024]{1,0:T(8,128)(2,1)S(1)}, u32[]{:S(2)}, u32[]{:S(2)}) %collective-permute-start.4) | collective-permute-done | bytes 393248 | tf_op jit(solution)/shard_map/ppermute | solution.py:185
  14.0 1.7 %collective-permute-start.5 = (bf16[192,1024]{1,0:T(8,128)(2,1)S(1)}, bf16[192,1024]{1,0:T(8,128)(2,1)S(1)}, u32[]{:S(2)}, u32[]{:S(2)}) collective-permute-start(bf16[192,1024]{1,0:T(8,128)(2,1)S(1)} %collective-permute-done.4.refs_3_), channel_id=1, source_target_pairs={{0,2},{2,0},{4,6},{6,4},{8,10},{10,8},{12,14},{14,12},{16,18},{18,... | collective-permute-start | bytes 1179656 | tf_op jit(solution)/shard_map/ppermute | solution.py:185
  15.7 0.0 collective-permute-done.6.refs_2_
  15.7 1.6 %collective-permute-start.7 = (bf16[192,1024]{1,0:T(8,128)(2,1)S(1)}, bf16[192,1024]{1,0:T(8,128)(2,1)S(1)}, u32[]{:S(2)}, u32[]{:S(2)}) collective-permute-start(bf16[192,1024]{1,0:T(8,128)(2,1)S(1)} %collective-permute-done.6.refs_2_), channel_id=1, source_target_pairs={{0,8},{2,10},{4,12},{6,14},{8,0},{10,2},{12,4},{14,6},{16,24},{18,... | collective-permute-start | bytes 1179656 | tf_op jit(solution)/shard_map/ppermute | solution.py:185
  17.3 0.2 collective-permute-done.2.refs_1_
  17.5 1.3 %collective-permute-start.3 = (bf16[192,1024]{1,0:T(8,128)(2,1)S(1)}, bf16[192,1024]{1,0:T(8,128)(2,1)S(1)}, u32[]{:S(2)}, u32[]{:S(2)}) collective-permute-start(bf16[192,1024]{1,0:T(8,128)(2,1)S(1)} %collective-permute-done.2.refs_1_), channel_id=1, source_target_pairs={{0,4},{2,6},{4,0},{6,2},{8,12},{10,14},{12,8},{14,10},{16,20},{18,... | collective-permute-start | bytes 1179656 | tf_op jit(solution)/shard_map/ppermute | solution.py:185
  18.8 0.8 copy-done.6
  19.5 1.1 %convert_element_type.13 = bf16[128,1024]{1,0:T(8,128)(2,1)S(1)} convert(f32[128,1024]{1,0:T(8,128)} %param.3) | non-fusion elementwise | flops 131072 | bytes 786432 | tf_op jit(solution)/shard_map/convert_element_type | solution.py:243
  20.6 2.7 %collective-permute-start.1 = (bf16[128,1024]{1,0:T(8,128)(2,1)S(1)}, bf16[128,1024]{1,0:T(8,128)(2,1)S(1)}, u32[]{:S(2)}, u32[]{:S(2)}) collective-permute-start(bf16[128,1024]{1,0:T(8,128)(2,1)S(1)} %convert_element_type.13), channel_id=1, source_target_pairs={{0,16},{2,18},{4,20},{6,22},{8,24},{10,26},{12,28},{14,30},{16,0},... | collective-permute-start | bytes 786440 | tf_op jit(solution)/shard_map/ppermute | solution.py:185
  23.3 0.0 collective-permute-start
  23.3 10.3 %collective-permute-done.1 = bf16[128,1024]{1,0:T(8,128)(2,1)S(1)} collective-permute-done((bf16[128,1024]{1,0:T(8,128)(2,1)S(1)}, bf16[128,1024]{1,0:T(8,128)(2,1)S(1)}, u32[]{:S(2)}, u32[]{:S(2)}) %collective-permute-start.1) | collective-permute-done | bytes 262176 | tf_op jit(solution)/shard_map/ppermute | solution.py:185
  33.6 0.0 collective-permute-done.5.refs_1_
  33.6 0.0 collective-permute-done.7.refs_0_
  33.6 0.0 collective-permute-done.3.refs_0_
  33.6 0.0 copy-done.2
  33.6 0.1 collective-permute-start.8
  33.7 0.0 copy-done.4
  33.7 0.1 collective-permute-start.10
  33.8 0.0 copy-start.1
  33.9 0.0 copy-start.3
  33.9 0.0 copy-start.5
  33.9 2.4 %collective-permute-start.9 = (bf16[96,1024]{1,0:T(8,128)(2,1)S(1)}, bf16[96,1024]{1,0:T(8,128)(2,1)S(1)}, u32[]{:S(2)}, u32[]{:S(2)}) collective-permute-start(bf16[96,1024]{1,0:T(8,128)(2,1)S(1)} %slice.402), channel_id=1, source_target_pairs={{0,2},{2,0},{4,6},{6,4},{8,10},{10,8},{12,14},{14,12},{16,18},{18,... | collective-permute-start | bytes 589832 | tf_op jit(solution)/shard_map/ppermute | solution.py:185
  36.3 0.0 collective-permute-done
  36.3 0.0 collective-permute-done.8
  36.3 0.1 pad_maximum_fusion.cents
  36.4 1.0 first_pass.4
  37.4 1.8 %first_pass.3 = (f32[2,4,192]{2,1,0:T(4,128)S(1)}, f32[1,768]{1,0:T(1,128)S(1)}, bf16[768,1024]{1,0:T(8,128)(2,1)S(1)}) custom-call(bf16[512,1024]{1,0:T(8,128)(2,1)S(1)} %pad_maximum_fusion.cents, bf16[192,1024]{1,0:T(8,128)(2,1)S(1)} %copy-done.1, bf16[192,1024]{1,0:T(8,128)(2,1)S(1)} %copy-done.7, bf16[192,1024]{1,0:T(8,128)(2,1)S(1)} %copy-done.5, ...), custom_call_target="tpu_custom_call" | custom-call | flops 805306368 | bytes 1572864 | tf_op jit(solution)/shard_map/first_pass/pallas_call | solution.py:67
  39.2 1.9 %collective-permute-done.10 = bf16[96,1024]{1,0:T(8,128)(2,1)S(1)} collective-permute-done((bf16[96,1024]{1,0:T(8,128)(2,1)S(1)}, bf16[96,1024]{1,0:T(8,128)(2,1)S(1)}, u32[]{:S(2)}, u32[]{:S(2)}) %collective-permute-start.10) | collective-permute-done | bytes 196640 | tf_op jit(solution)/shard_map/ppermute | solution.py:185
  41.1 0.5 collective-permute-done.9
  41.7 1.0 first_pass.5
  42.8 8.9 %all_to_all.10 = f32[8,2,8,192]{3,2,1,0:T(8,128)S(1)} all-to-all(f32[8,2,8,192]{3,2,1,0:T(8,128)S(1)} %broadcast_in_dim.2), channel_id=1, replica_groups={{0,2,4,6,8,10,12,14},{16,18,20,22,24,26,28,30},{1,3,5,7,9,11,13,15},{17..., dimensions={0} | all-to-all | bytes 196608 | tf_op jit(solution)/shard_map/all_to_all | solution.py:229
  52.1 0.1 pad_maximum_fusion.8
  52.2 0.1 pad_maximum_fusion.7.refs_0_
  52.2 2.8 %sums_pass.3 = f32[256,1152]{1,0:T(8,128)S(1)} custom-call(bf16[512,1024]{1,0:T(8,128)(2,1)S(1)} %pad_maximum_fusion.cents, f32[2,768]{1,0:T(2,128)S(1)} %pad_maximum_fusion.7.refs_0_, f32[2,384]{1,0:T(2,128)S(1)} %get-tuple-element.112.refs_1_, f32[2,384]{1,0:T(2,128)S(1)} %get-tuple-element.113.refs_2_, f32[1,768]{1,0:T(1,128)S(1)} %get-tuple-element.42.refs_3_.refs_0_, ...), custom_call_target="tpu_custom_call" | custom-call | flops 1610612736 | bytes 3145728 | tf_op jit(solution)/shard_map/sums_pass/pallas_call | solution.py:106
  55.1 0.1 collective-permute-start.12
  55.2 2.8 %sums_pass.2 = f32[256,1152]{1,0:T(8,128)S(1)} custom-call(bf16[512,1024]{1,0:T(8,128)(2,1)S(1)} %pad_maximum_fusion.cents, f32[2,768]{1,0:T(2,128)S(1)} %pad_maximum_fusion.7.refs_0_, f32[2,384]{1,0:T(2,128)S(1)} %get-tuple-element.112.refs_1_, f32[2,384]{1,0:T(2,128)S(1)} %get-tuple-element.113.refs_2_, f32[1,768]{1,0:T(1,128)S(1)} %get-tuple-element.42.refs_3_.refs_0_, ...), custom_call_target="tpu_custom_call" | custom-call | flops 1610612736 | bytes 3145728 | tf_op jit(solution)/shard_map/sums_pass/pallas_call | solution.py:106
  58.0 0.5 collective-permute-start.11
  58.5 0.0 collective-permute-done.12
  58.6 0.1 slice_add_fusion
  58.7 0.0 copy-start.8
  58.7 2.8 %collective-permute-start.13 = (bf16[128,1152]{1,0:T(8,128)(2,1)S(1)}, bf16[128,1152]{1,0:T(8,128)(2,1)S(1)}, u32[]{:S(2)}, u32[]{:S(2)}) collective-permute-start(bf16[128,1152]{1,0:T(8,128)(2,1)S(1)} %pad_maximum_fusion.4), channel_id=1, source_target_pairs={{0,16},{2,18},{4,20},{6,22},{8,24},{10,26},{12,28},{14,30},{16,0},... | collective-permute-start | bytes 884744 | tf_op jit(solution)/shard_map/ppermute | solution.py:185
  61.6 0.0 collective-permute-done.11
  61.6 0.1 slice_add_fusion.1
  61.6 13.4 %collective-permute-done.13 = bf16[128,1152]{1,0:T(8,128)(2,1)S(1)} collective-permute-done((bf16[128,1152]{1,0:T(8,128)(2,1)S(1)}, bf16[128,1152]{1,0:T(8,128)(2,1)S(1)}, u32[]{:S(2)}, u32[]{:S(2)}) %collective-permute-start.13) | collective-permute-done | bytes 294944 | tf_op jit(solution)/shard_map/ppermute | solution.py:185
  75.1 0.2 fusion.5
  75.3 0.0 copy-done.8
  75.3 0.9 fusion.25
  76.2 0.0 collective-permute-start.15
  76.3 0.0 collective-permute-start.14
  76.3 1.5 %collective-permute-done.15 = bf16[128,1024]{1,0:T(8,128)(2,1)S(1)} collective-permute-done((bf16[128,1024]{1,0:T(8,128)(2,1)S(1)}, bf16[128,1024]{1,0:T(8,128)(2,1)S(1)}, u32[]{:S(2)}, u32[]{:S(2)}) %collective-permute-start.15) | collective-permute-done | bytes 262176 | tf_op jit(solution)/shard_map/ppermute | solution.py:188
  77.8 1.6 %second_pass.2 = (f32[3,4,192]{2,1,0:T(4,128)S(1)}, f32[3,2,192]{2,1,0:T(2,128)S(1)}, f32[3,2,192]{2,1,0:T(2,128)S(1)}) custom-call(bf16[256,1024]{1,0:T(8,128)(2,1)S(1)} %pad_maximum_fusion.1.cents, f32[1,768]{1,0:T(1,128)S(1)} %get-tuple-element.42.refs_3_.refs_0_, f32[1,384]{1,0:T(1,128)S(1)} %get-tuple-element.43.refs_4_.refs_1_, ...), custom_call_target="tpu_custom_call" | custom-call | flops 805306368 | bytes 3145728 | tf_op jit(solution)/shard_map/second_pass/pallas_call | solution.py:147
  79.4 12.2 %collective-permute-done.14 = bf16[128,1024]{1,0:T(8,128)(2,1)} collective-permute-done((bf16[128,1024]{1,0:T(8,128)(2,1)S(1)}, bf16[128,1024]{1,0:T(8,128)(2,1)}, u32[]{:S(2)}, u32[]{:S(2)}) %collective-permute-start.14) | collective-permute-done | bytes 262176 | tf_op jit(solution)/shard_map/ppermute | solution.py:185
  91.6 0.0 collective-permute-start.16
  91.7 1.7 %collective-permute-done.16 = bf16[128,1024]{1,0:T(8,128)(2,1)S(1)} collective-permute-done((bf16[128,1024]{1,0:T(8,128)(2,1)}, bf16[128,1024]{1,0:T(8,128)(2,1)S(1)}, u32[]{:S(2)}, u32[]{:S(2)}) %collective-permute-start.16) | collective-permute-done | bytes 262176 | tf_op jit(solution)/shard_map/ppermute | solution.py:188
  93.3 1.0 pad_maximum_fusion.2.cents
  94.3 1.6 %second_pass.3 = (f32[3,4,192]{2,1,0:T(4,128)S(1)}, f32[3,2,192]{2,1,0:T(2,128)S(1)}, f32[3,2,192]{2,1,0:T(2,128)S(1)}) custom-call(bf16[256,1024]{1,0:T(8,128)(2,1)S(1)} %pad_maximum_fusion.2.cents, f32[1,768]{1,0:T(1,128)S(1)} %get-tuple-element.42.refs_3_.refs_0_, f32[1,384]{1,0:T(1,128)S(1)} %get-tuple-element.43.refs_4_.refs_1_, ...), custom_call_target="tpu_custom_call" | custom-call | flops 805306368 | bytes 3145728 | tf_op jit(solution)/shard_map/second_pass/pallas_call | solution.py:147
  96.1 0.1 stack.73
  96.2 8.1 %all_to_all.11 = f32[8,3,192]{2,1,0:T(4,128)S(1)} all-to-all(f32[8,3,192]{2,1,0:T(4,128)S(1)} %copy.69), channel_id=1, replica_groups={{0,2,4,6,8,10,12,14},{16,18,20,22,24,26,28,30},{1,3,5,7,9,11,13,15},{17..., dimensions={0} | all-to-all | bytes 36864 | tf_op jit(solution)/shard_map/all_to_all | solution.py:229
  104.4 0.6 divide_subtract_fusion
  (76 shorter events, 1.0 us)
Async XLA Ops:
  1.8 12.2 %collective-permute-start.4 = (bf16[192,1024]{1,0:T(8,128)(2,1)S(1)}, bf16[192,1024]{1,0:T(8,128)(2,1)S(1)}, u32[]{:S(2)}, u32[]{:S(2)}) collective-permute-start(bf16[192,1024]{1,0:T(8,128)(2,1)S(1)} %convert_element_type.14.refs_0_), channel_id=1, source_target_pairs={{0,8},{2,10},{4,12},{6,14},{8,0},{10,2},{12,4},{14,6},{16,24},{18,... | collective-permute-start | bytes 1179656 | tf_op jit(solution)/shard_map/ppermute | solution.py:185
  4.9 10.8 %collective-permute-start.6 = (bf16[192,1024]{1,0:T(8,128)(2,1)S(1)}, bf16[192,1024]{1,0:T(8,128)(2,1)S(1)}, u32[]{:S(2)}, u32[]{:S(2)}) collective-permute-start(bf16[192,1024]{1,0:T(8,128)(2,1)S(1)} %convert_element_type.14.refs_0_), channel_id=1, source_target_pairs={{0,4},{2,6},{4,0},{6,2},{8,12},{10,14},{12,8},{14,10},{16,20},{18,... | collective-permute-start | bytes 1179656 | tf_op jit(solution)/shard_map/ppermute | solution.py:185
  6.4 11.0 %collective-permute-start.2 = (bf16[192,1024]{1,0:T(8,128)(2,1)S(1)}, bf16[192,1024]{1,0:T(8,128)(2,1)S(1)}, u32[]{:S(2)}, u32[]{:S(2)}) collective-permute-start(bf16[192,1024]{1,0:T(8,128)(2,1)S(1)} %convert_element_type.14.refs_0_), channel_id=1, source_target_pairs={{0,2},{2,0},{4,6},{6,4},{8,10},{10,8},{12,14},{14,12},{16,18},{18,... | collective-permute-start | bytes 1179656 | tf_op jit(solution)/shard_map/ppermute | solution.py:185
  7.9 0.7 copy-start
  14.0 19.6 %copy-start.2 = (bf16[192,1024]{1,0:T(8,128)(2,1)}, bf16[192,1024]{1,0:T(8,128)(2,1)S(1)}, u32[]{:S(2)}) copy-start(bf16[192,1024]{1,0:T(8,128)(2,1)S(1)} %collective-permute-done.4.refs_3_) | copy-start | bytes 1179652
  14.0 19.6 %collective-permute-start.5 = (bf16[192,1024]{1,0:T(8,128)(2,1)S(1)}, bf16[192,1024]{1,0:T(8,128)(2,1)S(1)}, u32[]{:S(2)}, u32[]{:S(2)}) collective-permute-start(bf16[192,1024]{1,0:T(8,128)(2,1)S(1)} %collective-permute-done.4.refs_3_), channel_id=1, source_target_pairs={{0,2},{2,0},{4,6},{6,4},{8,10},{10,8},{12,14},{14,12},{16,18},{18,... | collective-permute-start | bytes 1179656 | tf_op jit(solution)/shard_map/ppermute | solution.py:185
  15.7 18.0 %copy-start.4 = (bf16[192,1024]{1,0:T(8,128)(2,1)}, bf16[192,1024]{1,0:T(8,128)(2,1)S(1)}, u32[]{:S(2)}) copy-start(bf16[192,1024]{1,0:T(8,128)(2,1)S(1)} %collective-permute-done.6.refs_2_) | copy-start | bytes 1179652
  15.7 17.9 %collective-permute-start.7 = (bf16[192,1024]{1,0:T(8,128)(2,1)S(1)}, bf16[192,1024]{1,0:T(8,128)(2,1)S(1)}, u32[]{:S(2)}, u32[]{:S(2)}) collective-permute-start(bf16[192,1024]{1,0:T(8,128)(2,1)S(1)} %collective-permute-done.6.refs_2_), channel_id=1, source_target_pairs={{0,8},{2,10},{4,12},{6,14},{8,0},{10,2},{12,4},{14,6},{16,24},{18,... | collective-permute-start | bytes 1179656 | tf_op jit(solution)/shard_map/ppermute | solution.py:185
  17.5 16.1 %collective-permute-start.3 = (bf16[192,1024]{1,0:T(8,128)(2,1)S(1)}, bf16[192,1024]{1,0:T(8,128)(2,1)S(1)}, u32[]{:S(2)}, u32[]{:S(2)}) collective-permute-start(bf16[192,1024]{1,0:T(8,128)(2,1)S(1)} %collective-permute-done.2.refs_1_), channel_id=1, source_target_pairs={{0,4},{2,6},{4,0},{6,2},{8,12},{10,14},{12,8},{14,10},{16,20},{18,... | collective-permute-start | bytes 1179656 | tf_op jit(solution)/shard_map/ppermute | solution.py:185
  18.8 0.8 copy-start.6
  20.6 13.0 %collective-permute-start.1 = (bf16[128,1024]{1,0:T(8,128)(2,1)S(1)}, bf16[128,1024]{1,0:T(8,128)(2,1)S(1)}, u32[]{:S(2)}, u32[]{:S(2)}) collective-permute-start(bf16[128,1024]{1,0:T(8,128)(2,1)S(1)} %convert_element_type.13), channel_id=1, source_target_pairs={{0,16},{2,18},{4,20},{6,22},{8,24},{10,26},{12,28},{14,30},{16,0},... | collective-permute-start | bytes 786440 | tf_op jit(solution)/shard_map/ppermute | solution.py:185
  23.3 13.0 %collective-permute-start = (bf16[128,1024]{1,0:T(8,128)(2,1)S(1)}, bf16[128,1024]{1,0:T(8,128)(2,1)S(1)}, u32[]{:S(2)}, u32[]{:S(2)}) collective-permute-start(bf16[128,1024]{1,0:T(8,128)(2,1)S(1)} %convert_element_type.13), channel_id=1, source_target_pairs={{0,1},{1,0},{2,3},{3,2},{4,5},{5,4},{6,7},{7,6},{8,9},{9,8},{10,11... | collective-permute-start | bytes 786440 | tf_op jit(solution)/shard_map/ppermute | solution.py:188
  33.6 2.7 %collective-permute-start.8 = (bf16[128,1024]{1,0:T(8,128)(2,1)S(1)}, bf16[128,1024]{1,0:T(8,128)(2,1)S(1)}, u32[]{:S(2)}, u32[]{:S(2)}) collective-permute-start(bf16[128,1024]{1,0:T(8,128)(2,1)S(1)} %collective-permute-done.1), channel_id=1, source_target_pairs={{0,1},{1,0},{2,3},{3,2},{4,5},{5,4},{6,7},{7,6},{8,9},{9,8},{10,11... | collective-permute-start | bytes 786440 | tf_op jit(solution)/shard_map/ppermute | solution.py:188
  33.7 7.3 %collective-permute-start.10 = (bf16[96,1024]{1,0:T(8,128)(2,1)S(1)}, bf16[96,1024]{1,0:T(8,128)(2,1)S(1)}, u32[]{:S(2)}, u32[]{:S(2)}) collective-permute-start(bf16[96,1024]{1,0:T(8,128)(2,1)S(1)} %slice.403), channel_id=1, source_target_pairs={{0,4},{2,6},{4,0},{6,2},{8,12},{10,14},{12,8},{14,10},{16,20},{18,... | collective-permute-start | bytes 589832 | tf_op jit(solution)/shard_map/ppermute | solution.py:185
  33.8 3.5 %copy-start.1 = (bf16[192,1024]{1,0:T(8,128)(2,1)S(1)}, bf16[192,1024]{1,0:T(8,128)(2,1)}, u32[]{:S(2)}) copy-start(bf16[192,1024]{1,0:T(8,128)(2,1)} %copy-done) | copy-start | bytes 1179652
  33.9 3.5 %copy-start.3 = (bf16[192,1024]{1,0:T(8,128)(2,1)S(1)}, bf16[192,1024]{1,0:T(8,128)(2,1)}, u32[]{:S(2)}) copy-start(bf16[192,1024]{1,0:T(8,128)(2,1)} %copy-done.2) | copy-start | bytes 1179652
  33.9 3.5 %copy-start.5 = (bf16[192,1024]{1,0:T(8,128)(2,1)S(1)}, bf16[192,1024]{1,0:T(8,128)(2,1)}, u32[]{:S(2)}) copy-start(bf16[192,1024]{1,0:T(8,128)(2,1)} %copy-done.4) | copy-start | bytes 1179652
  33.9 3.5 %copy-start.7 = (bf16[192,1024]{1,0:T(8,128)(2,1)S(1)}, bf16[192,1024]{1,0:T(8,128)(2,1)}, u32[]{:S(2)}) copy-start(bf16[192,1024]{1,0:T(8,128)(2,1)} %copy-done.6) | copy-start | bytes 1179652
  33.9 7.7 %collective-permute-start.9 = (bf16[96,1024]{1,0:T(8,128)(2,1)S(1)}, bf16[96,1024]{1,0:T(8,128)(2,1)S(1)}, u32[]{:S(2)}, u32[]{:S(2)}) collective-permute-start(bf16[96,1024]{1,0:T(8,128)(2,1)S(1)} %slice.402), channel_id=1, source_target_pairs={{0,2},{2,0},{4,6},{6,4},{8,10},{10,8},{12,14},{14,12},{16,18},{18,... | collective-permute-start | bytes 589832 | tf_op jit(solution)/shard_map/ppermute | solution.py:185
  55.1 3.5 %collective-permute-start.12 = (f32[128,1152]{1,0:T(8,128)S(1)}, f32[128,1152]{1,0:T(8,128)S(1)}, u32[]{:S(2)}, u32[]{:S(2)}) collective-permute-start(f32[128,1152]{1,0:T(8,128)S(1)} %slice.455), channel_id=1, source_target_pairs={{0,1},{1,0},{2,3},{3,2},{4,5},{5,4},{6,7},{7,6},{8,9},{9,8},{10,11... | collective-permute-start | bytes 1769480 | tf_op jit(solution)/shard_map/ppermute | solution.py:188
  58.0 3.6 %collective-permute-start.11 = (f32[128,1152]{1,0:T(8,128)S(1)}, f32[128,1152]{1,0:T(8,128)S(1)}, u32[]{:S(2)}, u32[]{:S(2)}) collective-permute-start(f32[128,1152]{1,0:T(8,128)S(1)} %slice.452), channel_id=1, source_target_pairs={{0,1},{1,0},{2,3},{3,2},{4,5},{5,4},{6,7},{7,6},{8,9},{9,8},{10,11... | collective-permute-start | bytes 1769480 | tf_op jit(solution)/shard_map/ppermute | solution.py:188
  58.7 16.6 %copy-start.8 = (f32[128,1024]{1,0:T(8,128)S(1)}, f32[128,1024]{1,0:T(8,128)}, u32[]{:S(2)}) copy-start(f32[128,1024]{1,0:T(8,128)} %param.3) | copy-start | bytes 1572868
  58.7 16.4 %collective-permute-start.13 = (bf16[128,1152]{1,0:T(8,128)(2,1)S(1)}, bf16[128,1152]{1,0:T(8,128)(2,1)S(1)}, u32[]{:S(2)}, u32[]{:S(2)}) collective-permute-start(bf16[128,1152]{1,0:T(8,128)(2,1)S(1)} %pad_maximum_fusion.4), channel_id=1, source_target_pairs={{0,16},{2,18},{4,20},{6,22},{8,24},{10,26},{12,28},{14,30},{16,0},... | collective-permute-start | bytes 884744 | tf_op jit(solution)/shard_map/ppermute | solution.py:185
  76.2 1.5 %collective-permute-start.15 = (bf16[128,1024]{1,0:T(8,128)(2,1)S(1)}, bf16[128,1024]{1,0:T(8,128)(2,1)S(1)}, u32[]{:S(2)}, u32[]{:S(2)}) collective-permute-start(bf16[128,1024]{1,0:T(8,128)(2,1)S(1)} %get-tuple-element.62), channel_id=1, source_target_pairs={{0,1},{1,0},{2,3},{3,2},{4,5},{5,4},{6,7},{7,6},{8,9},{9,8},{10,11... | collective-permute-start | bytes 786440 | tf_op jit(solution)/shard_map/ppermute | solution.py:188
  76.3 15.3 %collective-permute-start.14 = (bf16[128,1024]{1,0:T(8,128)(2,1)S(1)}, bf16[128,1024]{1,0:T(8,128)(2,1)}, u32[]{:S(2)}, u32[]{:S(2)}) collective-permute-start(bf16[128,1024]{1,0:T(8,128)(2,1)S(1)} %get-tuple-element.62), channel_id=1, source_target_pairs={{0,16},{2,18},{4,20},{6,22},{8,24},{10,26},{12,28},{14,30},{16,0},... | collective-permute-start | bytes 786440 | tf_op jit(solution)/shard_map/ppermute | solution.py:185
  91.6 1.7 %collective-permute-start.16 = (bf16[128,1024]{1,0:T(8,128)(2,1)}, bf16[128,1024]{1,0:T(8,128)(2,1)S(1)}, u32[]{:S(2)}, u32[]{:S(2)}) collective-permute-start(bf16[128,1024]{1,0:T(8,128)(2,1)} %collective-permute-done.14), channel_id=1, source_target_pairs={{0,1},{1,0},{2,3},{3,2},{4,5},{5,4},{6,7},{7,6},{8,9},{9,8},{10,11... | collective-permute-start | bytes 786440 | tf_op jit(solution)/shard_map/ppermute | solution.py:188

commit v4 on v3

--- a/solution.py
+++ b/solution.py
@@ -12,7 +12,7 @@
 CUBE = 8
 GROUPS = ((0, 1, 2, 4), (3, 5), (6, 7))
 VMEM = pl.BlockSpec(memory_space=pltpu.VMEM)
-GRANT = 20 << 20
+GRANT = 12 << 20
 
 
 def params():
@@ -236,7 +236,7 @@
 
     def on_device(embeddings, centroids):
         shard, width = embeddings.shape
-        half = shard // 2
+        third = shard // 3
         chunk = {0: embeddings.astype(jnp.bfloat16)}
         for bit in (1, 2, 4):
             chunk[bit] = flip(chunk[0], bit)
@@ -245,10 +245,14 @@
         chunk[3] = flip(chunk[1], 2)
         chunk[6] = flip(chunk[2], 4)
         chunk[5] = flip(chunk[4], 1)
-        parts = (flip(chunk[6][:half], 1), flip(chunk[5][half:], 2))
+        parts = (
+            flip(chunk[6][:third], 1),
+            flip(chunk[5][third : 2 * third], 2),
+            flip(chunk[3][2 * third :], 4),
+        )
         near = gather_cent(near_own)
         n_near = near.shape[0]
-        far_own = hold(far_own, chunk[3], chunk[5], chunk[6])[0]
+        far_own = hold(far_own, chunk[1], chunk[2], chunk[4])[0]
         piece = jnp.concatenate([near, gather_cent(far_own)], axis=0)
         passes = [first_pass(piece, [chunk[b] for b in bits]) for bits in GROUPS[:2]]
         parts, passes = hold(parts, passes)

time: 105 us -> 105 us (level)
  waiting for transfers between devices: 47.1 us -> 43.3 us
  blocking collectives: 17 us -> 18.9 us
    ppermute x11 -> x12, waiting for transfers between devices: 43.9 us -> 40.1 us  [flip(): return lax.ppermute(value, 'dp', [(i, i ^ bits) for i in range(n_dp)])]
    all_to_all x2, blocking collectives: 17 us -> 18.9 us  [exchange(): return lax.all_to_all(value, 'dp', 0, 0, axis_index_groups=groups)]
    ppermute x11 -> x12, starting transfers between devices: 18.6 us -> 17.9 us  [flip(): return lax.ppermute(value, 'dp', [(i, i ^ bits) for i in range(n_dp)])]
  transfers between devices with their start and end apart: 17 -> 18, of which waited for: 9 -> 7; matrix products, arithmetic and copies ran while one was open for 1% -> 2% of each run, Pallas kernels for 7% -> 7%
where the time goes in v4:
time: 105 us; the launch traced here: 104 us
  waiting for transfers between devices  43.3 us (41%)
  starting transfers between devices  19 us (18%)
  blocking collectives  18.9 us (18%)
  Pallas kernels  12.5 us (12%)
  other arithmetic  6.83 us (7%)
  local copies, waits for them, and re-layouts  2.49 us (2%)
  between operations  1.13 us (1%)
    ppermute x12, waiting for transfers between devices, flip(): return lax.ppermute(value, 'dp', [(i, i ^ bits) for i in range(n_dp)])  40.1 us
    all_to_all x2, blocking collectives, exchange(): return lax.all_to_all(value, 'dp', 0, 0, axis_index_groups=groups)  18.9 us
    ppermute x12, starting transfers between devices, flip(): return lax.ppermute(value, 'dp', [(i, i ^ bits) for i in range(n_dp)])  17.9 us
    pallas_call x2, Pallas kernels, sums_pass(): pl.pallas_call(functools.partial(sums_kernel, first, last, n), out_shape=...  5.55 us
    pallas_call x3, Pallas kernels, first_pass(): pl.pallas_call(functools.partial(first_kernel, n, shard), out_shape=(jax....  3.75 us
    ppermute x6, waiting for transfers between devices, across(): return lax.ppermute(value, 'cent', [(i, i ^ bits) for i in range(n_cent)])  3.22 us
    pallas_call x2, Pallas kernels, second_pass(): pl.pallas_call(functools.partial(second_kernel, shard, n), out_shape=tupl...  3.16 us
  transfers between devices with their start and end apart: 18, of which 7 were waited for; matrix products, arithmetic and copies ran while one was open for 2% of the time, Pallas kernels for 7%

profile of v4, /device:TPU:0, one launch (start us, length us, event | category | flops | bytes accessed | tf_op | source)
XLA Modules:
  0.0 104.2 jit_solution(17361884938251426240)
XLA Ops:
  0.6 1.2 %convert_element_type.14.refs_0_ = bf16[192,1024]{1,0:T(8,128)(2,1)S(1)} convert(f32[192,1024]{1,0:T(8,128)} %param.2) | non-fusion elementwise | flops 196608 | bytes 1179648 | tf_op jit(solution)/shard_map/convert_element_type | solution.py:240
  1.8 3.0 %collective-permute-start.2 = (bf16[192,1024]{1,0:T(8,128)(2,1)S(1)}, bf16[192,1024]{1,0:T(8,128)(2,1)S(1)}, u32[]{:S(2)}, u32[]{:S(2)}) collective-permute-start(bf16[192,1024]{1,0:T(8,128)(2,1)S(1)} %convert_element_type.14.refs_0_), channel_id=1, source_target_pairs={{0,2},{2,0},{4,6},{6,4},{8,10},{10,8},{12,14},{14,12},{16,18},{18,... | collective-permute-start | bytes 1179656 | tf_op jit(solution)/shard_map/ppermute | solution.py:185
  4.8 1.5 %collective-permute-start.3 = (bf16[192,1024]{1,0:T(8,128)(2,1)S(1)}, bf16[192,1024]{1,0:T(8,128)(2,1)S(1)}, u32[]{:S(2)}, u32[]{:S(2)}) collective-permute-start(bf16[192,1024]{1,0:T(8,128)(2,1)S(1)} %convert_element_type.14.refs_0_), channel_id=1, source_target_pairs={{0,4},{2,6},{4,0},{6,2},{8,12},{10,14},{12,8},{14,10},{16,20},{18,... | collective-permute-start | bytes 1179656 | tf_op jit(solution)/shard_map/ppermute | solution.py:185
  6.3 1.6 %collective-permute-start.4 = (bf16[192,1024]{1,0:T(8,128)(2,1)S(1)}, bf16[192,1024]{1,0:T(8,128)(2,1)S(1)}, u32[]{:S(2)}, u32[]{:S(2)}) collective-permute-start(bf16[192,1024]{1,0:T(8,128)(2,1)S(1)} %convert_element_type.14.refs_0_), channel_id=1, source_target_pairs={{0,8},{2,10},{4,12},{6,14},{8,0},{10,2},{12,4},{14,6},{16,24},{18,... | collective-permute-start | bytes 1179656 | tf_op jit(solution)/shard_map/ppermute | solution.py:185
  7.9 1.1 %convert_element_type.13 = bf16[128,1024]{1,0:T(8,128)(2,1)S(1)} convert(f32[128,1024]{1,0:T(8,128)} %param.3) | non-fusion elementwise | flops 131072 | bytes 786432 | tf_op jit(solution)/shard_map/convert_element_type | solution.py:243
  9.0 2.7 %collective-permute-start.1 = (bf16[128,1024]{1,0:T(8,128)(2,1)S(1)}, bf16[128,1024]{1,0:T(8,128)(2,1)S(1)}, u32[]{:S(2)}, u32[]{:S(2)}) collective-permute-start(bf16[128,1024]{1,0:T(8,128)(2,1)S(1)} %convert_element_type.13), channel_id=1, source_target_pairs={{0,16},{2,18},{4,20},{6,22},{8,24},{10,26},{12,28},{14,30},{16,0},... | collective-permute-start | bytes 786440 | tf_op jit(solution)/shard_map/ppermute | solution.py:185
  11.7 2.3 %collective-permute-done.2.refs_1_ = bf16[192,1024]{1,0:T(8,128)(2,1)S(1)} collective-permute-done((bf16[192,1024]{1,0:T(8,128)(2,1)S(1)}, bf16[192,1024]{1,0:T(8,128)(2,1)S(1)}, u32[]{:S(2)}, u32[]{:S(2)}) %collective-permute-start.2) | collective-permute-done | bytes 393248 | tf_op jit(solution)/shard_map/ppermute | solution.py:185
  13.9 1.8 %collective-permute-start.10 = (bf16[192,1024]{1,0:T(8,128)(2,1)S(1)}, bf16[192,1024]{1,0:T(8,128)(2,1)S(1)}, u32[]{:S(2)}, u32[]{:S(2)}) collective-permute-start(bf16[192,1024]{1,0:T(8,128)(2,1)S(1)} %collective-permute-done.2.refs_1_), channel_id=1, source_target_pairs={{0,4},{2,6},{4,0},{6,2},{8,12},{10,14},{12,8},{14,10},{16,20},{18,... | collective-permute-start | bytes 1179656 | tf_op jit(solution)/shard_map/ppermute | solution.py:185
  15.7 0.0 collective-permute-done.3.refs_2_
  15.7 1.6 %collective-permute-start.6 = (bf16[192,1024]{1,0:T(8,128)(2,1)S(1)}, bf16[192,1024]{1,0:T(8,128)(2,1)S(1)}, u32[]{:S(2)}, u32[]{:S(2)}) collective-permute-start(bf16[192,1024]{1,0:T(8,128)(2,1)S(1)} %collective-permute-done.3.refs_2_), channel_id=1, source_target_pairs={{0,8},{2,10},{4,12},{6,14},{8,0},{10,2},{12,4},{14,6},{16,24},{18,... | collective-permute-start | bytes 1179656 | tf_op jit(solution)/shard_map/ppermute | solution.py:185
  17.3 6.7 %collective-permute-done.4.refs_3_ = bf16[192,1024]{1,0:T(8,128)(2,1)S(1)} collective-permute-done((bf16[192,1024]{1,0:T(8,128)(2,1)S(1)}, bf16[192,1024]{1,0:T(8,128)(2,1)S(1)}, u32[]{:S(2)}, u32[]{:S(2)}) %collective-permute-start.4) | collective-permute-done | bytes 393248 | tf_op jit(solution)/shard_map/ppermute | solution.py:185
  24.0 0.5 collective-permute-start.8
  24.6 0.0 collective-permute-start
  24.6 0.0 collective-permute-done.1
  24.6 0.5 collective-permute-start.5
  25.1 0.0 collective-permute-done.10.refs_0_
  25.1 1.6 %collective-permute-start.11 = (bf16[64,1024]{1,0:T(8,128)(2,1)S(1)}, bf16[64,1024]{1,0:T(8,128)(2,1)S(1)}, u32[]{:S(2)}, u32[]{:S(2)}) collective-permute-start(bf16[64,1024]{1,0:T(8,128)(2,1)S(1)} %slice.408), channel_id=1, source_target_pairs={{0,8},{2,10},{4,12},{6,14},{8,0},{10,2},{12,4},{14,6},{16,24},{18,... | collective-permute-start | bytes 393224 | tf_op jit(solution)/shard_map/ppermute | solution.py:185
  26.7 5.4 %collective-permute-done.6.refs_0_ = bf16[192,1024]{1,0:T(8,128)(2,1)S(1)} collective-permute-done((bf16[192,1024]{1,0:T(8,128)(2,1)S(1)}, bf16[192,1024]{1,0:T(8,128)(2,1)S(1)}, u32[]{:S(2)}, u32[]{:S(2)}) %collective-permute-start.6) | collective-permute-done | bytes 393248 | tf_op jit(solution)/shard_map/ppermute | solution.py:185
  32.1 0.6 collective-permute-start.7
  32.7 0.0 collective-permute-done.8.refs_1_
  32.7 0.4 collective-permute-start.9
  33.1 0.0 collective-permute-done
  33.1 0.0 collective-permute-done.5
  33.1 0.0 copy-done
  33.1 0.0 copy-done.2
  33.1 1.0 pad_maximum_fusion.cents
  34.2 0.0 copy-start.1
  34.2 1.0 copy-done.1
  35.2 1.0 copy-done.3
  36.2 1.7 %first_pass.3 = (f32[2,4,192]{2,1,0:T(4,128)S(1)}, f32[1,768]{1,0:T(1,128)S(1)}, bf16[768,1024]{1,0:T(8,128)(2,1)S(1)}) custom-call(bf16[512,1024]{1,0:T(8,128)(2,1)S(1)} %pad_maximum_fusion.cents, bf16[192,1024]{1,0:T(8,128)(2,1)S(1)} %convert_element_type.14.refs_0_, bf16[192,1024]{1,0:T(8,128)(2,1)S(1)} %collective-permute-done.2.refs_1_, ...), custom_call_target="tpu_custom_call" | custom-call | flops 805306368 | bytes 1572864 | tf_op jit(solution)/shard_map/first_pass/pallas_call | solution.py:67
  37.9 1.0 first_pass.4
  38.9 0.0 collective-permute-done.11
  38.9 0.0 collective-permute-done.7
  38.9 0.0 collective-permute-done.9
  39.1 1.0 first_pass.5
  40.2 10.8 %all_to_all.10 = f32[8,2,8,192]{3,2,1,0:T(8,128)S(1)} all-to-all(f32[8,2,8,192]{3,2,1,0:T(8,128)S(1)} %broadcast_in_dim.2), channel_id=1, replica_groups={{0,2,4,6,8,10,12,14},{16,18,20,22,24,26,28,30},{1,3,5,7,9,11,13,15},{17..., dimensions={0} | all-to-all | bytes 196608 | tf_op jit(solution)/shard_map/all_to_all | solution.py:229
  51.4 0.1 pad_maximum_fusion.8
  51.5 0.1 pad_maximum_fusion.7.refs_0_
  51.5 2.8 %sums_pass.3 = f32[256,1152]{1,0:T(8,128)S(1)} custom-call(bf16[512,1024]{1,0:T(8,128)(2,1)S(1)} %pad_maximum_fusion.cents, f32[2,768]{1,0:T(2,128)S(1)} %pad_maximum_fusion.7.refs_0_, f32[2,384]{1,0:T(2,128)S(1)} %get-tuple-element.114.refs_1_, f32[2,384]{1,0:T(2,128)S(1)} %get-tuple-element.115.refs_2_, f32[1,768]{1,0:T(1,128)S(1)} %get-tuple-element.44.refs_3_.refs_0_, ...), custom_call_target="tpu_custom_call" | custom-call | flops 1610612736 | bytes 3145728 | tf_op jit(solution)/shard_map/sums_pass/pallas_call | solution.py:106
  54.4 0.1 collective-permute-start.13
  54.5 2.8 %sums_pass.2 = f32[256,1152]{1,0:T(8,128)S(1)} custom-call(bf16[512,1024]{1,0:T(8,128)(2,1)S(1)} %pad_maximum_fusion.cents, f32[2,768]{1,0:T(2,128)S(1)} %pad_maximum_fusion.7.refs_0_, f32[2,384]{1,0:T(2,128)S(1)} %get-tuple-element.114.refs_1_, f32[2,384]{1,0:T(2,128)S(1)} %get-tuple-element.115.refs_2_, f32[1,768]{1,0:T(1,128)S(1)} %get-tuple-element.44.refs_3_.refs_0_, ...), custom_call_target="tpu_custom_call" | custom-call | flops 1610612736 | bytes 3145728 | tf_op jit(solution)/shard_map/sums_pass/pallas_call | solution.py:106
  57.3 0.6 collective-permute-start.12
  57.8 0.0 collective-permute-done.13
  57.8 0.1 slice_add_fusion
  58.0 0.0 copy-start.4
  58.0 2.7 %collective-permute-start.14 = (bf16[128,1152]{1,0:T(8,128)(2,1)S(1)}, bf16[128,1152]{1,0:T(8,128)(2,1)S(1)}, u32[]{:S(2)}, u32[]{:S(2)}) collective-permute-start(bf16[128,1152]{1,0:T(8,128)(2,1)S(1)} %pad_maximum_fusion.4), channel_id=1, source_target_pairs={{0,16},{2,18},{4,20},{6,22},{8,24},{10,26},{12,28},{14,30},{16,0},... | collective-permute-start | bytes 884744 | tf_op jit(solution)/shard_map/ppermute | solution.py:185
  60.7 0.0 collective-permute-done.12
  60.7 0.1 slice_add_fusion.1
  60.8 13.5 %collective-permute-done.14 = bf16[128,1152]{1,0:T(8,128)(2,1)S(1)} collective-permute-done((bf16[128,1152]{1,0:T(8,128)(2,1)S(1)}, bf16[128,1152]{1,0:T(8,128)(2,1)S(1)}, u32[]{:S(2)}, u32[]{:S(2)}) %collective-permute-start.14) | collective-permute-done | bytes 294944 | tf_op jit(solution)/shard_map/ppermute | solution.py:185
  74.3 0.2 fusion.5
  74.5 0.0 copy-done.4
  74.5 1.0 fusion.25
  75.4 0.0 collective-permute-start.16
  75.5 0.0 collective-permute-start.15
  75.5 1.5 %collective-permute-done.16 = bf16[128,1024]{1,0:T(8,128)(2,1)S(1)} collective-permute-done((bf16[128,1024]{1,0:T(8,128)(2,1)S(1)}, bf16[128,1024]{1,0:T(8,128)(2,1)S(1)}, u32[]{:S(2)}, u32[]{:S(2)}) %collective-permute-start.16) | collective-permute-done | bytes 262176 | tf_op jit(solution)/shard_map/ppermute | solution.py:188
  77.0 1.6 %second_pass.2 = (f32[3,4,192]{2,1,0:T(4,128)S(1)}, f32[3,2,192]{2,1,0:T(2,128)S(1)}, f32[3,2,192]{2,1,0:T(2,128)S(1)}) custom-call(bf16[256,1024]{1,0:T(8,128)(2,1)S(1)} %pad_maximum_fusion.1.cents, f32[1,768]{1,0:T(1,128)S(1)} %get-tuple-element.44.refs_3_.refs_0_, f32[1,384]{1,0:T(1,128)S(1)} %get-tuple-element.45.refs_4_.refs_1_, ...), custom_call_target="tpu_custom_call" | custom-call | flops 805306368 | bytes 3145728 | tf_op jit(solution)/shard_map/second_pass/pallas_call | solution.py:147
  78.6 12.2 %collective-permute-done.15 = bf16[128,1024]{1,0:T(8,128)(2,1)} collective-permute-done((bf16[128,1024]{1,0:T(8,128)(2,1)S(1)}, bf16[128,1024]{1,0:T(8,128)(2,1)}, u32[]{:S(2)}, u32[]{:S(2)}) %collective-permute-start.15) | collective-permute-done | bytes 262176 | tf_op jit(solution)/shard_map/ppermute | solution.py:185
  90.8 0.0 collective-permute-start.17
  90.9 1.7 %collective-permute-done.17 = bf16[128,1024]{1,0:T(8,128)(2,1)S(1)} collective-permute-done((bf16[128,1024]{1,0:T(8,128)(2,1)}, bf16[128,1024]{1,0:T(8,128)(2,1)S(1)}, u32[]{:S(2)}, u32[]{:S(2)}) %collective-permute-start.17) | collective-permute-done | bytes 262176 | tf_op jit(solution)/shard_map/ppermute | solution.py:188
  92.5 1.0 pad_maximum_fusion.2.cents
  93.5 1.6 %second_pass.3 = (f32[3,4,192]{2,1,0:T(4,128)S(1)}, f32[3,2,192]{2,1,0:T(2,128)S(1)}, f32[3,2,192]{2,1,0:T(2,128)S(1)}) custom-call(bf16[256,1024]{1,0:T(8,128)(2,1)S(1)} %pad_maximum_fusion.2.cents, f32[1,768]{1,0:T(1,128)S(1)} %get-tuple-element.44.refs_3_.refs_0_, f32[1,384]{1,0:T(1,128)S(1)} %get-tuple-element.45.refs_4_.refs_1_, ...), custom_call_target="tpu_custom_call" | custom-call | flops 805306368 | bytes 3145728 | tf_op jit(solution)/shard_map/second_pass/pallas_call | solution.py:147
  95.3 0.1 stack.73
  95.4 8.1 %all_to_all.11 = f32[8,3,192]{2,1,0:T(4,128)S(1)} all-to-all(f32[8,3,192]{2,1,0:T(4,128)S(1)} %copy.69), channel_id=1, replica_groups={{0,2,4,6,8,10,12,14},{16,18,20,22,24,26,28,30},{1,3,5,7,9,11,13,15},{17..., dimensions={0} | all-to-all | bytes 36864 | tf_op jit(solution)/shard_map/all_to_all | solution.py:229
  103.6 0.6 divide_subtract_fusion
  (71 shorter events, 1.0 us)
Async XLA Ops:
  1.8 12.1 %collective-permute-start.2 = (bf16[192,1024]{1,0:T(8,128)(2,1)S(1)}, bf16[192,1024]{1,0:T(8,128)(2,1)S(1)}, u32[]{:S(2)}, u32[]{:S(2)}) collective-permute-start(bf16[192,1024]{1,0:T(8,128)(2,1)S(1)} %convert_element_type.14.refs_0_), channel_id=1, source_target_pairs={{0,2},{2,0},{4,6},{6,4},{8,10},{10,8},{12,14},{14,12},{16,18},{18,... | collective-permute-start | bytes 1179656 | tf_op jit(solution)/shard_map/ppermute | solution.py:185
  4.8 10.9 %collective-permute-start.3 = (bf16[192,1024]{1,0:T(8,128)(2,1)S(1)}, bf16[192,1024]{1,0:T(8,128)(2,1)S(1)}, u32[]{:S(2)}, u32[]{:S(2)}) collective-permute-start(bf16[192,1024]{1,0:T(8,128)(2,1)S(1)} %convert_element_type.14.refs_0_), channel_id=1, source_target_pairs={{0,4},{2,6},{4,0},{6,2},{8,12},{10,14},{12,8},{14,10},{16,20},{18,... | collective-permute-start | bytes 1179656 | tf_op jit(solution)/shard_map/ppermute | solution.py:185
  6.3 17.7 %collective-permute-start.4 = (bf16[192,1024]{1,0:T(8,128)(2,1)S(1)}, bf16[192,1024]{1,0:T(8,128)(2,1)S(1)}, u32[]{:S(2)}, u32[]{:S(2)}) collective-permute-start(bf16[192,1024]{1,0:T(8,128)(2,1)S(1)} %convert_element_type.14.refs_0_), channel_id=1, source_target_pairs={{0,8},{2,10},{4,12},{6,14},{8,0},{10,2},{12,4},{14,6},{16,24},{18,... | collective-permute-start | bytes 1179656 | tf_op jit(solution)/shard_map/ppermute | solution.py:185
  9.0 15.6 %collective-permute-start.1 = (bf16[128,1024]{1,0:T(8,128)(2,1)S(1)}, bf16[128,1024]{1,0:T(8,128)(2,1)S(1)}, u32[]{:S(2)}, u32[]{:S(2)}) collective-permute-start(bf16[128,1024]{1,0:T(8,128)(2,1)S(1)} %convert_element_type.13), channel_id=1, source_target_pairs={{0,16},{2,18},{4,20},{6,22},{8,24},{10,26},{12,28},{14,30},{16,0},... | collective-permute-start | bytes 786440 | tf_op jit(solution)/shard_map/ppermute | solution.py:185
  13.9 11.1 %collective-permute-start.10 = (bf16[192,1024]{1,0:T(8,128)(2,1)S(1)}, bf16[192,1024]{1,0:T(8,128)(2,1)S(1)}, u32[]{:S(2)}, u32[]{:S(2)}) collective-permute-start(bf16[192,1024]{1,0:T(8,128)(2,1)S(1)} %collective-permute-done.2.refs_1_), channel_id=1, source_target_pairs={{0,4},{2,6},{4,0},{6,2},{8,12},{10,14},{12,8},{14,10},{16,20},{18,... | collective-permute-start | bytes 1179656 | tf_op jit(solution)/shard_map/ppermute | solution.py:185
  15.7 17.4 %copy-start = (bf16[192,1024]{1,0:T(8,128)(2,1)}, bf16[192,1024]{1,0:T(8,128)(2,1)S(1)}, u32[]{:S(2)}) copy-start(bf16[192,1024]{1,0:T(8,128)(2,1)S(1)} %collective-permute-done.3.refs_2_) | copy-start | bytes 1179652
  15.7 16.4 %collective-permute-start.6 = (bf16[192,1024]{1,0:T(8,128)(2,1)S(1)}, bf16[192,1024]{1,0:T(8,128)(2,1)S(1)}, u32[]{:S(2)}, u32[]{:S(2)}) collective-permute-start(bf16[192,1024]{1,0:T(8,128)(2,1)S(1)} %collective-permute-done.3.refs_2_), channel_id=1, source_target_pairs={{0,8},{2,10},{4,12},{6,14},{8,0},{10,2},{12,4},{14,6},{16,24},{18,... | collective-permute-start | bytes 1179656 | tf_op jit(solution)/shard_map/ppermute | solution.py:185
  24.0 9.1 %copy-start.2 = (bf16[192,1024]{1,0:T(8,128)(2,1)}, bf16[192,1024]{1,0:T(8,128)(2,1)S(1)}, u32[]{:S(2)}) copy-start(bf16[192,1024]{1,0:T(8,128)(2,1)S(1)} %collective-permute-done.4.refs_3_) | copy-start | bytes 1179652
  24.0 8.7 %collective-permute-start.8 = (bf16[192,1024]{1,0:T(8,128)(2,1)S(1)}, bf16[192,1024]{1,0:T(8,128)(2,1)S(1)}, u32[]{:S(2)}, u32[]{:S(2)}) collective-permute-start(bf16[192,1024]{1,0:T(8,128)(2,1)S(1)} %collective-permute-done.4.refs_3_), channel_id=1, source_target_pairs={{0,2},{2,0},{4,6},{6,4},{8,10},{10,8},{12,14},{14,12},{16,18},{18,... | collective-permute-start | bytes 1179656 | tf_op jit(solution)/shard_map/ppermute | solution.py:185
  24.6 8.6 %collective-permute-start = (bf16[128,1024]{1,0:T(8,128)(2,1)S(1)}, bf16[128,1024]{1,0:T(8,128)(2,1)S(1)}, u32[]{:S(2)}, u32[]{:S(2)}) collective-permute-start(bf16[128,1024]{1,0:T(8,128)(2,1)S(1)} %convert_element_type.13), channel_id=1, source_target_pairs={{0,1},{1,0},{2,3},{3,2},{4,5},{5,4},{6,7},{7,6},{8,9},{9,8},{10,11... | collective-permute-start | bytes 786440 | tf_op jit(solution)/shard_map/ppermute | solution.py:188
  24.6 8.6 %collective-permute-start.5 = (bf16[128,1024]{1,0:T(8,128)(2,1)S(1)}, bf16[128,1024]{1,0:T(8,128)(2,1)}, u32[]{:S(2)}, u32[]{:S(2)}) collective-permute-start(bf16[128,1024]{1,0:T(8,128)(2,1)S(1)} %collective-permute-done.1), channel_id=1, source_target_pairs={{0,1},{1,0},{2,3},{3,2},{4,5},{5,4},{6,7},{7,6},{8,9},{9,8},{10,11... | collective-permute-start | bytes 786440 | tf_op jit(solution)/shard_map/ppermute | solution.py:188
  25.1 13.8 %collective-permute-start.11 = (bf16[64,1024]{1,0:T(8,128)(2,1)S(1)}, bf16[64,1024]{1,0:T(8,128)(2,1)S(1)}, u32[]{:S(2)}, u32[]{:S(2)}) collective-permute-start(bf16[64,1024]{1,0:T(8,128)(2,1)S(1)} %slice.408), channel_id=1, source_target_pairs={{0,8},{2,10},{4,12},{6,14},{8,0},{10,2},{12,4},{14,6},{16,24},{18,... | collective-permute-start | bytes 393224 | tf_op jit(solution)/shard_map/ppermute | solution.py:185
  32.1 6.8 %collective-permute-start.7 = (bf16[64,1024]{1,0:T(8,128)(2,1)S(1)}, bf16[64,1024]{1,0:T(8,128)(2,1)S(1)}, u32[]{:S(2)}, u32[]{:S(2)}) collective-permute-start(bf16[64,1024]{1,0:T(8,128)(2,1)S(1)} %slice.406), channel_id=1, source_target_pairs={{0,2},{2,0},{4,6},{6,4},{8,10},{10,8},{12,14},{14,12},{16,18},{18,... | collective-permute-start | bytes 393224 | tf_op jit(solution)/shard_map/ppermute | solution.py:185
  32.7 6.2 %collective-permute-start.9 = (bf16[64,1024]{1,0:T(8,128)(2,1)S(1)}, bf16[64,1024]{1,0:T(8,128)(2,1)S(1)}, u32[]{:S(2)}, u32[]{:S(2)}) collective-permute-start(bf16[64,1024]{1,0:T(8,128)(2,1)S(1)} %slice.407), channel_id=1, source_target_pairs={{0,4},{2,6},{4,0},{6,2},{8,12},{10,14},{12,8},{14,10},{16,20},{18,... | collective-permute-start | bytes 393224 | tf_op jit(solution)/shard_map/ppermute | solution.py:185
  34.2 1.0 copy-start.1
  35.2 1.0 copy-start.3
  54.4 3.5 %collective-permute-start.13 = (f32[128,1152]{1,0:T(8,128)S(1)}, f32[128,1152]{1,0:T(8,128)S(1)}, u32[]{:S(2)}, u32[]{:S(2)}) collective-permute-start(f32[128,1152]{1,0:T(8,128)S(1)} %slice.460), channel_id=1, source_target_pairs={{0,1},{1,0},{2,3},{3,2},{4,5},{5,4},{6,7},{7,6},{8,9},{9,8},{10,11... | collective-permute-start | bytes 1769480 | tf_op jit(solution)/shard_map/ppermute | solution.py:188
  57.3 3.4 %collective-permute-start.12 = (f32[128,1152]{1,0:T(8,128)S(1)}, f32[128,1152]{1,0:T(8,128)S(1)}, u32[]{:S(2)}, u32[]{:S(2)}) collective-permute-start(f32[128,1152]{1,0:T(8,128)S(1)} %slice.457), channel_id=1, source_target_pairs={{0,1},{1,0},{2,3},{3,2},{4,5},{5,4},{6,7},{7,6},{8,9},{9,8},{10,11... | collective-permute-start | bytes 1769480 | tf_op jit(solution)/shard_map/ppermute | solution.py:188
  58.0 16.5 %copy-start.4 = (f32[128,1024]{1,0:T(8,128)S(1)}, f32[128,1024]{1,0:T(8,128)}, u32[]{:S(2)}) copy-start(f32[128,1024]{1,0:T(8,128)} %param.3) | copy-start | bytes 1572868
  58.0 16.2 %collective-permute-start.14 = (bf16[128,1152]{1,0:T(8,128)(2,1)S(1)}, bf16[128,1152]{1,0:T(8,128)(2,1)S(1)}, u32[]{:S(2)}, u32[]{:S(2)}) collective-permute-start(bf16[128,1152]{1,0:T(8,128)(2,1)S(1)} %pad_maximum_fusion.4), channel_id=1, source_target_pairs={{0,16},{2,18},{4,20},{6,22},{8,24},{10,26},{12,28},{14,30},{16,0},... | collective-permute-start | bytes 884744 | tf_op jit(solution)/shard_map/ppermute | solution.py:185
  75.4 1.5 %collective-permute-start.16 = (bf16[128,1024]{1,0:T(8,128)(2,1)S(1)}, bf16[128,1024]{1,0:T(8,128)(2,1)S(1)}, u32[]{:S(2)}, u32[]{:S(2)}) collective-permute-start(bf16[128,1024]{1,0:T(8,128)(2,1)S(1)} %get-tuple-element.64), channel_id=1, source_target_pairs={{0,1},{1,0},{2,3},{3,2},{4,5},{5,4},{6,7},{7,6},{8,9},{9,8},{10,11... | collective-permute-start | bytes 786440 | tf_op jit(solution)/shard_map/ppermute | solution.py:188
  75.5 15.3 %collective-permute-start.15 = (bf16[128,1024]{1,0:T(8,128)(2,1)S(1)}, bf16[128,1024]{1,0:T(8,128)(2,1)}, u32[]{:S(2)}, u32[]{:S(2)}) collective-permute-start(bf16[128,1024]{1,0:T(8,128)(2,1)S(1)} %get-tuple-element.64), channel_id=1, source_target_pairs={{0,16},{2,18},{4,20},{6,22},{8,24},{10,26},{12,28},{14,30},{16,0},... | collective-permute-start | bytes 786440 | tf_op jit(solution)/shard_map/ppermute | solution.py:185
  90.8 1.7 %collective-permute-start.17 = (bf16[128,1024]{1,0:T(8,128)(2,1)}, bf16[128,1024]{1,0:T(8,128)(2,1)S(1)}, u32[]{:S(2)}, u32[]{:S(2)}) collective-permute-start(bf16[128,1024]{1,0:T(8,128)(2,1)} %collective-permute-done.15), channel_id=1, source_target_pairs={{0,1},{1,0},{2,3},{3,2},{4,5},{5,4},{6,7},{7,6},{8,9},{9,8},{10,11... | collective-permute-start | bytes 786440 | tf_op jit(solution)/shard_map/ppermute | solution.py:188

commit v5 on v3

--- a/solution.py
+++ b/solution.py
@@ -10,9 +10,10 @@
 softness_level = 32.0
 prior_mass = 4.0
 CUBE = 8
-GROUPS = ((0, 1, 2, 4), (3, 5), (6, 7))
+GROUPS = ((0, 1, 2, 4), (3, 5, 6, 7))
 VMEM = pl.BlockSpec(memory_space=pltpu.VMEM)
-GRANT = 20 << 20
+HBM = pl.BlockSpec(memory_space=pltpu.HBM)
+GRANT = 12 << 20
 
 
 def params():
@@ -38,15 +39,38 @@
     return -(row_sq - 2.0 * inner + cent_sq) * (0.5 / softness_level)
 
 
-def first_kernel(n, shard, cents, *refs):
-    chunks = refs[:n]
-    stats_ref, row_sq_ref, rows_ref = refs[n:]
-    for i in range(n):
-        rows_ref[i * shard : (i + 1) * shard, :] = chunks[i][...]
+def fetch(sources, target, sems):
+    copies, at = [], 0
+    for i, source in enumerate(sources):
+        n = source.shape[0]
+        copy = pltpu.make_async_copy(source, target.at[pl.ds(at, n)], sems.at[i])
+        copy.start()
+        copies.append(copy)
+        at += n
+    return copies
+
+
+def first_kernel(n, n_blocks, shard, last, *refs):
+    blocks, chunks, refs = refs[:n_blocks], refs[n_blocks : n_blocks + n], refs[n_blocks + n :]
+    stats_ref, row_sq_ref, rows_ref = refs[:3]
+    sems = refs[-1]
+    cents, copies = blocks[0], []
+    if n_blocks > 1:
+        cents, at = refs[3], 0
+        for block in blocks:
+            cents[at : at + block.shape[0], :] = block[...]
+            at += block.shape[0]
+    if last:
+        for i in range(n):
+            rows_ref[i * shard : (i + 1) * shard, :] = chunks[i][...]
+    else:
+        copies = fetch(chunks, rows_ref, sems)
     piece = cents[...]
     cent_sq = centroid_squares(piece)
     tile = 2 * shard
     for j in range(n // 2):
+        for copy in copies[2 * j : 2 * j + 2]:
+            copy.wait()
         span = slice(j * tile, (j + 1) * tile)
         rows = rows_ref[span, :]
         row_sq = row_squares(rows)
@@ -59,26 +83,33 @@
             stats_ref[1, 2 * j + i : 2 * j + i + 1, :] = total[:, i * shard : (i + 1) * shard]
 
 
-def first_pass(cents, chunks):
-    n = len(chunks)
+def first_pass(blocks, chunks, last=False):
+    n, n_blocks = len(chunks), len(blocks)
     shard, width = chunks[0].shape
-    n_k = cents.shape[0]
+    n_k = sum(b.shape[0] for b in blocks)
     n_rows = n * shard
-    return pl.pallas_call(
-        functools.partial(first_kernel, n, shard),
-        out_shape=(
-            jax.ShapeDtypeStruct((2, n, shard), jnp.float32),
-            jax.ShapeDtypeStruct((1, n_rows), jnp.float32),
-            jax.ShapeDtypeStruct((n_rows, width), jnp.bfloat16),
-        ),
-        in_specs=[VMEM] * (1 + n),
-        out_specs=(VMEM,) * 3,
+    outs = [
+        jax.ShapeDtypeStruct((2, n, shard), jnp.float32),
+        jax.ShapeDtypeStruct((1, n_rows), jnp.float32),
+        jax.ShapeDtypeStruct((n_rows, width), jnp.bfloat16),
+    ]
+    if n_blocks > 1:
+        outs.append(jax.ShapeDtypeStruct((n_k, width), jnp.bfloat16))
+    out = pl.pallas_call(
+        functools.partial(first_kernel, n, n_blocks, shard, last),
+        out_shape=tuple(outs),
+        in_specs=[VMEM] * n_blocks + [VMEM if last else HBM] * n,
+        out_specs=(VMEM,) * len(outs),
+        scratch_shapes=[pltpu.SemaphoreType.DMA((n,))],
         compiler_params=params(),
         cost_estimate=pl.CostEstimate(
-            flops=2 * n_k * n_rows * width, bytes_accessed=2 * n_rows * width, transcendentals=n_k * n_rows
+            flops=(16 if n_blocks > 1 else 2) * n_k * n_rows * width,
+            bytes_accessed=2 * n_rows * width,
+            transcendentals=n_k * n_rows,
         ),
         name="first_pass",
-    )(cents, *chunks)
+    )(*blocks, *chunks)
+    return out[:3], (out[3] if n_blocks > 1 else blocks[0])
 
 
 def sums_kernel(first, last, n, cents, *refs):
@@ -144,7 +175,7 @@
     n = len(rows)
     n_k, width = cents.shape
     n_rows = sum(r.shape[0] for r in rows)
-    return pl.pallas_call(
+    out = pl.pallas_call(
         functools.partial(second_kernel, shard, n),
         out_shape=tuple(jax.ShapeDtypeStruct((3, r.shape[0] // shard, shard), jnp.float32) for r in rows),
         in_specs=[VMEM] * (1 + 2 * n),
@@ -155,6 +186,7 @@
         ),
         name="second_pass",
     )(cents, *row_sqs, *rows)
+    return by_chunk(out)
 
 
 def hold(*values):
@@ -188,11 +220,12 @@
         return lax.ppermute(value, "cent", [(i, i ^ bits) for i in range(n_cent)])
 
     def gather_cent(value):
+        blocks = [value]
         bits = 1
         while bits < n_cent:
-            value = jnp.concatenate([value, across(value, bits)], axis=0)
+            blocks = blocks + [across(b, bits) for b in blocks]
             bits *= 2
-        return value
+        return blocks
 
     def scatter_cent(value):
         bits = n_cent // 2
@@ -236,24 +269,26 @@
 
     def on_device(embeddings, centroids):
         shard, width = embeddings.shape
+        per_device = centroids.shape[0]
+        cuts = [per_device * 3 // 8] if top_bit == CUBE and per_device % 64 == 0 else []
         half = shard // 2
         chunk = {0: embeddings.astype(jnp.bfloat16)}
         for bit in (1, 2, 4):
             chunk[bit] = flip(chunk[0], bit)
         near_own = gather_near(centroids.astype(jnp.bfloat16))
         far_own = flip(near_own, top_bit)
-        chunk[3] = flip(chunk[1], 2)
-        chunk[6] = flip(chunk[2], 4)
+        chunk[3] = jnp.concatenate([flip(chunk[2][:half], 1), flip(chunk[1][half:], 2)], axis=0)
         chunk[5] = flip(chunk[4], 1)
-        parts = (flip(chunk[6][:half], 1), flip(chunk[5][half:], 2))
+        chunk[6] = flip(chunk[4], 2)
+        chunk[7] = flip(chunk[3], 4)
         near = gather_cent(near_own)
-        n_near = near.shape[0]
-        far_own = hold(far_own, chunk[3], chunk[5], chunk[6])[0]
-        piece = jnp.concatenate([near, gather_cent(far_own)], axis=0)
-        passes = [first_pass(piece, [chunk[b] for b in bits]) for bits in GROUPS[:2]]
-        parts, passes = hold(parts, passes)
-        chunk[7] = jnp.concatenate(parts, axis=0)
-        passes.append(first_pass(piece, [chunk[b] for b in GROUPS[2]]))
+        n_near = len(near) * near_own.shape[0]
+        far_own = hold(far_own, chunk[1], chunk[2], chunk[4])[0]
+        done, piece = first_pass(near + gather_cent(far_own), [chunk[b] for b in GROUPS[0]])
+        chunk[7], done = hold(chunk[7], done)
+        passes = [done]
+        for bits in GROUPS[1:]:
+            passes.append(first_pass([piece], [chunk[b] for b in bits], bits == GROUPS[-1])[0])
         local, row_sqs, rows = zip(*passes)
 
         stats = by_position(by_chunk(local))
@@ -268,18 +303,28 @@
         coarse = lax.reduce_precision(count, 8, 7)
         lane = lax.broadcasted_iota(jnp.int32, count.shape, 1)
         far = jnp.concatenate([far[:, :width], jnp.where(lane < 64, coarse, count - coarse)], axis=1)
-        far = flip(far.astype(jnp.bfloat16), top_bit).astype(jnp.float32)
+        far = [flip(p, top_bit) for p in jnp.split(far.astype(jnp.bfloat16), cuts, axis=0)]
         near = scatter_cent(sums_pass(piece, final, row_sqs, rows, 0, n_near))
-        counts = near[:, width : width + 1] + (far[:, width : width + 1] + far[:, width + 64 : width + 65])
-        sums = scatter_near(jnp.concatenate([near[:, :width] + far[:, :width], jnp.broadcast_to(counts, count.shape)], axis=1))
-        updated = (sums[:, :width] + prior_mass * centroids) / (sums[:, width : width + 1] + prior_mass)
-
-        near_own = gather_near(updated.astype(jnp.bfloat16))
-        far_own = flip(near_own, top_bit)
-        near = second_pass(gather_cent(near_own), row_sqs, rows, shard)
-        far_own, near = hold(far_own, near)
-        far = second_pass(gather_cent(far_own), row_sqs, rows, shard)
-        stats = merge(by_chunk(near), by_chunk(far))
+        updated, near_own = [], []
+        for p, (here, there) in enumerate(zip(jnp.split(near, cuts, axis=0), far)):
+            if p:
+                there = hold(there, near_own[-1])[0]
+            there = there.astype(jnp.float32)
+            counts = there[:, width : width + 1] + there[:, width + 64 : width + 65]
+            there = jnp.concatenate([there[:, :width], jnp.broadcast_to(counts, (there.shape[0], 128))], axis=1)
+            sums = scatter_near(here + there)
+            at = cuts[0] if p else 0
+            prior = prior_mass * centroids[at : at + sums.shape[0]]
+            updated.append((sums[:, :width] + prior) / (sums[:, width : width + 1] + prior_mass))
+            near_own.append(gather_near(updated[-1].astype(jnp.bfloat16)))
+        far_own = [flip(p, top_bit) for p in near_own]
+        near = [b for p in near_own for b in gather_cent(p)]
+        stats = [second_pass(jnp.concatenate(near, axis=0), row_sqs, rows, shard)]
+        for p in far_own:
+            p, stats[-1] = hold(p, stats[-1]) if p is far_own[-1] else (p, stats[-1])
+            stats.append(second_pass(jnp.concatenate(gather_cent(p), axis=0), row_sqs, rows, shard))
+        stats = functools.reduce(merge, stats)
+        updated = jnp.concatenate(updated, axis=0)
         stats = to_owner(by_position(stats))
         drop = stats[:, 0] - jnp.max(stats[:, 0], axis=0)
         factor = jnp.exp(drop)

time: 105 us -> 99.4 us (0.947)
  blocking collectives: 17 us -> 10.8 us
  waiting for transfers between devices: 47.1 us -> 42.8 us
  starting transfers between devices: 19.3 us -> 23.4 us
  other arithmetic: 5.84 us -> 4.43 us
  Pallas kernels: 12.5 us -> 13.8 us
    ppermute x11 -> x13, waiting for transfers between devices: 43.9 us -> 37.4 us  [flip(): return lax.ppermute(value, 'dp', [(i, i ^ bits) for i in range(n_dp)])]
    all_to_all x2 -> x1, blocking collectives: 17 us -> 10.8 us  [exchange(): return lax.all_to_all(value, 'dp', 0, 0, axis_index_groups=groups)]
    all_to_all x0 -> x1, waiting for transfers between devices: none -> 4.81 us  [exchange(): return lax.all_to_all(value, 'dp', 0, 0, axis_index_groups=groups)]
    all_to_all x0 -> x1, starting transfers between devices: none -> 3.33 us  [exchange(): return lax.all_to_all(value, 'dp', 0, 0, axis_index_groups=groups)]
    ppermute x6 -> x8, waiting for transfers between devices: 3.22 us -> 0.63 us  [across(): return lax.ppermute(value, 'cent', [(i, i ^ bits) for i in range(n_cent)])]
    unnamed x27 -> x8, local copies, waits for them, and re-layouts: 1.6 us -> 0.06 us
    slice x2 -> x4, local copies, waits for them, and re-layouts: 0.03 us -> 1.44 us  [the longest x1 0.7 us: on_device(): chunk[1][half:]]
    pallas_call x3 -> x2, Pallas kernels: 3.77 us -> 4.84 us  [first_pass(): pl.pallas_call(functools.partial(first_kernel, n, n_blocks, shard, last),...]
  transfers between devices with their start and end apart: 17 -> 22, of which waited for: 9 -> 10; matrix products, arithmetic and copies ran while one was open for 1% -> 4% of each run, Pallas kernels for 7% -> 8%
where the time goes in v5:
time: 99.4 us; the launch traced here: 99.1 us
  waiting for transfers between devices  42.8 us (43%)
  starting transfers between devices  23.4 us (24%)
  Pallas kernels  13.8 us (14%)
  blocking collectives  10.8 us (11%)
  other arithmetic  4.43 us (4%)
  local copies, waits for them, and re-layouts  2.63 us (3%)
  between operations  1.22 us (1%)
    ppermute x13, waiting for transfers between devices, flip(): return lax.ppermute(value, 'dp', [(i, i ^ bits) for i in range(n_dp)])  37.4 us
    ppermute x13, starting transfers between devices, flip(): return lax.ppermute(value, 'dp', [(i, i ^ bits) for i in range(n_dp)])  18.8 us
    all_to_all x1, blocking collectives, exchange(): return lax.all_to_all(value, 'dp', 0, 0, axis_index_groups=groups)  10.8 us
    pallas_call x2, Pallas kernels, first_pass(): pl.pallas_call(functools.partial(first_kernel, n, n_blocks, shard, last),...  4.84 us
    pallas_call x2, Pallas kernels, sums_pass(): pl.pallas_call(functools.partial(sums_kernel, first, last, n), out_shape=...  4.81 us
    all_to_all x1, waiting for transfers between devices, exchange(): return lax.all_to_all(value, 'dp', 0, 0, axis_index_groups=groups)  4.81 us
    pallas_call x3, Pallas kernels, second_pass(): pl.pallas_call(functools.partial(second_kernel, shard, n), out_shape=tupl...  4.1 us
    all_to_all x1, starting transfers between devices, exchange(): return lax.all_to_all(value, 'dp', 0, 0, axis_index_groups=groups)  3.33 us
  transfers between devices with their start and end apart: 22, of which 10 were waited for; matrix products, arithmetic and copies ran while one was open for 4% of the time, Pallas kernels for 8%

profile of v5, /device:TPU:0, one launch (start us, length us, event | category | flops | bytes accessed | tf_op | source)
XLA Modules:
  0.0 99.1 jit_solution(18111060526320819216)
XLA Ops:
  0.6 1.2 %convert_element_type.20.refs_4_ = bf16[192,1024]{1,0:T(8,128)(2,1)S(1)} convert(f32[192,1024]{1,0:T(8,128)} %param.2) | non-fusion elementwise | flops 196608 | bytes 1179648 | tf_op jit(solution)/shard_map/convert_element_type | solution.py:275
  1.9 3.0 %collective-permute-start.3 = (bf16[192,1024]{1,0:T(8,128)(2,1)S(1)}, bf16[192,1024]{1,0:T(8,128)(2,1)S(1)}, u32[]{:S(2)}, u32[]{:S(2)}) collective-permute-start(bf16[192,1024]{1,0:T(8,128)(2,1)S(1)} %convert_element_type.20.refs_4_), channel_id=1, source_target_pairs={{0,4},{2,6},{4,0},{6,2},{8,12},{10,14},{12,8},{14,10},{16,20},{18,... | collective-permute-start | bytes 1179656 | tf_op jit(solution)/shard_map/ppermute | solution.py:217
  4.9 1.5 %collective-permute-start.2 = (bf16[192,1024]{1,0:T(8,128)(2,1)S(1)}, bf16[192,1024]{1,0:T(8,128)(2,1)S(1)}, u32[]{:S(2)}, u32[]{:S(2)}) collective-permute-start(bf16[192,1024]{1,0:T(8,128)(2,1)S(1)} %convert_element_type.20.refs_4_), channel_id=1, source_target_pairs={{0,2},{2,0},{4,6},{6,4},{8,10},{10,8},{12,14},{14,12},{16,18},{18,... | collective-permute-start | bytes 1179656 | tf_op jit(solution)/shard_map/ppermute | solution.py:217
  6.4 1.6 %collective-permute-start.4 = (bf16[192,1024]{1,0:T(8,128)(2,1)S(1)}, bf16[192,1024]{1,0:T(8,128)(2,1)S(1)}, u32[]{:S(2)}, u32[]{:S(2)}) collective-permute-start(bf16[192,1024]{1,0:T(8,128)(2,1)S(1)} %convert_element_type.20.refs_4_), channel_id=1, source_target_pairs={{0,8},{2,10},{4,12},{6,14},{8,0},{10,2},{12,4},{14,6},{16,24},{18,... | collective-permute-start | bytes 1179656 | tf_op jit(solution)/shard_map/ppermute | solution.py:217
  8.0 2.7 %collective-permute-start.1 = (bf16[128,1024]{1,0:T(8,128)(2,1)S(1)}, bf16[128,1024]{1,0:T(8,128)(2,1)S(1)}, u32[]{:S(2)}, u32[]{:S(2)}) collective-permute-start(bf16[128,1024]{1,0:T(8,128)(2,1)S(1)} %convert_element_type.19.refs_0_), channel_id=1, source_target_pairs={{0,16},{2,18},{4,20},{6,22},{8,24},{10,26},{12,28},{14,30},{16,0},... | collective-permute-start | bytes 786440 | tf_op jit(solution)/shard_map/ppermute | solution.py:217
  10.7 3.4 %collective-permute-done.3.refs_6_ = bf16[192,1024]{1,0:T(8,128)(2,1)S(1)} collective-permute-done((bf16[192,1024]{1,0:T(8,128)(2,1)S(1)}, bf16[192,1024]{1,0:T(8,128)(2,1)S(1)}, u32[]{:S(2)}, u32[]{:S(2)}) %collective-permute-start.3) | collective-permute-done | bytes 393248 | tf_op jit(solution)/shard_map/ppermute | solution.py:217
  14.0 0.7 slice.468
  14.7 1.7 %collective-permute-start.6 = (bf16[96,1024]{1,0:T(8,128)(2,1)}, bf16[96,1024]{1,0:T(8,128)(2,1)S(1)}, u32[]{:S(2)}, u32[]{:S(2)}) collective-permute-start(bf16[96,1024]{1,0:T(8,128)(2,1)} %slice.468), channel_id=1, source_target_pairs={{0,2},{2,0},{4,6},{6,4},{8,10},{10,8},{12,14},{14,12},{16,18},{18,... | collective-permute-start | bytes 589832 | tf_op jit(solution)/shard_map/ppermute | solution.py:217
  16.4 0.0 collective-permute-done.2.refs_5_
  16.4 0.7 slice.469
  17.1 1.5 %collective-permute-start.7 = (bf16[96,1024]{1,0:T(8,128)(2,1)}, bf16[96,1024]{1,0:T(8,128)(2,1)S(1)}, u32[]{:S(2)}, u32[]{:S(2)}) collective-permute-start(bf16[96,1024]{1,0:T(8,128)(2,1)} %slice.469), channel_id=1, source_target_pairs={{0,4},{2,6},{4,0},{6,2},{8,12},{10,14},{12,8},{14,10},{16,20},{18,... | collective-permute-start | bytes 589832 | tf_op jit(solution)/shard_map/ppermute | solution.py:217
  18.7 0.0 collective-permute-start
  18.7 2.8 %collective-permute-done.1.refs_2_ = bf16[128,1024]{1,0:T(8,128)(2,1)S(1)} collective-permute-done((bf16[128,1024]{1,0:T(8,128)(2,1)S(1)}, bf16[128,1024]{1,0:T(8,128)(2,1)S(1)}, u32[]{:S(2)}, u32[]{:S(2)}) %collective-permute-start.1) | collective-permute-done | bytes 262176 | tf_op jit(solution)/shard_map/ppermute | solution.py:217
  21.4 0.9 collective-permute-done.4.refs_7_
  22.3 0.0 collective-permute-start.5
  22.3 0.5 collective-permute-start.10
  22.8 0.0 collective-permute-done.6
  22.8 0.4 collective-permute-start.9
  23.2 0.0 collective-permute-done.7
  23.3 2.8 %collective-permute-start.8 = (bf16[192,1024]{1,0:T(8,128)(2,1)S(1)}, bf16[192,1024]{1,0:T(8,128)(2,1)S(1)}, u32[]{:S(2)}, u32[]{:S(2)}) collective-permute-start(bf16[192,1024]{1,0:T(8,128)(2,1)S(1)} %constant_dynamic-update-slice_fusion.refs_1_), channel_id=1, source_target_pairs={{0,8},{2,10},{4,12},{6,14},{8,0},{10,2},{12,4},{14,6},{16,24},{18,... | collective-permute-start | bytes 1179656 | tf_op jit(solution)/shard_map/ppermute | solution.py:217
  26.1 3.1 %first_pass.2 = (f32[2,4,192]{2,1,0:T(4,128)S(1)}, f32[1,768]{1,0:T(1,128)S(1)}, bf16[768,1024]{1,0:T(8,128)(2,1)S(1)}, bf16[512,1024]{1,0:T(8,128)(2,1)S(1)}) custom-call(bf16[128,1024]{1,0:T(8,128)(2,1)S(1)} %convert_element_type.19.refs_0_, bf16[128,1024]{1,0:T(8,128)(2,1)S(1)} %collective-permute-done.refs_1_, ...), custom_call_target="tpu_custom_call" | custom-call | flops 6442450944 | bytes 1572864 | tf_op jit(solution)/shard_map/first_pass/pallas_call | solution.py:98
  29.2 6.1 %collective-permute-done.8.refs_4_ = bf16[192,1024]{1,0:T(8,128)(2,1)S(1)} collective-permute-done((bf16[192,1024]{1,0:T(8,128)(2,1)S(1)}, bf16[192,1024]{1,0:T(8,128)(2,1)S(1)}, u32[]{:S(2)}, u32[]{:S(2)}) %collective-permute-start.8) | collective-permute-done | bytes 393248 | tf_op jit(solution)/shard_map/ppermute | solution.py:217
  35.3 0.0 collective-permute-done.10.refs_3_
  35.4 1.8 %first_pass.3 = (f32[2,4,192]{2,1,0:T(4,128)S(1)}, f32[1,768]{1,0:T(1,128)S(1)}, bf16[768,1024]{1,0:T(8,128)(2,1)S(1)}) custom-call(bf16[512,1024]{1,0:T(8,128)(2,1)S(1)} %get-tuple-element.24.refs_0_.cents, bf16[192,1024]{1,0:T(8,128)(2,1)S(1)} %constant_dynamic-update-slice_fusion.refs_1_, bf16[192,1024]{1,0:T(8,128)(2,1)S(1)} %collective-permute-done.9.refs_2_, ...), custom_call_target="tpu_custom_call" | custom-call | flops 805306368 | bytes 1572864 | tf_op jit(solution)/shard_map/first_pass/pallas_call | solution.py:98
  37.4 10.8 %all_to_all.10 = f32[8,2,8,192]{3,2,1,0:T(8,128)S(1)} all-to-all(f32[8,2,8,192]{3,2,1,0:T(8,128)S(1)} %broadcast_in_dim.10), channel_id=1, replica_groups={{0,2,4,6,8,10,12,14},{16,18,20,22,24,26,28,30},{1,3,5,7,9,11,13,15},{17..., dimensions={0} | all-to-all | bytes 196608 | tf_op jit(solution)/shard_map/all_to_all | solution.py:262
  48.5 0.1 pad_maximum_fusion.11
  48.6 2.4 %sums_pass.3 = f32[256,1152]{1,0:T(8,128)S(1)} custom-call(bf16[512,1024]{1,0:T(8,128)(2,1)S(1)} %get-tuple-element.24.refs_0_.cents, f32[2,768]{1,0:T(2,128)S(1)} %get-tuple-element.95.refs_0_, f32[2,768]{1,0:T(2,128)S(1)} %get-tuple-element.96.refs_1_, f32[1,768]{1,0:T(1,128)S(1)} %get-tuple-element.31.refs_2_.refs_0_, ...), custom_call_target="tpu_custom_call" | custom-call | flops 1610612736 | bytes 3145728 | tf_op jit(solution)/shard_map/sums_pass/pallas_call | solution.py:137
  51.0 0.1 collective-permute-start.12
  51.1 2.4 %sums_pass.2 = f32[256,1152]{1,0:T(8,128)S(1)} custom-call(bf16[512,1024]{1,0:T(8,128)(2,1)S(1)} %get-tuple-element.24.refs_0_.cents, f32[2,768]{1,0:T(2,128)S(1)} %get-tuple-element.95.refs_0_, f32[2,768]{1,0:T(2,128)S(1)} %get-tuple-element.96.refs_1_, f32[1,768]{1,0:T(1,128)S(1)} %get-tuple-element.31.refs_2_.refs_0_, ...), custom_call_target="tpu_custom_call" | custom-call | flops 1610612736 | bytes 3145728 | tf_op jit(solution)/shard_map/sums_pass/pallas_call | solution.py:137
  53.6 0.6 collective-permute-start.11
  54.1 0.1 slice_add_fusion
  54.3 1.6 %collective-permute-start.13 = (bf16[48,1152]{1,0:T(8,128)(2,1)S(1)}, bf16[48,1152]{1,0:T(8,128)(2,1)S(1)}, u32[]{:S(2)}, u32[]{:S(2)}) collective-permute-start(bf16[48,1152]{1,0:T(8,128)(2,1)S(1)} %pad_maximum_fusion.5), channel_id=1, source_target_pairs={{0,16},{2,18},{4,20},{6,22},{8,24},{10,26},{12,28},{14,30},{16,0},... | collective-permute-start | bytes 331784 | tf_op jit(solution)/shard_map/ppermute | solution.py:217
  56.0 1.4 %collective-permute-start.14 = (bf16[80,1152]{1,0:T(8,128)(2,1)S(1)}, bf16[80,1152]{1,0:T(8,128)(2,1)S(1)}, u32[]{:S(2)}, u32[]{:S(2)}) collective-permute-start(bf16[80,1152]{1,0:T(8,128)(2,1)S(1)} %pad_maximum_fusion.4), channel_id=1, source_target_pairs={{0,16},{2,18},{4,20},{6,22},{8,24},{10,26},{12,28},{14,30},{16,0},... | collective-permute-start | bytes 552968 | tf_op jit(solution)/shard_map/ppermute | solution.py:217
  57.4 0.1 slice_add_fusion.1
  57.5 9.4 %collective-permute-done.13 = bf16[48,1152]{1,0:T(8,128)(2,1)S(1)} collective-permute-done((bf16[48,1152]{1,0:T(8,128)(2,1)S(1)}, bf16[48,1152]{1,0:T(8,128)(2,1)S(1)}, u32[]{:S(2)}, u32[]{:S(2)}) %collective-permute-start.13) | collective-permute-done | bytes 110624 | tf_op jit(solution)/shard_map/ppermute | solution.py:217
  66.9 0.2 fusion.9
  67.1 0.1 broadcast_in_dim.24
  67.2 0.1 fusion.8
  67.3 0.1 fusion.31
  67.4 0.1 collective-permute-start.15
  67.5 0.1 collective-permute-start.18
  67.6 3.0 %collective-permute-done.14 = bf16[80,1152]{1,0:T(8,128)(2,1)S(1)} collective-permute-done((bf16[80,1152]{1,0:T(8,128)(2,1)S(1)}, bf16[80,1152]{1,0:T(8,128)(2,1)S(1)}, u32[]{:S(2)}, u32[]{:S(2)}) %collective-permute-start.14) | collective-permute-done | bytes 184352 | tf_op jit(solution)/shard_map/ppermute | solution.py:217
  70.6 0.2 fusion.7
  70.8 0.1 broadcast_in_dim.26
  70.8 0.1 slice_add_fusion.2
  70.9 0.1 fusion.6
  71.0 4.3 %collective-permute-done.18 = bf16[48,1024]{1,0:T(8,128)(2,1)S(1)} collective-permute-done((bf16[48,1024]{1,0:T(8,128)(2,1)S(1)}, bf16[48,1024]{1,0:T(8,128)(2,1)S(1)}, u32[]{:S(2)}, u32[]{:S(2)}) %collective-permute-start.18) | collective-permute-done | bytes 98336 | tf_op jit(solution)/shard_map/ppermute | solution.py:217
  75.3 0.1 collective-permute-start.19
  75.4 0.1 fusion.29
  75.5 0.5 collective-permute-start.16
  76.0 0.0 collective-permute-start.17
  76.0 0.6 collective-permute-done.19
  76.6 1.2 %second_pass.4 = (f32[3,4,192]{2,1,0:T(4,128)S(1)}, f32[3,4,192]{2,1,0:T(4,128)S(1)}) custom-call(bf16[96,1024]{1,0:T(8,128)(2,1)S(1)} %pad_maximum_fusion.3.cents, f32[1,768]{1,0:T(1,128)S(1)} %get-tuple-element.31.refs_2_.refs_0_, f32[1,768]{1,0:T(1,128)S(1)} %get-tuple-element.32.refs_3_.refs_1_, bf16[768,1024]{1,0:T(8,128)(2,1)S(1)} %get-tuple-element.33.refs_4_.refs_2_, ...), custom_call_target="tpu_custom_call" | custom-call | flops 301989888 | bytes 3145728 | tf_op jit(solution)/shard_map/second_pass/pallas_call | solution.py:178
  77.9 7.6 %collective-permute-done.17 = bf16[80,1024]{1,0:T(8,128)(2,1)S(1)} collective-permute-done((bf16[80,1024]{1,0:T(8,128)(2,1)S(1)}, bf16[80,1024]{1,0:T(8,128)(2,1)S(1)}, u32[]{:S(2)}, u32[]{:S(2)}) %collective-permute-start.17) | collective-permute-done | bytes 163872 | tf_op jit(solution)/shard_map/ppermute | solution.py:217
  85.5 0.0 collective-permute-start.20
  85.6 1.6 %second_pass.3 = (f32[3,4,192]{2,1,0:T(4,128)S(1)}, f32[3,4,192]{2,1,0:T(4,128)S(1)}) custom-call(bf16[256,1024]{1,0:T(8,128)(2,1)S(1)} %pad_maximum_fusion.1.cents, f32[1,768]{1,0:T(1,128)S(1)} %get-tuple-element.31.refs_2_.refs_0_, f32[1,768]{1,0:T(1,128)S(1)} %get-tuple-element.32.refs_3_.refs_1_, ...), custom_call_target="tpu_custom_call" | custom-call | flops 805306368 | bytes 3145728 | tf_op jit(solution)/shard_map/second_pass/pallas_call | solution.py:178
  87.3 0.0 collective-permute-done.20
  87.3 1.3 %second_pass.5 = (f32[3,4,192]{2,1,0:T(4,128)S(1)}, f32[3,4,192]{2,1,0:T(4,128)S(1)}) custom-call(bf16[160,1024]{1,0:T(8,128)(2,1)S(1)} %pad_maximum_fusion.2.cents, f32[1,768]{1,0:T(1,128)S(1)} %get-tuple-element.31.refs_2_.refs_0_, f32[1,768]{1,0:T(1,128)S(1)} %get-tuple-element.32.refs_3_.refs_1_, ...), custom_call_target="tpu_custom_call" | custom-call | flops 503316480 | bytes 3145728 | tf_op jit(solution)/shard_map/second_pass/pallas_call | solution.py:178
  88.7 0.1 stack.78
  88.9 0.6 copy.69
  89.5 3.3 %all-to-all-start.1 = ((f32[8,3,192]{2,1,0:T(4,128)}), f32[8,3,192]{2,1,0:T(4,128)S(1)}, u32[]{:S(2)}, u32[]{:S(2)}) async-start(f32[8,3,192]{2,1,0:T(4,128)} %copy.69), calls=%async_computation.1 | async-start | bytes 65536 | tf_op jit(solution)/shard_map/all_to_all | solution.py:262
  92.8 0.8 pad_maximum_fusion
  93.7 4.8 %all-to-all-done.1 = f32[8,3,192]{2,1,0:T(4,128)S(1)} async-done(((f32[8,3,192]{2,1,0:T(4,128)}), f32[8,3,192]{2,1,0:T(4,128)S(1)}, u32[]{:S(2)}, u32[]{:S(2)}) %all-to-all-start.1) | async-done | bytes 18464 | tf_op jit(solution)/shard_map/all_to_all | solution.py:262
  98.5 0.6 divide_subtract_fusion
  (86 shorter events, 1.1 us)
Async XLA Ops:
  0.6 7.4 %copy-start = (f32[128,1024]{1,0:T(8,128)S(1)}, f32[128,1024]{1,0:T(8,128)}, u32[]{:S(2)}) copy-start(f32[128,1024]{1,0:T(8,128)} %param.3) | copy-start | bytes 1572868
  1.9 12.1 %collective-permute-start.3 = (bf16[192,1024]{1,0:T(8,128)(2,1)S(1)}, bf16[192,1024]{1,0:T(8,128)(2,1)S(1)}, u32[]{:S(2)}, u32[]{:S(2)}) collective-permute-start(bf16[192,1024]{1,0:T(8,128)(2,1)S(1)} %convert_element_type.20.refs_4_), channel_id=1, source_target_pairs={{0,4},{2,6},{4,0},{6,2},{8,12},{10,14},{12,8},{14,10},{16,20},{18,... | collective-permute-start | bytes 1179656 | tf_op jit(solution)/shard_map/ppermute | solution.py:217
  4.9 11.5 %collective-permute-start.2 = (bf16[192,1024]{1,0:T(8,128)(2,1)S(1)}, bf16[192,1024]{1,0:T(8,128)(2,1)S(1)}, u32[]{:S(2)}, u32[]{:S(2)}) collective-permute-start(bf16[192,1024]{1,0:T(8,128)(2,1)S(1)} %convert_element_type.20.refs_4_), channel_id=1, source_target_pairs={{0,2},{2,0},{4,6},{6,4},{8,10},{10,8},{12,14},{14,12},{16,18},{18,... | collective-permute-start | bytes 1179656 | tf_op jit(solution)/shard_map/ppermute | solution.py:217
  6.4 15.9 %collective-permute-start.4 = (bf16[192,1024]{1,0:T(8,128)(2,1)S(1)}, bf16[192,1024]{1,0:T(8,128)(2,1)S(1)}, u32[]{:S(2)}, u32[]{:S(2)}) collective-permute-start(bf16[192,1024]{1,0:T(8,128)(2,1)S(1)} %convert_element_type.20.refs_4_), channel_id=1, source_target_pairs={{0,8},{2,10},{4,12},{6,14},{8,0},{10,2},{12,4},{14,6},{16,24},{18,... | collective-permute-start | bytes 1179656 | tf_op jit(solution)/shard_map/ppermute | solution.py:217
  8.0 13.4 %collective-permute-start.1 = (bf16[128,1024]{1,0:T(8,128)(2,1)S(1)}, bf16[128,1024]{1,0:T(8,128)(2,1)S(1)}, u32[]{:S(2)}, u32[]{:S(2)}) collective-permute-start(bf16[128,1024]{1,0:T(8,128)(2,1)S(1)} %convert_element_type.19.refs_0_), channel_id=1, source_target_pairs={{0,16},{2,18},{4,20},{6,22},{8,24},{10,26},{12,28},{14,30},{16,0},... | collective-permute-start | bytes 786440 | tf_op jit(solution)/shard_map/ppermute | solution.py:217
  14.7 8.1 %collective-permute-start.6 = (bf16[96,1024]{1,0:T(8,128)(2,1)}, bf16[96,1024]{1,0:T(8,128)(2,1)S(1)}, u32[]{:S(2)}, u32[]{:S(2)}) collective-permute-start(bf16[96,1024]{1,0:T(8,128)(2,1)} %slice.468), channel_id=1, source_target_pairs={{0,2},{2,0},{4,6},{6,4},{8,10},{10,8},{12,14},{14,12},{16,18},{18,... | collective-permute-start | bytes 589832 | tf_op jit(solution)/shard_map/ppermute | solution.py:217
  17.1 6.1 %collective-permute-start.7 = (bf16[96,1024]{1,0:T(8,128)(2,1)}, bf16[96,1024]{1,0:T(8,128)(2,1)S(1)}, u32[]{:S(2)}, u32[]{:S(2)}) collective-permute-start(bf16[96,1024]{1,0:T(8,128)(2,1)} %slice.469), channel_id=1, source_target_pairs={{0,4},{2,6},{4,0},{6,2},{8,12},{10,14},{12,8},{14,10},{16,20},{18,... | collective-permute-start | bytes 589832 | tf_op jit(solution)/shard_map/ppermute | solution.py:217
  18.7 7.4 %collective-permute-start = (bf16[128,1024]{1,0:T(8,128)(2,1)S(1)}, bf16[128,1024]{1,0:T(8,128)(2,1)S(1)}, u32[]{:S(2)}, u32[]{:S(2)}) collective-permute-start(bf16[128,1024]{1,0:T(8,128)(2,1)S(1)} %convert_element_type.19.refs_0_), channel_id=1, source_target_pairs={{0,1},{1,0},{2,3},{3,2},{4,5},{5,4},{6,7},{7,6},{8,9},{9,8},{10,11... | collective-permute-start | bytes 786440 | tf_op jit(solution)/shard_map/ppermute | solution.py:220
  22.3 3.8 %collective-permute-start.5 = (bf16[128,1024]{1,0:T(8,128)(2,1)S(1)}, bf16[128,1024]{1,0:T(8,128)(2,1)S(1)}, u32[]{:S(2)}, u32[]{:S(2)}) collective-permute-start(bf16[128,1024]{1,0:T(8,128)(2,1)S(1)} %collective-permute-done.1.refs_2_), channel_id=1, source_target_pairs={{0,1},{1,0},{2,3},{3,2},{4,5},{5,4},{6,7},{7,6},{8,9},{9,8},{10,11... | collective-permute-start | bytes 786440 | tf_op jit(solution)/shard_map/ppermute | solution.py:220
  22.3 13.0 %collective-permute-start.10 = (bf16[192,1024]{1,0:T(8,128)(2,1)S(1)}, bf16[192,1024]{1,0:T(8,128)(2,1)S(1)}, u32[]{:S(2)}, u32[]{:S(2)}) collective-permute-start(bf16[192,1024]{1,0:T(8,128)(2,1)S(1)} %collective-permute-done.4.refs_7_), channel_id=1, source_target_pairs={{0,4},{2,6},{4,0},{6,2},{8,12},{10,14},{12,8},{14,10},{16,20},{18,... | collective-permute-start | bytes 1179656 | tf_op jit(solution)/shard_map/ppermute | solution.py:217
  22.8 12.5 %collective-permute-start.9 = (bf16[192,1024]{1,0:T(8,128)(2,1)S(1)}, bf16[192,1024]{1,0:T(8,128)(2,1)S(1)}, u32[]{:S(2)}, u32[]{:S(2)}) collective-permute-start(bf16[192,1024]{1,0:T(8,128)(2,1)S(1)} %collective-permute-done.4.refs_7_), channel_id=1, source_target_pairs={{0,2},{2,0},{4,6},{6,4},{8,10},{10,8},{12,14},{14,12},{16,18},{18,... | collective-permute-start | bytes 1179656 | tf_op jit(solution)/shard_map/ppermute | solution.py:217
  23.3 12.0 %collective-permute-start.8 = (bf16[192,1024]{1,0:T(8,128)(2,1)S(1)}, bf16[192,1024]{1,0:T(8,128)(2,1)S(1)}, u32[]{:S(2)}, u32[]{:S(2)}) collective-permute-start(bf16[192,1024]{1,0:T(8,128)(2,1)S(1)} %constant_dynamic-update-slice_fusion.refs_1_), channel_id=1, source_target_pairs={{0,8},{2,10},{4,12},{6,14},{8,0},{10,2},{12,4},{14,6},{16,24},{18,... | collective-permute-start | bytes 1179656 | tf_op jit(solution)/shard_map/ppermute | solution.py:217
  51.0 3.1 %collective-permute-start.12 = (f32[128,1152]{1,0:T(8,128)S(1)}, f32[128,1152]{1,0:T(8,128)S(1)}, u32[]{:S(2)}, u32[]{:S(2)}) collective-permute-start(f32[128,1152]{1,0:T(8,128)S(1)} %slice.521), channel_id=1, source_target_pairs={{0,1},{1,0},{2,3},{3,2},{4,5},{5,4},{6,7},{7,6},{8,9},{9,8},{10,11... | collective-permute-start | bytes 1769480 | tf_op jit(solution)/shard_map/ppermute | solution.py:220
  53.6 3.8 %collective-permute-start.11 = (f32[128,1152]{1,0:T(8,128)S(1)}, f32[128,1152]{1,0:T(8,128)S(1)}, u32[]{:S(2)}, u32[]{:S(2)}) collective-permute-start(f32[128,1152]{1,0:T(8,128)S(1)} %slice.519), channel_id=1, source_target_pairs={{0,1},{1,0},{2,3},{3,2},{4,5},{5,4},{6,7},{7,6},{8,9},{9,8},{10,11... | collective-permute-start | bytes 1769480 | tf_op jit(solution)/shard_map/ppermute | solution.py:220
  54.3 12.5 %collective-permute-start.13 = (bf16[48,1152]{1,0:T(8,128)(2,1)S(1)}, bf16[48,1152]{1,0:T(8,128)(2,1)S(1)}, u32[]{:S(2)}, u32[]{:S(2)}) collective-permute-start(bf16[48,1152]{1,0:T(8,128)(2,1)S(1)} %pad_maximum_fusion.5), channel_id=1, source_target_pairs={{0,16},{2,18},{4,20},{6,22},{8,24},{10,26},{12,28},{14,30},{16,0},... | collective-permute-start | bytes 331784 | tf_op jit(solution)/shard_map/ppermute | solution.py:217
  56.0 14.6 %collective-permute-start.14 = (bf16[80,1152]{1,0:T(8,128)(2,1)S(1)}, bf16[80,1152]{1,0:T(8,128)(2,1)S(1)}, u32[]{:S(2)}, u32[]{:S(2)}) collective-permute-start(bf16[80,1152]{1,0:T(8,128)(2,1)S(1)} %pad_maximum_fusion.4), channel_id=1, source_target_pairs={{0,16},{2,18},{4,20},{6,22},{8,24},{10,26},{12,28},{14,30},{16,0},... | collective-permute-start | bytes 552968 | tf_op jit(solution)/shard_map/ppermute | solution.py:217
  67.4 18.1 %collective-permute-start.15 = (bf16[48,1024]{1,0:T(8,128)(2,1)S(1)}, bf16[48,1024]{1,0:T(8,128)(2,1)S(1)}, u32[]{:S(2)}, u32[]{:S(2)}) collective-permute-start(bf16[48,1024]{1,0:T(8,128)(2,1)S(1)} %get-tuple-element.48), channel_id=1, source_target_pairs={{0,1},{1,0},{2,3},{3,2},{4,5},{5,4},{6,7},{7,6},{8,9},{9,8},{10,11... | collective-permute-start | bytes 294920 | tf_op jit(solution)/shard_map/ppermute | solution.py:220
  67.5 7.9 %collective-permute-start.18 = (bf16[48,1024]{1,0:T(8,128)(2,1)S(1)}, bf16[48,1024]{1,0:T(8,128)(2,1)S(1)}, u32[]{:S(2)}, u32[]{:S(2)}) collective-permute-start(bf16[48,1024]{1,0:T(8,128)(2,1)S(1)} %get-tuple-element.48), channel_id=1, source_target_pairs={{0,16},{2,18},{4,20},{6,22},{8,24},{10,26},{12,28},{14,30},{16,0},... | collective-permute-start | bytes 294920 | tf_op jit(solution)/shard_map/ppermute | solution.py:217
  75.3 1.3 %collective-permute-start.19 = (bf16[48,1024]{1,0:T(8,128)(2,1)S(1)}, bf16[48,1024]{1,0:T(8,128)(2,1)S(1)}, u32[]{:S(2)}, u32[]{:S(2)}) collective-permute-start(bf16[48,1024]{1,0:T(8,128)(2,1)S(1)} %collective-permute-done.18), channel_id=1, source_target_pairs={{0,1},{1,0},{2,3},{3,2},{4,5},{5,4},{6,7},{7,6},{8,9},{9,8},{10,11... | collective-permute-start | bytes 294920 | tf_op jit(solution)/shard_map/ppermute | solution.py:220
  75.5 10.0 %collective-permute-start.16 = (bf16[80,1024]{1,0:T(8,128)(2,1)S(1)}, bf16[80,1024]{1,0:T(8,128)(2,1)S(1)}, u32[]{:S(2)}, u32[]{:S(2)}) collective-permute-start(bf16[80,1024]{1,0:T(8,128)(2,1)S(1)} %get-tuple-element.46), channel_id=1, source_target_pairs={{0,1},{1,0},{2,3},{3,2},{4,5},{5,4},{6,7},{7,6},{8,9},{9,8},{10,11... | collective-permute-start | bytes 491528 | tf_op jit(solution)/shard_map/ppermute | solution.py:220
  76.0 9.5 %collective-permute-start.17 = (bf16[80,1024]{1,0:T(8,128)(2,1)S(1)}, bf16[80,1024]{1,0:T(8,128)(2,1)S(1)}, u32[]{:S(2)}, u32[]{:S(2)}) collective-permute-start(bf16[80,1024]{1,0:T(8,128)(2,1)S(1)} %get-tuple-element.46), channel_id=1, source_target_pairs={{0,16},{2,18},{4,20},{6,22},{8,24},{10,26},{12,28},{14,30},{16,0},... | collective-permute-start | bytes 491528 | tf_op jit(solution)/shard_map/ppermute | solution.py:217
  85.5 1.8 %collective-permute-start.20 = (bf16[80,1024]{1,0:T(8,128)(2,1)S(1)}, bf16[80,1024]{1,0:T(8,128)(2,1)S(1)}, u32[]{:S(2)}, u32[]{:S(2)}) collective-permute-start(bf16[80,1024]{1,0:T(8,128)(2,1)S(1)} %collective-permute-done.17), channel_id=1, source_target_pairs={{0,1},{1,0},{2,3},{3,2},{4,5},{5,4},{6,7},{7,6},{8,9},{9,8},{10,11... | collective-permute-start | bytes 491528 | tf_op jit(solution)/shard_map/ppermute | solution.py:220
  89.5 9.0 %all-to-all-start.1 = ((f32[8,3,192]{2,1,0:T(4,128)}), f32[8,3,192]{2,1,0:T(4,128)S(1)}, u32[]{:S(2)}, u32[]{:S(2)}) async-start(f32[8,3,192]{2,1,0:T(4,128)} %copy.69), calls=%async_computation.1 | async-start | bytes 65536 | tf_op jit(solution)/shard_map/all_to_all | solution.py:262

commit v6 on v5

--- a/solution.py
+++ b/solution.py
@@ -318,6 +318,7 @@
             updated.append((sums[:, :width] + prior) / (sums[:, width : width + 1] + prior_mass))
             near_own.append(gather_near(updated[-1].astype(jnp.bfloat16)))
         far_own = [flip(p, top_bit) for p in near_own]
+        far_own[0] = hold(far_own[0], near_own[-1])[0]
         near = [b for p in near_own for b in gather_cent(p)]
         stats = [second_pass(jnp.concatenate(near, axis=0), row_sqs, rows, shard)]
         for p in far_own:

time: 99.4 us -> 99.3 us (level)
  no operation moved by 1% of the time
where the time goes in v6:
time: 99.3 us; the launch traced here: 99 us
  waiting for transfers between devices  42.8 us (43%)
  starting transfers between devices  23.4 us (24%)
  Pallas kernels  13.7 us (14%)
  blocking collectives  10.8 us (11%)
  other arithmetic  4.44 us (4%)
  local copies, waits for them, and re-layouts  2.63 us (3%)
  between operations  1.22 us (1%)
    ppermute x13, waiting for transfers between devices, flip(): return lax.ppermute(value, 'dp', [(i, i ^ bits) for i in range(n_dp)])  37.2 us
    ppermute x13, starting transfers between devices, flip(): return lax.ppermute(value, 'dp', [(i, i ^ bits) for i in range(n_dp)])  18.8 us
    all_to_all x1, blocking collectives, exchange(): return lax.all_to_all(value, 'dp', 0, 0, axis_index_groups=groups)  10.8 us
    pallas_call x2, Pallas kernels, first_pass(): pl.pallas_call(functools.partial(first_kernel, n, n_blocks, shard, last),...  4.84 us
    pallas_call x2, Pallas kernels, sums_pass(): pl.pallas_call(functools.partial(sums_kernel, first, last, n), out_shape=...  4.81 us
    all_to_all x1, waiting for transfers between devices, exchange(): return lax.all_to_all(value, 'dp', 0, 0, axis_index_groups=groups)  4.81 us
    pallas_call x3, Pallas kernels, second_pass(): pl.pallas_call(functools.partial(second_kernel, shard, n), out_shape=tupl...  4.1 us
    all_to_all x1, starting transfers between devices, exchange(): return lax.all_to_all(value, 'dp', 0, 0, axis_index_groups=groups)  3.33 us
  transfers between devices with their start and end apart: 22, of which 10 were waited for; matrix products, arithmetic and copies ran while one was open for 4% of the time, Pallas kernels for 8%

profile of v6, /device:TPU:0, one launch (start us, length us, event | category | flops | bytes accessed | tf_op | source)
XLA Modules:
  0.0 99.0 jit_solution(5348991536130824520)
XLA Ops:
  0.6 1.2 %convert_element_type.20.refs_4_ = bf16[192,1024]{1,0:T(8,128)(2,1)S(1)} convert(f32[192,1024]{1,0:T(8,128)} %param.2) | non-fusion elementwise | flops 196608 | bytes 1179648 | tf_op jit(solution)/shard_map/convert_element_type | solution.py:275
  1.9 3.0 %collective-permute-start.3 = (bf16[192,1024]{1,0:T(8,128)(2,1)S(1)}, bf16[192,1024]{1,0:T(8,128)(2,1)S(1)}, u32[]{:S(2)}, u32[]{:S(2)}) collective-permute-start(bf16[192,1024]{1,0:T(8,128)(2,1)S(1)} %convert_element_type.20.refs_4_), channel_id=1, source_target_pairs={{0,4},{2,6},{4,0},{6,2},{8,12},{10,14},{12,8},{14,10},{16,20},{18,... | collective-permute-start | bytes 1179656 | tf_op jit(solution)/shard_map/ppermute | solution.py:217
  4.9 1.5 %collective-permute-start.2 = (bf16[192,1024]{1,0:T(8,128)(2,1)S(1)}, bf16[192,1024]{1,0:T(8,128)(2,1)S(1)}, u32[]{:S(2)}, u32[]{:S(2)}) collective-permute-start(bf16[192,1024]{1,0:T(8,128)(2,1)S(1)} %convert_element_type.20.refs_4_), channel_id=1, source_target_pairs={{0,2},{2,0},{4,6},{6,4},{8,10},{10,8},{12,14},{14,12},{16,18},{18,... | collective-permute-start | bytes 1179656 | tf_op jit(solution)/shard_map/ppermute | solution.py:217
  6.4 1.6 %collective-permute-start.4 = (bf16[192,1024]{1,0:T(8,128)(2,1)S(1)}, bf16[192,1024]{1,0:T(8,128)(2,1)S(1)}, u32[]{:S(2)}, u32[]{:S(2)}) collective-permute-start(bf16[192,1024]{1,0:T(8,128)(2,1)S(1)} %convert_element_type.20.refs_4_), channel_id=1, source_target_pairs={{0,8},{2,10},{4,12},{6,14},{8,0},{10,2},{12,4},{14,6},{16,24},{18,... | collective-permute-start | bytes 1179656 | tf_op jit(solution)/shard_map/ppermute | solution.py:217
  8.0 2.7 %collective-permute-start.1 = (bf16[128,1024]{1,0:T(8,128)(2,1)S(1)}, bf16[128,1024]{1,0:T(8,128)(2,1)S(1)}, u32[]{:S(2)}, u32[]{:S(2)}) collective-permute-start(bf16[128,1024]{1,0:T(8,128)(2,1)S(1)} %convert_element_type.19.refs_0_), channel_id=1, source_target_pairs={{0,16},{2,18},{4,20},{6,22},{8,24},{10,26},{12,28},{14,30},{16,0},... | collective-permute-start | bytes 786440 | tf_op jit(solution)/shard_map/ppermute | solution.py:217
  10.7 3.4 %collective-permute-done.3.refs_6_ = bf16[192,1024]{1,0:T(8,128)(2,1)S(1)} collective-permute-done((bf16[192,1024]{1,0:T(8,128)(2,1)S(1)}, bf16[192,1024]{1,0:T(8,128)(2,1)S(1)}, u32[]{:S(2)}, u32[]{:S(2)}) %collective-permute-start.3) | collective-permute-done | bytes 393248 | tf_op jit(solution)/shard_map/ppermute | solution.py:217
  14.0 0.7 slice.468
  14.7 1.7 %collective-permute-start.6 = (bf16[96,1024]{1,0:T(8,128)(2,1)}, bf16[96,1024]{1,0:T(8,128)(2,1)S(1)}, u32[]{:S(2)}, u32[]{:S(2)}) collective-permute-start(bf16[96,1024]{1,0:T(8,128)(2,1)} %slice.468), channel_id=1, source_target_pairs={{0,2},{2,0},{4,6},{6,4},{8,10},{10,8},{12,14},{14,12},{16,18},{18,... | collective-permute-start | bytes 589832 | tf_op jit(solution)/shard_map/ppermute | solution.py:217
  16.4 0.0 collective-permute-done.2.refs_5_
  16.4 0.7 slice.469
  17.1 1.5 %collective-permute-start.7 = (bf16[96,1024]{1,0:T(8,128)(2,1)}, bf16[96,1024]{1,0:T(8,128)(2,1)S(1)}, u32[]{:S(2)}, u32[]{:S(2)}) collective-permute-start(bf16[96,1024]{1,0:T(8,128)(2,1)} %slice.469), channel_id=1, source_target_pairs={{0,4},{2,6},{4,0},{6,2},{8,12},{10,14},{12,8},{14,10},{16,20},{18,... | collective-permute-start | bytes 589832 | tf_op jit(solution)/shard_map/ppermute | solution.py:217
  18.7 0.0 collective-permute-start
  18.7 2.8 %collective-permute-done.1.refs_2_ = bf16[128,1024]{1,0:T(8,128)(2,1)S(1)} collective-permute-done((bf16[128,1024]{1,0:T(8,128)(2,1)S(1)}, bf16[128,1024]{1,0:T(8,128)(2,1)S(1)}, u32[]{:S(2)}, u32[]{:S(2)}) %collective-permute-start.1) | collective-permute-done | bytes 262176 | tf_op jit(solution)/shard_map/ppermute | solution.py:217
  21.4 0.9 collective-permute-done.4.refs_7_
  22.3 0.0 collective-permute-start.5
  22.3 0.5 collective-permute-start.10
  22.8 0.4 collective-permute-start.9
  23.2 0.0 collective-permute-done.7
  23.3 2.8 %collective-permute-start.8 = (bf16[192,1024]{1,0:T(8,128)(2,1)S(1)}, bf16[192,1024]{1,0:T(8,128)(2,1)S(1)}, u32[]{:S(2)}, u32[]{:S(2)}) collective-permute-start(bf16[192,1024]{1,0:T(8,128)(2,1)S(1)} %constant_dynamic-update-slice_fusion.refs_1_), channel_id=1, source_target_pairs={{0,8},{2,10},{4,12},{6,14},{8,0},{10,2},{12,4},{14,6},{16,24},{18,... | collective-permute-start | bytes 1179656 | tf_op jit(solution)/shard_map/ppermute | solution.py:217
  26.1 3.1 %first_pass.2 = (f32[2,4,192]{2,1,0:T(4,128)S(1)}, f32[1,768]{1,0:T(1,128)S(1)}, bf16[768,1024]{1,0:T(8,128)(2,1)S(1)}, bf16[512,1024]{1,0:T(8,128)(2,1)S(1)}) custom-call(bf16[128,1024]{1,0:T(8,128)(2,1)S(1)} %convert_element_type.19.refs_0_, bf16[128,1024]{1,0:T(8,128)(2,1)S(1)} %collective-permute-done.refs_1_, ...), custom_call_target="tpu_custom_call" | custom-call | flops 6442450944 | bytes 1572864 | tf_op jit(solution)/shard_map/first_pass/pallas_call | solution.py:98
  29.2 6.1 %collective-permute-done.8.refs_4_ = bf16[192,1024]{1,0:T(8,128)(2,1)S(1)} collective-permute-done((bf16[192,1024]{1,0:T(8,128)(2,1)S(1)}, bf16[192,1024]{1,0:T(8,128)(2,1)S(1)}, u32[]{:S(2)}, u32[]{:S(2)}) %collective-permute-start.8) | collective-permute-done | bytes 393248 | tf_op jit(solution)/shard_map/ppermute | solution.py:217
  35.3 0.0 collective-permute-done.10.refs_3_
  35.4 1.8 %first_pass.3 = (f32[2,4,192]{2,1,0:T(4,128)S(1)}, f32[1,768]{1,0:T(1,128)S(1)}, bf16[768,1024]{1,0:T(8,128)(2,1)S(1)}) custom-call(bf16[512,1024]{1,0:T(8,128)(2,1)S(1)} %get-tuple-element.25.refs_0_.cents, bf16[192,1024]{1,0:T(8,128)(2,1)S(1)} %constant_dynamic-update-slice_fusion.refs_1_, bf16[192,1024]{1,0:T(8,128)(2,1)S(1)} %collective-permute-done.9.refs_2_, ...), custom_call_target="tpu_custom_call" | custom-call | flops 805306368 | bytes 1572864 | tf_op jit(solution)/shard_map/first_pass/pallas_call | solution.py:98
  37.4 10.8 %all_to_all.10 = f32[8,2,8,192]{3,2,1,0:T(8,128)S(1)} all-to-all(f32[8,2,8,192]{3,2,1,0:T(8,128)S(1)} %broadcast_in_dim.10), channel_id=1, replica_groups={{0,2,4,6,8,10,12,14},{16,18,20,22,24,26,28,30},{1,3,5,7,9,11,13,15},{17..., dimensions={0} | all-to-all | bytes 196608 | tf_op jit(solution)/shard_map/all_to_all | solution.py:262
  48.5 0.1 pad_maximum_fusion.11
  48.6 2.4 %sums_pass.3 = f32[256,1152]{1,0:T(8,128)S(1)} custom-call(bf16[512,1024]{1,0:T(8,128)(2,1)S(1)} %get-tuple-element.25.refs_0_.cents, f32[2,768]{1,0:T(2,128)S(1)} %get-tuple-element.97.refs_0_, f32[2,768]{1,0:T(2,128)S(1)} %get-tuple-element.98.refs_1_, f32[1,768]{1,0:T(1,128)S(1)} %get-tuple-element.32.refs_2_.refs_0_, ...), custom_call_target="tpu_custom_call" | custom-call | flops 1610612736 | bytes 3145728 | tf_op jit(solution)/shard_map/sums_pass/pallas_call | solution.py:137
  51.0 0.1 collective-permute-start.12
  51.1 2.4 %sums_pass.2 = f32[256,1152]{1,0:T(8,128)S(1)} custom-call(bf16[512,1024]{1,0:T(8,128)(2,1)S(1)} %get-tuple-element.25.refs_0_.cents, f32[2,768]{1,0:T(2,128)S(1)} %get-tuple-element.97.refs_0_, f32[2,768]{1,0:T(2,128)S(1)} %get-tuple-element.98.refs_1_, f32[1,768]{1,0:T(1,128)S(1)} %get-tuple-element.32.refs_2_.refs_0_, ...), custom_call_target="tpu_custom_call" | custom-call | flops 1610612736 | bytes 3145728 | tf_op jit(solution)/shard_map/sums_pass/pallas_call | solution.py:137
  53.6 0.6 collective-permute-start.11
  54.1 0.1 slice_add_fusion
  54.3 1.6 %collective-permute-start.13 = (bf16[48,1152]{1,0:T(8,128)(2,1)S(1)}, bf16[48,1152]{1,0:T(8,128)(2,1)S(1)}, u32[]{:S(2)}, u32[]{:S(2)}) collective-permute-start(bf16[48,1152]{1,0:T(8,128)(2,1)S(1)} %pad_maximum_fusion.5), channel_id=1, source_target_pairs={{0,16},{2,18},{4,20},{6,22},{8,24},{10,26},{12,28},{14,30},{16,0},... | collective-permute-start | bytes 331784 | tf_op jit(solution)/shard_map/ppermute | solution.py:217
  56.0 1.4 %collective-permute-start.14 = (bf16[80,1152]{1,0:T(8,128)(2,1)S(1)}, bf16[80,1152]{1,0:T(8,128)(2,1)S(1)}, u32[]{:S(2)}, u32[]{:S(2)}) collective-permute-start(bf16[80,1152]{1,0:T(8,128)(2,1)S(1)} %pad_maximum_fusion.4), channel_id=1, source_target_pairs={{0,16},{2,18},{4,20},{6,22},{8,24},{10,26},{12,28},{14,30},{16,0},... | collective-permute-start | bytes 552968 | tf_op jit(solution)/shard_map/ppermute | solution.py:217
  57.4 0.1 slice_add_fusion.1
  57.5 9.4 %collective-permute-done.13 = bf16[48,1152]{1,0:T(8,128)(2,1)S(1)} collective-permute-done((bf16[48,1152]{1,0:T(8,128)(2,1)S(1)}, bf16[48,1152]{1,0:T(8,128)(2,1)S(1)}, u32[]{:S(2)}, u32[]{:S(2)}) %collective-permute-start.13) | collective-permute-done | bytes 110624 | tf_op jit(solution)/shard_map/ppermute | solution.py:217
  66.9 0.2 fusion.9
  67.1 0.1 broadcast_in_dim.24
  67.2 0.1 fusion.8
  67.3 0.1 fusion.31
  67.4 0.1 collective-permute-start.18
  67.5 5.4 %collective-permute-done.14 = bf16[80,1152]{1,0:T(8,128)(2,1)S(1)} collective-permute-done((bf16[80,1152]{1,0:T(8,128)(2,1)S(1)}, bf16[80,1152]{1,0:T(8,128)(2,1)S(1)}, u32[]{:S(2)}, u32[]{:S(2)}) %collective-permute-start.14) | collective-permute-done | bytes 184352 | tf_op jit(solution)/shard_map/ppermute | solution.py:217
  73.0 0.2 fusion.7
  73.1 0.1 broadcast_in_dim.26
  73.2 0.1 slice_add_fusion.2
  73.3 0.1 fusion.6
  73.4 0.1 fusion.29
  73.5 1.2 %collective-permute-done.18 = bf16[48,1024]{1,0:T(8,128)(2,1)S(1)} collective-permute-done((bf16[48,1024]{1,0:T(8,128)(2,1)S(1)}, bf16[48,1024]{1,0:T(8,128)(2,1)S(1)}, u32[]{:S(2)}, u32[]{:S(2)}) %collective-permute-start.18) | collective-permute-done | bytes 98336 | tf_op jit(solution)/shard_map/ppermute | solution.py:217
  74.7 0.0 collective-permute-start.19
  74.7 0.5 collective-permute-start.15
  75.2 0.0 collective-permute-start.16
  75.2 0.0 collective-permute-start.17
  75.3 0.8 collective-permute-done.19
  76.1 1.2 %second_pass.4 = (f32[3,4,192]{2,1,0:T(4,128)S(1)}, f32[3,4,192]{2,1,0:T(4,128)S(1)}) custom-call(bf16[96,1024]{1,0:T(8,128)(2,1)S(1)} %pad_maximum_fusion.3.cents, f32[1,768]{1,0:T(1,128)S(1)} %get-tuple-element.32.refs_2_.refs_0_, f32[1,768]{1,0:T(1,128)S(1)} %get-tuple-element.33.refs_3_.refs_1_, bf16[768,1024]{1,0:T(8,128)(2,1)S(1)} %get-tuple-element.34.refs_4_.refs_2_, ...), custom_call_target="tpu_custom_call" | custom-call | flops 301989888 | bytes 3145728 | tf_op jit(solution)/shard_map/second_pass/pallas_call | solution.py:178
  77.3 8.1 %collective-permute-done.17 = bf16[80,1024]{1,0:T(8,128)(2,1)S(1)} collective-permute-done((bf16[80,1024]{1,0:T(8,128)(2,1)S(1)}, bf16[80,1024]{1,0:T(8,128)(2,1)S(1)}, u32[]{:S(2)}, u32[]{:S(2)}) %collective-permute-start.17) | collective-permute-done | bytes 163872 | tf_op jit(solution)/shard_map/ppermute | solution.py:217
  85.4 0.1 collective-permute-start.20
  85.4 0.0 collective-permute-done.15
  85.5 0.0 collective-permute-done.16
  85.5 1.6 %second_pass.3 = (f32[3,4,192]{2,1,0:T(4,128)S(1)}, f32[3,4,192]{2,1,0:T(4,128)S(1)}) custom-call(bf16[256,1024]{1,0:T(8,128)(2,1)S(1)} %pad_maximum_fusion.1.cents, f32[1,768]{1,0:T(1,128)S(1)} %get-tuple-element.32.refs_2_.refs_0_, f32[1,768]{1,0:T(1,128)S(1)} %get-tuple-element.33.refs_3_.refs_1_, ...), custom_call_target="tpu_custom_call" | custom-call | flops 805306368 | bytes 3145728 | tf_op jit(solution)/shard_map/second_pass/pallas_call | solution.py:178
  87.2 1.3 %second_pass.5 = (f32[3,4,192]{2,1,0:T(4,128)S(1)}, f32[3,4,192]{2,1,0:T(4,128)S(1)}) custom-call(bf16[160,1024]{1,0:T(8,128)(2,1)S(1)} %pad_maximum_fusion.2.cents, f32[1,768]{1,0:T(1,128)S(1)} %get-tuple-element.32.refs_2_.refs_0_, f32[1,768]{1,0:T(1,128)S(1)} %get-tuple-element.33.refs_3_.refs_1_, ...), custom_call_target="tpu_custom_call" | custom-call | flops 503316480 | bytes 3145728 | tf_op jit(solution)/shard_map/second_pass/pallas_call | solution.py:178
  88.6 0.1 stack.78
  88.8 0.6 copy.69
  89.4 3.3 %all-to-all-start.1 = ((f32[8,3,192]{2,1,0:T(4,128)}), f32[8,3,192]{2,1,0:T(4,128)S(1)}, u32[]{:S(2)}, u32[]{:S(2)}) async-start(f32[8,3,192]{2,1,0:T(4,128)} %copy.69), calls=%async_computation.1 | async-start | bytes 65536 | tf_op jit(solution)/shard_map/all_to_all | solution.py:262
  92.7 0.8 pad_maximum_fusion
  93.6 4.8 %all-to-all-done.1 = f32[8,3,192]{2,1,0:T(4,128)S(1)} async-done(((f32[8,3,192]{2,1,0:T(4,128)}), f32[8,3,192]{2,1,0:T(4,128)S(1)}, u32[]{:S(2)}, u32[]{:S(2)}) %all-to-all-start.1) | async-done | bytes 18464 | tf_op jit(solution)/shard_map/all_to_all | solution.py:262
  98.4 0.6 divide_subtract_fusion
  (86 shorter events, 1.1 us)
Async XLA Ops:
  0.6 7.4 %copy-start = (f32[128,1024]{1,0:T(8,128)S(1)}, f32[128,1024]{1,0:T(8,128)}, u32[]{:S(2)}) copy-start(f32[128,1024]{1,0:T(8,128)} %param.3) | copy-start | bytes 1572868
  1.9 12.1 %collective-permute-start.3 = (bf16[192,1024]{1,0:T(8,128)(2,1)S(1)}, bf16[192,1024]{1,0:T(8,128)(2,1)S(1)}, u32[]{:S(2)}, u32[]{:S(2)}) collective-permute-start(bf16[192,1024]{1,0:T(8,128)(2,1)S(1)} %convert_element_type.20.refs_4_), channel_id=1, source_target_pairs={{0,4},{2,6},{4,0},{6,2},{8,12},{10,14},{12,8},{14,10},{16,20},{18,... | collective-permute-start | bytes 1179656 | tf_op jit(solution)/shard_map/ppermute | solution.py:217
  4.9 11.5 %collective-permute-start.2 = (bf16[192,1024]{1,0:T(8,128)(2,1)S(1)}, bf16[192,1024]{1,0:T(8,128)(2,1)S(1)}, u32[]{:S(2)}, u32[]{:S(2)}) collective-permute-start(bf16[192,1024]{1,0:T(8,128)(2,1)S(1)} %convert_element_type.20.refs_4_), channel_id=1, source_target_pairs={{0,2},{2,0},{4,6},{6,4},{8,10},{10,8},{12,14},{14,12},{16,18},{18,... | collective-permute-start | bytes 1179656 | tf_op jit(solution)/shard_map/ppermute | solution.py:217
  6.4 15.9 %collective-permute-start.4 = (bf16[192,1024]{1,0:T(8,128)(2,1)S(1)}, bf16[192,1024]{1,0:T(8,128)(2,1)S(1)}, u32[]{:S(2)}, u32[]{:S(2)}) collective-permute-start(bf16[192,1024]{1,0:T(8,128)(2,1)S(1)} %convert_element_type.20.refs_4_), channel_id=1, source_target_pairs={{0,8},{2,10},{4,12},{6,14},{8,0},{10,2},{12,4},{14,6},{16,24},{18,... | collective-permute-start | bytes 1179656 | tf_op jit(solution)/shard_map/ppermute | solution.py:217
  8.0 13.4 %collective-permute-start.1 = (bf16[128,1024]{1,0:T(8,128)(2,1)S(1)}, bf16[128,1024]{1,0:T(8,128)(2,1)S(1)}, u32[]{:S(2)}, u32[]{:S(2)}) collective-permute-start(bf16[128,1024]{1,0:T(8,128)(2,1)S(1)} %convert_element_type.19.refs_0_), channel_id=1, source_target_pairs={{0,16},{2,18},{4,20},{6,22},{8,24},{10,26},{12,28},{14,30},{16,0},... | collective-permute-start | bytes 786440 | tf_op jit(solution)/shard_map/ppermute | solution.py:217
  14.7 8.1 %collective-permute-start.6 = (bf16[96,1024]{1,0:T(8,128)(2,1)}, bf16[96,1024]{1,0:T(8,128)(2,1)S(1)}, u32[]{:S(2)}, u32[]{:S(2)}) collective-permute-start(bf16[96,1024]{1,0:T(8,128)(2,1)} %slice.468), channel_id=1, source_target_pairs={{0,2},{2,0},{4,6},{6,4},{8,10},{10,8},{12,14},{14,12},{16,18},{18,... | collective-permute-start | bytes 589832 | tf_op jit(solution)/shard_map/ppermute | solution.py:217
  17.1 6.1 %collective-permute-start.7 = (bf16[96,1024]{1,0:T(8,128)(2,1)}, bf16[96,1024]{1,0:T(8,128)(2,1)S(1)}, u32[]{:S(2)}, u32[]{:S(2)}) collective-permute-start(bf16[96,1024]{1,0:T(8,128)(2,1)} %slice.469), channel_id=1, source_target_pairs={{0,4},{2,6},{4,0},{6,2},{8,12},{10,14},{12,8},{14,10},{16,20},{18,... | collective-permute-start | bytes 589832 | tf_op jit(solution)/shard_map/ppermute | solution.py:217
  18.7 7.4 %collective-permute-start = (bf16[128,1024]{1,0:T(8,128)(2,1)S(1)}, bf16[128,1024]{1,0:T(8,128)(2,1)S(1)}, u32[]{:S(2)}, u32[]{:S(2)}) collective-permute-start(bf16[128,1024]{1,0:T(8,128)(2,1)S(1)} %convert_element_type.19.refs_0_), channel_id=1, source_target_pairs={{0,1},{1,0},{2,3},{3,2},{4,5},{5,4},{6,7},{7,6},{8,9},{9,8},{10,11... | collective-permute-start | bytes 786440 | tf_op jit(solution)/shard_map/ppermute | solution.py:220
  22.3 3.8 %collective-permute-start.5 = (bf16[128,1024]{1,0:T(8,128)(2,1)S(1)}, bf16[128,1024]{1,0:T(8,128)(2,1)S(1)}, u32[]{:S(2)}, u32[]{:S(2)}) collective-permute-start(bf16[128,1024]{1,0:T(8,128)(2,1)S(1)} %collective-permute-done.1.refs_2_), channel_id=1, source_target_pairs={{0,1},{1,0},{2,3},{3,2},{4,5},{5,4},{6,7},{7,6},{8,9},{9,8},{10,11... | collective-permute-start | bytes 786440 | tf_op jit(solution)/shard_map/ppermute | solution.py:220
  22.3 13.0 %collective-permute-start.10 = (bf16[192,1024]{1,0:T(8,128)(2,1)S(1)}, bf16[192,1024]{1,0:T(8,128)(2,1)S(1)}, u32[]{:S(2)}, u32[]{:S(2)}) collective-permute-start(bf16[192,1024]{1,0:T(8,128)(2,1)S(1)} %collective-permute-done.4.refs_7_), channel_id=1, source_target_pairs={{0,4},{2,6},{4,0},{6,2},{8,12},{10,14},{12,8},{14,10},{16,20},{18,... | collective-permute-start | bytes 1179656 | tf_op jit(solution)/shard_map/ppermute | solution.py:217
  22.8 12.5 %collective-permute-start.9 = (bf16[192,1024]{1,0:T(8,128)(2,1)S(1)}, bf16[192,1024]{1,0:T(8,128)(2,1)S(1)}, u32[]{:S(2)}, u32[]{:S(2)}) collective-permute-start(bf16[192,1024]{1,0:T(8,128)(2,1)S(1)} %collective-permute-done.4.refs_7_), channel_id=1, source_target_pairs={{0,2},{2,0},{4,6},{6,4},{8,10},{10,8},{12,14},{14,12},{16,18},{18,... | collective-permute-start | bytes 1179656 | tf_op jit(solution)/shard_map/ppermute | solution.py:217
  23.3 12.0 %collective-permute-start.8 = (bf16[192,1024]{1,0:T(8,128)(2,1)S(1)}, bf16[192,1024]{1,0:T(8,128)(2,1)S(1)}, u32[]{:S(2)}, u32[]{:S(2)}) collective-permute-start(bf16[192,1024]{1,0:T(8,128)(2,1)S(1)} %constant_dynamic-update-slice_fusion.refs_1_), channel_id=1, source_target_pairs={{0,8},{2,10},{4,12},{6,14},{8,0},{10,2},{12,4},{14,6},{16,24},{18,... | collective-permute-start | bytes 1179656 | tf_op jit(solution)/shard_map/ppermute | solution.py:217
  51.0 3.1 %collective-permute-start.12 = (f32[128,1152]{1,0:T(8,128)S(1)}, f32[128,1152]{1,0:T(8,128)S(1)}, u32[]{:S(2)}, u32[]{:S(2)}) collective-permute-start(f32[128,1152]{1,0:T(8,128)S(1)} %slice.521), channel_id=1, source_target_pairs={{0,1},{1,0},{2,3},{3,2},{4,5},{5,4},{6,7},{7,6},{8,9},{9,8},{10,11... | collective-permute-start | bytes 1769480 | tf_op jit(solution)/shard_map/ppermute | solution.py:220
  53.6 3.8 %collective-permute-start.11 = (f32[128,1152]{1,0:T(8,128)S(1)}, f32[128,1152]{1,0:T(8,128)S(1)}, u32[]{:S(2)}, u32[]{:S(2)}) collective-permute-start(f32[128,1152]{1,0:T(8,128)S(1)} %slice.519), channel_id=1, source_target_pairs={{0,1},{1,0},{2,3},{3,2},{4,5},{5,4},{6,7},{7,6},{8,9},{9,8},{10,11... | collective-permute-start | bytes 1769480 | tf_op jit(solution)/shard_map/ppermute | solution.py:220
  54.3 12.5 %collective-permute-start.13 = (bf16[48,1152]{1,0:T(8,128)(2,1)S(1)}, bf16[48,1152]{1,0:T(8,128)(2,1)S(1)}, u32[]{:S(2)}, u32[]{:S(2)}) collective-permute-start(bf16[48,1152]{1,0:T(8,128)(2,1)S(1)} %pad_maximum_fusion.5), channel_id=1, source_target_pairs={{0,16},{2,18},{4,20},{6,22},{8,24},{10,26},{12,28},{14,30},{16,0},... | collective-permute-start | bytes 331784 | tf_op jit(solution)/shard_map/ppermute | solution.py:217
  56.0 16.9 %collective-permute-start.14 = (bf16[80,1152]{1,0:T(8,128)(2,1)S(1)}, bf16[80,1152]{1,0:T(8,128)(2,1)S(1)}, u32[]{:S(2)}, u32[]{:S(2)}) collective-permute-start(bf16[80,1152]{1,0:T(8,128)(2,1)S(1)} %pad_maximum_fusion.4), channel_id=1, source_target_pairs={{0,16},{2,18},{4,20},{6,22},{8,24},{10,26},{12,28},{14,30},{16,0},... | collective-permute-start | bytes 552968 | tf_op jit(solution)/shard_map/ppermute | solution.py:217
  67.4 7.3 %collective-permute-start.18 = (bf16[48,1024]{1,0:T(8,128)(2,1)S(1)}, bf16[48,1024]{1,0:T(8,128)(2,1)S(1)}, u32[]{:S(2)}, u32[]{:S(2)}) collective-permute-start(bf16[48,1024]{1,0:T(8,128)(2,1)S(1)} %get-tuple-element.50), channel_id=1, source_target_pairs={{0,16},{2,18},{4,20},{6,22},{8,24},{10,26},{12,28},{14,30},{16,0},... | collective-permute-start | bytes 294920 | tf_op jit(solution)/shard_map/ppermute | solution.py:217
  74.7 1.3 %collective-permute-start.19 = (bf16[48,1024]{1,0:T(8,128)(2,1)S(1)}, bf16[48,1024]{1,0:T(8,128)(2,1)S(1)}, u32[]{:S(2)}, u32[]{:S(2)}) collective-permute-start(bf16[48,1024]{1,0:T(8,128)(2,1)S(1)} %collective-permute-done.18), channel_id=1, source_target_pairs={{0,1},{1,0},{2,3},{3,2},{4,5},{5,4},{6,7},{7,6},{8,9},{9,8},{10,11... | collective-permute-start | bytes 294920 | tf_op jit(solution)/shard_map/ppermute | solution.py:220
  74.7 10.7 %collective-permute-start.15 = (bf16[48,1024]{1,0:T(8,128)(2,1)S(1)}, bf16[48,1024]{1,0:T(8,128)(2,1)S(1)}, u32[]{:S(2)}, u32[]{:S(2)}) collective-permute-start(bf16[48,1024]{1,0:T(8,128)(2,1)S(1)} %get-tuple-element.50), channel_id=1, source_target_pairs={{0,1},{1,0},{2,3},{3,2},{4,5},{5,4},{6,7},{7,6},{8,9},{9,8},{10,11... | collective-permute-start | bytes 294920 | tf_op jit(solution)/shard_map/ppermute | solution.py:220
  75.2 10.2 %collective-permute-start.16 = (bf16[80,1024]{1,0:T(8,128)(2,1)S(1)}, bf16[80,1024]{1,0:T(8,128)(2,1)S(1)}, u32[]{:S(2)}, u32[]{:S(2)}) collective-permute-start(bf16[80,1024]{1,0:T(8,128)(2,1)S(1)} %get-tuple-element.48), channel_id=1, source_target_pairs={{0,1},{1,0},{2,3},{3,2},{4,5},{5,4},{6,7},{7,6},{8,9},{9,8},{10,11... | collective-permute-start | bytes 491528 | tf_op jit(solution)/shard_map/ppermute | solution.py:220
  75.2 10.1 %collective-permute-start.17 = (bf16[80,1024]{1,0:T(8,128)(2,1)S(1)}, bf16[80,1024]{1,0:T(8,128)(2,1)S(1)}, u32[]{:S(2)}, u32[]{:S(2)}) collective-permute-start(bf16[80,1024]{1,0:T(8,128)(2,1)S(1)} %get-tuple-element.48), channel_id=1, source_target_pairs={{0,16},{2,18},{4,20},{6,22},{8,24},{10,26},{12,28},{14,30},{16,0},... | collective-permute-start | bytes 491528 | tf_op jit(solution)/shard_map/ppermute | solution.py:217
  85.4 1.8 %collective-permute-start.20 = (bf16[80,1024]{1,0:T(8,128)(2,1)S(1)}, bf16[80,1024]{1,0:T(8,128)(2,1)S(1)}, u32[]{:S(2)}, u32[]{:S(2)}) collective-permute-start(bf16[80,1024]{1,0:T(8,128)(2,1)S(1)} %collective-permute-done.17), channel_id=1, source_target_pairs={{0,1},{1,0},{2,3},{3,2},{4,5},{5,4},{6,7},{7,6},{8,9},{9,8},{10,11... | collective-permute-start | bytes 491528 | tf_op jit(solution)/shard_map/ppermute | solution.py:220
  89.4 9.0 %all-to-all-start.1 = ((f32[8,3,192]{2,1,0:T(4,128)}), f32[8,3,192]{2,1,0:T(4,128)S(1)}, u32[]{:S(2)}, u32[]{:S(2)}) async-start(f32[8,3,192]{2,1,0:T(4,128)} %copy.69), calls=%async_computation.1 | async-start | bytes 65536 | tf_op jit(solution)/shard_map/all_to_all | solution.py:262

commit v7 on v5

--- a/solution.py
+++ b/solution.py
@@ -10,7 +10,7 @@
 softness_level = 32.0
 prior_mass = 4.0
 CUBE = 8
-GROUPS = ((0, 1, 2, 4), (3, 5, 6, 7))
+GROUPS = ((0, 1, 2, 3), (4, 5), (6, 7))
 VMEM = pl.BlockSpec(memory_space=pltpu.VMEM)
 HBM = pl.BlockSpec(memory_space=pltpu.HBM)
 GRANT = 12 << 20
@@ -211,10 +211,17 @@
 def solution(mesh):
     n_dp = mesh.shape["dp"]
     n_cent = mesh.shape["cent"]
-    top_bit = n_dp // 2
+    high = n_dp // 2
+    top_bit = n_dp // 4
 
     def flip(value, bits):
         return lax.ppermute(value, "dp", [(i, i ^ bits) for i in range(n_dp)])
+
+    def member(place):
+        return (place & 3) | (high if place & 4 else 0)
+
+    def rows_from(value, place):
+        return flip(value, member(place))
 
     def across(value, bits):
         return lax.ppermute(value, "cent", [(i, i ^ bits) for i in range(n_cent)])
@@ -236,7 +243,7 @@
         return value
 
     def gather_near(value):
-        bits = CUBE
+        bits = 4
         while bits < top_bit:
             value = jnp.concatenate([value, flip(value, bits)], axis=0)
             bits *= 2
@@ -244,21 +251,21 @@
 
     def scatter_near(value):
         bits = top_bit // 2
-        while bits >= CUBE:
+        while bits >= 4:
             half = value.shape[0] // 2
             value = value[:half] + flip(value[half:], bits)
             bits //= 2
         return value
 
     def by_position(stats):
-        place = lax.axis_index("dp") % CUBE
+        place = lax.axis_index("dp")
         for bit in (1, 2, 4):
             swapped = jnp.stack([stats[:, b ^ bit] for b in range(CUBE)], axis=1)
-            stats = jnp.where((place & bit) != 0, swapped, stats)
+            stats = jnp.where((place & member(bit)) != 0, swapped, stats)
         return stats
 
     def exchange(value):
-        groups = [list(range(i, i + CUBE)) for i in range(0, n_dp, CUBE)]
+        groups = [[i + member(place) for place in range(CUBE)] for i in range(0, high, 4)]
         return lax.all_to_all(value, "dp", 0, 0, axis_index_groups=groups)
 
     def everywhere(stats):
@@ -269,26 +276,25 @@
 
     def on_device(embeddings, centroids):
         shard, width = embeddings.shape
-        per_device = centroids.shape[0]
-        cuts = [per_device * 3 // 8] if top_bit == CUBE and per_device % 64 == 0 else []
         half = shard // 2
         chunk = {0: embeddings.astype(jnp.bfloat16)}
-        for bit in (1, 2, 4):
-            chunk[bit] = flip(chunk[0], bit)
+        for bit in (4, 1, 2):
+            chunk[bit] = rows_from(chunk[0], bit)
         near_own = gather_near(centroids.astype(jnp.bfloat16))
         far_own = flip(near_own, top_bit)
-        chunk[3] = jnp.concatenate([flip(chunk[2][:half], 1), flip(chunk[1][half:], 2)], axis=0)
-        chunk[5] = flip(chunk[4], 1)
-        chunk[6] = flip(chunk[4], 2)
-        chunk[7] = flip(chunk[3], 4)
+        chunk[3] = rows_from(chunk[1], 2)
+        chunk[4], chunk[3], chunk[2], far_own = hold(chunk[4], chunk[3], chunk[2], far_own)
+        chunk[5] = rows_from(chunk[4], 1)
+        chunk[6] = rows_from(chunk[4], 2)
         near = gather_cent(near_own)
         n_near = len(near) * near_own.shape[0]
-        far_own = hold(far_own, chunk[1], chunk[2], chunk[4])[0]
         done, piece = first_pass(near + gather_cent(far_own), [chunk[b] for b in GROUPS[0]])
-        chunk[7], done = hold(chunk[7], done)
-        passes = [done]
-        for bits in GROUPS[1:]:
-            passes.append(first_pass([piece], [chunk[b] for b in bits], bits == GROUPS[-1])[0])
+        chunk[5], chunk[6], done = hold(chunk[5], chunk[6], done)
+        parts = (rows_from(chunk[6][:half], 1), rows_from(chunk[5][half:], 2))
+        passes = [done, first_pass([piece], [chunk[b] for b in GROUPS[1]])[0]]
+        parts, passes = hold(parts, passes)
+        chunk[7] = jnp.concatenate(parts, axis=0)
+        passes.append(first_pass([piece], [chunk[b] for b in GROUPS[2]], True)[0])
         local, row_sqs, rows = zip(*passes)
 
         stats = by_position(by_chunk(local))
@@ -303,28 +309,19 @@
         coarse = lax.reduce_precision(count, 8, 7)
         lane = lax.broadcasted_iota(jnp.int32, count.shape, 1)
         far = jnp.concatenate([far[:, :width], jnp.where(lane < 64, coarse, count - coarse)], axis=1)
-        far = [flip(p, top_bit) for p in jnp.split(far.astype(jnp.bfloat16), cuts, axis=0)]
+        far = flip(far.astype(jnp.bfloat16), top_bit).astype(jnp.float32)
         near = scatter_cent(sums_pass(piece, final, row_sqs, rows, 0, n_near))
-        updated, near_own = [], []
-        for p, (here, there) in enumerate(zip(jnp.split(near, cuts, axis=0), far)):
-            if p:
-                there = hold(there, near_own[-1])[0]
-            there = there.astype(jnp.float32)
-            counts = there[:, width : width + 1] + there[:, width + 64 : width + 65]
-            there = jnp.concatenate([there[:, :width], jnp.broadcast_to(counts, (there.shape[0], 128))], axis=1)
-            sums = scatter_near(here + there)
-            at = cuts[0] if p else 0
-            prior = prior_mass * centroids[at : at + sums.shape[0]]
-            updated.append((sums[:, :width] + prior) / (sums[:, width : width + 1] + prior_mass))
-            near_own.append(gather_near(updated[-1].astype(jnp.bfloat16)))
-        far_own = [flip(p, top_bit) for p in near_own]
-        near = [b for p in near_own for b in gather_cent(p)]
-        stats = [second_pass(jnp.concatenate(near, axis=0), row_sqs, rows, shard)]
-        for p in far_own:
-            p, stats[-1] = hold(p, stats[-1]) if p is far_own[-1] else (p, stats[-1])
-            stats.append(second_pass(jnp.concatenate(gather_cent(p), axis=0), row_sqs, rows, shard))
-        stats = functools.reduce(merge, stats)
-        updated = jnp.concatenate(updated, axis=0)
+        counts = far[:, width : width + 1] + far[:, width + 64 : width + 65]
+        far = jnp.concatenate([far[:, :width], jnp.broadcast_to(counts, count.shape)], axis=1)
+        sums = scatter_near(near + far)
+        updated = (sums[:, :width] + prior_mass * centroids) / (sums[:, width : width + 1] + prior_mass)
+        near_own = gather_near(updated.astype(jnp.bfloat16))
+        far_own = flip(near_own, top_bit)
+        stats = second_pass(jnp.concatenate(gather_cent(near_own), axis=0), row_sqs, rows, shard)
+        far_own, stats = hold(far_own, stats)
+        far = gather_cent(far_own)
+        stats = merge(stats, second_pass(far_own, row_sqs, rows, shard))
+        stats = merge(stats, second_pass(jnp.concatenate(far[1:], axis=0), row_sqs, rows, shard))
         stats = to_owner(by_position(stats))
         drop = stats[:, 0] - jnp.max(stats[:, 0], axis=0)
         factor = jnp.exp(drop)

time: 99.4 us -> 105 us (1.056)
  blocking collectives: 10.8 us -> 19.9 us
  starting transfers between devices: 23.4 us -> 19.4 us
  waiting for transfers between devices: 42.8 us -> 40.3 us
  Pallas kernels: 13.8 us -> 15.3 us
    all_to_all x1 -> x2, blocking collectives: 10.8 us -> 19.9 us  [exchange(): return lax.all_to_all(value, 'dp', 0, 0, axis_index_groups=groups)]
    all_to_all x1 -> x0, waiting for transfers between devices: 4.81 us -> none  [exchange(): return lax.all_to_all(value, 'dp', 0, 0, axis_index_groups=groups)]
    all_to_all x1 -> x0, starting transfers between devices: 3.33 us -> none  [exchange(): return lax.all_to_all(value, 'dp', 0, 0, axis_index_groups=groups)]
    ppermute x13 -> x11, waiting for transfers between devices: 37.4 us -> 40 us  [flip(): return lax.ppermute(value, 'dp', [(i, i ^ bits) for i in range(n_dp)])]
    unnamed x8 -> x15, local copies, waits for them, and re-layouts: 0.06 us -> 1.87 us
    pallas_call x2 -> x3, Pallas kernels: 4.84 us -> 5.72 us  [first_pass(): pl.pallas_call(functools.partial(first_kernel, n, n_blocks, shard, last),...]
    ppermute x13 -> x11, starting transfers between devices: 18.8 us -> 18.7 us  [flip(): return lax.ppermute(value, 'dp', [(i, i ^ bits) for i in range(n_dp)])]
  transfers between devices with their start and end apart: 22 -> 17, of which waited for: 10 -> 9; matrix products, arithmetic and copies ran while one was open for 4% -> 1% of each run, Pallas kernels for 8% -> 10%
where the time goes in v7:
time: 105 us
  waiting for transfers between devices  40.3 us (38%)
  blocking collectives  19.9 us (19%)
  starting transfers between devices  19.4 us (18%)
  Pallas kernels  15.3 us (15%)
  other arithmetic  5.04 us (5%)
  local copies, waits for them, and re-layouts  3.66 us (3%)
  between operations  1.14 us (1%)
    ppermute x11, waiting for transfers between devices, flip(): return lax.ppermute(value, 'dp', [(i, i ^ bits) for i in range(n_dp)])  40 us
    all_to_all x2, blocking collectives, exchange(): return lax.all_to_all(value, 'dp', 0, 0, axis_index_groups=groups)  19.9 us
    ppermute x11, starting transfers between devices, flip(): return lax.ppermute(value, 'dp', [(i, i ^ bits) for i in range(n_dp)])  18.7 us
    pallas_call x3, Pallas kernels, first_pass(): pl.pallas_call(functools.partial(first_kernel, n, n_blocks, shard, last),...  5.72 us
    pallas_call x2, Pallas kernels, sums_pass(): pl.pallas_call(functools.partial(sums_kernel, first, last, n), out_shape=...  5.56 us
    pallas_call x3, Pallas kernels, second_pass(): pl.pallas_call(functools.partial(second_kernel, shard, n), out_shape=tupl...  4.05 us
  transfers between devices with their start and end apart: 17, of which 9 were waited for; matrix products, arithmetic and copies ran while one was open for 1% of the time, Pallas kernels for 10%

profile of v7, /device:TPU:0, one launch (start us, length us, event | category | flops | bytes accessed | tf_op | source)
XLA Modules:
  0.0 104.7 jit_solution(16597553604470681218)
XLA Ops:
  0.6 0.0 copy-start.2
  0.6 1.2 %convert_element_type.14.refs_4_ = bf16[192,1024]{1,0:T(8,128)(2,1)S(1)} convert(f32[192,1024]{1,0:T(8,128)} %param.2) | non-fusion elementwise | flops 196608 | bytes 1179648 | tf_op jit(solution)/shard_map/convert_element_type | solution.py:280
  1.9 3.0 %collective-permute-start.2 = (bf16[192,1024]{1,0:T(8,128)(2,1)S(1)}, bf16[192,1024]{1,0:T(8,128)(2,1)S(1)}, u32[]{:S(2)}, u32[]{:S(2)}) collective-permute-start(bf16[192,1024]{1,0:T(8,128)(2,1)S(1)} %convert_element_type.14.refs_4_), channel_id=1, source_target_pairs={{0,2},{2,0},{4,6},{6,4},{8,10},{10,8},{12,14},{14,12},{16,18},{18,... | collective-permute-start | bytes 1179656 | tf_op jit(solution)/shard_map/ppermute | solution.py:218
  4.9 2.6 %collective-permute-start.1 = (bf16[192,1024]{1,0:T(8,128)(2,1)S(1)}, bf16[192,1024]{1,0:T(8,128)(2,1)S(1)}, u32[]{:S(2)}, u32[]{:S(2)}) collective-permute-start(bf16[192,1024]{1,0:T(8,128)(2,1)S(1)} %convert_element_type.14.refs_4_), channel_id=1, source_target_pairs={{0,16},{2,18},{4,20},{6,22},{8,24},{10,26},{12,28},{14,30},{16,0},... | collective-permute-start | bytes 1179656 | tf_op jit(solution)/shard_map/ppermute | solution.py:218
  7.5 1.5 %collective-permute-start.4 = (bf16[192,1024]{1,0:T(8,128)(2,1)S(1)}, bf16[192,1024]{1,0:T(8,128)(2,1)S(1)}, u32[]{:S(2)}, u32[]{:S(2)}) collective-permute-start(bf16[192,1024]{1,0:T(8,128)(2,1)S(1)} %convert_element_type.14.refs_4_), channel_id=1, source_target_pairs={{0,4},{2,6},{4,0},{6,2},{8,12},{10,14},{12,8},{14,10},{16,20},{18,... | collective-permute-start | bytes 1179656 | tf_op jit(solution)/shard_map/ppermute | solution.py:218
  9.0 5.0 %collective-permute-done.2.refs_5_ = bf16[192,1024]{1,0:T(8,128)(2,1)S(1)} collective-permute-done((bf16[192,1024]{1,0:T(8,128)(2,1)S(1)}, bf16[192,1024]{1,0:T(8,128)(2,1)S(1)}, u32[]{:S(2)}, u32[]{:S(2)}) %collective-permute-start.2) | collective-permute-done | bytes 393248 | tf_op jit(solution)/shard_map/ppermute | solution.py:218
  14.0 1.8 %collective-permute-start.3 = (bf16[192,1024]{1,0:T(8,128)(2,1)S(1)}, bf16[192,1024]{1,0:T(8,128)(2,1)S(1)}, u32[]{:S(2)}, u32[]{:S(2)}) collective-permute-start(bf16[192,1024]{1,0:T(8,128)(2,1)S(1)} %collective-permute-done.2.refs_5_), channel_id=1, source_target_pairs={{0,4},{2,6},{4,0},{6,2},{8,12},{10,14},{12,8},{14,10},{16,20},{18,... | collective-permute-start | bytes 1179656 | tf_op jit(solution)/shard_map/ppermute | solution.py:218
  15.8 0.0 copy-done.2
  15.8 1.6 %collective-permute-start.5 = (bf16[128,1024]{1,0:T(8,128)(2,1)S(1)}, bf16[128,1024]{1,0:T(8,128)(2,1)S(1)}, u32[]{:S(2)}, u32[]{:S(2)}) collective-permute-start(bf16[128,1024]{1,0:T(8,128)(2,1)S(1)} %convert_element_type.13.refs_0_), channel_id=1, source_target_pairs={{0,8},{2,10},{4,12},{6,14},{8,0},{10,2},{12,4},{14,6},{16,24},{18,... | collective-permute-start | bytes 786440 | tf_op jit(solution)/shard_map/ppermute | solution.py:218
  17.5 0.0 collective-permute-start
  17.5 12.6 %collective-permute-done.5.refs_2_ = bf16[128,1024]{1,0:T(8,128)(2,1)S(1)} collective-permute-done((bf16[128,1024]{1,0:T(8,128)(2,1)S(1)}, bf16[128,1024]{1,0:T(8,128)(2,1)S(1)}, u32[]{:S(2)}, u32[]{:S(2)}) %collective-permute-start.5) | collective-permute-done | bytes 262176 | tf_op jit(solution)/shard_map/ppermute | solution.py:218
  30.1 0.0 collective-permute-done.1.refs_1_
  30.1 0.0 collective-permute-done.4.refs_6_
  30.1 0.0 collective-permute-done.3.refs_7_
  30.1 0.1 collective-permute-start.6
  30.2 0.9 collective-permute-start.7
  31.1 1.2 %collective-permute-start.8 = (bf16[192,1024]{1,0:T(8,128)(2,1)S(1)}, bf16[192,1024]{1,0:T(8,128)(2,1)S(1)}, u32[]{:S(2)}, u32[]{:S(2)}) collective-permute-start(bf16[192,1024]{1,0:T(8,128)(2,1)S(1)} %collective-permute-done.1.refs_1_), channel_id=1, source_target_pairs={{0,4},{2,6},{4,0},{6,2},{8,12},{10,14},{12,8},{14,10},{16,20},{18,... | collective-permute-start | bytes 1179656 | tf_op jit(solution)/shard_map/ppermute | solution.py:218
  32.3 0.0 collective-permute-done.refs_1_
  32.3 0.0 collective-permute-done.6.refs_3_
  32.3 3.0 %first_pass.3 = (f32[2,4,192]{2,1,0:T(4,128)S(1)}, f32[1,768]{1,0:T(1,128)S(1)}, bf16[768,1024]{1,0:T(8,128)(2,1)S(1)}, bf16[512,1024]{1,0:T(8,128)(2,1)S(1)}) custom-call(bf16[128,1024]{1,0:T(8,128)(2,1)S(1)} %convert_element_type.13.refs_0_, bf16[128,1024]{1,0:T(8,128)(2,1)S(1)} %collective-permute-done.refs_1_, ...), custom_call_target="tpu_custom_call" | custom-call | flops 6442450944 | bytes 1572864 | tf_op jit(solution)/shard_map/first_pass/pallas_call | solution.py:98
  35.3 0.0 copy-done
  35.3 6.4 %collective-permute-done.7.refs_2_ = bf16[192,1024]{1,0:T(8,128)(2,1)S(1)} collective-permute-done((bf16[192,1024]{1,0:T(8,128)(2,1)S(1)}, bf16[192,1024]{1,0:T(8,128)(2,1)S(1)}, u32[]{:S(2)}, u32[]{:S(2)}) %collective-permute-start.7) | collective-permute-done | bytes 393248 | tf_op jit(solution)/shard_map/ppermute | solution.py:218
  41.7 0.5 collective-permute-done.8.refs_1_
  42.2 0.7 slice.326
  42.9 1.2 %collective-permute-start.10 = (bf16[96,1024]{1,0:T(8,128)(2,1)}, bf16[96,1024]{1,0:T(8,128)(2,1)}, u32[]{:S(2)}, u32[]{:S(2)}) collective-permute-start(bf16[96,1024]{1,0:T(8,128)(2,1)} %slice.326), channel_id=1, source_target_pairs={{0,4},{2,6},{4,0},{6,2},{8,12},{10,14},{12,8},{14,10},{16,20},{18,... | collective-permute-start | bytes 589832 | tf_op jit(solution)/shard_map/ppermute | solution.py:218
  44.1 0.7 slice.325
  44.8 0.6 collective-permute-start.9
  45.4 1.0 copy-done.1
  46.4 1.7 %first_pass.4 = (f32[2,2,192]{2,1,0:T(2,128)S(1)}, f32[1,384]{1,0:T(1,128)S(1)}, bf16[384,1024]{1,0:T(8,128)(2,1)S(1)}) custom-call(bf16[512,1024]{1,0:T(8,128)(2,1)S(1)} %get-tuple-element.43.refs_0_.cents, bf16[192,1024]{1,0:T(8,128)(2,1)S(1)} %copy-done.1, bf16[192,1024]{1,0:T(8,128)(2,1)S(1)} %collective-permute-done.7.refs_2_), custom_call_target="tpu_custom_call" | custom-call | flops 402653184 | bytes 786432 | tf_op jit(solution)/shard_map/first_pass/pallas_call | solution.py:98
  48.1 1.3 %collective-permute-done.10 = bf16[96,1024]{1,0:T(8,128)(2,1)} collective-permute-done((bf16[96,1024]{1,0:T(8,128)(2,1)}, bf16[96,1024]{1,0:T(8,128)(2,1)}, u32[]{:S(2)}, u32[]{:S(2)}) %collective-permute-start.10) | collective-permute-done | bytes 196640 | tf_op jit(solution)/shard_map/ppermute | solution.py:218
  49.4 1.6 %collective-permute-done.9 = bf16[96,1024]{1,0:T(8,128)(2,1)} collective-permute-done((bf16[96,1024]{1,0:T(8,128)(2,1)}, bf16[96,1024]{1,0:T(8,128)(2,1)}, u32[]{:S(2)}, u32[]{:S(2)}) %collective-permute-start.9) | collective-permute-done | bytes 196640 | tf_op jit(solution)/shard_map/ppermute | solution.py:218
  51.0 1.0 %pad_maximum_fusion.1.refs_2_ = bf16[192,1024]{1,0:T(8,128)(2,1)S(1)} fusion(bf16[96,1024]{1,0:T(8,128)(2,1)} %collective-permute-done.10, bf16[96,1024]{1,0:T(8,128)(2,1)} %collective-permute-done.9), kind=kLoop, calls=%fused_computation.7 | loop fusion | flops 786432 | bytes 786432 | tf_op jit(solution)/shard_map/concatenate | solution.py:296
  52.0 1.0 first_pass.5
  53.3 10.9 %all_to_all.10 = f32[8,2,8,192]{3,2,1,0:T(8,128)S(1)} all-to-all(f32[8,2,8,192]{3,2,1,0:T(8,128)S(1)} %broadcast_in_dim.6), channel_id=1, replica_groups={{0,2,4,6,16,18,20,22},{8,10,12,14,24,26,28,30},{1,3,5,7,17,19,21,23},{9..., dimensions={0} | all-to-all | bytes 196608 | tf_op jit(solution)/shard_map/all_to_all | solution.py:269
  64.6 0.1 pad_maximum_fusion.9
  64.6 0.1 pad_maximum_fusion.8.refs_0_
  64.7 2.8 %sums_pass.3 = f32[256,1152]{1,0:T(8,128)S(1)} custom-call(bf16[512,1024]{1,0:T(8,128)(2,1)S(1)} %get-tuple-element.43.refs_0_.cents, f32[2,768]{1,0:T(2,128)S(1)} %pad_maximum_fusion.8.refs_0_, f32[2,384]{1,0:T(2,128)S(1)} %get-tuple-element.123.refs_1_, f32[2,384]{1,0:T(2,128)S(1)} %get-tuple-element.124.refs_2_, ...), custom_call_target="tpu_custom_call" | custom-call | flops 1610612736 | bytes 3145728 | tf_op jit(solution)/shard_map/sums_pass/pallas_call | solution.py:137
  67.6 0.1 collective-permute-start.12
  67.6 2.8 %sums_pass.2 = f32[256,1152]{1,0:T(8,128)S(1)} custom-call(bf16[512,1024]{1,0:T(8,128)(2,1)S(1)} %get-tuple-element.43.refs_0_.cents, f32[2,768]{1,0:T(2,128)S(1)} %pad_maximum_fusion.8.refs_0_, f32[2,384]{1,0:T(2,128)S(1)} %get-tuple-element.123.refs_1_, f32[2,384]{1,0:T(2,128)S(1)} %get-tuple-element.124.refs_2_, ...), custom_call_target="tpu_custom_call" | custom-call | flops 1610612736 | bytes 3145728 | tf_op jit(solution)/shard_map/sums_pass/pallas_call | solution.py:137
  70.5 0.6 collective-permute-start.11
  71.0 0.0 collective-permute-done.12
  71.0 0.1 slice_add_fusion
  71.2 2.6 %collective-permute-start.13 = (bf16[128,1152]{1,0:T(8,128)(2,1)S(1)}, bf16[128,1152]{1,0:T(8,128)(2,1)S(1)}, u32[]{:S(2)}, u32[]{:S(2)}) collective-permute-start(bf16[128,1152]{1,0:T(8,128)(2,1)S(1)} %pad_maximum_fusion.2), channel_id=1, source_target_pairs={{0,8},{2,10},{4,12},{6,14},{8,0},{10,2},{12,4},{14,6},{16,24},{18,... | collective-permute-start | bytes 884744 | tf_op jit(solution)/shard_map/ppermute | solution.py:218
  73.8 7.2 %collective-permute-done.13 = bf16[128,1152]{1,0:T(8,128)(2,1)S(1)} collective-permute-done((bf16[128,1152]{1,0:T(8,128)(2,1)S(1)}, bf16[128,1152]{1,0:T(8,128)(2,1)S(1)}, u32[]{:S(2)}, u32[]{:S(2)}) %collective-permute-start.13) | collective-permute-done | bytes 294944 | tf_op jit(solution)/shard_map/ppermute | solution.py:218
  81.1 0.2 fusion.4
  81.2 0.0 collective-permute-done.11
  81.3 0.1 broadcast_in_dim.8
  81.3 0.0 copy-start.3
  81.3 0.1 fusion
  81.5 0.1 fusion.3
  81.6 0.8 copy-done.3
  82.4 0.9 fusion.27
  83.3 0.0 collective-permute-start.15
  83.3 1.7 %collective-permute-start.14 = (bf16[128,1024]{1,0:T(8,128)(2,1)S(1)}, bf16[128,1024]{1,0:T(8,128)(2,1)S(1)}, u32[]{:S(2)}, u32[]{:S(2)}) collective-permute-start(bf16[128,1024]{1,0:T(8,128)(2,1)S(1)} %get-tuple-element.80), channel_id=1, source_target_pairs={{0,8},{2,10},{4,12},{6,14},{8,0},{10,2},{12,4},{14,6},{16,24},{18,... | collective-permute-start | bytes 786440 | tf_op jit(solution)/shard_map/ppermute | solution.py:218
  85.1 0.0 collective-permute-done.15
  85.1 1.6 %second_pass.3 = (f32[3,4,192]{2,1,0:T(4,128)S(1)}, f32[3,2,192]{2,1,0:T(2,128)S(1)}, f32[3,2,192]{2,1,0:T(2,128)S(1)}) custom-call(bf16[256,1024]{1,0:T(8,128)(2,1)S(1)} %pad_maximum_fusion.cents, f32[1,768]{1,0:T(1,128)S(1)} %get-tuple-element.61.refs_3_.refs_0_, f32[1,384]{1,0:T(1,128)S(1)} %get-tuple-element.62.refs_4_.refs_1_, ...), custom_call_target="tpu_custom_call" | custom-call | flops 805306368 | bytes 3145728 | tf_op jit(solution)/shard_map/second_pass/pallas_call | solution.py:178
  86.7 5.3 %collective-permute-done.14.cents = bf16[128,1024]{1,0:T(8,128)(2,1)S(1)} collective-permute-done((bf16[128,1024]{1,0:T(8,128)(2,1)S(1)}, bf16[128,1024]{1,0:T(8,128)(2,1)S(1)}, u32[]{:S(2)}, u32[]{:S(2)}) %collective-permute-start.14) | collective-permute-done | bytes 262176 | tf_op jit(solution)/shard_map/ppermute | solution.py:218
  92.0 0.0 collective-permute-start.16
  92.0 1.2 %second_pass.4 = (f32[3,4,192]{2,1,0:T(4,128)S(1)}, f32[3,2,192]{2,1,0:T(2,128)S(1)}, f32[3,2,192]{2,1,0:T(2,128)S(1)}) custom-call(bf16[128,1024]{1,0:T(8,128)(2,1)S(1)} %collective-permute-done.14.cents, f32[1,768]{1,0:T(1,128)S(1)} %get-tuple-element.61.refs_3_.refs_0_, f32[1,384]{1,0:T(1,128)S(1)} %get-tuple-element.62.refs_4_.refs_1_, ...), custom_call_target="tpu_custom_call" | custom-call | flops 402653184 | bytes 3145728 | tf_op jit(solution)/shard_map/second_pass/pallas_call | solution.py:178
  93.3 0.3 collective-permute-done.16.cents
  93.6 1.2 %second_pass.5 = (f32[3,4,192]{2,1,0:T(4,128)S(1)}, f32[3,2,192]{2,1,0:T(2,128)S(1)}, f32[3,2,192]{2,1,0:T(2,128)S(1)}) custom-call(bf16[128,1024]{1,0:T(8,128)(2,1)S(1)} %collective-permute-done.16.cents, f32[1,768]{1,0:T(1,128)S(1)} %get-tuple-element.61.refs_3_.refs_0_, f32[1,384]{1,0:T(1,128)S(1)} %get-tuple-element.62.refs_4_.refs_1_, ...), custom_call_target="tpu_custom_call" | custom-call | flops 402653184 | bytes 3145728 | tf_op jit(solution)/shard_map/second_pass/pallas_call | solution.py:178
  94.9 0.1 stack.78
  95.1 9.0 %all_to_all.11 = f32[8,3,192]{2,1,0:T(4,128)S(1)} all-to-all(f32[8,3,192]{2,1,0:T(4,128)S(1)} %copy.74), channel_id=1, replica_groups={{0,2,4,6,16,18,20,22},{8,10,12,14,24,26,28,30},{1,3,5,7,17,19,21,23},{9..., dimensions={0} | all-to-all | bytes 36864 | tf_op jit(solution)/shard_map/all_to_all | solution.py:269
  104.1 0.6 divide_subtract_fusion
  (62 shorter events, 1.0 us)
Async XLA Ops:
  0.6 15.1 %copy-start.2 = (f32[128,1024]{1,0:T(8,128)S(1)}, f32[128,1024]{1,0:T(8,128)}, u32[]{:S(2)}) copy-start(f32[128,1024]{1,0:T(8,128)} %param.3) | copy-start | bytes 1572868
  1.9 12.1 %collective-permute-start.2 = (bf16[192,1024]{1,0:T(8,128)(2,1)S(1)}, bf16[192,1024]{1,0:T(8,128)(2,1)S(1)}, u32[]{:S(2)}, u32[]{:S(2)}) collective-permute-start(bf16[192,1024]{1,0:T(8,128)(2,1)S(1)} %convert_element_type.14.refs_4_), channel_id=1, source_target_pairs={{0,2},{2,0},{4,6},{6,4},{8,10},{10,8},{12,14},{14,12},{16,18},{18,... | collective-permute-start | bytes 1179656 | tf_op jit(solution)/shard_map/ppermute | solution.py:218
  4.9 25.2 %collective-permute-start.1 = (bf16[192,1024]{1,0:T(8,128)(2,1)S(1)}, bf16[192,1024]{1,0:T(8,128)(2,1)S(1)}, u32[]{:S(2)}, u32[]{:S(2)}) collective-permute-start(bf16[192,1024]{1,0:T(8,128)(2,1)S(1)} %convert_element_type.14.refs_4_), channel_id=1, source_target_pairs={{0,16},{2,18},{4,20},{6,22},{8,24},{10,26},{12,28},{14,30},{16,0},... | collective-permute-start | bytes 1179656 | tf_op jit(solution)/shard_map/ppermute | solution.py:218
  7.5 22.6 %collective-permute-start.4 = (bf16[192,1024]{1,0:T(8,128)(2,1)S(1)}, bf16[192,1024]{1,0:T(8,128)(2,1)S(1)}, u32[]{:S(2)}, u32[]{:S(2)}) collective-permute-start(bf16[192,1024]{1,0:T(8,128)(2,1)S(1)} %convert_element_type.14.refs_4_), channel_id=1, source_target_pairs={{0,4},{2,6},{4,0},{6,2},{8,12},{10,14},{12,8},{14,10},{16,20},{18,... | collective-permute-start | bytes 1179656 | tf_op jit(solution)/shard_map/ppermute | solution.py:218
  14.0 16.1 %collective-permute-start.3 = (bf16[192,1024]{1,0:T(8,128)(2,1)S(1)}, bf16[192,1024]{1,0:T(8,128)(2,1)S(1)}, u32[]{:S(2)}, u32[]{:S(2)}) collective-permute-start(bf16[192,1024]{1,0:T(8,128)(2,1)S(1)} %collective-permute-done.2.refs_5_), channel_id=1, source_target_pairs={{0,4},{2,6},{4,0},{6,2},{8,12},{10,14},{12,8},{14,10},{16,20},{18,... | collective-permute-start | bytes 1179656 | tf_op jit(solution)/shard_map/ppermute | solution.py:218
  15.8 14.3 %collective-permute-start.5 = (bf16[128,1024]{1,0:T(8,128)(2,1)S(1)}, bf16[128,1024]{1,0:T(8,128)(2,1)S(1)}, u32[]{:S(2)}, u32[]{:S(2)}) collective-permute-start(bf16[128,1024]{1,0:T(8,128)(2,1)S(1)} %convert_element_type.13.refs_0_), channel_id=1, source_target_pairs={{0,8},{2,10},{4,12},{6,14},{8,0},{10,2},{12,4},{14,6},{16,24},{18,... | collective-permute-start | bytes 786440 | tf_op jit(solution)/shard_map/ppermute | solution.py:218
  17.5 14.8 %collective-permute-start = (bf16[128,1024]{1,0:T(8,128)(2,1)S(1)}, bf16[128,1024]{1,0:T(8,128)(2,1)S(1)}, u32[]{:S(2)}, u32[]{:S(2)}) collective-permute-start(bf16[128,1024]{1,0:T(8,128)(2,1)S(1)} %convert_element_type.13.refs_0_), channel_id=1, source_target_pairs={{0,1},{1,0},{2,3},{3,2},{4,5},{5,4},{6,7},{7,6},{8,9},{9,8},{10,11... | collective-permute-start | bytes 786440 | tf_op jit(solution)/shard_map/ppermute | solution.py:227
  30.1 5.2 %copy-start = (bf16[192,1024]{1,0:T(8,128)(2,1)}, bf16[192,1024]{1,0:T(8,128)(2,1)S(1)}, u32[]{:S(2)}) copy-start(bf16[192,1024]{1,0:T(8,128)(2,1)S(1)} %collective-permute-done.1.refs_1_) | copy-start | bytes 1179652
  30.1 2.1 %collective-permute-start.6 = (bf16[128,1024]{1,0:T(8,128)(2,1)S(1)}, bf16[128,1024]{1,0:T(8,128)(2,1)S(1)}, u32[]{:S(2)}, u32[]{:S(2)}) collective-permute-start(bf16[128,1024]{1,0:T(8,128)(2,1)S(1)} %collective-permute-done.5.refs_2_), channel_id=1, source_target_pairs={{0,1},{1,0},{2,3},{3,2},{4,5},{5,4},{6,7},{7,6},{8,9},{9,8},{10,11... | collective-permute-start | bytes 786440 | tf_op jit(solution)/shard_map/ppermute | solution.py:227
  30.2 11.5 %collective-permute-start.7 = (bf16[192,1024]{1,0:T(8,128)(2,1)S(1)}, bf16[192,1024]{1,0:T(8,128)(2,1)S(1)}, u32[]{:S(2)}, u32[]{:S(2)}) collective-permute-start(bf16[192,1024]{1,0:T(8,128)(2,1)S(1)} %collective-permute-done.1.refs_1_), channel_id=1, source_target_pairs={{0,2},{2,0},{4,6},{6,4},{8,10},{10,8},{12,14},{14,12},{16,18},{18,... | collective-permute-start | bytes 1179656 | tf_op jit(solution)/shard_map/ppermute | solution.py:218
  31.1 11.2 %collective-permute-start.8 = (bf16[192,1024]{1,0:T(8,128)(2,1)S(1)}, bf16[192,1024]{1,0:T(8,128)(2,1)S(1)}, u32[]{:S(2)}, u32[]{:S(2)}) collective-permute-start(bf16[192,1024]{1,0:T(8,128)(2,1)S(1)} %collective-permute-done.1.refs_1_), channel_id=1, source_target_pairs={{0,4},{2,6},{4,0},{6,2},{8,12},{10,14},{12,8},{14,10},{16,20},{18,... | collective-permute-start | bytes 1179656 | tf_op jit(solution)/shard_map/ppermute | solution.py:218
  42.9 6.5 %collective-permute-start.10 = (bf16[96,1024]{1,0:T(8,128)(2,1)}, bf16[96,1024]{1,0:T(8,128)(2,1)}, u32[]{:S(2)}, u32[]{:S(2)}) collective-permute-start(bf16[96,1024]{1,0:T(8,128)(2,1)} %slice.326), channel_id=1, source_target_pairs={{0,4},{2,6},{4,0},{6,2},{8,12},{10,14},{12,8},{14,10},{16,20},{18,... | collective-permute-start | bytes 589832 | tf_op jit(solution)/shard_map/ppermute | solution.py:218
  44.8 6.2 %collective-permute-start.9 = (bf16[96,1024]{1,0:T(8,128)(2,1)}, bf16[96,1024]{1,0:T(8,128)(2,1)}, u32[]{:S(2)}, u32[]{:S(2)}) collective-permute-start(bf16[96,1024]{1,0:T(8,128)(2,1)} %slice.325), channel_id=1, source_target_pairs={{0,2},{2,0},{4,6},{6,4},{8,10},{10,8},{12,14},{14,12},{16,18},{18,... | collective-permute-start | bytes 589832 | tf_op jit(solution)/shard_map/ppermute | solution.py:218
  45.4 1.0 copy-start.1
  67.6 3.5 %collective-permute-start.12 = (f32[128,1152]{1,0:T(8,128)S(1)}, f32[128,1152]{1,0:T(8,128)S(1)}, u32[]{:S(2)}, u32[]{:S(2)}) collective-permute-start(f32[128,1152]{1,0:T(8,128)S(1)} %slice.451), channel_id=1, source_target_pairs={{0,1},{1,0},{2,3},{3,2},{4,5},{5,4},{6,7},{7,6},{8,9},{9,8},{10,11... | collective-permute-start | bytes 1769480 | tf_op jit(solution)/shard_map/ppermute | solution.py:227
  70.5 10.8 %collective-permute-start.11 = (f32[128,1152]{1,0:T(8,128)S(1)}, f32[128,1152]{1,0:T(8,128)S(1)}, u32[]{:S(2)}, u32[]{:S(2)}) collective-permute-start(f32[128,1152]{1,0:T(8,128)S(1)} %slice.449), channel_id=1, source_target_pairs={{0,1},{1,0},{2,3},{3,2},{4,5},{5,4},{6,7},{7,6},{8,9},{9,8},{10,11... | collective-permute-start | bytes 1769480 | tf_op jit(solution)/shard_map/ppermute | solution.py:227
  71.2 9.8 %collective-permute-start.13 = (bf16[128,1152]{1,0:T(8,128)(2,1)S(1)}, bf16[128,1152]{1,0:T(8,128)(2,1)S(1)}, u32[]{:S(2)}, u32[]{:S(2)}) collective-permute-start(bf16[128,1152]{1,0:T(8,128)(2,1)S(1)} %pad_maximum_fusion.2), channel_id=1, source_target_pairs={{0,8},{2,10},{4,12},{6,14},{8,0},{10,2},{12,4},{14,6},{16,24},{18,... | collective-permute-start | bytes 884744 | tf_op jit(solution)/shard_map/ppermute | solution.py:218
  81.3 1.1 %copy-start.3 = (f32[128,1024]{1,0:T(8,128)S(1)}, f32[128,1024]{1,0:T(8,128)}, u32[]{:S(2)}) copy-start(f32[128,1024]{1,0:T(8,128)} %param.3) | copy-start | bytes 1572868
  83.3 1.7 %collective-permute-start.15 = (bf16[128,1024]{1,0:T(8,128)(2,1)S(1)}, bf16[128,1024]{1,0:T(8,128)(2,1)S(1)}, u32[]{:S(2)}, u32[]{:S(2)}) collective-permute-start(bf16[128,1024]{1,0:T(8,128)(2,1)S(1)} %get-tuple-element.80), channel_id=1, source_target_pairs={{0,1},{1,0},{2,3},{3,2},{4,5},{5,4},{6,7},{7,6},{8,9},{9,8},{10,11... | collective-permute-start | bytes 786440 | tf_op jit(solution)/shard_map/ppermute | solution.py:227
  83.3 8.7 %collective-permute-start.14 = (bf16[128,1024]{1,0:T(8,128)(2,1)S(1)}, bf16[128,1024]{1,0:T(8,128)(2,1)S(1)}, u32[]{:S(2)}, u32[]{:S(2)}) collective-permute-start(bf16[128,1024]{1,0:T(8,128)(2,1)S(1)} %get-tuple-element.80), channel_id=1, source_target_pairs={{0,8},{2,10},{4,12},{6,14},{8,0},{10,2},{12,4},{14,6},{16,24},{18,... | collective-permute-start | bytes 786440 | tf_op jit(solution)/shard_map/ppermute | solution.py:218
  92.0 1.5 %collective-permute-start.16 = (bf16[128,1024]{1,0:T(8,128)(2,1)S(1)}, bf16[128,1024]{1,0:T(8,128)(2,1)S(1)}, u32[]{:S(2)}, u32[]{:S(2)}) collective-permute-start(bf16[128,1024]{1,0:T(8,128)(2,1)S(1)} %collective-permute-done.14.cents), channel_id=1, source_target_pairs={{0,1},{1,0},{2,3},{3,2},{4,5},{5,4},{6,7},{7,6},{8,9},{9,8},{10,11... | collective-permute-start | bytes 786440 | tf_op jit(solution)/shard_map/ppermute | solution.py:227

commit v8 on v7

--- a/solution.py
+++ b/solution.py
@@ -103,7 +103,7 @@
         scratch_shapes=[pltpu.SemaphoreType.DMA((n,))],
         compiler_params=params(),
         cost_estimate=pl.CostEstimate(
-            flops=(16 if n_blocks > 1 else 2) * n_k * n_rows * width,
+            flops=2 * n_k * n_rows * width,
             bytes_accessed=2 * n_rows * width,
             transcendentals=n_k * n_rows,
         ),
@@ -280,17 +280,16 @@
         chunk = {0: embeddings.astype(jnp.bfloat16)}
         for bit in (4, 1, 2):
             chunk[bit] = rows_from(chunk[0], bit)
+        chunk[3] = rows_from(chunk[1], 2)
         near_own = gather_near(centroids.astype(jnp.bfloat16))
         far_own = flip(near_own, top_bit)
-        chunk[3] = rows_from(chunk[1], 2)
-        chunk[4], chunk[3], chunk[2], far_own = hold(chunk[4], chunk[3], chunk[2], far_own)
+        chunk[4], chunk[3], chunk[2] = hold(chunk[4], chunk[3], chunk[2])
         chunk[5] = rows_from(chunk[4], 1)
         chunk[6] = rows_from(chunk[4], 2)
+        parts = (rows_from(chunk[3][:half], 4), rows_from(chunk[4][half:], 3))
         near = gather_cent(near_own)
         n_near = len(near) * near_own.shape[0]
         done, piece = first_pass(near + gather_cent(far_own), [chunk[b] for b in GROUPS[0]])
-        chunk[5], chunk[6], done = hold(chunk[5], chunk[6], done)
-        parts = (rows_from(chunk[6][:half], 1), rows_from(chunk[5][half:], 2))
         passes = [done, first_pass([piece], [chunk[b] for b in GROUPS[1]])[0]]
         parts, passes = hold(parts, passes)
         chunk[7] = jnp.concatenate(parts, axis=0)

time: 105 us -> 99.4 us (0.947)
  waiting for transfers between devices: 40.3 us -> 34.7 us
  blocking collectives: 19.9 us -> 18.7 us
  starting transfers between devices: 19.4 us -> 20.5 us
  Pallas kernels: 15.3 us -> 16.4 us
    ppermute x11, waiting for transfers between devices: 40 us -> 34.4 us  [flip(): return lax.ppermute(value, 'dp', [(i, i ^ bits) for i in range(n_dp)])]
    ppermute x11, starting transfers between devices: 18.7 us -> 19.8 us  [flip(): return lax.ppermute(value, 'dp', [(i, i ^ bits) for i in range(n_dp)])]
    all_to_all x2, blocking collectives: 19.9 us -> 18.7 us  [exchange(): return lax.all_to_all(value, 'dp', 0, 0, axis_index_groups=groups)]
  transfers between devices with their start and end apart: 17 -> 17, of which waited for: 9 -> 8; matrix products, arithmetic and copies ran while one was open for 1% -> 3% of each run, Pallas kernels for 10% -> 11%
where the time goes in v8:
time: 99.4 us; the launch traced here: 99.1 us
  waiting for transfers between devices  34.7 us (35%)
  starting transfers between devices  20.5 us (21%)
  blocking collectives  18.7 us (19%)
  Pallas kernels  16.4 us (16%)
  other arithmetic  4.99 us (5%)
  local copies, waits for them, and re-layouts  2.7 us (3%)
  between operations  1.14 us (1%)
    ppermute x11, waiting for transfers between devices, flip(): return lax.ppermute(value, 'dp', [(i, i ^ bits) for i in range(n_dp)])  34.4 us
    ppermute x11, starting transfers between devices, flip(): return lax.ppermute(value, 'dp', [(i, i ^ bits) for i in range(n_dp)])  19.8 us
    all_to_all x2, blocking collectives, exchange(): return lax.all_to_all(value, 'dp', 0, 0, axis_index_groups=groups)  18.7 us
    pallas_call x3, Pallas kernels, first_pass(): pl.pallas_call(functools.partial(first_kernel, n, n_blocks, shard, last),...  6.72 us
    pallas_call x2, Pallas kernels, sums_pass(): pl.pallas_call(functools.partial(sums_kernel, first, last, n), out_shape=...  5.58 us
    pallas_call x3, Pallas kernels, second_pass(): pl.pallas_call(functools.partial(second_kernel, shard, n), out_shape=tupl...  4.06 us
  transfers between devices with their start and end apart: 17, of which 8 were waited for; matrix products, arithmetic and copies ran while one was open for 3% of the time, Pallas kernels for 11%

profile of v8, /device:TPU:0, one launch (start us, length us, event | category | flops | bytes accessed | tf_op | source)
XLA Modules:
  0.0 99.1 jit_solution(7504896936002054096)
XLA Ops:
  0.6 0.0 copy-start
  0.6 1.2 %convert_element_type.14.refs_4_ = bf16[192,1024]{1,0:T(8,128)(2,1)S(1)} convert(f32[192,1024]{1,0:T(8,128)} %param.2) | non-fusion elementwise | flops 196608 | bytes 1179648 | tf_op jit(solution)/shard_map/convert_element_type | solution.py:280
  1.9 3.0 %collective-permute-start.3 = (bf16[192,1024]{1,0:T(8,128)(2,1)S(1)}, bf16[192,1024]{1,0:T(8,128)(2,1)S(1)}, u32[]{:S(2)}, u32[]{:S(2)}) collective-permute-start(bf16[192,1024]{1,0:T(8,128)(2,1)S(1)} %convert_element_type.14.refs_4_), channel_id=1, source_target_pairs={{0,2},{2,0},{4,6},{6,4},{8,10},{10,8},{12,14},{14,12},{16,18},{18,... | collective-permute-start | bytes 1179656 | tf_op jit(solution)/shard_map/ppermute | solution.py:218
  4.9 2.6 %collective-permute-start.4 = (bf16[192,1024]{1,0:T(8,128)(2,1)S(1)}, bf16[192,1024]{1,0:T(8,128)(2,1)S(1)}, u32[]{:S(2)}, u32[]{:S(2)}) collective-permute-start(bf16[192,1024]{1,0:T(8,128)(2,1)S(1)} %convert_element_type.14.refs_4_), channel_id=1, source_target_pairs={{0,16},{2,18},{4,20},{6,22},{8,24},{10,26},{12,28},{14,30},{16,0},... | collective-permute-start | bytes 1179656 | tf_op jit(solution)/shard_map/ppermute | solution.py:218
  7.5 1.5 %collective-permute-start.6 = (bf16[192,1024]{1,0:T(8,128)(2,1)S(1)}, bf16[192,1024]{1,0:T(8,128)(2,1)S(1)}, u32[]{:S(2)}, u32[]{:S(2)}) collective-permute-start(bf16[192,1024]{1,0:T(8,128)(2,1)S(1)} %convert_element_type.14.refs_4_), channel_id=1, source_target_pairs={{0,4},{2,6},{4,0},{6,2},{8,12},{10,14},{12,8},{14,10},{16,20},{18,... | collective-permute-start | bytes 1179656 | tf_op jit(solution)/shard_map/ppermute | solution.py:218
  9.0 5.0 %collective-permute-done.3.refs_5_ = bf16[192,1024]{1,0:T(8,128)(2,1)S(1)} collective-permute-done((bf16[192,1024]{1,0:T(8,128)(2,1)S(1)}, bf16[192,1024]{1,0:T(8,128)(2,1)S(1)}, u32[]{:S(2)}, u32[]{:S(2)}) %collective-permute-start.3) | collective-permute-done | bytes 393248 | tf_op jit(solution)/shard_map/ppermute | solution.py:218
  14.0 1.8 %collective-permute-start.5 = (bf16[192,1024]{1,0:T(8,128)(2,1)S(1)}, bf16[192,1024]{1,0:T(8,128)(2,1)S(1)}, u32[]{:S(2)}, u32[]{:S(2)}) collective-permute-start(bf16[192,1024]{1,0:T(8,128)(2,1)S(1)} %collective-permute-done.3.refs_5_), channel_id=1, source_target_pairs={{0,4},{2,6},{4,0},{6,2},{8,12},{10,14},{12,8},{14,10},{16,20},{18,... | collective-permute-start | bytes 1179656 | tf_op jit(solution)/shard_map/ppermute | solution.py:218
  15.8 0.0 copy-done
  15.8 1.6 %collective-permute-start.1 = (bf16[128,1024]{1,0:T(8,128)(2,1)S(1)}, bf16[128,1024]{1,0:T(8,128)(2,1)S(1)}, u32[]{:S(2)}, u32[]{:S(2)}) collective-permute-start(bf16[128,1024]{1,0:T(8,128)(2,1)S(1)} %convert_element_type.13.refs_0_), channel_id=1, source_target_pairs={{0,8},{2,10},{4,12},{6,14},{8,0},{10,2},{12,4},{14,6},{16,24},{18,... | collective-permute-start | bytes 786440 | tf_op jit(solution)/shard_map/ppermute | solution.py:218
  17.5 0.0 collective-permute-start
  17.5 7.4 %collective-permute-done.4.refs_1_ = bf16[192,1024]{1,0:T(8,128)(2,1)S(1)} collective-permute-done((bf16[192,1024]{1,0:T(8,128)(2,1)S(1)}, bf16[192,1024]{1,0:T(8,128)(2,1)S(1)}, u32[]{:S(2)}, u32[]{:S(2)}) %collective-permute-start.4) | collective-permute-done | bytes 393248 | tf_op jit(solution)/shard_map/ppermute | solution.py:218
  24.9 0.0 collective-permute-done.6.refs_6_
  24.9 1.3 %collective-permute-done.5.refs_7_ = bf16[192,1024]{1,0:T(8,128)(2,1)S(1)} collective-permute-done((bf16[192,1024]{1,0:T(8,128)(2,1)S(1)}, bf16[192,1024]{1,0:T(8,128)(2,1)S(1)}, u32[]{:S(2)}, u32[]{:S(2)}) %collective-permute-start.5) | collective-permute-done | bytes 393248 | tf_op jit(solution)/shard_map/ppermute | solution.py:218
  26.2 0.5 collective-permute-start.9
  26.7 3.4 %collective-permute-done.1.refs_2_ = bf16[128,1024]{1,0:T(8,128)(2,1)S(1)} collective-permute-done((bf16[128,1024]{1,0:T(8,128)(2,1)S(1)}, bf16[128,1024]{1,0:T(8,128)(2,1)S(1)}, u32[]{:S(2)}, u32[]{:S(2)}) %collective-permute-start.1) | collective-permute-done | bytes 262176 | tf_op jit(solution)/shard_map/ppermute | solution.py:218
  30.1 0.0 collective-permute-start.2
  30.1 0.6 collective-permute-start.10
  30.7 0.7 slice.326
  31.4 1.7 %collective-permute-start.8 = (bf16[96,1024]{1,0:T(8,128)(2,1)}, bf16[96,1024]{1,0:T(8,128)(2,1)}, u32[]{:S(2)}, u32[]{:S(2)}) collective-permute-start(bf16[96,1024]{1,0:T(8,128)(2,1)} %slice.326), channel_id=1, source_target_pairs={{0,6},{2,4},{4,2},{6,0},{8,14},{10,12},{12,10},{14,8},{16,22},{18,... | collective-permute-start | bytes 589832 | tf_op jit(solution)/shard_map/ppermute | solution.py:218
  33.1 0.7 slice.325
  33.8 0.0 collective-permute-done.refs_1_
  33.8 1.6 %collective-permute-start.7 = (bf16[96,1024]{1,0:T(8,128)(2,1)}, bf16[96,1024]{1,0:T(8,128)(2,1)}, u32[]{:S(2)}, u32[]{:S(2)}) collective-permute-start(bf16[96,1024]{1,0:T(8,128)(2,1)} %slice.325), channel_id=1, source_target_pairs={{0,16},{2,18},{4,20},{6,22},{8,24},{10,26},{12,28},{14,30},{16,0},... | collective-permute-start | bytes 589832 | tf_op jit(solution)/shard_map/ppermute | solution.py:218
  35.4 0.0 collective-permute-done.2.refs_3_
  35.4 4.0 %first_pass.3 = (f32[2,4,192]{2,1,0:T(4,128)S(1)}, f32[1,768]{1,0:T(1,128)S(1)}, bf16[768,1024]{1,0:T(8,128)(2,1)S(1)}, bf16[512,1024]{1,0:T(8,128)(2,1)S(1)}) custom-call(bf16[128,1024]{1,0:T(8,128)(2,1)S(1)} %convert_element_type.13.refs_0_, bf16[128,1024]{1,0:T(8,128)(2,1)S(1)} %collective-permute-done.refs_1_, ...), custom_call_target="tpu_custom_call" | custom-call | flops 805306368 | bytes 1572864 | tf_op jit(solution)/shard_map/first_pass/pallas_call | solution.py:98
  39.4 0.0 collective-permute-done.9.refs_2_
  39.4 1.7 %first_pass.4 = (f32[2,2,192]{2,1,0:T(2,128)S(1)}, f32[1,384]{1,0:T(1,128)S(1)}, bf16[384,1024]{1,0:T(8,128)(2,1)S(1)}) custom-call(bf16[512,1024]{1,0:T(8,128)(2,1)S(1)} %get-tuple-element.36.refs_0_.cents, bf16[192,1024]{1,0:T(8,128)(2,1)S(1)} %collective-permute-done.4.refs_1_, bf16[192,1024]{1,0:T(8,128)(2,1)S(1)} %collective-permute-done.9.refs_2_), custom_call_target="tpu_custom_call" | custom-call | flops 402653184 | bytes 786432 | tf_op jit(solution)/shard_map/first_pass/pallas_call | solution.py:98
  41.1 0.0 collective-permute-done.8
  41.1 4.8 %collective-permute-done.7 = bf16[96,1024]{1,0:T(8,128)(2,1)} collective-permute-done((bf16[96,1024]{1,0:T(8,128)(2,1)}, bf16[96,1024]{1,0:T(8,128)(2,1)}, u32[]{:S(2)}, u32[]{:S(2)}) %collective-permute-start.7) | collective-permute-done | bytes 196640 | tf_op jit(solution)/shard_map/ppermute | solution.py:218
  45.9 1.0 %pad_maximum_fusion.1.refs_2_ = bf16[192,1024]{1,0:T(8,128)(2,1)S(1)} fusion(bf16[96,1024]{1,0:T(8,128)(2,1)} %collective-permute-done.8, bf16[96,1024]{1,0:T(8,128)(2,1)} %collective-permute-done.7), kind=kLoop, calls=%fused_computation.7 | loop fusion | flops 786432 | bytes 786432 | tf_op jit(solution)/shard_map/concatenate | solution.py:295
  47.0 0.0 collective-permute-done.10.refs_1_
  47.0 1.0 %first_pass.5 = (f32[2,2,192]{2,1,0:T(2,128)S(1)}, f32[1,384]{1,0:T(1,128)S(1)}, bf16[384,1024]{1,0:T(8,128)(2,1)S(1)}) custom-call(bf16[512,1024]{1,0:T(8,128)(2,1)S(1)} %get-tuple-element.36.refs_0_.cents, bf16[192,1024]{1,0:T(8,128)(2,1)S(1)} %collective-permute-done.10.refs_1_, bf16[192,1024]{1,0:T(8,128)(2,1)S(1)} %pad_maximum_fusion.1.refs_2_), custom_call_target="tpu_custom_call" | custom-call | flops 402653184 | bytes 786432 | tf_op jit(solution)/shard_map/first_pass/pallas_call | solution.py:98
  48.3 9.7 %all_to_all.10 = f32[8,2,8,192]{3,2,1,0:T(8,128)S(1)} all-to-all(f32[8,2,8,192]{3,2,1,0:T(8,128)S(1)} %broadcast_in_dim.6), channel_id=1, replica_groups={{0,2,4,6,16,18,20,22},{8,10,12,14,24,26,28,30},{1,3,5,7,17,19,21,23},{9..., dimensions={0} | all-to-all | bytes 196608 | tf_op jit(solution)/shard_map/all_to_all | solution.py:269
  58.4 0.1 pad_maximum_fusion.9
  58.4 0.1 pad_maximum_fusion.8.refs_0_
  58.5 2.8 %sums_pass.3 = f32[256,1152]{1,0:T(8,128)S(1)} custom-call(bf16[512,1024]{1,0:T(8,128)(2,1)S(1)} %get-tuple-element.36.refs_0_.cents, f32[2,768]{1,0:T(2,128)S(1)} %pad_maximum_fusion.8.refs_0_, f32[2,384]{1,0:T(2,128)S(1)} %get-tuple-element.111.refs_1_, f32[2,384]{1,0:T(2,128)S(1)} %get-tuple-element.112.refs_2_, ...), custom_call_target="tpu_custom_call" | custom-call | flops 1610612736 | bytes 3145728 | tf_op jit(solution)/shard_map/sums_pass/pallas_call | solution.py:137
  61.4 0.1 collective-permute-start.12
  61.5 2.8 %sums_pass.2 = f32[256,1152]{1,0:T(8,128)S(1)} custom-call(bf16[512,1024]{1,0:T(8,128)(2,1)S(1)} %get-tuple-element.36.refs_0_.cents, f32[2,768]{1,0:T(2,128)S(1)} %pad_maximum_fusion.8.refs_0_, f32[2,384]{1,0:T(2,128)S(1)} %get-tuple-element.111.refs_1_, f32[2,384]{1,0:T(2,128)S(1)} %get-tuple-element.112.refs_2_, ...), custom_call_target="tpu_custom_call" | custom-call | flops 1610612736 | bytes 3145728 | tf_op jit(solution)/shard_map/sums_pass/pallas_call | solution.py:137
  64.3 0.6 collective-permute-start.11
  64.9 0.0 collective-permute-done.12
  64.9 0.1 slice_add_fusion
  65.0 3.1 %collective-permute-start.13 = (bf16[128,1152]{1,0:T(8,128)(2,1)S(1)}, bf16[128,1152]{1,0:T(8,128)(2,1)S(1)}, u32[]{:S(2)}, u32[]{:S(2)}) collective-permute-start(bf16[128,1152]{1,0:T(8,128)(2,1)S(1)} %pad_maximum_fusion.2), channel_id=1, source_target_pairs={{0,8},{2,10},{4,12},{6,14},{8,0},{10,2},{12,4},{14,6},{16,24},{18,... | collective-permute-start | bytes 884744 | tf_op jit(solution)/shard_map/ppermute | solution.py:218
  68.2 7.2 %collective-permute-done.13 = bf16[128,1152]{1,0:T(8,128)(2,1)S(1)} collective-permute-done((bf16[128,1152]{1,0:T(8,128)(2,1)S(1)}, bf16[128,1152]{1,0:T(8,128)(2,1)S(1)}, u32[]{:S(2)}, u32[]{:S(2)}) %collective-permute-start.13) | collective-permute-done | bytes 294944 | tf_op jit(solution)/shard_map/ppermute | solution.py:218
  75.5 0.2 fusion.4
  75.6 0.0 collective-permute-done.11
  75.6 0.1 broadcast_in_dim.8
  75.7 0.0 copy-start.1
  75.7 0.1 fusion
  75.8 0.1 fusion.3
  75.9 0.8 copy-done.1
  76.8 0.9 fusion.27
  77.7 0.0 collective-permute-start.15
  77.7 1.7 %collective-permute-start.14 = (bf16[128,1024]{1,0:T(8,128)(2,1)S(1)}, bf16[128,1024]{1,0:T(8,128)(2,1)S(1)}, u32[]{:S(2)}, u32[]{:S(2)}) collective-permute-start(bf16[128,1024]{1,0:T(8,128)(2,1)S(1)} %get-tuple-element.68), channel_id=1, source_target_pairs={{0,8},{2,10},{4,12},{6,14},{8,0},{10,2},{12,4},{14,6},{16,24},{18,... | collective-permute-start | bytes 786440 | tf_op jit(solution)/shard_map/ppermute | solution.py:218
  79.5 0.0 collective-permute-done.15
  79.5 1.6 %second_pass.3 = (f32[3,4,192]{2,1,0:T(4,128)S(1)}, f32[3,2,192]{2,1,0:T(2,128)S(1)}, f32[3,2,192]{2,1,0:T(2,128)S(1)}) custom-call(bf16[256,1024]{1,0:T(8,128)(2,1)S(1)} %pad_maximum_fusion.cents, f32[1,768]{1,0:T(1,128)S(1)} %get-tuple-element.49.refs_3_.refs_0_, f32[1,384]{1,0:T(1,128)S(1)} %get-tuple-element.50.refs_4_.refs_1_, ...), custom_call_target="tpu_custom_call" | custom-call | flops 805306368 | bytes 3145728 | tf_op jit(solution)/shard_map/second_pass/pallas_call | solution.py:178
  81.1 5.3 %collective-permute-done.14.cents = bf16[128,1024]{1,0:T(8,128)(2,1)S(1)} collective-permute-done((bf16[128,1024]{1,0:T(8,128)(2,1)S(1)}, bf16[128,1024]{1,0:T(8,128)(2,1)S(1)}, u32[]{:S(2)}, u32[]{:S(2)}) %collective-permute-start.14) | collective-permute-done | bytes 262176 | tf_op jit(solution)/shard_map/ppermute | solution.py:218
  86.4 0.0 collective-permute-start.16
  86.4 1.2 %second_pass.4 = (f32[3,4,192]{2,1,0:T(4,128)S(1)}, f32[3,2,192]{2,1,0:T(2,128)S(1)}, f32[3,2,192]{2,1,0:T(2,128)S(1)}) custom-call(bf16[128,1024]{1,0:T(8,128)(2,1)S(1)} %collective-permute-done.14.cents, f32[1,768]{1,0:T(1,128)S(1)} %get-tuple-element.49.refs_3_.refs_0_, f32[1,384]{1,0:T(1,128)S(1)} %get-tuple-element.50.refs_4_.refs_1_, ...), custom_call_target="tpu_custom_call" | custom-call | flops 402653184 | bytes 3145728 | tf_op jit(solution)/shard_map/second_pass/pallas_call | solution.py:178
  87.7 0.3 collective-permute-done.16.cents
  88.0 1.2 %second_pass.5 = (f32[3,4,192]{2,1,0:T(4,128)S(1)}, f32[3,2,192]{2,1,0:T(2,128)S(1)}, f32[3,2,192]{2,1,0:T(2,128)S(1)}) custom-call(bf16[128,1024]{1,0:T(8,128)(2,1)S(1)} %collective-permute-done.16.cents, f32[1,768]{1,0:T(1,128)S(1)} %get-tuple-element.49.refs_3_.refs_0_, f32[1,384]{1,0:T(1,128)S(1)} %get-tuple-element.50.refs_4_.refs_1_, ...), custom_call_target="tpu_custom_call" | custom-call | flops 402653184 | bytes 3145728 | tf_op jit(solution)/shard_map/second_pass/pallas_call | solution.py:178
  89.3 0.1 stack.78
  89.5 9.0 %all_to_all.11 = f32[8,3,192]{2,1,0:T(4,128)S(1)} all-to-all(f32[8,3,192]{2,1,0:T(4,128)S(1)} %copy.74), channel_id=1, replica_groups={{0,2,4,6,16,18,20,22},{8,10,12,14,24,26,28,30},{1,3,5,7,17,19,21,23},{9..., dimensions={0} | all-to-all | bytes 36864 | tf_op jit(solution)/shard_map/all_to_all | solution.py:269
  98.5 0.6 divide_subtract_fusion
  (60 shorter events, 1.0 us)
Async XLA Ops:
  0.6 15.1 %copy-start = (f32[128,1024]{1,0:T(8,128)S(1)}, f32[128,1024]{1,0:T(8,128)}, u32[]{:S(2)}) copy-start(f32[128,1024]{1,0:T(8,128)} %param.3) | copy-start | bytes 1572868
  1.9 12.1 %collective-permute-start.3 = (bf16[192,1024]{1,0:T(8,128)(2,1)S(1)}, bf16[192,1024]{1,0:T(8,128)(2,1)S(1)}, u32[]{:S(2)}, u32[]{:S(2)}) collective-permute-start(bf16[192,1024]{1,0:T(8,128)(2,1)S(1)} %convert_element_type.14.refs_4_), channel_id=1, source_target_pairs={{0,2},{2,0},{4,6},{6,4},{8,10},{10,8},{12,14},{14,12},{16,18},{18,... | collective-permute-start | bytes 1179656 | tf_op jit(solution)/shard_map/ppermute | solution.py:218
  4.9 20.0 %collective-permute-start.4 = (bf16[192,1024]{1,0:T(8,128)(2,1)S(1)}, bf16[192,1024]{1,0:T(8,128)(2,1)S(1)}, u32[]{:S(2)}, u32[]{:S(2)}) collective-permute-start(bf16[192,1024]{1,0:T(8,128)(2,1)S(1)} %convert_element_type.14.refs_4_), channel_id=1, source_target_pairs={{0,16},{2,18},{4,20},{6,22},{8,24},{10,26},{12,28},{14,30},{16,0},... | collective-permute-start | bytes 1179656 | tf_op jit(solution)/shard_map/ppermute | solution.py:218
  7.5 17.4 %collective-permute-start.6 = (bf16[192,1024]{1,0:T(8,128)(2,1)S(1)}, bf16[192,1024]{1,0:T(8,128)(2,1)S(1)}, u32[]{:S(2)}, u32[]{:S(2)}) collective-permute-start(bf16[192,1024]{1,0:T(8,128)(2,1)S(1)} %convert_element_type.14.refs_4_), channel_id=1, source_target_pairs={{0,4},{2,6},{4,0},{6,2},{8,12},{10,14},{12,8},{14,10},{16,20},{18,... | collective-permute-start | bytes 1179656 | tf_op jit(solution)/shard_map/ppermute | solution.py:218
  14.0 12.2 %collective-permute-start.5 = (bf16[192,1024]{1,0:T(8,128)(2,1)S(1)}, bf16[192,1024]{1,0:T(8,128)(2,1)S(1)}, u32[]{:S(2)}, u32[]{:S(2)}) collective-permute-start(bf16[192,1024]{1,0:T(8,128)(2,1)S(1)} %collective-permute-done.3.refs_5_), channel_id=1, source_target_pairs={{0,4},{2,6},{4,0},{6,2},{8,12},{10,14},{12,8},{14,10},{16,20},{18,... | collective-permute-start | bytes 1179656 | tf_op jit(solution)/shard_map/ppermute | solution.py:218
  15.8 14.3 %collective-permute-start.1 = (bf16[128,1024]{1,0:T(8,128)(2,1)S(1)}, bf16[128,1024]{1,0:T(8,128)(2,1)S(1)}, u32[]{:S(2)}, u32[]{:S(2)}) collective-permute-start(bf16[128,1024]{1,0:T(8,128)(2,1)S(1)} %convert_element_type.13.refs_0_), channel_id=1, source_target_pairs={{0,8},{2,10},{4,12},{6,14},{8,0},{10,2},{12,4},{14,6},{16,24},{18,... | collective-permute-start | bytes 786440 | tf_op jit(solution)/shard_map/ppermute | solution.py:218
  17.5 16.3 %collective-permute-start = (bf16[128,1024]{1,0:T(8,128)(2,1)S(1)}, bf16[128,1024]{1,0:T(8,128)(2,1)S(1)}, u32[]{:S(2)}, u32[]{:S(2)}) collective-permute-start(bf16[128,1024]{1,0:T(8,128)(2,1)S(1)} %convert_element_type.13.refs_0_), channel_id=1, source_target_pairs={{0,1},{1,0},{2,3},{3,2},{4,5},{5,4},{6,7},{7,6},{8,9},{9,8},{10,11... | collective-permute-start | bytes 786440 | tf_op jit(solution)/shard_map/ppermute | solution.py:227
  26.2 13.2 %collective-permute-start.9 = (bf16[192,1024]{1,0:T(8,128)(2,1)S(1)}, bf16[192,1024]{1,0:T(8,128)(2,1)S(1)}, u32[]{:S(2)}, u32[]{:S(2)}) collective-permute-start(bf16[192,1024]{1,0:T(8,128)(2,1)S(1)} %collective-permute-done.4.refs_1_), channel_id=1, source_target_pairs={{0,2},{2,0},{4,6},{6,4},{8,10},{10,8},{12,14},{14,12},{16,18},{18,... | collective-permute-start | bytes 1179656 | tf_op jit(solution)/shard_map/ppermute | solution.py:218
  30.1 5.3 %collective-permute-start.2 = (bf16[128,1024]{1,0:T(8,128)(2,1)S(1)}, bf16[128,1024]{1,0:T(8,128)(2,1)}, u32[]{:S(2)}, u32[]{:S(2)}) collective-permute-start(bf16[128,1024]{1,0:T(8,128)(2,1)S(1)} %collective-permute-done.1.refs_2_), channel_id=1, source_target_pairs={{0,1},{1,0},{2,3},{3,2},{4,5},{5,4},{6,7},{7,6},{8,9},{9,8},{10,11... | collective-permute-start | bytes 786440 | tf_op jit(solution)/shard_map/ppermute | solution.py:227
  30.1 16.9 %collective-permute-start.10 = (bf16[192,1024]{1,0:T(8,128)(2,1)S(1)}, bf16[192,1024]{1,0:T(8,128)(2,1)S(1)}, u32[]{:S(2)}, u32[]{:S(2)}) collective-permute-start(bf16[192,1024]{1,0:T(8,128)(2,1)S(1)} %collective-permute-done.4.refs_1_), channel_id=1, source_target_pairs={{0,4},{2,6},{4,0},{6,2},{8,12},{10,14},{12,8},{14,10},{16,20},{18,... | collective-permute-start | bytes 1179656 | tf_op jit(solution)/shard_map/ppermute | solution.py:218
  31.4 9.7 %collective-permute-start.8 = (bf16[96,1024]{1,0:T(8,128)(2,1)}, bf16[96,1024]{1,0:T(8,128)(2,1)}, u32[]{:S(2)}, u32[]{:S(2)}) collective-permute-start(bf16[96,1024]{1,0:T(8,128)(2,1)} %slice.326), channel_id=1, source_target_pairs={{0,6},{2,4},{4,2},{6,0},{8,14},{10,12},{12,10},{14,8},{16,22},{18,... | collective-permute-start | bytes 589832 | tf_op jit(solution)/shard_map/ppermute | solution.py:218
  33.8 12.2 %collective-permute-start.7 = (bf16[96,1024]{1,0:T(8,128)(2,1)}, bf16[96,1024]{1,0:T(8,128)(2,1)}, u32[]{:S(2)}, u32[]{:S(2)}) collective-permute-start(bf16[96,1024]{1,0:T(8,128)(2,1)} %slice.325), channel_id=1, source_target_pairs={{0,16},{2,18},{4,20},{6,22},{8,24},{10,26},{12,28},{14,30},{16,0},... | collective-permute-start | bytes 589832 | tf_op jit(solution)/shard_map/ppermute | solution.py:218
  61.4 3.5 %collective-permute-start.12 = (f32[128,1152]{1,0:T(8,128)S(1)}, f32[128,1152]{1,0:T(8,128)S(1)}, u32[]{:S(2)}, u32[]{:S(2)}) collective-permute-start(f32[128,1152]{1,0:T(8,128)S(1)} %slice.451), channel_id=1, source_target_pairs={{0,1},{1,0},{2,3},{3,2},{4,5},{5,4},{6,7},{7,6},{8,9},{9,8},{10,11... | collective-permute-start | bytes 1769480 | tf_op jit(solution)/shard_map/ppermute | solution.py:227
  64.3 11.3 %collective-permute-start.11 = (f32[128,1152]{1,0:T(8,128)S(1)}, f32[128,1152]{1,0:T(8,128)S(1)}, u32[]{:S(2)}, u32[]{:S(2)}) collective-permute-start(f32[128,1152]{1,0:T(8,128)S(1)} %slice.449), channel_id=1, source_target_pairs={{0,1},{1,0},{2,3},{3,2},{4,5},{5,4},{6,7},{7,6},{8,9},{9,8},{10,11... | collective-permute-start | bytes 1769480 | tf_op jit(solution)/shard_map/ppermute | solution.py:227
  65.0 10.3 %collective-permute-start.13 = (bf16[128,1152]{1,0:T(8,128)(2,1)S(1)}, bf16[128,1152]{1,0:T(8,128)(2,1)S(1)}, u32[]{:S(2)}, u32[]{:S(2)}) collective-permute-start(bf16[128,1152]{1,0:T(8,128)(2,1)S(1)} %pad_maximum_fusion.2), channel_id=1, source_target_pairs={{0,8},{2,10},{4,12},{6,14},{8,0},{10,2},{12,4},{14,6},{16,24},{18,... | collective-permute-start | bytes 884744 | tf_op jit(solution)/shard_map/ppermute | solution.py:218
  75.7 1.1 %copy-start.1 = (f32[128,1024]{1,0:T(8,128)S(1)}, f32[128,1024]{1,0:T(8,128)}, u32[]{:S(2)}) copy-start(f32[128,1024]{1,0:T(8,128)} %param.3) | copy-start | bytes 1572868
  77.7 1.7 %collective-permute-start.15 = (bf16[128,1024]{1,0:T(8,128)(2,1)S(1)}, bf16[128,1024]{1,0:T(8,128)(2,1)S(1)}, u32[]{:S(2)}, u32[]{:S(2)}) collective-permute-start(bf16[128,1024]{1,0:T(8,128)(2,1)S(1)} %get-tuple-element.68), channel_id=1, source_target_pairs={{0,1},{1,0},{2,3},{3,2},{4,5},{5,4},{6,7},{7,6},{8,9},{9,8},{10,11... | collective-permute-start | bytes 786440 | tf_op jit(solution)/shard_map/ppermute | solution.py:227
  77.7 8.7 %collective-permute-start.14 = (bf16[128,1024]{1,0:T(8,128)(2,1)S(1)}, bf16[128,1024]{1,0:T(8,128)(2,1)S(1)}, u32[]{:S(2)}, u32[]{:S(2)}) collective-permute-start(bf16[128,1024]{1,0:T(8,128)(2,1)S(1)} %get-tuple-element.68), channel_id=1, source_target_pairs={{0,8},{2,10},{4,12},{6,14},{8,0},{10,2},{12,4},{14,6},{16,24},{18,... | collective-permute-start | bytes 786440 | tf_op jit(solution)/shard_map/ppermute | solution.py:218
  86.4 1.5 %collective-permute-start.16 = (bf16[128,1024]{1,0:T(8,128)(2,1)S(1)}, bf16[128,1024]{1,0:T(8,128)(2,1)S(1)}, u32[]{:S(2)}, u32[]{:S(2)}) collective-permute-start(bf16[128,1024]{1,0:T(8,128)(2,1)S(1)} %collective-permute-done.14.cents), channel_id=1, source_target_pairs={{0,1},{1,0},{2,3},{3,2},{4,5},{5,4},{6,7},{7,6},{8,9},{9,8},{10,11... | collective-permute-start | bytes 786440 | tf_op jit(solution)/shard_map/ppermute | solution.py:227

commit v9 on v8

--- a/solution.py
+++ b/solution.py
@@ -50,8 +50,8 @@
     return copies
 
 
-def first_kernel(n, n_blocks, shard, last, *refs):
-    blocks, chunks, refs = refs[:n_blocks], refs[n_blocks : n_blocks + n], refs[n_blocks + n :]
+def first_kernel(n, n_blocks, n_chunks, shard, last, *refs):
+    blocks, chunks, refs = refs[:n_blocks], refs[n_blocks : n_blocks + n_chunks], refs[n_blocks + n_chunks :]
     stats_ref, row_sq_ref, rows_ref = refs[:3]
     sems = refs[-1]
     cents, copies = blocks[0], []
@@ -61,8 +61,10 @@
             cents[at : at + block.shape[0], :] = block[...]
             at += block.shape[0]
     if last:
-        for i in range(n):
-            rows_ref[i * shard : (i + 1) * shard, :] = chunks[i][...]
+        at = 0
+        for chunk in chunks:
+            rows_ref[at : at + chunk.shape[0], :] = chunk[...]
+            at += chunk.shape[0]
     else:
         copies = fetch(chunks, rows_ref, sems)
     piece = cents[...]
@@ -84,10 +86,11 @@
 
 
 def first_pass(blocks, chunks, last=False):
-    n, n_blocks = len(chunks), len(blocks)
+    n_blocks, n_chunks = len(blocks), len(chunks)
     shard, width = chunks[0].shape
     n_k = sum(b.shape[0] for b in blocks)
-    n_rows = n * shard
+    n_rows = sum(c.shape[0] for c in chunks)
+    n = n_rows // shard
     outs = [
         jax.ShapeDtypeStruct((2, n, shard), jnp.float32),
         jax.ShapeDtypeStruct((1, n_rows), jnp.float32),
@@ -96,11 +99,11 @@
     if n_blocks > 1:
         outs.append(jax.ShapeDtypeStruct((n_k, width), jnp.bfloat16))
     out = pl.pallas_call(
-        functools.partial(first_kernel, n, n_blocks, shard, last),
+        functools.partial(first_kernel, n, n_blocks, n_chunks, shard, last),
         out_shape=tuple(outs),
-        in_specs=[VMEM] * n_blocks + [VMEM if last else HBM] * n,
+        in_specs=[VMEM] * n_blocks + [VMEM if last else HBM] * n_chunks,
         out_specs=(VMEM,) * len(outs),
-        scratch_shapes=[pltpu.SemaphoreType.DMA((n,))],
+        scratch_shapes=[pltpu.SemaphoreType.DMA((n_chunks,))],
         compiler_params=params(),
         cost_estimate=pl.CostEstimate(
             flops=2 * n_k * n_rows * width,
@@ -283,17 +286,17 @@
         chunk[3] = rows_from(chunk[1], 2)
         near_own = gather_near(centroids.astype(jnp.bfloat16))
         far_own = flip(near_own, top_bit)
-        chunk[4], chunk[3], chunk[2] = hold(chunk[4], chunk[3], chunk[2])
+        near = gather_cent(near_own)
+        n_near = len(near) * near_own.shape[0]
+        far = gather_cent(far_own)
+        chunk[4], chunk[3], chunk[2], far = hold(chunk[4], chunk[3], chunk[2], far)
         chunk[5] = rows_from(chunk[4], 1)
         chunk[6] = rows_from(chunk[4], 2)
         parts = (rows_from(chunk[3][:half], 4), rows_from(chunk[4][half:], 3))
-        near = gather_cent(near_own)
-        n_near = len(near) * near_own.shape[0]
-        done, piece = first_pass(near + gather_cent(far_own), [chunk[b] for b in GROUPS[0]])
+        done, piece = first_pass(near + far, [chunk[b] for b in GROUPS[0]])
         passes = [done, first_pass([piece], [chunk[b] for b in GROUPS[1]])[0]]
         parts, passes = hold(parts, passes)
-        chunk[7] = jnp.concatenate(parts, axis=0)
-        passes.append(first_pass([piece], [chunk[b] for b in GROUPS[2]], True)[0])
+        passes.append(first_pass([piece], [chunk[GROUPS[2][0]], *parts], True)[0])
         local, row_sqs, rows = zip(*passes)
 
         stats = by_position(by_chunk(local))

time: 99.4 us -> 96.1 us (0.967)
  local copies, waits for them, and re-layouts: 2.7 us -> 5.99 us
  starting transfers between devices: 20.5 us -> 17.4 us
  waiting for transfers between devices: 34.7 us -> 32 us
  other arithmetic: 4.99 us -> 3.94 us
    unnamed x11 -> x19, local copies, waits for them, and re-layouts: 0.91 us -> 4.2 us
    ppermute x11, starting transfers between devices: 19.8 us -> 16.7 us  [flip(): return lax.ppermute(value, 'dp', [(i, i ^ bits) for i in range(n_dp)])]
    ppermute x11, waiting for transfers between devices: 34.4 us -> 31.3 us  [flip(): return lax.ppermute(value, 'dp', [(i, i ^ bits) for i in range(n_dp)])]
    concatenate x1 -> x0, other arithmetic: 1.05 us -> none  [on_device(): chunk[7] = jnp.concatenate(parts, axis=0)]
  transfers between devices with their start and end apart: 17 -> 17, of which waited for: 8 -> 10; matrix products, arithmetic and copies ran while one was open for 3% -> 2% of each run, Pallas kernels for 11% -> 12%
where the time goes in v9:
time: 96.1 us; the launch traced here: 95.8 us
  waiting for transfers between devices  32 us (33%)
  blocking collectives  19 us (20%)
  starting transfers between devices  17.4 us (18%)
  Pallas kernels  16.4 us (17%)
  local copies, waits for them, and re-layouts  5.99 us (6%)
  other arithmetic  3.94 us (4%)
  between operations  1.12 us (1%)
    ppermute x11, waiting for transfers between devices, flip(): return lax.ppermute(value, 'dp', [(i, i ^ bits) for i in range(n_dp)])  31.3 us
    all_to_all x2, blocking collectives, exchange(): return lax.all_to_all(value, 'dp', 0, 0, axis_index_groups=groups)  19 us
    ppermute x11, starting transfers between devices, flip(): return lax.ppermute(value, 'dp', [(i, i ^ bits) for i in range(n_dp)])  16.7 us
    pallas_call x3, Pallas kernels, first_pass(): pl.pallas_call(functools.partial(first_kernel, n, n_blocks, n_chunks, sha...  6.72 us
    pallas_call x2, Pallas kernels, sums_pass(): pl.pallas_call(functools.partial(sums_kernel, first, last, n), out_shape=...  5.58 us
    unnamed x19, local copies, waits for them, and re-layouts  4.2 us
    pallas_call x3, Pallas kernels, second_pass(): pl.pallas_call(functools.partial(second_kernel, shard, n), out_shape=tupl...  4.07 us
  transfers between devices with their start and end apart: 17, of which 10 were waited for; matrix products, arithmetic and copies ran while one was open for 2% of the time, Pallas kernels for 12%

profile of v9, /device:TPU:0, one launch (start us, length us, event | category | flops | bytes accessed | tf_op | source)
XLA Modules:
  0.0 95.8 jit_solution(7868069668367325630)
XLA Ops:
  0.6 0.0 copy-start.4
  0.6 1.2 %convert_element_type.14.refs_4_ = bf16[192,1024]{1,0:T(8,128)(2,1)S(1)} convert(f32[192,1024]{1,0:T(8,128)} %param.2) | non-fusion elementwise | flops 196608 | bytes 1179648 | tf_op jit(solution)/shard_map/convert_element_type | solution.py:283
  1.9 3.0 %collective-permute-start.2 = (bf16[192,1024]{1,0:T(8,128)(2,1)S(1)}, bf16[192,1024]{1,0:T(8,128)(2,1)S(1)}, u32[]{:S(2)}, u32[]{:S(2)}) collective-permute-start(bf16[192,1024]{1,0:T(8,128)(2,1)S(1)} %convert_element_type.14.refs_4_), channel_id=1, source_target_pairs={{0,2},{2,0},{4,6},{6,4},{8,10},{10,8},{12,14},{14,12},{16,18},{18,... | collective-permute-start | bytes 1179656 | tf_op jit(solution)/shard_map/ppermute | solution.py:221
  4.9 1.6 %collective-permute-start.5 = (bf16[128,1024]{1,0:T(8,128)(2,1)S(1)}, bf16[128,1024]{1,0:T(8,128)(2,1)S(1)}, u32[]{:S(2)}, u32[]{:S(2)}) collective-permute-start(bf16[128,1024]{1,0:T(8,128)(2,1)S(1)} %convert_element_type.13.refs_0_), channel_id=1, source_target_pairs={{0,8},{2,10},{4,12},{6,14},{8,0},{10,2},{12,4},{14,6},{16,24},{18,... | collective-permute-start | bytes 786440 | tf_op jit(solution)/shard_map/ppermute | solution.py:221
  6.6 2.6 %collective-permute-start.1 = (bf16[192,1024]{1,0:T(8,128)(2,1)S(1)}, bf16[192,1024]{1,0:T(8,128)(2,1)S(1)}, u32[]{:S(2)}, u32[]{:S(2)}) collective-permute-start(bf16[192,1024]{1,0:T(8,128)(2,1)S(1)} %convert_element_type.14.refs_4_), channel_id=1, source_target_pairs={{0,16},{2,18},{4,20},{6,22},{8,24},{10,26},{12,28},{14,30},{16,0},... | collective-permute-start | bytes 1179656 | tf_op jit(solution)/shard_map/ppermute | solution.py:221
  9.2 1.5 %collective-permute-start.4 = (bf16[192,1024]{1,0:T(8,128)(2,1)S(1)}, bf16[192,1024]{1,0:T(8,128)(2,1)S(1)}, u32[]{:S(2)}, u32[]{:S(2)}) collective-permute-start(bf16[192,1024]{1,0:T(8,128)(2,1)S(1)} %convert_element_type.14.refs_4_), channel_id=1, source_target_pairs={{0,4},{2,6},{4,0},{6,2},{8,12},{10,14},{12,8},{14,10},{16,20},{18,... | collective-permute-start | bytes 1179656 | tf_op jit(solution)/shard_map/ppermute | solution.py:221
  10.7 3.3 %collective-permute-done.2.refs_5_ = bf16[192,1024]{1,0:T(8,128)(2,1)S(1)} collective-permute-done((bf16[192,1024]{1,0:T(8,128)(2,1)S(1)}, bf16[192,1024]{1,0:T(8,128)(2,1)S(1)}, u32[]{:S(2)}, u32[]{:S(2)}) %collective-permute-start.2) | collective-permute-done | bytes 393248 | tf_op jit(solution)/shard_map/ppermute | solution.py:221
  14.0 1.8 %collective-permute-start.3 = (bf16[192,1024]{1,0:T(8,128)(2,1)S(1)}, bf16[192,1024]{1,0:T(8,128)(2,1)S(1)}, u32[]{:S(2)}, u32[]{:S(2)}) collective-permute-start(bf16[192,1024]{1,0:T(8,128)(2,1)S(1)} %collective-permute-done.2.refs_5_), channel_id=1, source_target_pairs={{0,4},{2,6},{4,0},{6,2},{8,12},{10,14},{12,8},{14,10},{16,20},{18,... | collective-permute-start | bytes 1179656 | tf_op jit(solution)/shard_map/ppermute | solution.py:221
  15.8 2.5 %collective-permute-done.5.refs_2_ = bf16[128,1024]{1,0:T(8,128)(2,1)S(1)} collective-permute-done((bf16[128,1024]{1,0:T(8,128)(2,1)S(1)}, bf16[128,1024]{1,0:T(8,128)(2,1)S(1)}, u32[]{:S(2)}, u32[]{:S(2)}) %collective-permute-start.5) | collective-permute-done | bytes 262176 | tf_op jit(solution)/shard_map/ppermute | solution.py:221
  18.3 0.0 collective-permute-start.6
  18.3 0.7 copy-done
  19.0 7.3 %collective-permute-done.1.refs_1_ = bf16[192,1024]{1,0:T(8,128)(2,1)S(1)} collective-permute-done((bf16[192,1024]{1,0:T(8,128)(2,1)S(1)}, bf16[192,1024]{1,0:T(8,128)(2,1)S(1)}, u32[]{:S(2)}, u32[]{:S(2)}) %collective-permute-start.1) | collective-permute-done | bytes 393248 | tf_op jit(solution)/shard_map/ppermute | solution.py:221
  26.2 0.0 collective-permute-done.4.refs_6_
  26.2 0.0 collective-permute-done.6.refs_3_
  26.3 0.7 copy-done.2
  26.9 0.7 collective-permute-done.3.refs_7_
  27.6 0.5 collective-permute-start.9
  28.1 1.5 %collective-permute-start.10 = (bf16[192,1024]{1,0:T(8,128)(2,1)S(1)}, bf16[192,1024]{1,0:T(8,128)(2,1)S(1)}, u32[]{:S(2)}, u32[]{:S(2)}) collective-permute-start(bf16[192,1024]{1,0:T(8,128)(2,1)S(1)} %collective-permute-done.1.refs_1_), channel_id=1, source_target_pairs={{0,4},{2,6},{4,0},{6,2},{8,12},{10,14},{12,8},{14,10},{16,20},{18,... | collective-permute-start | bytes 1179656 | tf_op jit(solution)/shard_map/ppermute | solution.py:221
  29.7 0.0 collective-permute-start
  29.7 0.7 slice.326
  30.4 1.4 %collective-permute-start.8 = (bf16[96,1024]{1,0:T(8,128)(2,1)}, bf16[96,1024]{1,0:T(8,128)(2,1)S(1)}, u32[]{:S(2)}, u32[]{:S(2)}) collective-permute-start(bf16[96,1024]{1,0:T(8,128)(2,1)} %slice.326), channel_id=1, source_target_pairs={{0,6},{2,4},{4,2},{6,0},{8,14},{10,12},{12,10},{14,8},{16,22},{18,... | collective-permute-start | bytes 589832 | tf_op jit(solution)/shard_map/ppermute | solution.py:221
  31.8 0.7 slice.325
  32.5 0.3 collective-permute-start.7
  32.8 0.0 collective-permute-done.refs_1_
  32.8 0.9 copy-done.1
  33.8 0.9 copy-done.3
  34.7 4.0 %first_pass.3 = (f32[2,4,192]{2,1,0:T(4,128)S(1)}, f32[1,768]{1,0:T(1,128)S(1)}, bf16[768,1024]{1,0:T(8,128)(2,1)S(1)}, bf16[512,1024]{1,0:T(8,128)(2,1)S(1)}) custom-call(bf16[128,1024]{1,0:T(8,128)(2,1)S(1)} %convert_element_type.13.refs_0_, bf16[128,1024]{1,0:T(8,128)(2,1)} %collective-permute-done.refs_1_, bf16[128,1024]{1,0:T(8,128)(2,1)S(1)} %copy-done.1, ...), custom_call_target="tpu_custom_call" | custom-call | flops 805306368 | bytes 1572864 | tf_op jit(solution)/shard_map/first_pass/pallas_call | solution.py:101
  38.8 0.0 collective-permute-done.9.refs_2_
  38.8 1.7 %first_pass.4 = (f32[2,2,192]{2,1,0:T(2,128)S(1)}, f32[1,384]{1,0:T(1,128)S(1)}, bf16[384,1024]{1,0:T(8,128)(2,1)S(1)}) custom-call(bf16[512,1024]{1,0:T(8,128)(2,1)S(1)} %get-tuple-element.40.refs_0_.cents, bf16[192,1024]{1,0:T(8,128)(2,1)S(1)} %collective-permute-done.1.refs_1_, bf16[192,1024]{1,0:T(8,128)(2,1)S(1)} %collective-permute-done.9.refs_2_), custom_call_target="tpu_custom_call" | custom-call | flops 402653184 | bytes 786432 | tf_op jit(solution)/shard_map/first_pass/pallas_call | solution.py:101
  40.5 1.4 %collective-permute-done.8.refs_3_ = bf16[96,1024]{1,0:T(8,128)(2,1)S(1)} collective-permute-done((bf16[96,1024]{1,0:T(8,128)(2,1)}, bf16[96,1024]{1,0:T(8,128)(2,1)S(1)}, u32[]{:S(2)}, u32[]{:S(2)}) %collective-permute-start.8) | collective-permute-done | bytes 196640 | tf_op jit(solution)/shard_map/ppermute | solution.py:221
  41.9 2.9 %collective-permute-done.7.refs_2_ = bf16[96,1024]{1,0:T(8,128)(2,1)S(1)} collective-permute-done((bf16[96,1024]{1,0:T(8,128)(2,1)}, bf16[96,1024]{1,0:T(8,128)(2,1)S(1)}, u32[]{:S(2)}, u32[]{:S(2)}) %collective-permute-start.7) | collective-permute-done | bytes 196640 | tf_op jit(solution)/shard_map/ppermute | solution.py:221
  44.7 0.0 collective-permute-done.10.refs_1_
  44.7 1.0 %first_pass.5 = (f32[2,2,192]{2,1,0:T(2,128)S(1)}, f32[1,384]{1,0:T(1,128)S(1)}, bf16[384,1024]{1,0:T(8,128)(2,1)S(1)}) custom-call(bf16[512,1024]{1,0:T(8,128)(2,1)S(1)} %get-tuple-element.40.refs_0_.cents, bf16[192,1024]{1,0:T(8,128)(2,1)S(1)} %collective-permute-done.10.refs_1_, bf16[96,1024]{1,0:T(8,128)(2,1)S(1)} %collective-permute-done.7.refs_2_, ...), custom_call_target="tpu_custom_call" | custom-call | flops 402653184 | bytes 786432 | tf_op jit(solution)/shard_map/first_pass/pallas_call | solution.py:101
  46.0 9.9 %all_to_all.10 = f32[8,2,8,192]{3,2,1,0:T(8,128)S(1)} all-to-all(f32[8,2,8,192]{3,2,1,0:T(8,128)S(1)} %broadcast_in_dim.6), channel_id=1, replica_groups={{0,2,4,6,16,18,20,22},{8,10,12,14,24,26,28,30},{1,3,5,7,17,19,21,23},{9..., dimensions={0} | all-to-all | bytes 196608 | tf_op jit(solution)/shard_map/all_to_all | solution.py:272
  56.3 0.1 pad_maximum_fusion.8
  56.3 0.1 pad_maximum_fusion.7.refs_0_
  56.4 2.8 %sums_pass.3 = f32[256,1152]{1,0:T(8,128)S(1)} custom-call(bf16[512,1024]{1,0:T(8,128)(2,1)S(1)} %get-tuple-element.40.refs_0_.cents, f32[2,768]{1,0:T(2,128)S(1)} %pad_maximum_fusion.7.refs_0_, f32[2,384]{1,0:T(2,128)S(1)} %get-tuple-element.115.refs_1_, f32[2,384]{1,0:T(2,128)S(1)} %get-tuple-element.116.refs_2_, ...), custom_call_target="tpu_custom_call" | custom-call | flops 1610612736 | bytes 3145728 | tf_op jit(solution)/shard_map/sums_pass/pallas_call | solution.py:140
  59.3 0.1 collective-permute-start.12
  59.4 2.8 %sums_pass.2 = f32[256,1152]{1,0:T(8,128)S(1)} custom-call(bf16[512,1024]{1,0:T(8,128)(2,1)S(1)} %get-tuple-element.40.refs_0_.cents, f32[2,768]{1,0:T(2,128)S(1)} %pad_maximum_fusion.7.refs_0_, f32[2,384]{1,0:T(2,128)S(1)} %get-tuple-element.115.refs_1_, f32[2,384]{1,0:T(2,128)S(1)} %get-tuple-element.116.refs_2_, ...), custom_call_target="tpu_custom_call" | custom-call | flops 1610612736 | bytes 3145728 | tf_op jit(solution)/shard_map/sums_pass/pallas_call | solution.py:140
  62.2 0.6 collective-permute-start.11
  62.8 0.0 collective-permute-done.12
  62.8 0.1 slice_add_fusion
  62.9 1.2 %collective-permute-start.13 = (bf16[128,1152]{1,0:T(8,128)(2,1)S(1)}, bf16[128,1152]{1,0:T(8,128)(2,1)S(1)}, u32[]{:S(2)}, u32[]{:S(2)}) collective-permute-start(bf16[128,1152]{1,0:T(8,128)(2,1)S(1)} %pad_maximum_fusion.1), channel_id=1, source_target_pairs={{0,8},{2,10},{4,12},{6,14},{8,0},{10,2},{12,4},{14,6},{16,24},{18,... | collective-permute-start | bytes 884744 | tf_op jit(solution)/shard_map/ppermute | solution.py:221
  64.1 7.8 %collective-permute-done.13 = bf16[128,1152]{1,0:T(8,128)(2,1)S(1)} collective-permute-done((bf16[128,1152]{1,0:T(8,128)(2,1)S(1)}, bf16[128,1152]{1,0:T(8,128)(2,1)S(1)}, u32[]{:S(2)}, u32[]{:S(2)}) %collective-permute-start.13) | collective-permute-done | bytes 294944 | tf_op jit(solution)/shard_map/ppermute | solution.py:221
  72.0 0.2 fusion.4
  72.2 0.0 collective-permute-done.11
  72.2 0.1 broadcast_in_dim.8
  72.3 0.0 copy-start.5
  72.3 0.1 fusion
  72.4 0.1 fusion.3
  72.5 0.8 copy-done.5
  73.3 0.9 fusion.27
  74.3 0.0 collective-permute-start.15
  74.3 1.2 %collective-permute-start.14 = (bf16[128,1024]{1,0:T(8,128)(2,1)S(1)}, bf16[128,1024]{1,0:T(8,128)(2,1)S(1)}, u32[]{:S(2)}, u32[]{:S(2)}) collective-permute-start(bf16[128,1024]{1,0:T(8,128)(2,1)S(1)} %get-tuple-element.72), channel_id=1, source_target_pairs={{0,8},{2,10},{4,12},{6,14},{8,0},{10,2},{12,4},{14,6},{16,24},{18,... | collective-permute-start | bytes 786440 | tf_op jit(solution)/shard_map/ppermute | solution.py:221
  75.4 0.4 collective-permute-done.15
  75.8 1.6 %second_pass.3 = (f32[3,4,192]{2,1,0:T(4,128)S(1)}, f32[3,2,192]{2,1,0:T(2,128)S(1)}, f32[3,2,192]{2,1,0:T(2,128)S(1)}) custom-call(bf16[256,1024]{1,0:T(8,128)(2,1)S(1)} %pad_maximum_fusion.cents, f32[1,768]{1,0:T(1,128)S(1)} %get-tuple-element.53.refs_3_.refs_0_, f32[1,384]{1,0:T(1,128)S(1)} %get-tuple-element.54.refs_4_.refs_1_, ...), custom_call_target="tpu_custom_call" | custom-call | flops 805306368 | bytes 3145728 | tf_op jit(solution)/shard_map/second_pass/pallas_call | solution.py:181
  77.5 5.5 %collective-permute-done.14.cents = bf16[128,1024]{1,0:T(8,128)(2,1)S(1)} collective-permute-done((bf16[128,1024]{1,0:T(8,128)(2,1)S(1)}, bf16[128,1024]{1,0:T(8,128)(2,1)S(1)}, u32[]{:S(2)}, u32[]{:S(2)}) %collective-permute-start.14) | collective-permute-done | bytes 262176 | tf_op jit(solution)/shard_map/ppermute | solution.py:221
  83.0 0.0 collective-permute-start.16
  83.0 1.2 %second_pass.4 = (f32[3,4,192]{2,1,0:T(4,128)S(1)}, f32[3,2,192]{2,1,0:T(2,128)S(1)}, f32[3,2,192]{2,1,0:T(2,128)S(1)}) custom-call(bf16[128,1024]{1,0:T(8,128)(2,1)S(1)} %collective-permute-done.14.cents, f32[1,768]{1,0:T(1,128)S(1)} %get-tuple-element.53.refs_3_.refs_0_, f32[1,384]{1,0:T(1,128)S(1)} %get-tuple-element.54.refs_4_.refs_1_, ...), custom_call_target="tpu_custom_call" | custom-call | flops 402653184 | bytes 3145728 | tf_op jit(solution)/shard_map/second_pass/pallas_call | solution.py:181
  84.2 0.3 collective-permute-done.16.cents
  84.5 1.2 %second_pass.5 = (f32[3,4,192]{2,1,0:T(4,128)S(1)}, f32[3,2,192]{2,1,0:T(2,128)S(1)}, f32[3,2,192]{2,1,0:T(2,128)S(1)}) custom-call(bf16[128,1024]{1,0:T(8,128)(2,1)S(1)} %collective-permute-done.16.cents, f32[1,768]{1,0:T(1,128)S(1)} %get-tuple-element.53.refs_3_.refs_0_, f32[1,384]{1,0:T(1,128)S(1)} %get-tuple-element.54.refs_4_.refs_1_, ...), custom_call_target="tpu_custom_call" | custom-call | flops 402653184 | bytes 3145728 | tf_op jit(solution)/shard_map/second_pass/pallas_call | solution.py:181
  85.8 0.1 stack.78
  86.0 9.1 %all_to_all.11 = f32[8,3,192]{2,1,0:T(4,128)S(1)} all-to-all(f32[8,3,192]{2,1,0:T(4,128)S(1)} %copy.74), channel_id=1, replica_groups={{0,2,4,6,16,18,20,22},{8,10,12,14,24,26,28,30},{1,3,5,7,17,19,21,23},{9..., dimensions={0} | all-to-all | bytes 36864 | tf_op jit(solution)/shard_map/all_to_all | solution.py:272
  95.2 0.6 divide_subtract_fusion
  (65 shorter events, 1.0 us)
Async XLA Ops:
  0.6 4.3 %copy-start.4 = (f32[128,1024]{1,0:T(8,128)S(1)}, f32[128,1024]{1,0:T(8,128)}, u32[]{:S(2)}) copy-start(f32[128,1024]{1,0:T(8,128)} %param.3) | copy-start | bytes 1572868
  1.9 12.1 %collective-permute-start.2 = (bf16[192,1024]{1,0:T(8,128)(2,1)S(1)}, bf16[192,1024]{1,0:T(8,128)(2,1)S(1)}, u32[]{:S(2)}, u32[]{:S(2)}) collective-permute-start(bf16[192,1024]{1,0:T(8,128)(2,1)S(1)} %convert_element_type.14.refs_4_), channel_id=1, source_target_pairs={{0,2},{2,0},{4,6},{6,4},{8,10},{10,8},{12,14},{14,12},{16,18},{18,... | collective-permute-start | bytes 1179656 | tf_op jit(solution)/shard_map/ppermute | solution.py:221
  4.9 13.3 %collective-permute-start.5 = (bf16[128,1024]{1,0:T(8,128)(2,1)S(1)}, bf16[128,1024]{1,0:T(8,128)(2,1)S(1)}, u32[]{:S(2)}, u32[]{:S(2)}) collective-permute-start(bf16[128,1024]{1,0:T(8,128)(2,1)S(1)} %convert_element_type.13.refs_0_), channel_id=1, source_target_pairs={{0,8},{2,10},{4,12},{6,14},{8,0},{10,2},{12,4},{14,6},{16,24},{18,... | collective-permute-start | bytes 786440 | tf_op jit(solution)/shard_map/ppermute | solution.py:221
  6.6 19.7 %collective-permute-start.1 = (bf16[192,1024]{1,0:T(8,128)(2,1)S(1)}, bf16[192,1024]{1,0:T(8,128)(2,1)S(1)}, u32[]{:S(2)}, u32[]{:S(2)}) collective-permute-start(bf16[192,1024]{1,0:T(8,128)(2,1)S(1)} %convert_element_type.14.refs_4_), channel_id=1, source_target_pairs={{0,16},{2,18},{4,20},{6,22},{8,24},{10,26},{12,28},{14,30},{16,0},... | collective-permute-start | bytes 1179656 | tf_op jit(solution)/shard_map/ppermute | solution.py:221
  9.2 17.1 %collective-permute-start.4 = (bf16[192,1024]{1,0:T(8,128)(2,1)S(1)}, bf16[192,1024]{1,0:T(8,128)(2,1)S(1)}, u32[]{:S(2)}, u32[]{:S(2)}) collective-permute-start(bf16[192,1024]{1,0:T(8,128)(2,1)S(1)} %convert_element_type.14.refs_4_), channel_id=1, source_target_pairs={{0,4},{2,6},{4,0},{6,2},{8,12},{10,14},{12,8},{14,10},{16,20},{18,... | collective-permute-start | bytes 1179656 | tf_op jit(solution)/shard_map/ppermute | solution.py:221
  14.0 13.6 %collective-permute-start.3 = (bf16[192,1024]{1,0:T(8,128)(2,1)S(1)}, bf16[192,1024]{1,0:T(8,128)(2,1)S(1)}, u32[]{:S(2)}, u32[]{:S(2)}) collective-permute-start(bf16[192,1024]{1,0:T(8,128)(2,1)S(1)} %collective-permute-done.2.refs_5_), channel_id=1, source_target_pairs={{0,4},{2,6},{4,0},{6,2},{8,12},{10,14},{12,8},{14,10},{16,20},{18,... | collective-permute-start | bytes 1179656 | tf_op jit(solution)/shard_map/ppermute | solution.py:221
  18.3 8.0 %collective-permute-start.6 = (bf16[128,1024]{1,0:T(8,128)(2,1)S(1)}, bf16[128,1024]{1,0:T(8,128)(2,1)S(1)}, u32[]{:S(2)}, u32[]{:S(2)}) collective-permute-start(bf16[128,1024]{1,0:T(8,128)(2,1)S(1)} %collective-permute-done.5.refs_2_), channel_id=1, source_target_pairs={{0,1},{1,0},{2,3},{3,2},{4,5},{5,4},{6,7},{7,6},{8,9},{9,8},{10,11... | collective-permute-start | bytes 786440 | tf_op jit(solution)/shard_map/ppermute | solution.py:230
  18.3 0.7 copy-start
  26.2 0.7 copy-start.2
  27.6 11.2 %collective-permute-start.9 = (bf16[192,1024]{1,0:T(8,128)(2,1)S(1)}, bf16[192,1024]{1,0:T(8,128)(2,1)S(1)}, u32[]{:S(2)}, u32[]{:S(2)}) collective-permute-start(bf16[192,1024]{1,0:T(8,128)(2,1)S(1)} %collective-permute-done.1.refs_1_), channel_id=1, source_target_pairs={{0,2},{2,0},{4,6},{6,4},{8,10},{10,8},{12,14},{14,12},{16,18},{18,... | collective-permute-start | bytes 1179656 | tf_op jit(solution)/shard_map/ppermute | solution.py:221
  28.1 16.6 %collective-permute-start.10 = (bf16[192,1024]{1,0:T(8,128)(2,1)S(1)}, bf16[192,1024]{1,0:T(8,128)(2,1)S(1)}, u32[]{:S(2)}, u32[]{:S(2)}) collective-permute-start(bf16[192,1024]{1,0:T(8,128)(2,1)S(1)} %collective-permute-done.1.refs_1_), channel_id=1, source_target_pairs={{0,4},{2,6},{4,0},{6,2},{8,12},{10,14},{12,8},{14,10},{16,20},{18,... | collective-permute-start | bytes 1179656 | tf_op jit(solution)/shard_map/ppermute | solution.py:221
  29.7 3.2 %collective-permute-start = (bf16[128,1024]{1,0:T(8,128)(2,1)S(1)}, bf16[128,1024]{1,0:T(8,128)(2,1)}, u32[]{:S(2)}, u32[]{:S(2)}) collective-permute-start(bf16[128,1024]{1,0:T(8,128)(2,1)S(1)} %convert_element_type.13.refs_0_), channel_id=1, source_target_pairs={{0,1},{1,0},{2,3},{3,2},{4,5},{5,4},{6,7},{7,6},{8,9},{9,8},{10,11... | collective-permute-start | bytes 786440 | tf_op jit(solution)/shard_map/ppermute | solution.py:230
  30.4 11.5 %collective-permute-start.8 = (bf16[96,1024]{1,0:T(8,128)(2,1)}, bf16[96,1024]{1,0:T(8,128)(2,1)S(1)}, u32[]{:S(2)}, u32[]{:S(2)}) collective-permute-start(bf16[96,1024]{1,0:T(8,128)(2,1)} %slice.326), channel_id=1, source_target_pairs={{0,6},{2,4},{4,2},{6,0},{8,14},{10,12},{12,10},{14,8},{16,22},{18,... | collective-permute-start | bytes 589832 | tf_op jit(solution)/shard_map/ppermute | solution.py:221
  32.5 12.2 %collective-permute-start.7 = (bf16[96,1024]{1,0:T(8,128)(2,1)}, bf16[96,1024]{1,0:T(8,128)(2,1)S(1)}, u32[]{:S(2)}, u32[]{:S(2)}) collective-permute-start(bf16[96,1024]{1,0:T(8,128)(2,1)} %slice.325), channel_id=1, source_target_pairs={{0,16},{2,18},{4,20},{6,22},{8,24},{10,26},{12,28},{14,30},{16,0},... | collective-permute-start | bytes 589832 | tf_op jit(solution)/shard_map/ppermute | solution.py:221
  32.8 1.0 copy-start.1
  33.8 0.9 copy-start.3
  59.3 3.5 %collective-permute-start.12 = (f32[128,1152]{1,0:T(8,128)S(1)}, f32[128,1152]{1,0:T(8,128)S(1)}, u32[]{:S(2)}, u32[]{:S(2)}) collective-permute-start(f32[128,1152]{1,0:T(8,128)S(1)} %slice.451), channel_id=1, source_target_pairs={{0,1},{1,0},{2,3},{3,2},{4,5},{5,4},{6,7},{7,6},{8,9},{9,8},{10,11... | collective-permute-start | bytes 1769480 | tf_op jit(solution)/shard_map/ppermute | solution.py:230
  62.2 10.0 %collective-permute-start.11 = (f32[128,1152]{1,0:T(8,128)S(1)}, f32[128,1152]{1,0:T(8,128)S(1)}, u32[]{:S(2)}, u32[]{:S(2)}) collective-permute-start(f32[128,1152]{1,0:T(8,128)S(1)} %slice.449), channel_id=1, source_target_pairs={{0,1},{1,0},{2,3},{3,2},{4,5},{5,4},{6,7},{7,6},{8,9},{9,8},{10,11... | collective-permute-start | bytes 1769480 | tf_op jit(solution)/shard_map/ppermute | solution.py:230
  62.9 9.0 %collective-permute-start.13 = (bf16[128,1152]{1,0:T(8,128)(2,1)S(1)}, bf16[128,1152]{1,0:T(8,128)(2,1)S(1)}, u32[]{:S(2)}, u32[]{:S(2)}) collective-permute-start(bf16[128,1152]{1,0:T(8,128)(2,1)S(1)} %pad_maximum_fusion.1), channel_id=1, source_target_pairs={{0,8},{2,10},{4,12},{6,14},{8,0},{10,2},{12,4},{14,6},{16,24},{18,... | collective-permute-start | bytes 884744 | tf_op jit(solution)/shard_map/ppermute | solution.py:221
  72.3 1.1 %copy-start.5 = (f32[128,1024]{1,0:T(8,128)S(1)}, f32[128,1024]{1,0:T(8,128)}, u32[]{:S(2)}) copy-start(f32[128,1024]{1,0:T(8,128)} %param.3) | copy-start | bytes 1572868
  74.3 1.5 %collective-permute-start.15 = (bf16[128,1024]{1,0:T(8,128)(2,1)S(1)}, bf16[128,1024]{1,0:T(8,128)(2,1)S(1)}, u32[]{:S(2)}, u32[]{:S(2)}) collective-permute-start(bf16[128,1024]{1,0:T(8,128)(2,1)S(1)} %get-tuple-element.72), channel_id=1, source_target_pairs={{0,1},{1,0},{2,3},{3,2},{4,5},{5,4},{6,7},{7,6},{8,9},{9,8},{10,11... | collective-permute-start | bytes 786440 | tf_op jit(solution)/shard_map/ppermute | solution.py:230
  74.3 8.7 %collective-permute-start.14 = (bf16[128,1024]{1,0:T(8,128)(2,1)S(1)}, bf16[128,1024]{1,0:T(8,128)(2,1)S(1)}, u32[]{:S(2)}, u32[]{:S(2)}) collective-permute-start(bf16[128,1024]{1,0:T(8,128)(2,1)S(1)} %get-tuple-element.72), channel_id=1, source_target_pairs={{0,8},{2,10},{4,12},{6,14},{8,0},{10,2},{12,4},{14,6},{16,24},{18,... | collective-permute-start | bytes 786440 | tf_op jit(solution)/shard_map/ppermute | solution.py:221
  83.0 1.5 %collective-permute-start.16 = (bf16[128,1024]{1,0:T(8,128)(2,1)S(1)}, bf16[128,1024]{1,0:T(8,128)(2,1)S(1)}, u32[]{:S(2)}, u32[]{:S(2)}) collective-permute-start(bf16[128,1024]{1,0:T(8,128)(2,1)S(1)} %collective-permute-done.14.cents), channel_id=1, source_target_pairs={{0,1},{1,0},{2,3},{3,2},{4,5},{5,4},{6,7},{7,6},{8,9},{9,8},{10,11... | collective-permute-start | bytes 786440 | tf_op jit(solution)/shard_map/ppermute | solution.py:230

commit v10 on v9

--- a/solution.py
+++ b/solution.py
@@ -36,7 +36,8 @@
 
 def scores(piece, cent_sq, rows, row_sq):
     inner = lax.dot_general(piece, rows, (((1,), (1,)), ((), ())), preferred_element_type=jnp.float32)
-    return -(row_sq - 2.0 * inner + cent_sq) * (0.5 / softness_level)
+    scale = 0.5 / softness_level
+    return (2.0 * scale) * inner - scale * row_sq - scale * cent_sq
 
 
 def fetch(sources, target, sems):
@@ -116,31 +117,35 @@
 
 
 def sums_kernel(first, last, n, cents, *refs):
-    stats, row_sqs, rows = refs[:n], refs[n : 2 * n], refs[2 * n : 3 * n]
-    out_ref = refs[3 * n]
+    stats, row_sqs, rows, priors = refs[:n], refs[n : 2 * n], refs[2 * n : 3 * n], refs[3 * n : -1]
+    out_ref = refs[-1]
     width = cents.shape[1]
     piece = cents[first:last, :]
     cent_sq = centroid_squares(piece)
     counts = 0.0
     for s in range(n):
         score = scores(piece, cent_sq, rows[s][...], row_sqs[s][...])
-        resp = (jnp.exp(score - stats[s][0:1, :]) / stats[s][1:2, :]).astype(jnp.bfloat16)
+        resp = (jnp.exp(score - stats[s][0:1, :]) * (1.0 / stats[s][1:2, :])).astype(jnp.bfloat16)
         counts = counts + jnp.sum(resp.astype(jnp.float32), axis=1, keepdims=True)
         part = jnp.dot(resp, rows[s][...], preferred_element_type=jnp.float32)
         if s:
             part = part + out_ref[:, :width]
         out_ref[:, :width] = part
     out_ref[:, width:] = jnp.broadcast_to(counts, (last - first, 128))
-
-
-def sums_pass(cents, stats, row_sqs, rows, first, last):
+    for prior in priors:
+        held = prior.shape[0]
+        out_ref[:held, :width] += prior_mass * prior[...]
+        out_ref[:held, width:] += prior_mass
+
+
+def sums_pass(cents, stats, row_sqs, rows, first, last, priors=()):
     n = len(rows)
     width = rows[0].shape[1]
     n_rows = sum(r.shape[0] for r in rows)
     return pl.pallas_call(
         functools.partial(sums_kernel, first, last, n),
         out_shape=jax.ShapeDtypeStruct((last - first, width + 128), jnp.float32),
-        in_specs=[VMEM] * (1 + 3 * n),
+        in_specs=[VMEM] * (1 + 3 * n + len(priors)),
         out_specs=VMEM,
         compiler_params=params(),
         cost_estimate=pl.CostEstimate(
@@ -149,7 +154,7 @@
             transcendentals=(last - first) * n_rows,
         ),
         name="sums_pass",
-    )(cents, *stats, *row_sqs, *rows)
+    )(cents, *stats, *row_sqs, *rows, *priors)
 
 
 def second_kernel(shard, n, cents, *refs):
@@ -312,11 +317,11 @@
         lane = lax.broadcasted_iota(jnp.int32, count.shape, 1)
         far = jnp.concatenate([far[:, :width], jnp.where(lane < 64, coarse, count - coarse)], axis=1)
         far = flip(far.astype(jnp.bfloat16), top_bit).astype(jnp.float32)
-        near = scatter_cent(sums_pass(piece, final, row_sqs, rows, 0, n_near))
+        near = scatter_cent(sums_pass(piece, final, row_sqs, rows, 0, n_near, [centroids]))
         counts = far[:, width : width + 1] + far[:, width + 64 : width + 65]
         far = jnp.concatenate([far[:, :width], jnp.broadcast_to(counts, count.shape)], axis=1)
         sums = scatter_near(near + far)
-        updated = (sums[:, :width] + prior_mass * centroids) / (sums[:, width : width + 1] + prior_mass)
+        updated = sums[:, :width] / sums[:, width : width + 1]
         near_own = gather_near(updated.astype(jnp.bfloat16))
         far_own = flip(near_own, top_bit)
         stats = second_pass(jnp.concatenate(gather_cent(near_own), axis=0), row_sqs, rows, shard)

time: 96.1 us -> 95.3 us (level)
  waiting for transfers between devices: 32 us -> 30.4 us
  local copies, waits for them, and re-layouts: 5.99 us -> 7.01 us
    ppermute x11, waiting for transfers between devices: 31.3 us -> 29.7 us  [flip(): return lax.ppermute(value, 'dp', [(i, i ^ bits) for i in range(n_dp)])]
    unnamed x19 -> x21, local copies, waits for them, and re-layouts: 4.2 us -> 5.1 us
  transfers between devices with their start and end apart: 17 -> 17, of which waited for: 10 -> 9; matrix products, arithmetic and copies ran while one was open for 2% -> 2% of each run, Pallas kernels for 12% -> 12%
where the time goes in v10:
time: 95.3 us; the launch traced here: 95 us
  waiting for transfers between devices  30.4 us (32%)
  blocking collectives  19 us (20%)
  starting transfers between devices  17.3 us (18%)
  Pallas kernels  16.3 us (17%)
  local copies, waits for them, and re-layouts  7.01 us (7%)
  other arithmetic  3.88 us (4%)
  between operations  1.11 us (1%)
    ppermute x11, waiting for transfers between devices, flip(): return lax.ppermute(value, 'dp', [(i, i ^ bits) for i in range(n_dp)])  29.7 us
    all_to_all x2, blocking collectives, exchange(): return lax.all_to_all(value, 'dp', 0, 0, axis_index_groups=groups)  19 us
    ppermute x11, starting transfers between devices, flip(): return lax.ppermute(value, 'dp', [(i, i ^ bits) for i in range(n_dp)])  16.6 us
    pallas_call x3, Pallas kernels, first_pass(): pl.pallas_call(functools.partial(first_kernel, n, n_blocks, n_chunks, sha...  6.77 us
    pallas_call x2, Pallas kernels, sums_pass(): pl.pallas_call(functools.partial(sums_kernel, first, last, n), out_shape=...  5.55 us
    unnamed x21, local copies, waits for them, and re-layouts  5.1 us
    pallas_call x3, Pallas kernels, second_pass(): pl.pallas_call(functools.partial(second_kernel, shard, n), out_shape=tupl...  4.01 us
  transfers between devices with their start and end apart: 17, of which 9 were waited for; matrix products, arithmetic and copies ran while one was open for 2% of the time, Pallas kernels for 12%

profile of v10, /device:TPU:0, one launch (start us, length us, event | category | flops | bytes accessed | tf_op | source)
XLA Modules:
  0.0 95.0 jit_solution(14386808999900915480)
XLA Ops:
  0.6 0.0 copy-start
  0.6 1.2 %convert_element_type.14.refs_4_ = bf16[192,1024]{1,0:T(8,128)(2,1)S(1)} convert(f32[192,1024]{1,0:T(8,128)} %param.2) | non-fusion elementwise | flops 196608 | bytes 1179648 | tf_op jit(solution)/shard_map/convert_element_type | solution.py:288
  1.9 3.0 %collective-permute-start.2 = (bf16[192,1024]{1,0:T(8,128)(2,1)S(1)}, bf16[192,1024]{1,0:T(8,128)(2,1)S(1)}, u32[]{:S(2)}, u32[]{:S(2)}) collective-permute-start(bf16[192,1024]{1,0:T(8,128)(2,1)S(1)} %convert_element_type.14.refs_4_), channel_id=1, source_target_pairs={{0,2},{2,0},{4,6},{6,4},{8,10},{10,8},{12,14},{14,12},{16,18},{18,... | collective-permute-start | bytes 1179656 | tf_op jit(solution)/shard_map/ppermute | solution.py:226
  4.9 1.6 %collective-permute-start.5 = (bf16[128,1024]{1,0:T(8,128)(2,1)S(1)}, bf16[128,1024]{1,0:T(8,128)(2,1)S(1)}, u32[]{:S(2)}, u32[]{:S(2)}) collective-permute-start(bf16[128,1024]{1,0:T(8,128)(2,1)S(1)} %convert_element_type.13.refs_0_), channel_id=1, source_target_pairs={{0,8},{2,10},{4,12},{6,14},{8,0},{10,2},{12,4},{14,6},{16,24},{18,... | collective-permute-start | bytes 786440 | tf_op jit(solution)/shard_map/ppermute | solution.py:226
  6.6 2.6 %collective-permute-start.1 = (bf16[192,1024]{1,0:T(8,128)(2,1)S(1)}, bf16[192,1024]{1,0:T(8,128)(2,1)S(1)}, u32[]{:S(2)}, u32[]{:S(2)}) collective-permute-start(bf16[192,1024]{1,0:T(8,128)(2,1)S(1)} %convert_element_type.14.refs_4_), channel_id=1, source_target_pairs={{0,16},{2,18},{4,20},{6,22},{8,24},{10,26},{12,28},{14,30},{16,0},... | collective-permute-start | bytes 1179656 | tf_op jit(solution)/shard_map/ppermute | solution.py:226
  9.2 1.5 %collective-permute-start.4 = (bf16[192,1024]{1,0:T(8,128)(2,1)S(1)}, bf16[192,1024]{1,0:T(8,128)(2,1)S(1)}, u32[]{:S(2)}, u32[]{:S(2)}) collective-permute-start(bf16[192,1024]{1,0:T(8,128)(2,1)S(1)} %convert_element_type.14.refs_4_), channel_id=1, source_target_pairs={{0,4},{2,6},{4,0},{6,2},{8,12},{10,14},{12,8},{14,10},{16,20},{18,... | collective-permute-start | bytes 1179656 | tf_op jit(solution)/shard_map/ppermute | solution.py:226
  10.7 3.3 %collective-permute-done.2.refs_5_ = bf16[192,1024]{1,0:T(8,128)(2,1)S(1)} collective-permute-done((bf16[192,1024]{1,0:T(8,128)(2,1)S(1)}, bf16[192,1024]{1,0:T(8,128)(2,1)S(1)}, u32[]{:S(2)}, u32[]{:S(2)}) %collective-permute-start.2) | collective-permute-done | bytes 393248 | tf_op jit(solution)/shard_map/ppermute | solution.py:226
  14.0 1.8 %collective-permute-start.3 = (bf16[192,1024]{1,0:T(8,128)(2,1)S(1)}, bf16[192,1024]{1,0:T(8,128)(2,1)S(1)}, u32[]{:S(2)}, u32[]{:S(2)}) collective-permute-start(bf16[192,1024]{1,0:T(8,128)(2,1)S(1)} %collective-permute-done.2.refs_5_), channel_id=1, source_target_pairs={{0,4},{2,6},{4,0},{6,2},{8,12},{10,14},{12,8},{14,10},{16,20},{18,... | collective-permute-start | bytes 1179656 | tf_op jit(solution)/shard_map/ppermute | solution.py:226
  15.8 2.5 %collective-permute-done.5.refs_2_ = bf16[128,1024]{1,0:T(8,128)(2,1)S(1)} collective-permute-done((bf16[128,1024]{1,0:T(8,128)(2,1)S(1)}, bf16[128,1024]{1,0:T(8,128)(2,1)S(1)}, u32[]{:S(2)}, u32[]{:S(2)}) %collective-permute-start.5) | collective-permute-done | bytes 262176 | tf_op jit(solution)/shard_map/ppermute | solution.py:226
  18.3 0.0 collective-permute-start.6
  18.3 0.7 copy-done.3
  19.0 7.3 %collective-permute-done.1.refs_1_ = bf16[192,1024]{1,0:T(8,128)(2,1)S(1)} collective-permute-done((bf16[192,1024]{1,0:T(8,128)(2,1)S(1)}, bf16[192,1024]{1,0:T(8,128)(2,1)S(1)}, u32[]{:S(2)}, u32[]{:S(2)}) %collective-permute-start.1) | collective-permute-done | bytes 393248 | tf_op jit(solution)/shard_map/ppermute | solution.py:226
  26.2 0.0 collective-permute-done.4.refs_6_
  26.2 0.7 copy-done.1
  27.0 0.0 collective-permute-done.6.refs_3_
  27.0 0.7 copy-done.5
  27.7 0.0 collective-permute-done.3.refs_7_
  27.7 0.5 collective-permute-start.9
  28.2 1.5 %collective-permute-start.10 = (bf16[192,1024]{1,0:T(8,128)(2,1)S(1)}, bf16[192,1024]{1,0:T(8,128)(2,1)S(1)}, u32[]{:S(2)}, u32[]{:S(2)}) collective-permute-start(bf16[192,1024]{1,0:T(8,128)(2,1)S(1)} %collective-permute-done.1.refs_1_), channel_id=1, source_target_pairs={{0,4},{2,6},{4,0},{6,2},{8,12},{10,14},{12,8},{14,10},{16,20},{18,... | collective-permute-start | bytes 1179656 | tf_op jit(solution)/shard_map/ppermute | solution.py:226
  29.8 0.0 collective-permute-start
  29.8 0.7 slice.326
  30.5 1.4 %collective-permute-start.8 = (bf16[96,1024]{1,0:T(8,128)(2,1)}, bf16[96,1024]{1,0:T(8,128)(2,1)S(1)}, u32[]{:S(2)}, u32[]{:S(2)}) collective-permute-start(bf16[96,1024]{1,0:T(8,128)(2,1)} %slice.326), channel_id=1, source_target_pairs={{0,6},{2,4},{4,2},{6,0},{8,14},{10,12},{12,10},{14,8},{16,22},{18,... | collective-permute-start | bytes 589832 | tf_op jit(solution)/shard_map/ppermute | solution.py:226
  31.9 0.7 slice.325
  32.6 0.2 collective-permute-start.7
  32.8 0.0 collective-permute-done.refs_1_
  32.8 1.0 %copy-done.2 = bf16[192,1024]{1,0:T(8,128)(2,1)S(1)} copy-done((bf16[192,1024]{1,0:T(8,128)(2,1)S(1)}, bf16[192,1024]{1,0:T(8,128)(2,1)}, u32[]{:S(2)}) %copy-start.2) | copy-done | bytes 393240
  33.8 0.9 copy-done.4
  34.8 0.9 copy-done.6
  35.7 4.1 %first_pass.3 = (f32[2,4,192]{2,1,0:T(4,128)S(1)}, f32[1,768]{1,0:T(1,128)S(1)}, bf16[768,1024]{1,0:T(8,128)(2,1)S(1)}, bf16[512,1024]{1,0:T(8,128)(2,1)S(1)}) custom-call(bf16[128,1024]{1,0:T(8,128)(2,1)S(1)} %convert_element_type.13.refs_0_, bf16[128,1024]{1,0:T(8,128)(2,1)} %collective-permute-done.refs_1_, bf16[128,1024]{1,0:T(8,128)(2,1)S(1)} %copy-done.4, ...), custom_call_target="tpu_custom_call" | custom-call | flops 805306368 | bytes 1572864 | tf_op jit(solution)/shard_map/first_pass/pallas_call | solution.py:102
  39.8 0.0 collective-permute-done.9.refs_2_
  39.8 1.7 %first_pass.4 = (f32[2,2,192]{2,1,0:T(2,128)S(1)}, f32[1,384]{1,0:T(1,128)S(1)}, bf16[384,1024]{1,0:T(8,128)(2,1)S(1)}) custom-call(bf16[512,1024]{1,0:T(8,128)(2,1)S(1)} %get-tuple-element.40.refs_0_.cents, bf16[192,1024]{1,0:T(8,128)(2,1)S(1)} %collective-permute-done.1.refs_1_, bf16[192,1024]{1,0:T(8,128)(2,1)S(1)} %collective-permute-done.9.refs_2_), custom_call_target="tpu_custom_call" | custom-call | flops 402653184 | bytes 786432 | tf_op jit(solution)/shard_map/first_pass/pallas_call | solution.py:102
  41.5 0.8 collective-permute-done.8.refs_3_
  42.3 2.5 %collective-permute-done.7.refs_2_ = bf16[96,1024]{1,0:T(8,128)(2,1)S(1)} collective-permute-done((bf16[96,1024]{1,0:T(8,128)(2,1)}, bf16[96,1024]{1,0:T(8,128)(2,1)S(1)}, u32[]{:S(2)}, u32[]{:S(2)}) %collective-permute-start.7) | collective-permute-done | bytes 196640 | tf_op jit(solution)/shard_map/ppermute | solution.py:226
  44.8 0.0 collective-permute-done.10.refs_1_
  44.8 1.0 %first_pass.5 = (f32[2,2,192]{2,1,0:T(2,128)S(1)}, f32[1,384]{1,0:T(1,128)S(1)}, bf16[384,1024]{1,0:T(8,128)(2,1)S(1)}) custom-call(bf16[512,1024]{1,0:T(8,128)(2,1)S(1)} %get-tuple-element.40.refs_0_.cents, bf16[192,1024]{1,0:T(8,128)(2,1)S(1)} %collective-permute-done.10.refs_1_, bf16[96,1024]{1,0:T(8,128)(2,1)S(1)} %collective-permute-done.7.refs_2_, ...), custom_call_target="tpu_custom_call" | custom-call | flops 402653184 | bytes 786432 | tf_op jit(solution)/shard_map/first_pass/pallas_call | solution.py:102
  46.1 9.9 %all_to_all.10 = f32[8,2,8,192]{3,2,1,0:T(8,128)S(1)} all-to-all(f32[8,2,8,192]{3,2,1,0:T(8,128)S(1)} %broadcast_in_dim.6), channel_id=1, replica_groups={{0,2,4,6,16,18,20,22},{8,10,12,14,24,26,28,30},{1,3,5,7,17,19,21,23},{9..., dimensions={0} | all-to-all | bytes 196608 | tf_op jit(solution)/shard_map/all_to_all | solution.py:277
  56.3 0.1 pad_maximum_fusion.8
  56.4 0.1 pad_maximum_fusion.7.refs_0_
  56.5 2.8 %sums_pass.3 = f32[256,1152]{1,0:T(8,128)S(1)} custom-call(bf16[512,1024]{1,0:T(8,128)(2,1)S(1)} %get-tuple-element.40.refs_0_.cents, f32[2,768]{1,0:T(2,128)S(1)} %pad_maximum_fusion.7.refs_0_, f32[2,384]{1,0:T(2,128)S(1)} %get-tuple-element.115.refs_1_, f32[2,384]{1,0:T(2,128)S(1)} %get-tuple-element.116.refs_2_, ...), custom_call_target="tpu_custom_call" | custom-call | flops 1610612736 | bytes 3145728 | tf_op jit(solution)/shard_map/sums_pass/pallas_call | solution.py:145
  59.3 0.1 collective-permute-start.12
  59.4 2.8 %sums_pass.2 = f32[256,1152]{1,0:T(8,128)S(1)} custom-call(bf16[512,1024]{1,0:T(8,128)(2,1)S(1)} %get-tuple-element.40.refs_0_.cents, f32[2,768]{1,0:T(2,128)S(1)} %pad_maximum_fusion.7.refs_0_, f32[2,384]{1,0:T(2,128)S(1)} %get-tuple-element.115.refs_1_, f32[2,384]{1,0:T(2,128)S(1)} %get-tuple-element.116.refs_2_, ...), custom_call_target="tpu_custom_call" | custom-call | flops 1610612736 | bytes 3145728 | tf_op jit(solution)/shard_map/sums_pass/pallas_call | solution.py:145
  62.2 0.6 collective-permute-start.11
  62.8 0.0 collective-permute-done.12
  62.8 0.1 slice_add_fusion
  62.9 1.2 %collective-permute-start.13 = (bf16[128,1152]{1,0:T(8,128)(2,1)S(1)}, bf16[128,1152]{1,0:T(8,128)(2,1)S(1)}, u32[]{:S(2)}, u32[]{:S(2)}) collective-permute-start(bf16[128,1152]{1,0:T(8,128)(2,1)S(1)} %pad_maximum_fusion.1), channel_id=1, source_target_pairs={{0,8},{2,10},{4,12},{6,14},{8,0},{10,2},{12,4},{14,6},{16,24},{18,... | collective-permute-start | bytes 884744 | tf_op jit(solution)/shard_map/ppermute | solution.py:226
  64.2 7.8 %collective-permute-done.13 = bf16[128,1152]{1,0:T(8,128)(2,1)S(1)} collective-permute-done((bf16[128,1152]{1,0:T(8,128)(2,1)S(1)}, bf16[128,1152]{1,0:T(8,128)(2,1)S(1)}, u32[]{:S(2)}, u32[]{:S(2)}) %collective-permute-start.13) | collective-permute-done | bytes 294944 | tf_op jit(solution)/shard_map/ppermute | solution.py:226
  72.0 0.2 fusion.2
  72.2 0.0 collective-permute-done.11
  72.2 0.1 broadcast_in_dim.8
  72.3 0.1 fusion
  72.4 0.1 slice_reduce_fusion
  72.5 0.9 fusion.25
  73.5 0.0 collective-permute-start.15
  73.5 1.2 %collective-permute-start.14 = (bf16[128,1024]{1,0:T(8,128)(2,1)S(1)}, bf16[128,1024]{1,0:T(8,128)(2,1)S(1)}, u32[]{:S(2)}, u32[]{:S(2)}) collective-permute-start(bf16[128,1024]{1,0:T(8,128)(2,1)S(1)} %get-tuple-element.72), channel_id=1, source_target_pairs={{0,8},{2,10},{4,12},{6,14},{8,0},{10,2},{12,4},{14,6},{16,24},{18,... | collective-permute-start | bytes 786440 | tf_op jit(solution)/shard_map/ppermute | solution.py:226
  74.6 0.4 collective-permute-done.15
  75.0 1.6 %second_pass.3 = (f32[3,4,192]{2,1,0:T(4,128)S(1)}, f32[3,2,192]{2,1,0:T(2,128)S(1)}, f32[3,2,192]{2,1,0:T(2,128)S(1)}) custom-call(bf16[256,1024]{1,0:T(8,128)(2,1)S(1)} %pad_maximum_fusion.cents, f32[1,768]{1,0:T(1,128)S(1)} %get-tuple-element.53.refs_3_.refs_0_, f32[1,384]{1,0:T(1,128)S(1)} %get-tuple-element.54.refs_4_.refs_1_, ...), custom_call_target="tpu_custom_call" | custom-call | flops 805306368 | bytes 3145728 | tf_op jit(solution)/shard_map/second_pass/pallas_call | solution.py:186
  76.7 5.5 %collective-permute-done.14.cents = bf16[128,1024]{1,0:T(8,128)(2,1)S(1)} collective-permute-done((bf16[128,1024]{1,0:T(8,128)(2,1)S(1)}, bf16[128,1024]{1,0:T(8,128)(2,1)S(1)}, u32[]{:S(2)}, u32[]{:S(2)}) %collective-permute-start.14) | collective-permute-done | bytes 262176 | tf_op jit(solution)/shard_map/ppermute | solution.py:226
  82.2 0.0 collective-permute-start.16
  82.2 1.2 %second_pass.4 = (f32[3,4,192]{2,1,0:T(4,128)S(1)}, f32[3,2,192]{2,1,0:T(2,128)S(1)}, f32[3,2,192]{2,1,0:T(2,128)S(1)}) custom-call(bf16[128,1024]{1,0:T(8,128)(2,1)S(1)} %collective-permute-done.14.cents, f32[1,768]{1,0:T(1,128)S(1)} %get-tuple-element.53.refs_3_.refs_0_, f32[1,384]{1,0:T(1,128)S(1)} %get-tuple-element.54.refs_4_.refs_1_, ...), custom_call_target="tpu_custom_call" | custom-call | flops 402653184 | bytes 3145728 | tf_op jit(solution)/shard_map/second_pass/pallas_call | solution.py:186
  83.4 0.3 collective-permute-done.16.cents
  83.7 1.2 %second_pass.5 = (f32[3,4,192]{2,1,0:T(4,128)S(1)}, f32[3,2,192]{2,1,0:T(2,128)S(1)}, f32[3,2,192]{2,1,0:T(2,128)S(1)}) custom-call(bf16[128,1024]{1,0:T(8,128)(2,1)S(1)} %collective-permute-done.16.cents, f32[1,768]{1,0:T(1,128)S(1)} %get-tuple-element.53.refs_3_.refs_0_, f32[1,384]{1,0:T(1,128)S(1)} %get-tuple-element.54.refs_4_.refs_1_, ...), custom_call_target="tpu_custom_call" | custom-call | flops 402653184 | bytes 3145728 | tf_op jit(solution)/shard_map/second_pass/pallas_call | solution.py:186
  85.0 0.1 stack.78
  85.2 9.1 %all_to_all.11 = f32[8,3,192]{2,1,0:T(4,128)S(1)} all-to-all(f32[8,3,192]{2,1,0:T(4,128)S(1)} %copy.74), channel_id=1, replica_groups={{0,2,4,6,16,18,20,22},{8,10,12,14,24,26,28,30},{1,3,5,7,17,19,21,23},{9..., dimensions={0} | all-to-all | bytes 36864 | tf_op jit(solution)/shard_map/all_to_all | solution.py:277
  94.4 0.6 divide_subtract_fusion
  (67 shorter events, 1.0 us)
Async XLA Ops:
  0.6 4.3 %copy-start = (f32[128,1024]{1,0:T(8,128)S(1)}, f32[128,1024]{1,0:T(8,128)}, u32[]{:S(2)}) copy-start(f32[128,1024]{1,0:T(8,128)} %refs_9_.1) | copy-start | bytes 1572868
  1.9 12.1 %collective-permute-start.2 = (bf16[192,1024]{1,0:T(8,128)(2,1)S(1)}, bf16[192,1024]{1,0:T(8,128)(2,1)S(1)}, u32[]{:S(2)}, u32[]{:S(2)}) collective-permute-start(bf16[192,1024]{1,0:T(8,128)(2,1)S(1)} %convert_element_type.14.refs_4_), channel_id=1, source_target_pairs={{0,2},{2,0},{4,6},{6,4},{8,10},{10,8},{12,14},{14,12},{16,18},{18,... | collective-permute-start | bytes 1179656 | tf_op jit(solution)/shard_map/ppermute | solution.py:226
  4.9 13.3 %collective-permute-start.5 = (bf16[128,1024]{1,0:T(8,128)(2,1)S(1)}, bf16[128,1024]{1,0:T(8,128)(2,1)S(1)}, u32[]{:S(2)}, u32[]{:S(2)}) collective-permute-start(bf16[128,1024]{1,0:T(8,128)(2,1)S(1)} %convert_element_type.13.refs_0_), channel_id=1, source_target_pairs={{0,8},{2,10},{4,12},{6,14},{8,0},{10,2},{12,4},{14,6},{16,24},{18,... | collective-permute-start | bytes 786440 | tf_op jit(solution)/shard_map/ppermute | solution.py:226
  6.6 19.7 %collective-permute-start.1 = (bf16[192,1024]{1,0:T(8,128)(2,1)S(1)}, bf16[192,1024]{1,0:T(8,128)(2,1)S(1)}, u32[]{:S(2)}, u32[]{:S(2)}) collective-permute-start(bf16[192,1024]{1,0:T(8,128)(2,1)S(1)} %convert_element_type.14.refs_4_), channel_id=1, source_target_pairs={{0,16},{2,18},{4,20},{6,22},{8,24},{10,26},{12,28},{14,30},{16,0},... | collective-permute-start | bytes 1179656 | tf_op jit(solution)/shard_map/ppermute | solution.py:226
  9.2 17.1 %collective-permute-start.4 = (bf16[192,1024]{1,0:T(8,128)(2,1)S(1)}, bf16[192,1024]{1,0:T(8,128)(2,1)S(1)}, u32[]{:S(2)}, u32[]{:S(2)}) collective-permute-start(bf16[192,1024]{1,0:T(8,128)(2,1)S(1)} %convert_element_type.14.refs_4_), channel_id=1, source_target_pairs={{0,4},{2,6},{4,0},{6,2},{8,12},{10,14},{12,8},{14,10},{16,20},{18,... | collective-permute-start | bytes 1179656 | tf_op jit(solution)/shard_map/ppermute | solution.py:226
  14.0 13.7 %collective-permute-start.3 = (bf16[192,1024]{1,0:T(8,128)(2,1)S(1)}, bf16[192,1024]{1,0:T(8,128)(2,1)S(1)}, u32[]{:S(2)}, u32[]{:S(2)}) collective-permute-start(bf16[192,1024]{1,0:T(8,128)(2,1)S(1)} %collective-permute-done.2.refs_5_), channel_id=1, source_target_pairs={{0,4},{2,6},{4,0},{6,2},{8,12},{10,14},{12,8},{14,10},{16,20},{18,... | collective-permute-start | bytes 1179656 | tf_op jit(solution)/shard_map/ppermute | solution.py:226
  18.3 8.7 %collective-permute-start.6 = (bf16[128,1024]{1,0:T(8,128)(2,1)S(1)}, bf16[128,1024]{1,0:T(8,128)(2,1)S(1)}, u32[]{:S(2)}, u32[]{:S(2)}) collective-permute-start(bf16[128,1024]{1,0:T(8,128)(2,1)S(1)} %collective-permute-done.5.refs_2_), channel_id=1, source_target_pairs={{0,1},{1,0},{2,3},{3,2},{4,5},{5,4},{6,7},{7,6},{8,9},{9,8},{10,11... | collective-permute-start | bytes 786440 | tf_op jit(solution)/shard_map/ppermute | solution.py:235
  18.3 0.7 copy-start.3
  26.2 0.7 copy-start.1
  27.0 0.7 copy-start.5
  27.7 12.1 %collective-permute-start.9 = (bf16[192,1024]{1,0:T(8,128)(2,1)S(1)}, bf16[192,1024]{1,0:T(8,128)(2,1)S(1)}, u32[]{:S(2)}, u32[]{:S(2)}) collective-permute-start(bf16[192,1024]{1,0:T(8,128)(2,1)S(1)} %collective-permute-done.1.refs_1_), channel_id=1, source_target_pairs={{0,2},{2,0},{4,6},{6,4},{8,10},{10,8},{12,14},{14,12},{16,18},{18,... | collective-permute-start | bytes 1179656 | tf_op jit(solution)/shard_map/ppermute | solution.py:226
  28.2 16.5 %collective-permute-start.10 = (bf16[192,1024]{1,0:T(8,128)(2,1)S(1)}, bf16[192,1024]{1,0:T(8,128)(2,1)S(1)}, u32[]{:S(2)}, u32[]{:S(2)}) collective-permute-start(bf16[192,1024]{1,0:T(8,128)(2,1)S(1)} %collective-permute-done.1.refs_1_), channel_id=1, source_target_pairs={{0,4},{2,6},{4,0},{6,2},{8,12},{10,14},{12,8},{14,10},{16,20},{18,... | collective-permute-start | bytes 1179656 | tf_op jit(solution)/shard_map/ppermute | solution.py:226
  29.8 3.1 %collective-permute-start = (bf16[128,1024]{1,0:T(8,128)(2,1)S(1)}, bf16[128,1024]{1,0:T(8,128)(2,1)}, u32[]{:S(2)}, u32[]{:S(2)}) collective-permute-start(bf16[128,1024]{1,0:T(8,128)(2,1)S(1)} %convert_element_type.13.refs_0_), channel_id=1, source_target_pairs={{0,1},{1,0},{2,3},{3,2},{4,5},{5,4},{6,7},{7,6},{8,9},{9,8},{10,11... | collective-permute-start | bytes 786440 | tf_op jit(solution)/shard_map/ppermute | solution.py:235
  30.5 11.8 %collective-permute-start.8 = (bf16[96,1024]{1,0:T(8,128)(2,1)}, bf16[96,1024]{1,0:T(8,128)(2,1)S(1)}, u32[]{:S(2)}, u32[]{:S(2)}) collective-permute-start(bf16[96,1024]{1,0:T(8,128)(2,1)} %slice.326), channel_id=1, source_target_pairs={{0,6},{2,4},{4,2},{6,0},{8,14},{10,12},{12,10},{14,8},{16,22},{18,... | collective-permute-start | bytes 589832 | tf_op jit(solution)/shard_map/ppermute | solution.py:226
  32.6 12.2 %collective-permute-start.7 = (bf16[96,1024]{1,0:T(8,128)(2,1)}, bf16[96,1024]{1,0:T(8,128)(2,1)S(1)}, u32[]{:S(2)}, u32[]{:S(2)}) collective-permute-start(bf16[96,1024]{1,0:T(8,128)(2,1)} %slice.325), channel_id=1, source_target_pairs={{0,16},{2,18},{4,20},{6,22},{8,24},{10,26},{12,28},{14,30},{16,0},... | collective-permute-start | bytes 589832 | tf_op jit(solution)/shard_map/ppermute | solution.py:226
  32.8 1.0 %copy-start.2 = (bf16[192,1024]{1,0:T(8,128)(2,1)S(1)}, bf16[192,1024]{1,0:T(8,128)(2,1)}, u32[]{:S(2)}) copy-start(bf16[192,1024]{1,0:T(8,128)(2,1)} %copy-done.1) | copy-start | bytes 1179652
  33.8 0.9 %copy-start.4 = (bf16[128,1024]{1,0:T(8,128)(2,1)S(1)}, bf16[128,1024]{1,0:T(8,128)(2,1)}, u32[]{:S(2)}) copy-start(bf16[128,1024]{1,0:T(8,128)(2,1)} %copy-done.3) | copy-start | bytes 786436
  34.8 0.9 %copy-start.6 = (bf16[128,1024]{1,0:T(8,128)(2,1)S(1)}, bf16[128,1024]{1,0:T(8,128)(2,1)}, u32[]{:S(2)}) copy-start(bf16[128,1024]{1,0:T(8,128)(2,1)} %copy-done.5) | copy-start | bytes 786436
  59.3 3.5 %collective-permute-start.12 = (f32[128,1152]{1,0:T(8,128)S(1)}, f32[128,1152]{1,0:T(8,128)S(1)}, u32[]{:S(2)}, u32[]{:S(2)}) collective-permute-start(f32[128,1152]{1,0:T(8,128)S(1)} %slice.451), channel_id=1, source_target_pairs={{0,1},{1,0},{2,3},{3,2},{4,5},{5,4},{6,7},{7,6},{8,9},{9,8},{10,11... | collective-permute-start | bytes 1769480 | tf_op jit(solution)/shard_map/ppermute | solution.py:235
  62.2 10.0 %collective-permute-start.11 = (f32[128,1152]{1,0:T(8,128)S(1)}, f32[128,1152]{1,0:T(8,128)S(1)}, u32[]{:S(2)}, u32[]{:S(2)}) collective-permute-start(f32[128,1152]{1,0:T(8,128)S(1)} %slice.449), channel_id=1, source_target_pairs={{0,1},{1,0},{2,3},{3,2},{4,5},{5,4},{6,7},{7,6},{8,9},{9,8},{10,11... | collective-permute-start | bytes 1769480 | tf_op jit(solution)/shard_map/ppermute | solution.py:235
  62.9 9.0 %collective-permute-start.13 = (bf16[128,1152]{1,0:T(8,128)(2,1)S(1)}, bf16[128,1152]{1,0:T(8,128)(2,1)S(1)}, u32[]{:S(2)}, u32[]{:S(2)}) collective-permute-start(bf16[128,1152]{1,0:T(8,128)(2,1)S(1)} %pad_maximum_fusion.1), channel_id=1, source_target_pairs={{0,8},{2,10},{4,12},{6,14},{8,0},{10,2},{12,4},{14,6},{16,24},{18,... | collective-permute-start | bytes 884744 | tf_op jit(solution)/shard_map/ppermute | solution.py:226
  73.5 1.5 %collective-permute-start.15 = (bf16[128,1024]{1,0:T(8,128)(2,1)S(1)}, bf16[128,1024]{1,0:T(8,128)(2,1)S(1)}, u32[]{:S(2)}, u32[]{:S(2)}) collective-permute-start(bf16[128,1024]{1,0:T(8,128)(2,1)S(1)} %get-tuple-element.72), channel_id=1, source_target_pairs={{0,1},{1,0},{2,3},{3,2},{4,5},{5,4},{6,7},{7,6},{8,9},{9,8},{10,11... | collective-permute-start | bytes 786440 | tf_op jit(solution)/shard_map/ppermute | solution.py:235
  73.5 8.7 %collective-permute-start.14 = (bf16[128,1024]{1,0:T(8,128)(2,1)S(1)}, bf16[128,1024]{1,0:T(8,128)(2,1)S(1)}, u32[]{:S(2)}, u32[]{:S(2)}) collective-permute-start(bf16[128,1024]{1,0:T(8,128)(2,1)S(1)} %get-tuple-element.72), channel_id=1, source_target_pairs={{0,8},{2,10},{4,12},{6,14},{8,0},{10,2},{12,4},{14,6},{16,24},{18,... | collective-permute-start | bytes 786440 | tf_op jit(solution)/shard_map/ppermute | solution.py:226
  82.2 1.5 %collective-permute-start.16 = (bf16[128,1024]{1,0:T(8,128)(2,1)S(1)}, bf16[128,1024]{1,0:T(8,128)(2,1)S(1)}, u32[]{:S(2)}, u32[]{:S(2)}) collective-permute-start(bf16[128,1024]{1,0:T(8,128)(2,1)S(1)} %collective-permute-done.14.cents), channel_id=1, source_target_pairs={{0,1},{1,0},{2,3},{3,2},{4,5},{5,4},{6,7},{7,6},{8,9},{9,8},{10,11... | collective-permute-start | bytes 786440 | tf_op jit(solution)/shard_map/ppermute | solution.py:235

commit v11 on v10

--- a/solution.py
+++ b/solution.py
@@ -12,7 +12,6 @@
 CUBE = 8
 GROUPS = ((0, 1, 2, 3), (4, 5), (6, 7))
 VMEM = pl.BlockSpec(memory_space=pltpu.VMEM)
-HBM = pl.BlockSpec(memory_space=pltpu.HBM)
 GRANT = 12 << 20
 
 
@@ -40,40 +39,17 @@
     return (2.0 * scale) * inner - scale * row_sq - scale * cent_sq
 
 
-def fetch(sources, target, sems):
-    copies, at = [], 0
-    for i, source in enumerate(sources):
-        n = source.shape[0]
-        copy = pltpu.make_async_copy(source, target.at[pl.ds(at, n)], sems.at[i])
-        copy.start()
-        copies.append(copy)
-        at += n
-    return copies
-
-
-def first_kernel(n, n_blocks, n_chunks, shard, last, *refs):
-    blocks, chunks, refs = refs[:n_blocks], refs[n_blocks : n_blocks + n_chunks], refs[n_blocks + n_chunks :]
-    stats_ref, row_sq_ref, rows_ref = refs[:3]
-    sems = refs[-1]
-    cents, copies = blocks[0], []
-    if n_blocks > 1:
-        cents, at = refs[3], 0
-        for block in blocks:
-            cents[at : at + block.shape[0], :] = block[...]
-            at += block.shape[0]
-    if last:
-        at = 0
-        for chunk in chunks:
-            rows_ref[at : at + chunk.shape[0], :] = chunk[...]
-            at += chunk.shape[0]
-    else:
-        copies = fetch(chunks, rows_ref, sems)
+def first_kernel(n_chunks, shard, cents, *refs):
+    chunks = refs[:n_chunks]
+    stats_ref, row_sq_ref, rows_ref = refs[n_chunks:]
+    at = 0
+    for chunk in chunks:
+        rows_ref[at : at + chunk.shape[0], :] = chunk[...]
+        at += chunk.shape[0]
     piece = cents[...]
     cent_sq = centroid_squares(piece)
     tile = 2 * shard
-    for j in range(n // 2):
-        for copy in copies[2 * j : 2 * j + 2]:
-            copy.wait()
+    for j in range(at // tile):
         span = slice(j * tile, (j + 1) * tile)
         rows = rows_ref[span, :]
         row_sq = row_squares(rows)
@@ -86,34 +62,25 @@
             stats_ref[1, 2 * j + i : 2 * j + i + 1, :] = total[:, i * shard : (i + 1) * shard]
 
 
-def first_pass(blocks, chunks, last=False):
-    n_blocks, n_chunks = len(blocks), len(chunks)
+def first_pass(cents, chunks):
     shard, width = chunks[0].shape
-    n_k = sum(b.shape[0] for b in blocks)
+    n_k = cents.shape[0]
     n_rows = sum(c.shape[0] for c in chunks)
-    n = n_rows // shard
-    outs = [
-        jax.ShapeDtypeStruct((2, n, shard), jnp.float32),
-        jax.ShapeDtypeStruct((1, n_rows), jnp.float32),
-        jax.ShapeDtypeStruct((n_rows, width), jnp.bfloat16),
-    ]
-    if n_blocks > 1:
-        outs.append(jax.ShapeDtypeStruct((n_k, width), jnp.bfloat16))
-    out = pl.pallas_call(
-        functools.partial(first_kernel, n, n_blocks, n_chunks, shard, last),
-        out_shape=tuple(outs),
-        in_specs=[VMEM] * n_blocks + [VMEM if last else HBM] * n_chunks,
-        out_specs=(VMEM,) * len(outs),
-        scratch_shapes=[pltpu.SemaphoreType.DMA((n_chunks,))],
+    return pl.pallas_call(
+        functools.partial(first_kernel, len(chunks), shard),
+        out_shape=(
+            jax.ShapeDtypeStruct((2, n_rows // shard, shard), jnp.float32),
+            jax.ShapeDtypeStruct((1, n_rows), jnp.float32),
+            jax.ShapeDtypeStruct((n_rows, width), jnp.bfloat16),
+        ),
+        in_specs=[VMEM] * (1 + len(chunks)),
+        out_specs=(VMEM,) * 3,
         compiler_params=params(),
         cost_estimate=pl.CostEstimate(
-            flops=2 * n_k * n_rows * width,
-            bytes_accessed=2 * n_rows * width,
-            transcendentals=n_k * n_rows,
+            flops=2 * n_k * n_rows * width, bytes_accessed=2 * n_rows * width, transcendentals=n_k * n_rows
         ),
         name="first_pass",
-    )(*blocks, *chunks)
-    return out[:3], (out[3] if n_blocks > 1 else blocks[0])
+    )(cents, *chunks)
 
 
 def sums_kernel(first, last, n, cents, *refs):
@@ -298,10 +265,10 @@
         chunk[5] = rows_from(chunk[4], 1)
         chunk[6] = rows_from(chunk[4], 2)
         parts = (rows_from(chunk[3][:half], 4), rows_from(chunk[4][half:], 3))
-        done, piece = first_pass(near + far, [chunk[b] for b in GROUPS[0]])
-        passes = [done, first_pass([piece], [chunk[b] for b in GROUPS[1]])[0]]
+        piece = jnp.concatenate(near + far, axis=0)
+        passes = [first_pass(piece, [chunk[b] for b in bits]) for bits in GROUPS[:2]]
         parts, passes = hold(parts, passes)
-        passes.append(first_pass([piece], [chunk[GROUPS[2][0]], *parts], True)[0])
+        passes.append(first_pass(piece, [chunk[GROUPS[2][0]], *parts]))
         local, row_sqs, rows = zip(*passes)
 
         stats = by_position(by_chunk(local))

time: 95.3 us -> 93.1 us (0.977)
  local copies, waits for them, and re-layouts: 7.01 us -> 0.6 us
  waiting for transfers between devices: 30.4 us -> 34.4 us
  Pallas kernels: 16.3 us -> 13.3 us
  other arithmetic: 3.88 us -> 5.88 us
  starting transfers between devices: 17.3 us -> 18.7 us
    unnamed x21 -> x9, local copies, waits for them, and re-layouts: 5.1 us -> 0.06 us
    ppermute x11, waiting for transfers between devices: 29.7 us -> 34.1 us  [flip(): return lax.ppermute(value, 'dp', [(i, i ^ bits) for i in range(n_dp)])]
    pallas_call x3, Pallas kernels: 6.77 us -> 3.77 us  [first_pass(): pl.pallas_call(functools.partial(first_kernel, len(chunks), shard), out_s...]
    slice x2, local copies, waits for them, and re-layouts: 1.39 us -> 0.03 us  [on_device(): parts = (rows_from(chunk[3][:half], 4), rows_from(chunk[4][half:], 3))]
    convert_element_type x1, other arithmetic: 0.03 us -> 1.07 us  [on_device(): near_own = gather_near(centroids.astype(jnp.bfloat16))]
    concatenate x0 -> x1, other arithmetic: none -> 1.02 us  [on_device(): piece = jnp.concatenate(near + far, axis=0)]
  transfers between devices with their start and end apart: 17 -> 17, of which waited for: 9 -> 9; matrix products, arithmetic and copies ran while one was open for 2% -> 3% of each run, Pallas kernels for 12% -> 9%
where the time goes in v11:
time: 93.1 us; the launch traced here: 92.8 us
  waiting for transfers between devices  34.4 us (37%)
  blocking collectives  18.8 us (20%)
  starting transfers between devices  18.7 us (20%)
  Pallas kernels  13.3 us (14%)
  other arithmetic  5.88 us (6%)
  between operations  1.07 us (1%)
    ppermute x11, waiting for transfers between devices, flip(): return lax.ppermute(value, 'dp', [(i, i ^ bits) for i in range(n_dp)])  34.1 us
    all_to_all x2, blocking collectives, exchange(): return lax.all_to_all(value, 'dp', 0, 0, axis_index_groups=groups)  18.8 us
    ppermute x11, starting transfers between devices, flip(): return lax.ppermute(value, 'dp', [(i, i ^ bits) for i in range(n_dp)])  17.6 us
    pallas_call x2, Pallas kernels, sums_pass(): pl.pallas_call(functools.partial(sums_kernel, first, last, n), out_shape=...  5.56 us
    pallas_call x3, Pallas kernels, second_pass(): pl.pallas_call(functools.partial(second_kernel, shard, n), out_shape=tupl...  4.01 us
    pallas_call x3, Pallas kernels, first_pass(): pl.pallas_call(functools.partial(first_kernel, len(chunks), shard), out_s...  3.77 us
  transfers between devices with their start and end apart: 17, of which 9 were waited for; matrix products, arithmetic and copies ran while one was open for 3% of the time, Pallas kernels for 9%

profile of v11, /device:TPU:0, one launch (start us, length us, event | category | flops | bytes accessed | tf_op | source)
XLA Modules:
  0.0 92.8 jit_solution(7868857702469263785)
XLA Ops:
  0.6 1.2 %convert_element_type.14.refs_0_ = bf16[192,1024]{1,0:T(8,128)(2,1)S(1)} convert(f32[192,1024]{1,0:T(8,128)} %param.2) | non-fusion elementwise | flops 196608 | bytes 1179648 | tf_op jit(solution)/shard_map/convert_element_type | solution.py:255
  1.8 3.0 %collective-permute-start.2 = (bf16[192,1024]{1,0:T(8,128)(2,1)S(1)}, bf16[192,1024]{1,0:T(8,128)(2,1)S(1)}, u32[]{:S(2)}, u32[]{:S(2)}) collective-permute-start(bf16[192,1024]{1,0:T(8,128)(2,1)S(1)} %convert_element_type.14.refs_0_), channel_id=1, source_target_pairs={{0,2},{2,0},{4,6},{6,4},{8,10},{10,8},{12,14},{14,12},{16,18},{18,... | collective-permute-start | bytes 1179656 | tf_op jit(solution)/shard_map/ppermute | solution.py:193
  4.8 1.1 %convert_element_type.13 = bf16[128,1024]{1,0:T(8,128)(2,1)S(1)} convert(f32[128,1024]{1,0:T(8,128)} %refs_9_.1) | non-fusion elementwise | flops 131072 | bytes 786432 | tf_op jit(solution)/shard_map/convert_element_type | solution.py:259
  5.9 1.6 %collective-permute-start.5 = (bf16[128,1024]{1,0:T(8,128)(2,1)S(1)}, bf16[128,1024]{1,0:T(8,128)(2,1)S(1)}, u32[]{:S(2)}, u32[]{:S(2)}) collective-permute-start(bf16[128,1024]{1,0:T(8,128)(2,1)S(1)} %convert_element_type.13), channel_id=1, source_target_pairs={{0,8},{2,10},{4,12},{6,14},{8,0},{10,2},{12,4},{14,6},{16,24},{18,... | collective-permute-start | bytes 786440 | tf_op jit(solution)/shard_map/ppermute | solution.py:193
  7.5 2.6 %collective-permute-start.1 = (bf16[192,1024]{1,0:T(8,128)(2,1)S(1)}, bf16[192,1024]{1,0:T(8,128)(2,1)S(1)}, u32[]{:S(2)}, u32[]{:S(2)}) collective-permute-start(bf16[192,1024]{1,0:T(8,128)(2,1)S(1)} %convert_element_type.14.refs_0_), channel_id=1, source_target_pairs={{0,16},{2,18},{4,20},{6,22},{8,24},{10,26},{12,28},{14,30},{16,0},... | collective-permute-start | bytes 1179656 | tf_op jit(solution)/shard_map/ppermute | solution.py:193
  10.1 1.5 %collective-permute-start.4 = (bf16[192,1024]{1,0:T(8,128)(2,1)S(1)}, bf16[192,1024]{1,0:T(8,128)(2,1)S(1)}, u32[]{:S(2)}, u32[]{:S(2)}) collective-permute-start(bf16[192,1024]{1,0:T(8,128)(2,1)S(1)} %convert_element_type.14.refs_0_), channel_id=1, source_target_pairs={{0,4},{2,6},{4,0},{6,2},{8,12},{10,14},{12,8},{14,10},{16,20},{18,... | collective-permute-start | bytes 1179656 | tf_op jit(solution)/shard_map/ppermute | solution.py:193
  11.7 2.3 %collective-permute-done.2.refs_1_ = bf16[192,1024]{1,0:T(8,128)(2,1)S(1)} collective-permute-done((bf16[192,1024]{1,0:T(8,128)(2,1)S(1)}, bf16[192,1024]{1,0:T(8,128)(2,1)S(1)}, u32[]{:S(2)}, u32[]{:S(2)}) %collective-permute-start.2) | collective-permute-done | bytes 393248 | tf_op jit(solution)/shard_map/ppermute | solution.py:193
  13.9 1.8 %collective-permute-start.3 = (bf16[192,1024]{1,0:T(8,128)(2,1)S(1)}, bf16[192,1024]{1,0:T(8,128)(2,1)S(1)}, u32[]{:S(2)}, u32[]{:S(2)}) collective-permute-start(bf16[192,1024]{1,0:T(8,128)(2,1)S(1)} %collective-permute-done.2.refs_1_), channel_id=1, source_target_pairs={{0,4},{2,6},{4,0},{6,2},{8,12},{10,14},{12,8},{14,10},{16,20},{18,... | collective-permute-start | bytes 1179656 | tf_op jit(solution)/shard_map/ppermute | solution.py:193
  15.7 3.5 %collective-permute-done.5 = bf16[128,1024]{1,0:T(8,128)(2,1)S(1)} collective-permute-done((bf16[128,1024]{1,0:T(8,128)(2,1)S(1)}, bf16[128,1024]{1,0:T(8,128)(2,1)S(1)}, u32[]{:S(2)}, u32[]{:S(2)}) %collective-permute-start.5) | collective-permute-done | bytes 262176 | tf_op jit(solution)/shard_map/ppermute | solution.py:193
  19.2 0.0 collective-permute-start.6
  19.2 0.5 collective-permute-start
  19.7 7.5 %collective-permute-done.1.refs_0_ = bf16[192,1024]{1,0:T(8,128)(2,1)S(1)} collective-permute-done((bf16[192,1024]{1,0:T(8,128)(2,1)S(1)}, bf16[192,1024]{1,0:T(8,128)(2,1)S(1)}, u32[]{:S(2)}, u32[]{:S(2)}) %collective-permute-start.1) | collective-permute-done | bytes 393248 | tf_op jit(solution)/shard_map/ppermute | solution.py:193
  27.2 0.0 collective-permute-done.4.refs_2_
  27.2 0.0 collective-permute-done.6
  27.2 1.4 %collective-permute-done.3.refs_3_ = bf16[192,1024]{1,0:T(8,128)(2,1)S(1)} collective-permute-done((bf16[192,1024]{1,0:T(8,128)(2,1)S(1)}, bf16[192,1024]{1,0:T(8,128)(2,1)S(1)}, u32[]{:S(2)}, u32[]{:S(2)}) %collective-permute-start.3) | collective-permute-done | bytes 393248 | tf_op jit(solution)/shard_map/ppermute | solution.py:193
  28.6 0.5 collective-permute-start.9
  29.1 1.5 %collective-permute-start.10 = (bf16[192,1024]{1,0:T(8,128)(2,1)S(1)}, bf16[192,1024]{1,0:T(8,128)(2,1)S(1)}, u32[]{:S(2)}, u32[]{:S(2)}) collective-permute-start(bf16[192,1024]{1,0:T(8,128)(2,1)S(1)} %collective-permute-done.1.refs_0_), channel_id=1, source_target_pairs={{0,4},{2,6},{4,0},{6,2},{8,12},{10,14},{12,8},{14,10},{16,20},{18,... | collective-permute-start | bytes 1179656 | tf_op jit(solution)/shard_map/ppermute | solution.py:193
  30.6 1.5 %collective-permute-start.8 = (bf16[96,1024]{1,0:T(8,128)(2,1)S(1)}, bf16[96,1024]{1,0:T(8,128)(2,1)S(1)}, u32[]{:S(2)}, u32[]{:S(2)}) collective-permute-start(bf16[96,1024]{1,0:T(8,128)(2,1)S(1)} %slice.326), channel_id=1, source_target_pairs={{0,6},{2,4},{4,2},{6,0},{8,14},{10,12},{12,10},{14,8},{16,22},{18,... | collective-permute-start | bytes 589832 | tf_op jit(solution)/shard_map/ppermute | solution.py:193
  32.2 0.4 collective-permute-start.7
  32.6 0.0 collective-permute-done
  32.6 1.0 %pad_maximum_fusion.cents = bf16[512,1024]{1,0:T(8,128)(2,1)S(1)} fusion(bf16[128,1024]{1,0:T(8,128)(2,1)S(1)} %collective-permute-done.6, bf16[128,1024]{1,0:T(8,128)(2,1)S(1)} %collective-permute-done.5, bf16[128,1024]{1,0:T(8,128)(2,1)} %collective-permute-done, bf16[128,1024]{1,0:T(8,128)(2,1)S(1)} %convert_element_type.13), kind=kLoop, calls=%fused_computation | loop fusion | flops 4194304 | bytes 2097152 | tf_op jit(solution)/shard_map/concatenate | solution.py:268
  33.6 1.8 %first_pass.3 = (f32[2,4,192]{2,1,0:T(4,128)S(1)}, f32[1,768]{1,0:T(1,128)S(1)}, bf16[768,1024]{1,0:T(8,128)(2,1)S(1)}) custom-call(bf16[512,1024]{1,0:T(8,128)(2,1)S(1)} %pad_maximum_fusion.cents, bf16[192,1024]{1,0:T(8,128)(2,1)S(1)} %convert_element_type.14.refs_0_, bf16[192,1024]{1,0:T(8,128)(2,1)S(1)} %collective-permute-done.2.refs_1_, ...), custom_call_target="tpu_custom_call" | custom-call | flops 805306368 | bytes 1572864 | tf_op jit(solution)/shard_map/first_pass/pallas_call | solution.py:69
  35.3 4.4 %collective-permute-done.9.refs_1_ = bf16[192,1024]{1,0:T(8,128)(2,1)S(1)} collective-permute-done((bf16[192,1024]{1,0:T(8,128)(2,1)S(1)}, bf16[192,1024]{1,0:T(8,128)(2,1)S(1)}, u32[]{:S(2)}, u32[]{:S(2)}) %collective-permute-start.9) | collective-permute-done | bytes 393248 | tf_op jit(solution)/shard_map/ppermute | solution.py:193
  39.8 1.0 %first_pass.4 = (f32[2,2,192]{2,1,0:T(2,128)S(1)}, f32[1,384]{1,0:T(1,128)S(1)}, bf16[384,1024]{1,0:T(8,128)(2,1)S(1)}) custom-call(bf16[512,1024]{1,0:T(8,128)(2,1)S(1)} %pad_maximum_fusion.cents, bf16[192,1024]{1,0:T(8,128)(2,1)S(1)} %collective-permute-done.1.refs_0_, bf16[192,1024]{1,0:T(8,128)(2,1)S(1)} %collective-permute-done.9.refs_1_), custom_call_target="tpu_custom_call" | custom-call | flops 402653184 | bytes 786432 | tf_op jit(solution)/shard_map/first_pass/pallas_call | solution.py:69
  40.8 2.1 %collective-permute-done.8.refs_2_ = bf16[96,1024]{1,0:T(8,128)(2,1)S(1)} collective-permute-done((bf16[96,1024]{1,0:T(8,128)(2,1)S(1)}, bf16[96,1024]{1,0:T(8,128)(2,1)S(1)}, u32[]{:S(2)}, u32[]{:S(2)}) %collective-permute-start.8) | collective-permute-done | bytes 196640 | tf_op jit(solution)/shard_map/ppermute | solution.py:193
  42.8 0.0 collective-permute-done.7.refs_1_
  42.8 0.0 collective-permute-done.10.refs_0_
  42.8 1.0 %first_pass.5 = (f32[2,2,192]{2,1,0:T(2,128)S(1)}, f32[1,384]{1,0:T(1,128)S(1)}, bf16[384,1024]{1,0:T(8,128)(2,1)S(1)}) custom-call(bf16[512,1024]{1,0:T(8,128)(2,1)S(1)} %pad_maximum_fusion.cents, bf16[192,1024]{1,0:T(8,128)(2,1)S(1)} %collective-permute-done.10.refs_0_, bf16[96,1024]{1,0:T(8,128)(2,1)S(1)} %collective-permute-done.7.refs_1_, ...), custom_call_target="tpu_custom_call" | custom-call | flops 402653184 | bytes 786432 | tf_op jit(solution)/shard_map/first_pass/pallas_call | solution.py:69
  44.1 9.8 %all_to_all.10 = f32[8,2,8,192]{3,2,1,0:T(8,128)S(1)} all-to-all(f32[8,2,8,192]{3,2,1,0:T(8,128)S(1)} %broadcast_in_dim.6), channel_id=1, replica_groups={{0,2,4,6,16,18,20,22},{8,10,12,14,24,26,28,30},{1,3,5,7,17,19,21,23},{9..., dimensions={0} | all-to-all | bytes 196608 | tf_op jit(solution)/shard_map/all_to_all | solution.py:244
  54.3 0.1 pad_maximum_fusion.9
  54.3 0.1 pad_maximum_fusion.8.refs_0_
  54.4 0.0 copy-start
  54.4 2.8 %sums_pass.3 = f32[256,1152]{1,0:T(8,128)S(1)} custom-call(bf16[512,1024]{1,0:T(8,128)(2,1)S(1)} %pad_maximum_fusion.cents, f32[2,768]{1,0:T(2,128)S(1)} %pad_maximum_fusion.8.refs_0_, f32[2,384]{1,0:T(2,128)S(1)} %get-tuple-element.113.refs_1_, f32[2,384]{1,0:T(2,128)S(1)} %get-tuple-element.114.refs_2_, f32[1,768]{1,0:T(1,128)S(1)} %get-tuple-element.51.refs_3_.refs_0_, ...), custom_call_target="tpu_custom_call" | custom-call | flops 1610612736 | bytes 3145728 | tf_op jit(solution)/shard_map/sums_pass/pallas_call | solution.py:112
  57.2 0.1 collective-permute-start.12
  57.3 0.0 copy-done
  57.3 2.8 %sums_pass.2 = f32[256,1152]{1,0:T(8,128)S(1)} custom-call(bf16[512,1024]{1,0:T(8,128)(2,1)S(1)} %pad_maximum_fusion.cents, f32[2,768]{1,0:T(2,128)S(1)} %pad_maximum_fusion.8.refs_0_, f32[2,384]{1,0:T(2,128)S(1)} %get-tuple-element.113.refs_1_, f32[2,384]{1,0:T(2,128)S(1)} %get-tuple-element.114.refs_2_, f32[1,768]{1,0:T(1,128)S(1)} %get-tuple-element.51.refs_3_.refs_0_, ...), custom_call_target="tpu_custom_call" | custom-call | flops 1610612736 | bytes 3145728 | tf_op jit(solution)/shard_map/sums_pass/pallas_call | solution.py:112
  60.2 0.5 collective-permute-start.11
  60.7 0.0 collective-permute-done.12
  60.7 0.1 slice_add_fusion
  60.9 1.6 %collective-permute-start.13 = (bf16[128,1152]{1,0:T(8,128)(2,1)S(1)}, bf16[128,1152]{1,0:T(8,128)(2,1)S(1)}, u32[]{:S(2)}, u32[]{:S(2)}) collective-permute-start(bf16[128,1152]{1,0:T(8,128)(2,1)S(1)} %pad_maximum_fusion.2), channel_id=1, source_target_pairs={{0,8},{2,10},{4,12},{6,14},{8,0},{10,2},{12,4},{14,6},{16,24},{18,... | collective-permute-start | bytes 884744 | tf_op jit(solution)/shard_map/ppermute | solution.py:193
  62.5 7.4 %collective-permute-done.13 = bf16[128,1152]{1,0:T(8,128)(2,1)S(1)} collective-permute-done((bf16[128,1152]{1,0:T(8,128)(2,1)S(1)}, bf16[128,1152]{1,0:T(8,128)(2,1)S(1)}, u32[]{:S(2)}, u32[]{:S(2)}) %collective-permute-start.13) | collective-permute-done | bytes 294944 | tf_op jit(solution)/shard_map/ppermute | solution.py:193
  70.0 0.2 fusion.2
  70.2 0.0 collective-permute-done.11
  70.2 0.1 broadcast_in_dim.8
  70.3 0.1 fusion
  70.4 0.1 slice_reduce_fusion
  70.5 0.9 %fusion.25 = (bf16[128,1024]{1,0:T(8,128)(2,1)S(1)}, f32[128,1024]{1,0:T(8,128)}) fusion(f32[128]{0:T(128)S(1)} %slice_reduce_fusion, f32[128,1152]{1,0:T(8,128)S(1)} %fusion), kind=kLoop, calls=%fused_computation.110 | loop fusion | flops 262144 | bytes 1311232 | tf_op jit(solution)/shard_map/convert_element_type | solution.py:292
  71.4 0.0 collective-permute-start.15
  71.4 1.5 %collective-permute-start.14 = (bf16[128,1024]{1,0:T(8,128)(2,1)S(1)}, bf16[128,1024]{1,0:T(8,128)(2,1)S(1)}, u32[]{:S(2)}, u32[]{:S(2)}) collective-permute-start(bf16[128,1024]{1,0:T(8,128)(2,1)S(1)} %get-tuple-element.70), channel_id=1, source_target_pairs={{0,8},{2,10},{4,12},{6,14},{8,0},{10,2},{12,4},{14,6},{16,24},{18,... | collective-permute-start | bytes 786440 | tf_op jit(solution)/shard_map/ppermute | solution.py:193
  72.9 0.0 collective-permute-done.15
  73.0 1.6 %second_pass.3 = (f32[3,4,192]{2,1,0:T(4,128)S(1)}, f32[3,2,192]{2,1,0:T(2,128)S(1)}, f32[3,2,192]{2,1,0:T(2,128)S(1)}) custom-call(bf16[256,1024]{1,0:T(8,128)(2,1)S(1)} %pad_maximum_fusion.1.cents, f32[1,768]{1,0:T(1,128)S(1)} %get-tuple-element.51.refs_3_.refs_0_, f32[1,384]{1,0:T(1,128)S(1)} %get-tuple-element.52.refs_4_.refs_1_, ...), custom_call_target="tpu_custom_call" | custom-call | flops 805306368 | bytes 3145728 | tf_op jit(solution)/shard_map/second_pass/pallas_call | solution.py:153
  74.6 5.5 %collective-permute-done.14.cents = bf16[128,1024]{1,0:T(8,128)(2,1)S(1)} collective-permute-done((bf16[128,1024]{1,0:T(8,128)(2,1)S(1)}, bf16[128,1024]{1,0:T(8,128)(2,1)S(1)}, u32[]{:S(2)}, u32[]{:S(2)}) %collective-permute-start.14) | collective-permute-done | bytes 262176 | tf_op jit(solution)/shard_map/ppermute | solution.py:193
  80.2 0.0 collective-permute-start.16
  80.2 1.2 %second_pass.4 = (f32[3,4,192]{2,1,0:T(4,128)S(1)}, f32[3,2,192]{2,1,0:T(2,128)S(1)}, f32[3,2,192]{2,1,0:T(2,128)S(1)}) custom-call(bf16[128,1024]{1,0:T(8,128)(2,1)S(1)} %collective-permute-done.14.cents, f32[1,768]{1,0:T(1,128)S(1)} %get-tuple-element.51.refs_3_.refs_0_, f32[1,384]{1,0:T(1,128)S(1)} %get-tuple-element.52.refs_4_.refs_1_, ...), custom_call_target="tpu_custom_call" | custom-call | flops 402653184 | bytes 3145728 | tf_op jit(solution)/shard_map/second_pass/pallas_call | solution.py:153
  81.4 0.3 collective-permute-done.16.cents
  81.7 1.2 %second_pass.5 = (f32[3,4,192]{2,1,0:T(4,128)S(1)}, f32[3,2,192]{2,1,0:T(2,128)S(1)}, f32[3,2,192]{2,1,0:T(2,128)S(1)}) custom-call(bf16[128,1024]{1,0:T(8,128)(2,1)S(1)} %collective-permute-done.16.cents, f32[1,768]{1,0:T(1,128)S(1)} %get-tuple-element.51.refs_3_.refs_0_, f32[1,384]{1,0:T(1,128)S(1)} %get-tuple-element.52.refs_4_.refs_1_, ...), custom_call_target="tpu_custom_call" | custom-call | flops 402653184 | bytes 3145728 | tf_op jit(solution)/shard_map/second_pass/pallas_call | solution.py:153
  83.0 0.1 stack.78
  83.2 9.0 %all_to_all.11 = f32[8,3,192]{2,1,0:T(4,128)S(1)} all-to-all(f32[8,3,192]{2,1,0:T(4,128)S(1)} %copy.74), channel_id=1, replica_groups={{0,2,4,6,16,18,20,22},{8,10,12,14,24,26,28,30},{1,3,5,7,17,19,21,23},{9..., dimensions={0} | all-to-all | bytes 36864 | tf_op jit(solution)/shard_map/all_to_all | solution.py:244
  92.2 0.6 divide_subtract_fusion
  (61 shorter events, 1.0 us)
Async XLA Ops:
  1.8 12.1 %collective-permute-start.2 = (bf16[192,1024]{1,0:T(8,128)(2,1)S(1)}, bf16[192,1024]{1,0:T(8,128)(2,1)S(1)}, u32[]{:S(2)}, u32[]{:S(2)}) collective-permute-start(bf16[192,1024]{1,0:T(8,128)(2,1)S(1)} %convert_element_type.14.refs_0_), channel_id=1, source_target_pairs={{0,2},{2,0},{4,6},{6,4},{8,10},{10,8},{12,14},{14,12},{16,18},{18,... | collective-permute-start | bytes 1179656 | tf_op jit(solution)/shard_map/ppermute | solution.py:193
  5.9 13.3 %collective-permute-start.5 = (bf16[128,1024]{1,0:T(8,128)(2,1)S(1)}, bf16[128,1024]{1,0:T(8,128)(2,1)S(1)}, u32[]{:S(2)}, u32[]{:S(2)}) collective-permute-start(bf16[128,1024]{1,0:T(8,128)(2,1)S(1)} %convert_element_type.13), channel_id=1, source_target_pairs={{0,8},{2,10},{4,12},{6,14},{8,0},{10,2},{12,4},{14,6},{16,24},{18,... | collective-permute-start | bytes 786440 | tf_op jit(solution)/shard_map/ppermute | solution.py:193
  7.5 19.7 %collective-permute-start.1 = (bf16[192,1024]{1,0:T(8,128)(2,1)S(1)}, bf16[192,1024]{1,0:T(8,128)(2,1)S(1)}, u32[]{:S(2)}, u32[]{:S(2)}) collective-permute-start(bf16[192,1024]{1,0:T(8,128)(2,1)S(1)} %convert_element_type.14.refs_0_), channel_id=1, source_target_pairs={{0,16},{2,18},{4,20},{6,22},{8,24},{10,26},{12,28},{14,30},{16,0},... | collective-permute-start | bytes 1179656 | tf_op jit(solution)/shard_map/ppermute | solution.py:193
  10.1 17.1 %collective-permute-start.4 = (bf16[192,1024]{1,0:T(8,128)(2,1)S(1)}, bf16[192,1024]{1,0:T(8,128)(2,1)S(1)}, u32[]{:S(2)}, u32[]{:S(2)}) collective-permute-start(bf16[192,1024]{1,0:T(8,128)(2,1)S(1)} %convert_element_type.14.refs_0_), channel_id=1, source_target_pairs={{0,4},{2,6},{4,0},{6,2},{8,12},{10,14},{12,8},{14,10},{16,20},{18,... | collective-permute-start | bytes 1179656 | tf_op jit(solution)/shard_map/ppermute | solution.py:193
  13.9 14.6 %collective-permute-start.3 = (bf16[192,1024]{1,0:T(8,128)(2,1)S(1)}, bf16[192,1024]{1,0:T(8,128)(2,1)S(1)}, u32[]{:S(2)}, u32[]{:S(2)}) collective-permute-start(bf16[192,1024]{1,0:T(8,128)(2,1)S(1)} %collective-permute-done.2.refs_1_), channel_id=1, source_target_pairs={{0,4},{2,6},{4,0},{6,2},{8,12},{10,14},{12,8},{14,10},{16,20},{18,... | collective-permute-start | bytes 1179656 | tf_op jit(solution)/shard_map/ppermute | solution.py:193
  19.2 8.0 %collective-permute-start.6 = (bf16[128,1024]{1,0:T(8,128)(2,1)S(1)}, bf16[128,1024]{1,0:T(8,128)(2,1)S(1)}, u32[]{:S(2)}, u32[]{:S(2)}) collective-permute-start(bf16[128,1024]{1,0:T(8,128)(2,1)S(1)} %collective-permute-done.5), channel_id=1, source_target_pairs={{0,1},{1,0},{2,3},{3,2},{4,5},{5,4},{6,7},{7,6},{8,9},{9,8},{10,11... | collective-permute-start | bytes 786440 | tf_op jit(solution)/shard_map/ppermute | solution.py:202
  19.2 13.3 %collective-permute-start = (bf16[128,1024]{1,0:T(8,128)(2,1)S(1)}, bf16[128,1024]{1,0:T(8,128)(2,1)}, u32[]{:S(2)}, u32[]{:S(2)}) collective-permute-start(bf16[128,1024]{1,0:T(8,128)(2,1)S(1)} %convert_element_type.13), channel_id=1, source_target_pairs={{0,1},{1,0},{2,3},{3,2},{4,5},{5,4},{6,7},{7,6},{8,9},{9,8},{10,11... | collective-permute-start | bytes 786440 | tf_op jit(solution)/shard_map/ppermute | solution.py:202
  28.6 11.2 %collective-permute-start.9 = (bf16[192,1024]{1,0:T(8,128)(2,1)S(1)}, bf16[192,1024]{1,0:T(8,128)(2,1)S(1)}, u32[]{:S(2)}, u32[]{:S(2)}) collective-permute-start(bf16[192,1024]{1,0:T(8,128)(2,1)S(1)} %collective-permute-done.1.refs_0_), channel_id=1, source_target_pairs={{0,2},{2,0},{4,6},{6,4},{8,10},{10,8},{12,14},{14,12},{16,18},{18,... | collective-permute-start | bytes 1179656 | tf_op jit(solution)/shard_map/ppermute | solution.py:193
  29.1 13.7 %collective-permute-start.10 = (bf16[192,1024]{1,0:T(8,128)(2,1)S(1)}, bf16[192,1024]{1,0:T(8,128)(2,1)S(1)}, u32[]{:S(2)}, u32[]{:S(2)}) collective-permute-start(bf16[192,1024]{1,0:T(8,128)(2,1)S(1)} %collective-permute-done.1.refs_0_), channel_id=1, source_target_pairs={{0,4},{2,6},{4,0},{6,2},{8,12},{10,14},{12,8},{14,10},{16,20},{18,... | collective-permute-start | bytes 1179656 | tf_op jit(solution)/shard_map/ppermute | solution.py:193
  30.6 12.2 %collective-permute-start.8 = (bf16[96,1024]{1,0:T(8,128)(2,1)S(1)}, bf16[96,1024]{1,0:T(8,128)(2,1)S(1)}, u32[]{:S(2)}, u32[]{:S(2)}) collective-permute-start(bf16[96,1024]{1,0:T(8,128)(2,1)S(1)} %slice.326), channel_id=1, source_target_pairs={{0,6},{2,4},{4,2},{6,0},{8,14},{10,12},{12,10},{14,8},{16,22},{18,... | collective-permute-start | bytes 589832 | tf_op jit(solution)/shard_map/ppermute | solution.py:193
  32.2 10.7 %collective-permute-start.7 = (bf16[96,1024]{1,0:T(8,128)(2,1)S(1)}, bf16[96,1024]{1,0:T(8,128)(2,1)S(1)}, u32[]{:S(2)}, u32[]{:S(2)}) collective-permute-start(bf16[96,1024]{1,0:T(8,128)(2,1)S(1)} %slice.325), channel_id=1, source_target_pairs={{0,16},{2,18},{4,20},{6,22},{8,24},{10,26},{12,28},{14,30},{16,0},... | collective-permute-start | bytes 589832 | tf_op jit(solution)/shard_map/ppermute | solution.py:193
  54.4 2.9 %copy-start = (f32[128,1024]{1,0:T(8,128)S(1)}, f32[128,1024]{1,0:T(8,128)}, u32[]{:S(2)}) copy-start(f32[128,1024]{1,0:T(8,128)} %refs_9_.1) | copy-start | bytes 1572868
  57.2 3.5 %collective-permute-start.12 = (f32[128,1152]{1,0:T(8,128)S(1)}, f32[128,1152]{1,0:T(8,128)S(1)}, u32[]{:S(2)}, u32[]{:S(2)}) collective-permute-start(f32[128,1152]{1,0:T(8,128)S(1)} %slice.451), channel_id=1, source_target_pairs={{0,1},{1,0},{2,3},{3,2},{4,5},{5,4},{6,7},{7,6},{8,9},{9,8},{10,11... | collective-permute-start | bytes 1769480 | tf_op jit(solution)/shard_map/ppermute | solution.py:202
  60.2 10.0 %collective-permute-start.11 = (f32[128,1152]{1,0:T(8,128)S(1)}, f32[128,1152]{1,0:T(8,128)S(1)}, u32[]{:S(2)}, u32[]{:S(2)}) collective-permute-start(f32[128,1152]{1,0:T(8,128)S(1)} %slice.449), channel_id=1, source_target_pairs={{0,1},{1,0},{2,3},{3,2},{4,5},{5,4},{6,7},{7,6},{8,9},{9,8},{10,11... | collective-permute-start | bytes 1769480 | tf_op jit(solution)/shard_map/ppermute | solution.py:202
  60.9 9.0 %collective-permute-start.13 = (bf16[128,1152]{1,0:T(8,128)(2,1)S(1)}, bf16[128,1152]{1,0:T(8,128)(2,1)S(1)}, u32[]{:S(2)}, u32[]{:S(2)}) collective-permute-start(bf16[128,1152]{1,0:T(8,128)(2,1)S(1)} %pad_maximum_fusion.2), channel_id=1, source_target_pairs={{0,8},{2,10},{4,12},{6,14},{8,0},{10,2},{12,4},{14,6},{16,24},{18,... | collective-permute-start | bytes 884744 | tf_op jit(solution)/shard_map/ppermute | solution.py:193
  71.4 1.5 %collective-permute-start.15 = (bf16[128,1024]{1,0:T(8,128)(2,1)S(1)}, bf16[128,1024]{1,0:T(8,128)(2,1)S(1)}, u32[]{:S(2)}, u32[]{:S(2)}) collective-permute-start(bf16[128,1024]{1,0:T(8,128)(2,1)S(1)} %get-tuple-element.70), channel_id=1, source_target_pairs={{0,1},{1,0},{2,3},{3,2},{4,5},{5,4},{6,7},{7,6},{8,9},{9,8},{10,11... | collective-permute-start | bytes 786440 | tf_op jit(solution)/shard_map/ppermute | solution.py:202
  71.4 8.7 %collective-permute-start.14 = (bf16[128,1024]{1,0:T(8,128)(2,1)S(1)}, bf16[128,1024]{1,0:T(8,128)(2,1)S(1)}, u32[]{:S(2)}, u32[]{:S(2)}) collective-permute-start(bf16[128,1024]{1,0:T(8,128)(2,1)S(1)} %get-tuple-element.70), channel_id=1, source_target_pairs={{0,8},{2,10},{4,12},{6,14},{8,0},{10,2},{12,4},{14,6},{16,24},{18,... | collective-permute-start | bytes 786440 | tf_op jit(solution)/shard_map/ppermute | solution.py:193
  80.2 1.5 %collective-permute-start.16 = (bf16[128,1024]{1,0:T(8,128)(2,1)S(1)}, bf16[128,1024]{1,0:T(8,128)(2,1)S(1)}, u32[]{:S(2)}, u32[]{:S(2)}) collective-permute-start(bf16[128,1024]{1,0:T(8,128)(2,1)S(1)} %collective-permute-done.14.cents), channel_id=1, source_target_pairs={{0,1},{1,0},{2,3},{3,2},{4,5},{5,4},{6,7},{7,6},{8,9},{9,8},{10,11... | collective-permute-start | bytes 786440 | tf_op jit(solution)/shard_map/ppermute | solution.py:202

commit v12 on v11

v12 whole, which is shorter than its diff:
```python
import functools

import jax
import jax.numpy as jnp
from jax import lax
from jax.experimental import pallas as pl
from jax.experimental.pallas import tpu as pltpu
from jax.sharding import PartitionSpec as P

softness_level = 32.0
prior_mass = 4.0
CUBE = 8
VMEM = pl.BlockSpec(memory_space=pltpu.VMEM)
GRANT = 12 << 20


def params():
    return pltpu.CompilerParams(vmem_limit_bytes=GRANT)


def row_squares(rows):
    wide = rows.astype(jnp.float32)
    square = wide * wide
    part = square[:, :128]
    for j in range(128, square.shape[1], 128):
        part = part + square[:, j : j + 128]
    return jnp.sum(part.T, axis=0, keepdims=True)


def centroid_squares(piece):
    wide = piece.astype(jnp.float32)
    return jnp.sum(wide * wide, axis=1, keepdims=True)


def scores(piece, cent_sq, rows, row_sq):
    inner = lax.dot_general(piece, rows, (((1,), (1,)), ((), ())), preferred_element_type=jnp.float32)
    scale = 0.5 / softness_level
    return (2.0 * scale) * inner - scale * row_sq - scale * cent_sq


def cast_kernel(source, target):
    target[...] = source[...].astype(target.dtype)


def rounded(value):
    return pl.pallas_call(
        cast_kernel,
        out_shape=jax.ShapeDtypeStruct(value.shape, jnp.bfloat16),
        in_specs=[VMEM],
        out_specs=VMEM,
        compiler_params=params(),
        name="rounded",
    )(value)


def first_kernel(n_chunks, shard, start, cents, *refs):
    chunks = refs[:n_chunks]
    stats_ref, row_sq_ref, rows_ref = refs[-3:]
    at = start
    for chunk in chunks:
        rows_ref[at : at + chunk.shape[0], :] = chunk[...]
        at += chunk.shape[0]
    piece = cents[...]
    cent_sq = centroid_squares(piece)
    tile = 2 * shard
    for j in range((at - start) // tile):
        span = slice(j * tile, (j + 1) * tile)
        rows = rows_ref[start + j * tile : start + (j + 1) * tile, :]
        row_sq = row_squares(rows)
        score = scores(piece, cent_sq, rows, row_sq)
        top = jnp.max(score, axis=0, keepdims=True)
        total = jnp.sum(jnp.exp(score - top), axis=0, keepdims=True)
        row_sq_ref[:, span] = row_sq
        for i in range(2):
            stats_ref[0, 2 * j + i : 2 * j + i + 1, :] = top[:, i * shard : (i + 1) * shard]
            stats_ref[1, 2 * j + i : 2 * j + i + 1, :] = total[:, i * shard : (i + 1) * shard]


def first_pass(cents, chunks, start, held=None):
    shard, width = chunks[0].shape
    n_k = cents.shape[0]
    n_rows = sum(c.shape[0] for c in chunks)
    before = [] if held is None else [held]
    return pl.pallas_call(
        functools.partial(first_kernel, len(chunks), shard, start),
        out_shape=(
            jax.ShapeDtypeStruct((2, n_rows // shard, shard), jnp.float32),
            jax.ShapeDtypeStruct((1, n_rows), jnp.float32),
            jax.ShapeDtypeStruct((CUBE * shard, width), jnp.bfloat16),
        ),
        in_specs=[VMEM] * (1 + len(chunks) + len(before)),
        out_specs=(VMEM,) * 3,
        input_output_aliases={1 + len(chunks): 2} if before else {},
        compiler_params=params(),
        cost_estimate=pl.CostEstimate(
            flops=2 * n_k * n_rows * width, bytes_accessed=2 * n_rows * width, transcendentals=n_k * n_rows
        ),
        name="first_pass",
    )(cents, *chunks, *before)


def sums_kernel(first, last, cents, stats, row_sq, rows, *refs):
    priors, out_ref = refs[:-1], refs[-1]
    width = cents.shape[1]
    piece = cents[first:last, :]
    score = scores(piece, centroid_squares(piece), rows[...], row_sq[...])
    resp = (jnp.exp(score - stats[0:1, :]) * (1.0 / stats[1:2, :])).astype(jnp.bfloat16)
    counts = jnp.sum(resp.astype(jnp.float32), axis=1, keepdims=True)
    out_ref[:, :width] = jnp.dot(resp, rows[...], preferred_element_type=jnp.float32)
    out_ref[:, width:] = jnp.broadcast_to(counts, (last - first, 128))
    for prior in priors:
        held = prior.shape[0]
        out_ref[:held, :width] += prior_mass * prior[...]
        out_ref[:held, width:] += prior_mass


def sums_pass(cents, stats, row_sq, rows, first, last, priors=()):
    n_rows, width = rows.shape
    return pl.pallas_call(
        functools.partial(sums_kernel, first, last),
        out_shape=jax.ShapeDtypeStruct((last - first, width + 128), jnp.float32),
        in_specs=[VMEM] * (4 + len(priors)),
        out_specs=VMEM,
        compiler_params=params(),
        cost_estimate=pl.CostEstimate(
            flops=4 * (last - first) * n_rows * width,
            bytes_accessed=2 * n_rows * width,
            transcendentals=(last - first) * n_rows,
        ),
        name="sums_pass",
    )(cents, stats, row_sq, rows, *priors)


def second_kernel(shard, cents, row_sqs, rows, stats):
    piece = cents[...]
    cent_sq = centroid_squares(piece)
    tile = 2 * shard
    for j in range(rows.shape[0] // tile):
        span = slice(j * tile, (j + 1) * tile)
        score = scores(piece, cent_sq, rows[span, :], row_sqs[:, span])
        top = jnp.max(score, axis=0, keepdims=True)
        shifted = score - top
        weight = jnp.exp(shifted)
        total = jnp.sum(weight, axis=0, keepdims=True)
        spread = jnp.sum(weight * shifted, axis=0, keepdims=True)
        for i in range(2):
            part = slice(i * shard, (i + 1) * shard)
            at = slice(2 * j + i, 2 * j + i + 1)
            stats[0, at, :] = top[:, part]
            stats[1, at, :] = total[:, part]
            stats[2, at, :] = spread[:, part]


def second_pass(cents, row_sq, rows, shard):
    n_k, width = cents.shape
    n_rows = rows.shape[0]
    return pl.pallas_call(
        functools.partial(second_kernel, shard),
        out_shape=jax.ShapeDtypeStruct((3, n_rows // shard, shard), jnp.float32),
        in_specs=[VMEM] * 3,
        out_specs=VMEM,
        compiler_params=params(),
        cost_estimate=pl.CostEstimate(
            flops=2 * n_k * n_rows * width, bytes_accessed=2 * n_rows * width, transcendentals=n_k * n_rows
        ),
        name="second_pass",
    )(cents, row_sq, rows)


def hold(*values):
    return lax.optimization_barrier(values)


def merge(a, b):
    top = jnp.maximum(a[0], b[0])
    drops = (a[0] - top, b[0] - top)
    factors = (jnp.exp(drops[0]), jnp.exp(drops[1]))
    out = [top, factors[0] * a[1] + factors[1] * b[1]]
    if a.shape[0] == 3:
        out.append(factors[0] * (a[2] + drops[0] * a[1]) + factors[1] * (b[2] + drops[1] * b[1]))
    return jnp.stack(out)


def solution(mesh):
    n_dp = mesh.shape["dp"]
    n_cent = mesh.shape["cent"]
    high = n_dp // 2
    top_bit = n_dp // 4

    def flip(value, bits):
        return lax.ppermute(value, "dp", [(i, i ^ bits) for i in range(n_dp)])

    def member(place):
        return (place & 3) | (high if place & 4 else 0)

    def rows_from(value, place):
        return flip(value, member(place))

    def across(value, bits):
        return lax.ppermute(value, "cent", [(i, i ^ bits) for i in range(n_cent)])

    def gather_cent(value):
        blocks = [value]
        bits = 1
        while bits < n_cent:
            blocks = blocks + [across(b, bits) for b in blocks]
            bits *= 2
        return blocks

    def scatter_cent(value):
        bits = n_cent // 2
        while bits:
            half = value.shape[0] // 2
            value = value[:half] + across(value[half:], bits)
            bits //= 2
        return value

    def gather_near(value):
        bits = 4
        while bits < top_bit:
            value = jnp.concatenate([value, flip(value, bits)], axis=0)
            bits *= 2
        return value

    def scatter_near(value):
        bits = top_bit // 2
        while bits >= 4:
            half = value.shape[0] // 2
            value = value[:half] + flip(value[half:], bits)
            bits //= 2
        return value

    def by_position(stats):
        place = lax.axis_index("dp")
        for bit in (1, 2, 4):
            swapped = jnp.stack([stats[:, b ^ bit] for b in range(CUBE)], axis=1)
            stats = jnp.where((place & member(bit)) != 0, swapped, stats)
        return stats

    def exchange(value):
        groups = [[i + member(place) for place in range(CUBE)] for i in range(0, high, 4)]
        return lax.all_to_all(value, "dp", 0, 0, axis_index_groups=groups)

    def everywhere(stats):
        return exchange(jnp.broadcast_to(stats[None], (CUBE,) + stats.shape))

    def to_owner(stats):
        return exchange(stats.transpose(1, 0, 2))

    def on_device(embeddings, centroids):
        shard, width = embeddings.shape
        half = shard // 2
        chunk = {0: embeddings.astype(jnp.bfloat16)}
        for bit in (4, 1, 2):
            chunk[bit] = rows_from(chunk[0], bit)
        chunk[3] = rows_from(chunk[1], 2)
        near_own = gather_near(rounded(centroids))
        far_own = flip(near_own, top_bit)
        near = gather_cent(near_own)
        n_near = len(near) * near_own.shape[0]
        far = gather_cent(far_own)
        chunk[4], chunk[2], far = hold(chunk[4], chunk[2], far)
        chunk[5] = rows_from(chunk[4], 1)
        chunk[6] = rows_from(chunk[4], 2)
        parts = (rows_from(chunk[3][:half], 4), rows_from(chunk[4][half:], 3))
        piece = jnp.concatenate(near + far, axis=0)
        passes = [first_pass(piece, [chunk[b] for b in range(4)], 0)]
        passes.append(first_pass(piece, [chunk[4], chunk[5]], 4 * shard, passes[0][2]))
        parts, passes = hold(parts, passes)
        passes.append(first_pass(piece, [chunk[6], *parts], 6 * shard, passes[1][2]))
        rows = passes[2][2]
        row_sq = jnp.concatenate([p[1] for p in passes], axis=1)

        stats = by_position(jnp.concatenate([p[0] for p in passes], axis=1))
        stats = everywhere(stats)
        top = jnp.max(stats[:, 0], axis=0)
        total = jnp.sum(stats[:, 1] * jnp.exp(stats[:, 0] - top), axis=0)
        stats = by_position(jnp.stack([top, total]))
        final = stats.reshape(2, CUBE * shard)

        far = scatter_cent(sums_pass(piece, final, row_sq, rows, n_near, 2 * n_near))
        count = far[:, width:]
        coarse = lax.reduce_precision(count, 8, 7)
        lane = lax.broadcasted_iota(jnp.int32, count.shape, 1)
        far = jnp.concatenate([far[:, :width], jnp.where(lane < 64, coarse, count - coarse)], axis=1)
        far = flip(far.astype(jnp.bfloat16), top_bit).astype(jnp.float32)
        near = scatter_cent(sums_pass(piece, final, row_sq, rows, 0, n_near, [centroids]))
        counts = far[:, width : width + 1] + far[:, width + 64 : width + 65]
        far = jnp.concatenate([far[:, :width], jnp.broadcast_to(counts, count.shape)], axis=1)
        sums = scatter_near(near + far)
        updated = sums[:, :width] / sums[:, width : width + 1]
        near_own = gather_near(updated.astype(jnp.bfloat16))
        far_own = flip(near_own, top_bit)
        stats = second_pass(jnp.concatenate(gather_cent(near_own), axis=0), row_sq, rows, shard)
        far_own, stats = hold(far_own, stats)
        far = gather_cent(far_own)
        stats = merge(stats, second_pass(far_own, row_sq, rows, shard))
        stats = merge(stats, second_pass(jnp.concatenate(far[1:], axis=0), row_sq, rows, shard))
        stats = to_owner(by_position(stats))
        drop = stats[:, 0] - jnp.max(stats[:, 0], axis=0)
        factor = jnp.exp(drop)
        total = jnp.sum(factor * stats[:, 1], axis=0)
        spread = jnp.sum(factor * (stats[:, 2] + drop * stats[:, 1]), axis=0)
        entropy = jnp.log(total) - spread / total
        return (updated, entropy)

    in_specs = (P(("dp", "cent"), None), P(("dp", "cent"), None))
    out_specs = (P(("dp", "cent"), None), P(("dp", "cent")))
    return jax.shard_map(
        on_device, mesh=mesh, in_specs=in_specs, out_specs=out_specs, check_vma=False
    )
```

time: 93.1 us -> 96.1 us (1.032)
  blocking collectives: 18.8 us -> 8.97 us
  waiting for transfers between devices: 34.4 us -> 41.4 us
  local copies, waits for them, and re-layouts: 0.6 us -> 4.95 us
  starting transfers between devices: 18.7 us -> 22.1 us
  other arithmetic: 5.88 us -> 3.58 us
    all_to_all x2 -> x1, blocking collectives: 18.8 us -> 8.97 us  [exchange(): return lax.all_to_all(value, 'dp', 0, 0, axis_index_groups=groups)]
    all_to_all x0 -> x1, waiting for transfers between devices: none -> 6.38 us  [exchange(): return lax.all_to_all(value, 'dp', 0, 0, axis_index_groups=groups)]
    all_to_all x0 -> x1, starting transfers between devices: none -> 3.55 us  [exchange(): return lax.all_to_all(value, 'dp', 0, 0, axis_index_groups=groups)]
    unnamed x9 -> x15, local copies, waits for them, and re-layouts: 0.06 us -> 3.28 us
    convert_element_type x1 -> x0, other arithmetic: 1.07 us -> none  [on_device(): near_own = gather_near(centroids.astype(jnp.bfloat16))]
    pallas_call x8 -> x9, Pallas kernels: 13.3 us -> 13.6 us  [the longest x3 5.65 us: first_pass(): pl.pallas_call(functools.partial(first_kernel, len(chunks), shard, start)...]
  transfers between devices with their start and end apart: 17 -> 18, of which waited for: 9 -> 11; matrix products, arithmetic and copies ran while one was open for 3% -> 2% of each run, Pallas kernels for 9% -> 9%
where the time goes in v12:
time: 96.1 us; the launch traced here: 95.6 us
  waiting for transfers between devices  41.4 us (43%)
  starting transfers between devices  22.1 us (23%)
  Pallas kernels  13.6 us (14%)
  blocking collectives  8.97 us (9%)
  local copies, waits for them, and re-layouts  4.95 us (5%)
  other arithmetic  3.58 us (4%)
  between operations  1.02 us (1%)
    ppermute x11, waiting for transfers between devices, flip(): return lax.ppermute(value, 'dp', [(i, i ^ bits) for i in range(n_dp)])  34.7 us
    ppermute x11, starting transfers between devices, flip(): return lax.ppermute(value, 'dp', [(i, i ^ bits) for i in range(n_dp)])  17.7 us
    all_to_all x1, blocking collectives, exchange(): return lax.all_to_all(value, 'dp', 0, 0, axis_index_groups=groups)  8.97 us
    all_to_all x1, waiting for transfers between devices, exchange(): return lax.all_to_all(value, 'dp', 0, 0, axis_index_groups=groups)  6.38 us
    pallas_call x3, Pallas kernels, first_pass(): pl.pallas_call(functools.partial(first_kernel, len(chunks), shard, start)...  5.65 us
    pallas_call x2, Pallas kernels, sums_pass(): pl.pallas_call(functools.partial(sums_kernel, first, last), out_shape=jax...  3.98 us
    pallas_call x3, Pallas kernels, second_pass(): pl.pallas_call(functools.partial(second_kernel, shard), out_shape=jax.Sha...  3.94 us
    all_to_all x1, starting transfers between devices, exchange(): return lax.all_to_all(value, 'dp', 0, 0, axis_index_groups=groups)  3.55 us
  transfers between devices with their start and end apart: 18, of which 11 were waited for; matrix products, arithmetic and copies ran while one was open for 2% of the time, Pallas kernels for 9%

profile of v12, /device:TPU:0, one launch (start us, length us, event | category | flops | bytes accessed | tf_op | source)
XLA Modules:
  0.0 95.6 jit_solution(333611014130892977)
XLA Ops:
  0.6 1.2 %convert_element_type.10.refs_0_ = bf16[192,1024]{1,0:T(8,128)(2,1)S(1)} convert(f32[192,1024]{1,0:T(8,128)} %param.2) | non-fusion elementwise | flops 196608 | bytes 1179648 | tf_op jit(solution)/shard_map/convert_element_type | solution.py:253
  1.8 3.0 %collective-permute-start.5 = (bf16[192,1024]{1,0:T(8,128)(2,1)S(1)}, bf16[192,1024]{1,0:T(8,128)(2,1)S(1)}, u32[]{:S(2)}, u32[]{:S(2)}) collective-permute-start(bf16[192,1024]{1,0:T(8,128)(2,1)S(1)} %convert_element_type.10.refs_0_), channel_id=1, source_target_pairs={{0,2},{2,0},{4,6},{6,4},{8,10},{10,8},{12,14},{14,12},{16,18},{18,... | collective-permute-start | bytes 1179656 | tf_op jit(solution)/shard_map/ppermute | solution.py:191
  4.8 1.0 %copy-done.3 = f32[128,1024]{1,0:T(8,128)S(1)} copy-done((f32[128,1024]{1,0:T(8,128)S(1)}, f32[128,1024]{1,0:T(8,128)}, u32[]{:S(2)}) %copy-start.3) | copy-done | bytes 524312
  5.9 1.6 %collective-permute-start.3 = (bf16[128,1024]{1,0:T(8,128)(2,1)S(1)}, bf16[128,1024]{1,0:T(8,128)(2,1)S(1)}, u32[]{:S(2)}, u32[]{:S(2)}) collective-permute-start(bf16[128,1024]{1,0:T(8,128)(2,1)S(1)} %rounded.1), channel_id=1, source_target_pairs={{0,8},{2,10},{4,12},{6,14},{8,0},{10,2},{12,4},{14,6},{16,24},{18,... | collective-permute-start | bytes 786440 | tf_op jit(solution)/shard_map/ppermute | solution.py:191
  7.5 2.6 %collective-permute-start.1 = (bf16[192,1024]{1,0:T(8,128)(2,1)S(1)}, bf16[192,1024]{1,0:T(8,128)(2,1)S(1)}, u32[]{:S(2)}, u32[]{:S(2)}) collective-permute-start(bf16[192,1024]{1,0:T(8,128)(2,1)S(1)} %convert_element_type.10.refs_0_), channel_id=1, source_target_pairs={{0,16},{2,18},{4,20},{6,22},{8,24},{10,26},{12,28},{14,30},{16,0},... | collective-permute-start | bytes 1179656 | tf_op jit(solution)/shard_map/ppermute | solution.py:191
  10.1 1.5 %collective-permute-start.2 = (bf16[192,1024]{1,0:T(8,128)(2,1)S(1)}, bf16[192,1024]{1,0:T(8,128)(2,1)S(1)}, u32[]{:S(2)}, u32[]{:S(2)}) collective-permute-start(bf16[192,1024]{1,0:T(8,128)(2,1)S(1)} %convert_element_type.10.refs_0_), channel_id=1, source_target_pairs={{0,4},{2,6},{4,0},{6,2},{8,12},{10,14},{12,8},{14,10},{16,20},{18,... | collective-permute-start | bytes 1179656 | tf_op jit(solution)/shard_map/ppermute | solution.py:191
  11.6 7.6 %collective-permute-done.3 = bf16[128,1024]{1,0:T(8,128)(2,1)S(1)} collective-permute-done((bf16[128,1024]{1,0:T(8,128)(2,1)S(1)}, bf16[128,1024]{1,0:T(8,128)(2,1)S(1)}, u32[]{:S(2)}, u32[]{:S(2)}) %collective-permute-start.3) | collective-permute-done | bytes 262176 | tf_op jit(solution)/shard_map/ppermute | solution.py:191
  19.2 0.0 collective-permute-start.4
  19.2 0.0 collective-permute-done.5.refs_1_
  19.2 1.5 %collective-permute-start.6 = (bf16[192,1024]{1,0:T(8,128)(2,1)S(1)}, bf16[192,1024]{1,0:T(8,128)(2,1)S(1)}, u32[]{:S(2)}, u32[]{:S(2)}) collective-permute-start(bf16[192,1024]{1,0:T(8,128)(2,1)S(1)} %collective-permute-done.5.refs_1_), channel_id=1, source_target_pairs={{0,4},{2,6},{4,0},{6,2},{8,12},{10,14},{12,8},{14,10},{16,20},{18,... | collective-permute-start | bytes 1179656 | tf_op jit(solution)/shard_map/ppermute | solution.py:191
  20.8 0.2 collective-permute-start
  21.0 6.2 %collective-permute-done.1.refs_0_ = bf16[192,1024]{1,0:T(8,128)(2,1)S(1)} collective-permute-done((bf16[192,1024]{1,0:T(8,128)(2,1)S(1)}, bf16[192,1024]{1,0:T(8,128)(2,1)S(1)}, u32[]{:S(2)}, u32[]{:S(2)}) %collective-permute-start.1) | collective-permute-done | bytes 393248 | tf_op jit(solution)/shard_map/ppermute | solution.py:191
  27.2 0.0 collective-permute-done.2.refs_2_
  27.2 0.0 collective-permute-done.4
  27.2 0.5 collective-permute-start.9
  27.8 1.5 %collective-permute-start.10 = (bf16[192,1024]{1,0:T(8,128)(2,1)S(1)}, bf16[192,1024]{1,0:T(8,128)(2,1)}, u32[]{:S(2)}, u32[]{:S(2)}) collective-permute-start(bf16[192,1024]{1,0:T(8,128)(2,1)S(1)} %collective-permute-done.1.refs_0_), channel_id=1, source_target_pairs={{0,4},{2,6},{4,0},{6,2},{8,12},{10,14},{12,8},{14,10},{16,20},{18,... | collective-permute-start | bytes 1179656 | tf_op jit(solution)/shard_map/ppermute | solution.py:191
  29.3 1.5 %collective-permute-start.8 = (bf16[96,1024]{1,0:T(8,128)(2,1)S(1)}, bf16[96,1024]{1,0:T(8,128)(2,1)S(1)}, u32[]{:S(2)}, u32[]{:S(2)}) collective-permute-start(bf16[96,1024]{1,0:T(8,128)(2,1)S(1)} %slice.266), channel_id=1, source_target_pairs={{0,6},{2,4},{4,2},{6,0},{8,14},{10,12},{12,10},{14,8},{16,22},{18,... | collective-permute-start | bytes 589832 | tf_op jit(solution)/shard_map/ppermute | solution.py:191
  30.8 0.4 collective-permute-done.6.refs_3_
  31.2 0.6 collective-permute-start.7
  31.8 0.0 collective-permute-done
  31.8 0.1 pad_maximum_fusion.cents
  31.9 1.7 %first_pass.3 = (f32[2,4,192]{2,1,0:T(4,128)S(1)}, f32[1,768]{1,0:T(1,128)S(1)}, bf16[1536,1024]{1,0:T(8,128)(2,1)S(1)}) custom-call(bf16[512,1024]{1,0:T(8,128)(2,1)S(1)} %pad_maximum_fusion.cents, bf16[192,1024]{1,0:T(8,128)(2,1)S(1)} %convert_element_type.10.refs_0_, bf16[192,1024]{1,0:T(8,128)(2,1)S(1)} %collective-permute-done.5.refs_1_, ...), custom_call_target="tpu_custom_call" | custom-call | flops 805306368 | bytes 1572864 | tf_op jit(solution)/shard_map/first_pass/pallas_call | solution.py:84
  33.6 0.3 copy.37.refs_2_
  33.9 4.9 %collective-permute-done.9.refs_1_ = bf16[192,1024]{1,0:T(8,128)(2,1)} collective-permute-done((bf16[192,1024]{1,0:T(8,128)(2,1)S(1)}, bf16[192,1024]{1,0:T(8,128)(2,1)}, u32[]{:S(2)}, u32[]{:S(2)}) %collective-permute-start.9) | collective-permute-done | bytes 393248 | tf_op jit(solution)/shard_map/ppermute | solution.py:191
  38.8 2.0 %first_pass.4 = (f32[2,2,192]{2,1,0:T(2,128)S(1)}, f32[1,384]{1,0:T(1,128)S(1)}, bf16[1536,1024]{1,0:T(8,128)(2,1)S(1)}) custom-call(bf16[512,1024]{1,0:T(8,128)(2,1)S(1)} %pad_maximum_fusion.cents, bf16[192,1024]{1,0:T(8,128)(2,1)S(1)} %collective-permute-done.1.refs_0_, ...), custom_call_target="tpu_custom_call", output_to_operand_aliasing={{2}: (3, {})} | custom-call | flops 402653184 | bytes 786432 | tf_op jit(solution)/shard_map/first_pass/pallas_call | solution.py:84
  40.8 1.1 %collective-permute-done.8.refs_2_ = bf16[96,1024]{1,0:T(8,128)(2,1)S(1)} collective-permute-done((bf16[96,1024]{1,0:T(8,128)(2,1)S(1)}, bf16[96,1024]{1,0:T(8,128)(2,1)S(1)}, u32[]{:S(2)}, u32[]{:S(2)}) %collective-permute-start.8) | collective-permute-done | bytes 196640 | tf_op jit(solution)/shard_map/ppermute | solution.py:191
  41.9 0.4 collective-permute-done.7.refs_1_
  42.3 1.2 %collective-permute-done.10.refs_0_ = bf16[192,1024]{1,0:T(8,128)(2,1)} collective-permute-done((bf16[192,1024]{1,0:T(8,128)(2,1)S(1)}, bf16[192,1024]{1,0:T(8,128)(2,1)}, u32[]{:S(2)}, u32[]{:S(2)}) %collective-permute-start.10) | collective-permute-done | bytes 393248 | tf_op jit(solution)/shard_map/ppermute | solution.py:191
  43.5 2.0 %first_pass.5 = (f32[2,2,192]{2,1,0:T(2,128)S(1)}, f32[1,384]{1,0:T(1,128)S(1)}, bf16[1536,1024]{1,0:T(8,128)(2,1)S(1)}) custom-call(bf16[512,1024]{1,0:T(8,128)(2,1)S(1)} %pad_maximum_fusion.cents, bf16[192,1024]{1,0:T(8,128)(2,1)} %collective-permute-done.10.refs_0_, ...), custom_call_target="tpu_custom_call", output_to_operand_aliasing={{2}: (4, {})} | custom-call | flops 402653184 | bytes 786432 | tf_op jit(solution)/shard_map/first_pass/pallas_call | solution.py:84
  45.7 0.7 broadcast_in_dim.6
  46.3 3.6 %all-to-all-start = ((f32[8,2,8,192]{3,2,1,0:T(8,128)}), f32[8,2,8,192]{3,2,1,0:T(8,128)S(1)}, u32[]{:S(2)}, u32[]{:S(2)}) async-start(f32[8,2,8,192]{3,2,1,0:T(8,128)} %broadcast_in_dim.6), calls=%async_computation | async-start | bytes 262144 | tf_op jit(solution)/shard_map/all_to_all | solution.py:242
  49.9 0.7 constant_dynamic-update-slice_fusion.1
  50.6 6.4 %all-to-all-done = f32[8,2,8,192]{3,2,1,0:T(8,128)S(1)} async-done(((f32[8,2,8,192]{3,2,1,0:T(8,128)}), f32[8,2,8,192]{3,2,1,0:T(8,128)S(1)}, u32[]{:S(2)}, u32[]{:S(2)}) %all-to-all-start) | async-done | bytes 98336 | tf_op jit(solution)/shard_map/all_to_all | solution.py:242
  57.1 0.1 stack.71
  57.2 0.1 stack.73
  57.3 0.1 stack.72
  57.4 0.1 stack.69
  57.5 0.1 stack.70
  57.6 1.2 %copy-done.1 = bf16[512,1024]{1,0:T(8,128)(2,1)S(1)} copy-done((bf16[512,1024]{1,0:T(8,128)(2,1)S(1)}, bf16[512,1024]{1,0:T(8,128)(2,1)}, u32[]{:S(2)}) %copy-start.1) | copy-done | bytes 1048600
  58.8 2.0 %sums_pass.3 = f32[256,1152]{1,0:T(8,128)S(1)} custom-call(bf16[512,1024]{1,0:T(8,128)(2,1)S(1)} %copy-done.1, f32[2,1536]{1,0:T(2,128)S(1)} %fusion.9.stats, f32[1,1536]{1,0:T(1,128)S(1)} %constant_dynamic-update-slice_fusion.row_sq.row_sqs, bf16[1536,1024]{1,0:T(8,128)(2,1)S(1)} %get-tuple-element.43.rows), custom_call_target="tpu_custom_call" | custom-call | flops 1610612736 | bytes 3145728 | tf_op jit(solution)/shard_map/sums_pass/pallas_call | solution.py:119
  60.9 0.1 collective-permute-start.12
  61.0 2.0 %sums_pass.2 = f32[256,1152]{1,0:T(8,128)S(1)} custom-call(bf16[512,1024]{1,0:T(8,128)(2,1)S(1)} %copy-done.2, f32[2,1536]{1,0:T(2,128)S(1)} %fusion.9.stats, f32[1,1536]{1,0:T(1,128)S(1)} %constant_dynamic-update-slice_fusion.row_sq.row_sqs, bf16[1536,1024]{1,0:T(8,128)(2,1)S(1)} %get-tuple-element.43.rows, f32[128,1024]{1,0:T(8,128)S(1)} %copy-done.4), custom_call_target="tpu_custom_call" | custom-call | flops 1610612736 | bytes 3145728 | tf_op jit(solution)/shard_map/sums_pass/pallas_call | solution.py:119
  63.0 0.5 collective-permute-start.11
  63.6 0.0 collective-permute-done.12
  63.6 0.1 slice_add_fusion
  63.8 1.7 %collective-permute-start.13 = (bf16[128,1152]{1,0:T(8,128)(2,1)S(1)}, bf16[128,1152]{1,0:T(8,128)(2,1)S(1)}, u32[]{:S(2)}, u32[]{:S(2)}) collective-permute-start(bf16[128,1152]{1,0:T(8,128)(2,1)S(1)} %pad_maximum_fusion.2), channel_id=1, source_target_pairs={{0,8},{2,10},{4,12},{6,14},{8,0},{10,2},{12,4},{14,6},{16,24},{18,... | collective-permute-start | bytes 884744 | tf_op jit(solution)/shard_map/ppermute | solution.py:191
  65.4 7.3 %collective-permute-done.13 = bf16[128,1152]{1,0:T(8,128)(2,1)S(1)} collective-permute-done((bf16[128,1152]{1,0:T(8,128)(2,1)S(1)}, bf16[128,1152]{1,0:T(8,128)(2,1)S(1)}, u32[]{:S(2)}, u32[]{:S(2)}) %collective-permute-start.13) | collective-permute-done | bytes 294944 | tf_op jit(solution)/shard_map/ppermute | solution.py:191
  72.9 0.2 fusion.2
  73.1 0.0 collective-permute-done.11
  73.1 0.1 broadcast_in_dim.8
  73.1 0.1 fusion
  73.3 0.1 slice_reduce_fusion
  73.4 0.9 fusion.27
  74.3 0.0 collective-permute-start.15
  74.3 1.6 %collective-permute-start.14 = (bf16[128,1024]{1,0:T(8,128)(2,1)S(1)}, bf16[128,1024]{1,0:T(8,128)(2,1)S(1)}, u32[]{:S(2)}, u32[]{:S(2)}) collective-permute-start(bf16[128,1024]{1,0:T(8,128)(2,1)S(1)} %get-tuple-element.48), channel_id=1, source_target_pairs={{0,8},{2,10},{4,12},{6,14},{8,0},{10,2},{12,4},{14,6},{16,24},{18,... | collective-permute-start | bytes 786440 | tf_op jit(solution)/shard_map/ppermute | solution.py:191
  76.0 1.5 %second_pass.3 = f32[3,8,192]{2,1,0:T(8,128)S(1)} custom-call(bf16[256,1024]{1,0:T(8,128)(2,1)S(1)} %pad_maximum_fusion.1.cents, f32[1,1536]{1,0:T(1,128)S(1)} %constant_dynamic-update-slice_fusion.row_sq.row_sqs, bf16[1536,1024]{1,0:T(8,128)(2,1)S(1)} %get-tuple-element.43.rows), custom_call_target="tpu_custom_call" | custom-call | flops 805306368 | bytes 3145728 | tf_op jit(solution)/shard_map/second_pass/pallas_call | solution.py:157
  77.5 5.5 %collective-permute-done.14.cents = bf16[128,1024]{1,0:T(8,128)(2,1)S(1)} collective-permute-done((bf16[128,1024]{1,0:T(8,128)(2,1)S(1)}, bf16[128,1024]{1,0:T(8,128)(2,1)S(1)}, u32[]{:S(2)}, u32[]{:S(2)}) %collective-permute-start.14) | collective-permute-done | bytes 262176 | tf_op jit(solution)/shard_map/ppermute | solution.py:191
  83.0 0.0 collective-permute-start.16
  83.1 1.2 %second_pass.4 = f32[3,8,192]{2,1,0:T(8,128)S(1)} custom-call(bf16[128,1024]{1,0:T(8,128)(2,1)S(1)} %collective-permute-done.14.cents, f32[1,1536]{1,0:T(1,128)S(1)} %constant_dynamic-update-slice_fusion.row_sq.row_sqs, bf16[1536,1024]{1,0:T(8,128)(2,1)S(1)} %get-tuple-element.43.rows), custom_call_target="tpu_custom_call" | custom-call | flops 402653184 | bytes 3145728 | tf_op jit(solution)/shard_map/second_pass/pallas_call | solution.py:157
  84.2 0.3 collective-permute-done.16.cents
  84.6 1.2 %second_pass.5 = f32[3,8,192]{2,1,0:T(8,128)S(1)} custom-call(bf16[128,1024]{1,0:T(8,128)(2,1)S(1)} %collective-permute-done.16.cents, f32[1,1536]{1,0:T(1,128)S(1)} %constant_dynamic-update-slice_fusion.row_sq.row_sqs, bf16[1536,1024]{1,0:T(8,128)(2,1)S(1)} %get-tuple-element.43.rows), custom_call_target="tpu_custom_call" | custom-call | flops 402653184 | bytes 3145728 | tf_op jit(solution)/shard_map/second_pass/pallas_call | solution.py:157
  85.9 0.1 stack.76
  86.0 9.0 %all_to_all.10 = f32[8,3,192]{2,1,0:T(4,128)S(1)} all-to-all(f32[8,3,192]{2,1,0:T(4,128)S(1)} %copy.16), channel_id=1, replica_groups={{0,2,4,6,16,18,20,22},{8,10,12,14,24,26,28,30},{1,3,5,7,17,19,21,23},{9..., dimensions={0} | all-to-all | bytes 36864 | tf_op jit(solution)/shard_map/all_to_all | solution.py:242
  95.1 0.6 divide_subtract_fusion
  (54 shorter events, 0.8 us)
Async XLA Ops:
  1.8 17.4 %collective-permute-start.5 = (bf16[192,1024]{1,0:T(8,128)(2,1)S(1)}, bf16[192,1024]{1,0:T(8,128)(2,1)S(1)}, u32[]{:S(2)}, u32[]{:S(2)}) collective-permute-start(bf16[192,1024]{1,0:T(8,128)(2,1)S(1)} %convert_element_type.10.refs_0_), channel_id=1, source_target_pairs={{0,2},{2,0},{4,6},{6,4},{8,10},{10,8},{12,14},{14,12},{16,18},{18,... | collective-permute-start | bytes 1179656 | tf_op jit(solution)/shard_map/ppermute | solution.py:191
  4.8 1.0 %copy-start.3 = (f32[128,1024]{1,0:T(8,128)S(1)}, f32[128,1024]{1,0:T(8,128)}, u32[]{:S(2)}) copy-start(f32[128,1024]{1,0:T(8,128)} %refs_0_.1) | copy-start | bytes 1572868
  5.9 13.3 %collective-permute-start.3 = (bf16[128,1024]{1,0:T(8,128)(2,1)S(1)}, bf16[128,1024]{1,0:T(8,128)(2,1)S(1)}, u32[]{:S(2)}, u32[]{:S(2)}) collective-permute-start(bf16[128,1024]{1,0:T(8,128)(2,1)S(1)} %rounded.1), channel_id=1, source_target_pairs={{0,8},{2,10},{4,12},{6,14},{8,0},{10,2},{12,4},{14,6},{16,24},{18,... | collective-permute-start | bytes 786440 | tf_op jit(solution)/shard_map/ppermute | solution.py:191
  7.5 19.7 %collective-permute-start.1 = (bf16[192,1024]{1,0:T(8,128)(2,1)S(1)}, bf16[192,1024]{1,0:T(8,128)(2,1)S(1)}, u32[]{:S(2)}, u32[]{:S(2)}) collective-permute-start(bf16[192,1024]{1,0:T(8,128)(2,1)S(1)} %convert_element_type.10.refs_0_), channel_id=1, source_target_pairs={{0,16},{2,18},{4,20},{6,22},{8,24},{10,26},{12,28},{14,30},{16,0},... | collective-permute-start | bytes 1179656 | tf_op jit(solution)/shard_map/ppermute | solution.py:191
  10.1 17.1 %collective-permute-start.2 = (bf16[192,1024]{1,0:T(8,128)(2,1)S(1)}, bf16[192,1024]{1,0:T(8,128)(2,1)S(1)}, u32[]{:S(2)}, u32[]{:S(2)}) collective-permute-start(bf16[192,1024]{1,0:T(8,128)(2,1)S(1)} %convert_element_type.10.refs_0_), channel_id=1, source_target_pairs={{0,4},{2,6},{4,0},{6,2},{8,12},{10,14},{12,8},{14,10},{16,20},{18,... | collective-permute-start | bytes 1179656 | tf_op jit(solution)/shard_map/ppermute | solution.py:191
  19.2 8.0 %collective-permute-start.4 = (bf16[128,1024]{1,0:T(8,128)(2,1)S(1)}, bf16[128,1024]{1,0:T(8,128)(2,1)S(1)}, u32[]{:S(2)}, u32[]{:S(2)}) collective-permute-start(bf16[128,1024]{1,0:T(8,128)(2,1)S(1)} %collective-permute-done.3), channel_id=1, source_target_pairs={{0,1},{1,0},{2,3},{3,2},{4,5},{5,4},{6,7},{7,6},{8,9},{9,8},{10,11... | collective-permute-start | bytes 786440 | tf_op jit(solution)/shard_map/ppermute | solution.py:200
  19.2 11.9 %collective-permute-start.6 = (bf16[192,1024]{1,0:T(8,128)(2,1)S(1)}, bf16[192,1024]{1,0:T(8,128)(2,1)S(1)}, u32[]{:S(2)}, u32[]{:S(2)}) collective-permute-start(bf16[192,1024]{1,0:T(8,128)(2,1)S(1)} %collective-permute-done.5.refs_1_), channel_id=1, source_target_pairs={{0,4},{2,6},{4,0},{6,2},{8,12},{10,14},{12,8},{14,10},{16,20},{18,... | collective-permute-start | bytes 1179656 | tf_op jit(solution)/shard_map/ppermute | solution.py:191
  20.8 11.0 %collective-permute-start = (bf16[128,1024]{1,0:T(8,128)(2,1)S(1)}, bf16[128,1024]{1,0:T(8,128)(2,1)S(1)}, u32[]{:S(2)}, u32[]{:S(2)}) collective-permute-start(bf16[128,1024]{1,0:T(8,128)(2,1)S(1)} %rounded.1), channel_id=1, source_target_pairs={{0,1},{1,0},{2,3},{3,2},{4,5},{5,4},{6,7},{7,6},{8,9},{9,8},{10,11... | collective-permute-start | bytes 786440 | tf_op jit(solution)/shard_map/ppermute | solution.py:200
  27.2 11.6 %collective-permute-start.9 = (bf16[192,1024]{1,0:T(8,128)(2,1)S(1)}, bf16[192,1024]{1,0:T(8,128)(2,1)}, u32[]{:S(2)}, u32[]{:S(2)}) collective-permute-start(bf16[192,1024]{1,0:T(8,128)(2,1)S(1)} %collective-permute-done.1.refs_0_), channel_id=1, source_target_pairs={{0,2},{2,0},{4,6},{6,4},{8,10},{10,8},{12,14},{14,12},{16,18},{18,... | collective-permute-start | bytes 1179656 | tf_op jit(solution)/shard_map/ppermute | solution.py:191
  27.8 15.8 %collective-permute-start.10 = (bf16[192,1024]{1,0:T(8,128)(2,1)S(1)}, bf16[192,1024]{1,0:T(8,128)(2,1)}, u32[]{:S(2)}, u32[]{:S(2)}) collective-permute-start(bf16[192,1024]{1,0:T(8,128)(2,1)S(1)} %collective-permute-done.1.refs_0_), channel_id=1, source_target_pairs={{0,4},{2,6},{4,0},{6,2},{8,12},{10,14},{12,8},{14,10},{16,20},{18,... | collective-permute-start | bytes 1179656 | tf_op jit(solution)/shard_map/ppermute | solution.py:191
  29.3 12.6 %collective-permute-start.8 = (bf16[96,1024]{1,0:T(8,128)(2,1)S(1)}, bf16[96,1024]{1,0:T(8,128)(2,1)S(1)}, u32[]{:S(2)}, u32[]{:S(2)}) collective-permute-start(bf16[96,1024]{1,0:T(8,128)(2,1)S(1)} %slice.266), channel_id=1, source_target_pairs={{0,6},{2,4},{4,2},{6,0},{8,14},{10,12},{12,10},{14,8},{16,22},{18,... | collective-permute-start | bytes 589832 | tf_op jit(solution)/shard_map/ppermute | solution.py:191
  31.2 11.2 %collective-permute-start.7 = (bf16[96,1024]{1,0:T(8,128)(2,1)S(1)}, bf16[96,1024]{1,0:T(8,128)(2,1)S(1)}, u32[]{:S(2)}, u32[]{:S(2)}) collective-permute-start(bf16[96,1024]{1,0:T(8,128)(2,1)S(1)} %slice.334), channel_id=1, source_target_pairs={{0,16},{2,18},{4,20},{6,22},{8,24},{10,26},{12,28},{14,30},{16,0},... | collective-permute-start | bytes 589832 | tf_op jit(solution)/shard_map/ppermute | solution.py:191
  31.9 11.6 %copy-start = (bf16[512,1024]{1,0:T(8,128)(2,1)}, bf16[512,1024]{1,0:T(8,128)(2,1)S(1)}, u32[]{:S(2)}) copy-start(bf16[512,1024]{1,0:T(8,128)(2,1)S(1)} %pad_maximum_fusion.cents) | copy-start | bytes 3145732
  40.8 4.7 %copy-start.5 = (f32[1,384]{1,0:T(1,128)}, f32[1,384]{1,0:T(1,128)S(1)}, u32[]{:S(2)}) copy-start(f32[1,384]{1,0:T(1,128)S(1)} %get-tuple-element.41) | copy-start | bytes 4612
  46.3 10.7 %all-to-all-start = ((f32[8,2,8,192]{3,2,1,0:T(8,128)}), f32[8,2,8,192]{3,2,1,0:T(8,128)S(1)}, u32[]{:S(2)}, u32[]{:S(2)}) async-start(f32[8,2,8,192]{3,2,1,0:T(8,128)} %broadcast_in_dim.6), calls=%async_computation | async-start | bytes 262144 | tf_op jit(solution)/shard_map/all_to_all | solution.py:242
  57.6 1.2 %copy-start.1 = (bf16[512,1024]{1,0:T(8,128)(2,1)S(1)}, bf16[512,1024]{1,0:T(8,128)(2,1)}, u32[]{:S(2)}) copy-start(bf16[512,1024]{1,0:T(8,128)(2,1)} %copy-done) | copy-start | bytes 3145732
  58.8 2.1 %copy-start.2 = (bf16[512,1024]{1,0:T(8,128)(2,1)S(1)}, bf16[512,1024]{1,0:T(8,128)(2,1)}, u32[]{:S(2)}) copy-start(bf16[512,1024]{1,0:T(8,128)(2,1)} %copy-done) | copy-start | bytes 3145732
  58.8 2.1 %copy-start.4 = (f32[128,1024]{1,0:T(8,128)S(1)}, f32[128,1024]{1,0:T(8,128)}, u32[]{:S(2)}) copy-start(f32[128,1024]{1,0:T(8,128)} %refs_0_.1) | copy-start | bytes 1572868
  60.9 2.7 %collective-permute-start.12 = (f32[128,1152]{1,0:T(8,128)S(1)}, f32[128,1152]{1,0:T(8,128)S(1)}, u32[]{:S(2)}, u32[]{:S(2)}) collective-permute-start(f32[128,1152]{1,0:T(8,128)S(1)} %slice.368), channel_id=1, source_target_pairs={{0,1},{1,0},{2,3},{3,2},{4,5},{5,4},{6,7},{7,6},{8,9},{9,8},{10,11... | collective-permute-start | bytes 1769480 | tf_op jit(solution)/shard_map/ppermute | solution.py:200
  63.0 10.0 %collective-permute-start.11 = (f32[128,1152]{1,0:T(8,128)S(1)}, f32[128,1152]{1,0:T(8,128)S(1)}, u32[]{:S(2)}, u32[]{:S(2)}) collective-permute-start(f32[128,1152]{1,0:T(8,128)S(1)} %slice.366), channel_id=1, source_target_pairs={{0,1},{1,0},{2,3},{3,2},{4,5},{5,4},{6,7},{7,6},{8,9},{9,8},{10,11... | collective-permute-start | bytes 1769480 | tf_op jit(solution)/shard_map/ppermute | solution.py:200
  63.8 9.0 %collective-permute-start.13 = (bf16[128,1152]{1,0:T(8,128)(2,1)S(1)}, bf16[128,1152]{1,0:T(8,128)(2,1)S(1)}, u32[]{:S(2)}, u32[]{:S(2)}) collective-permute-start(bf16[128,1152]{1,0:T(8,128)(2,1)S(1)} %pad_maximum_fusion.2), channel_id=1, source_target_pairs={{0,8},{2,10},{4,12},{6,14},{8,0},{10,2},{12,4},{14,6},{16,24},{18,... | collective-permute-start | bytes 884744 | tf_op jit(solution)/shard_map/ppermute | solution.py:191
  74.3 1.6 %collective-permute-start.15 = (bf16[128,1024]{1,0:T(8,128)(2,1)S(1)}, bf16[128,1024]{1,0:T(8,128)(2,1)S(1)}, u32[]{:S(2)}, u32[]{:S(2)}) collective-permute-start(bf16[128,1024]{1,0:T(8,128)(2,1)S(1)} %get-tuple-element.48), channel_id=1, source_target_pairs={{0,1},{1,0},{2,3},{3,2},{4,5},{5,4},{6,7},{7,6},{8,9},{9,8},{10,11... | collective-permute-start | bytes 786440 | tf_op jit(solution)/shard_map/ppermute | solution.py:200
  74.3 8.7 %collective-permute-start.14 = (bf16[128,1024]{1,0:T(8,128)(2,1)S(1)}, bf16[128,1024]{1,0:T(8,128)(2,1)S(1)}, u32[]{:S(2)}, u32[]{:S(2)}) collective-permute-start(bf16[128,1024]{1,0:T(8,128)(2,1)S(1)} %get-tuple-element.48), channel_id=1, source_target_pairs={{0,8},{2,10},{4,12},{6,14},{8,0},{10,2},{12,4},{14,6},{16,24},{18,... | collective-permute-start | bytes 786440 | tf_op jit(solution)/shard_map/ppermute | solution.py:191
  83.0 1.5 %collective-permute-start.16 = (bf16[128,1024]{1,0:T(8,128)(2,1)S(1)}, bf16[128,1024]{1,0:T(8,128)(2,1)S(1)}, u32[]{:S(2)}, u32[]{:S(2)}) collective-permute-start(bf16[128,1024]{1,0:T(8,128)(2,1)S(1)} %collective-permute-done.14.cents), channel_id=1, source_target_pairs={{0,1},{1,0},{2,3},{3,2},{4,5},{5,4},{6,7},{7,6},{8,9},{9,8},{10,11... | collective-permute-start | bytes 786440 | tf_op jit(solution)/shard_map/ppermute | solution.py:200

commit v13 on v11

--- a/solution.py
+++ b/solution.py
@@ -15,8 +15,8 @@
 GRANT = 12 << 20
 
 
-def params():
-    return pltpu.CompilerParams(vmem_limit_bytes=GRANT)
+def params(grant=GRANT):
+    return pltpu.CompilerParams(vmem_limit_bytes=grant)
 
 
 def row_squares(rows):
@@ -39,18 +39,46 @@
     return (2.0 * scale) * inner - scale * row_sq - scale * cent_sq
 
 
-def first_kernel(n_chunks, shard, cents, *refs):
+def cast_kernel(n, *refs):
+    sources, targets, held, sems = refs[:n], refs[n : 2 * n], refs[2 * n : 3 * n], refs[3 * n]
+    copies = [pltpu.make_async_copy(sources[i], held[i], sems.at[i]) for i in range(n)]
+    for copy in copies:
+        copy.start()
+    for copy, target, value in zip(copies, targets, held):
+        copy.wait()
+        target[...] = value[...].astype(target.dtype)
+
+
+def rounded(*values):
+    n = len(values)
+    return pl.pallas_call(
+        functools.partial(cast_kernel, n),
+        out_shape=tuple(jax.ShapeDtypeStruct(v.shape, jnp.bfloat16) for v in values),
+        in_specs=[pl.BlockSpec(memory_space=pltpu.HBM)] * n,
+        out_specs=(VMEM,) * n,
+        scratch_shapes=[pltpu.VMEM(v.shape, v.dtype) for v in values] + [pltpu.SemaphoreType.DMA((n,))],
+        compiler_params=params(60 << 20),
+        name="rounded",
+    )(*values)
+
+
+def first_kernel(n_chunks, n_before, shard, cents, *refs):
     chunks = refs[:n_chunks]
-    stats_ref, row_sq_ref, rows_ref = refs[n_chunks:]
-    at = 0
+    stats_ref, row_sq_ref, rows_ref = refs[-3:]
+    start = 0
+    if n_before:
+        start = n_before
+        row_sq_ref[:, :start] = refs[n_chunks][...]
+        rows_ref[:start, :] = refs[n_chunks + 1][...]
+    at = start
     for chunk in chunks:
         rows_ref[at : at + chunk.shape[0], :] = chunk[...]
         at += chunk.shape[0]
     piece = cents[...]
     cent_sq = centroid_squares(piece)
     tile = 2 * shard
-    for j in range(at // tile):
-        span = slice(j * tile, (j + 1) * tile)
+    for j in range((at - start) // tile):
+        span = slice(start + j * tile, start + (j + 1) * tile)
         rows = rows_ref[span, :]
         row_sq = row_squares(rows)
         score = scores(piece, cent_sq, rows, row_sq)
@@ -62,25 +90,26 @@
             stats_ref[1, 2 * j + i : 2 * j + i + 1, :] = total[:, i * shard : (i + 1) * shard]
 
 
-def first_pass(cents, chunks):
+def first_pass(cents, chunks, before=()):
     shard, width = chunks[0].shape
     n_k = cents.shape[0]
     n_rows = sum(c.shape[0] for c in chunks)
+    n_before = before[1].shape[0] if before else 0
     return pl.pallas_call(
-        functools.partial(first_kernel, len(chunks), shard),
+        functools.partial(first_kernel, len(chunks), n_before, shard),
         out_shape=(
             jax.ShapeDtypeStruct((2, n_rows // shard, shard), jnp.float32),
-            jax.ShapeDtypeStruct((1, n_rows), jnp.float32),
-            jax.ShapeDtypeStruct((n_rows, width), jnp.bfloat16),
+            jax.ShapeDtypeStruct((1, n_before + n_rows), jnp.float32),
+            jax.ShapeDtypeStruct((n_before + n_rows, width), jnp.bfloat16),
         ),
-        in_specs=[VMEM] * (1 + len(chunks)),
+        in_specs=[VMEM] * (1 + len(chunks) + len(before)),
         out_specs=(VMEM,) * 3,
         compiler_params=params(),
         cost_estimate=pl.CostEstimate(
             flops=2 * n_k * n_rows * width, bytes_accessed=2 * n_rows * width, transcendentals=n_k * n_rows
         ),
         name="first_pass",
-    )(cents, *chunks)
+    )(cents, *chunks, *before)
 
 
 def sums_kernel(first, last, n, cents, *refs):
@@ -161,7 +190,7 @@
         ),
         name="second_pass",
     )(cents, *row_sqs, *rows)
-    return by_chunk(out)
+    return jnp.concatenate(out, axis=1)
 
 
 def hold(*values):
@@ -178,11 +207,6 @@
     return jnp.stack(out)
 
 
-def by_chunk(groups):
-    place = {b: (g, i) for g, bits in enumerate(GROUPS) for i, b in enumerate(bits)}
-    return jnp.stack([groups[place[b][0]][:, place[b][1]] for b in range(CUBE)], axis=1)
-
-
 def solution(mesh):
     n_dp = mesh.shape["dp"]
     n_cent = mesh.shape["cent"]
@@ -252,11 +276,12 @@
     def on_device(embeddings, centroids):
         shard, width = embeddings.shape
         half = shard // 2
-        chunk = {0: embeddings.astype(jnp.bfloat16)}
+        own, own_cents = rounded(embeddings, centroids)
+        chunk = {0: own}
         for bit in (4, 1, 2):
             chunk[bit] = rows_from(chunk[0], bit)
         chunk[3] = rows_from(chunk[1], 2)
-        near_own = gather_near(centroids.astype(jnp.bfloat16))
+        near_own = gather_near(own_cents)
         far_own = flip(near_own, top_bit)
         near = gather_cent(near_own)
         n_near = len(near) * near_own.shape[0]
@@ -268,15 +293,15 @@
         piece = jnp.concatenate(near + far, axis=0)
         passes = [first_pass(piece, [chunk[b] for b in bits]) for bits in GROUPS[:2]]
         parts, passes = hold(parts, passes)
-        passes.append(first_pass(piece, [chunk[GROUPS[2][0]], *parts]))
-        local, row_sqs, rows = zip(*passes)
-
-        stats = by_position(by_chunk(local))
+        passes.append(first_pass(piece, [chunk[GROUPS[2][0]], *parts], passes[1][1:]))
+        row_sqs, rows = zip(passes[0][1:], passes[2][1:])
+
+        stats = by_position(jnp.concatenate([p[0] for p in passes], axis=1))
         stats = everywhere(stats)
         top = jnp.max(stats[:, 0], axis=0)
         total = jnp.sum(stats[:, 1] * jnp.exp(stats[:, 0] - top), axis=0)
         stats = by_position(jnp.stack([top, total]))
-        final = [jnp.concatenate([stats[:, b] for b in bits], axis=1) for bits in GROUPS]
+        final = [stats[:, i : i + 4].reshape(2, 4 * shard) for i in (0, 4)]
 
         far = scatter_cent(sums_pass(piece, final, row_sqs, rows, n_near, 2 * n_near))
         count = far[:, width:]

time: 93.1 us -> 95.9 us (1.030)
  other arithmetic: 5.88 us -> 2.34 us
  local copies, waits for them, and re-layouts: 0.6 us -> 4.12 us
  waiting for transfers between devices: 34.4 us -> 37.7 us
  starting transfers between devices: 18.7 us -> 15.6 us
  blocking collectives: 18.8 us -> 20.2 us
  Pallas kernels: 13.3 us -> 14.6 us
    unnamed x9 -> x13, local copies, waits for them, and re-layouts: 0.06 us -> 3.31 us
    ppermute x11, starting transfers between devices: 17.6 us -> 14.9 us  [flip(): return lax.ppermute(value, 'dp', [(i, i ^ bits) for i in range(n_dp)])]
    convert_element_type x2 -> x0, other arithmetic: 2.25 us -> none  [the longest x1 1.18 us: on_device(): chunk = {0: embeddings.astype(jnp.bfloat16)}]
    pallas_call x3 -> x4, Pallas kernels: 3.77 us -> 5.94 us  [the longest x3 3.81 us: first_pass(): pl.pallas_call(functools.partial(first_kernel, len(chunks), n_before, sha...]
    ppermute x11, waiting for transfers between devices: 34.1 us -> 36.1 us  [flip(): return lax.ppermute(value, 'dp', [(i, i ^ bits) for i in range(n_dp)])]
    all_to_all x2, blocking collectives: 18.8 us -> 20.2 us  [exchange(): return lax.all_to_all(value, 'dp', 0, 0, axis_index_groups=groups)]
    ppermute x6, waiting for transfers between devices: 0.33 us -> 1.59 us  [across(): return lax.ppermute(value, 'cent', [(i, i ^ bits) for i in range(n_cent)])]
    concatenate x3 -> x1, other arithmetic: 1.17 us -> 0.01 us  [second_pass(): return jnp.concatenate(out, axis=1)]
  transfers between devices with their start and end apart: 17 -> 17, of which waited for: 9 -> 10; matrix products, arithmetic and copies ran while one was open for 3% -> 2% of each run, Pallas kernels for 9% -> 8%
where the time goes in v13:
time: 95.9 us; the launch traced here: 95.6 us
  waiting for transfers between devices  37.7 us (39%)
  blocking collectives  20.2 us (21%)
  starting transfers between devices  15.6 us (16%)
  Pallas kernels  14.6 us (15%)
  local copies, waits for them, and re-layouts  4.12 us (4%)
  other arithmetic  2.34 us (2%)
  between operations  1.05 us (1%)
    ppermute x11, waiting for transfers between devices, flip(): return lax.ppermute(value, 'dp', [(i, i ^ bits) for i in range(n_dp)])  36.1 us
    all_to_all x2, blocking collectives, exchange(): return lax.all_to_all(value, 'dp', 0, 0, axis_index_groups=groups)  20.2 us
    ppermute x11, starting transfers between devices, flip(): return lax.ppermute(value, 'dp', [(i, i ^ bits) for i in range(n_dp)])  14.9 us
    pallas_call x2, Pallas kernels, sums_pass(): pl.pallas_call(functools.partial(sums_kernel, first, last, n), out_shape=...  4.73 us
    pallas_call x3, Pallas kernels, second_pass(): pl.pallas_call(functools.partial(second_kernel, shard, n), out_shape=tupl...  3.94 us
    pallas_call x3, Pallas kernels, first_pass(): pl.pallas_call(functools.partial(first_kernel, len(chunks), n_before, sha...  3.81 us
    unnamed x13, local copies, waits for them, and re-layouts  3.31 us
    pallas_call x1, Pallas kernels, rounded(): pl.pallas_call(functools.partial(cast_kernel, n), out_shape=tuple((jax.Sh...  2.12 us
  transfers between devices with their start and end apart: 17, of which 10 were waited for; matrix products, arithmetic and copies ran while one was open for 2% of the time, Pallas kernels for 8%

profile of v13, /device:TPU:0, one launch (start us, length us, event | category | flops | bytes accessed | tf_op | source)
XLA Modules:
  0.0 95.6 jit_solution(8569613146838598469)
XLA Ops:
  0.6 2.1 %rounded.1 = (bf16[192,1024]{1,0:T(8,128)(2,1)}, bf16[128,1024]{1,0:T(8,128)(2,1)}) custom-call(f32[192,1024]{1,0:T(8,128)} %refs_0_.1, f32[128,1024]{1,0:T(8,128)} %refs_6_.1), custom_call_target="tpu_custom_call" | custom-call | tf_op jit(solution)/shard_map/rounded/pallas_call | solution.py:54
  2.8 3.0 %collective-permute-start.2 = (bf16[192,1024]{1,0:T(8,128)(2,1)}, bf16[192,1024]{1,0:T(8,128)(2,1)S(1)}, u32[]{:S(2)}, u32[]{:S(2)}) collective-permute-start(bf16[192,1024]{1,0:T(8,128)(2,1)} %get-tuple-element.35.refs_0_), channel_id=1, source_target_pairs={{0,2},{2,0},{4,6},{6,4},{8,10},{10,8},{12,14},{14,12},{16,18},{18,... | collective-permute-start | bytes 1179656 | tf_op jit(solution)/shard_map/ppermute | solution.py:217
  5.8 1.6 %collective-permute-start.5 = (bf16[128,1024]{1,0:T(8,128)(2,1)}, bf16[128,1024]{1,0:T(8,128)(2,1)S(1)}, u32[]{:S(2)}, u32[]{:S(2)}) collective-permute-start(bf16[128,1024]{1,0:T(8,128)(2,1)} %get-tuple-element.34), channel_id=1, source_target_pairs={{0,8},{2,10},{4,12},{6,14},{8,0},{10,2},{12,4},{14,6},{16,24},{18,... | collective-permute-start | bytes 786440 | tf_op jit(solution)/shard_map/ppermute | solution.py:217
  7.3 2.6 %collective-permute-start.1 = (bf16[192,1024]{1,0:T(8,128)(2,1)}, bf16[192,1024]{1,0:T(8,128)(2,1)S(1)}, u32[]{:S(2)}, u32[]{:S(2)}) collective-permute-start(bf16[192,1024]{1,0:T(8,128)(2,1)} %get-tuple-element.35.refs_0_), channel_id=1, source_target_pairs={{0,16},{2,18},{4,20},{6,22},{8,24},{10,26},{12,28},{14,30},{16,0},... | collective-permute-start | bytes 1179656 | tf_op jit(solution)/shard_map/ppermute | solution.py:217
  9.9 1.5 %collective-permute-start.4 = (bf16[192,1024]{1,0:T(8,128)(2,1)}, bf16[192,1024]{1,0:T(8,128)(2,1)S(1)}, u32[]{:S(2)}, u32[]{:S(2)}) collective-permute-start(bf16[192,1024]{1,0:T(8,128)(2,1)} %get-tuple-element.35.refs_0_), channel_id=1, source_target_pairs={{0,4},{2,6},{4,0},{6,2},{8,12},{10,14},{12,8},{14,10},{16,20},{18,... | collective-permute-start | bytes 1179656 | tf_op jit(solution)/shard_map/ppermute | solution.py:217
  11.4 3.6 %collective-permute-done.2.refs_1_ = bf16[192,1024]{1,0:T(8,128)(2,1)S(1)} collective-permute-done((bf16[192,1024]{1,0:T(8,128)(2,1)}, bf16[192,1024]{1,0:T(8,128)(2,1)S(1)}, u32[]{:S(2)}, u32[]{:S(2)}) %collective-permute-start.2) | collective-permute-done | bytes 393248 | tf_op jit(solution)/shard_map/ppermute | solution.py:217
  15.1 1.8 %collective-permute-start.3 = (bf16[192,1024]{1,0:T(8,128)(2,1)S(1)}, bf16[192,1024]{1,0:T(8,128)(2,1)S(1)}, u32[]{:S(2)}, u32[]{:S(2)}) collective-permute-start(bf16[192,1024]{1,0:T(8,128)(2,1)S(1)} %collective-permute-done.2.refs_1_), channel_id=1, source_target_pairs={{0,4},{2,6},{4,0},{6,2},{8,12},{10,14},{12,8},{14,10},{16,20},{18,... | collective-permute-start | bytes 1179656 | tf_op jit(solution)/shard_map/ppermute | solution.py:217
  16.9 2.4 %collective-permute-done.5 = bf16[128,1024]{1,0:T(8,128)(2,1)S(1)} collective-permute-done((bf16[128,1024]{1,0:T(8,128)(2,1)}, bf16[128,1024]{1,0:T(8,128)(2,1)S(1)}, u32[]{:S(2)}, u32[]{:S(2)}) %collective-permute-start.5) | collective-permute-done | bytes 262176 | tf_op jit(solution)/shard_map/ppermute | solution.py:217
  19.2 0.0 collective-permute-start.6
  19.2 0.5 collective-permute-start
  19.8 1.0 %constant_dynamic-update-slice_fusion.3 = bf16[512,1024]{1,0:T(8,128)(2,1)S(1)} fusion(bf16[128,1024]{1,0:T(8,128)(2,1)} %get-tuple-element.34), kind=kLoop, calls=%fused_computation.58 | loop fusion | bytes 524288
  20.7 0.0 copy-start.4
  20.7 6.5 %collective-permute-done.1.refs_0_ = bf16[192,1024]{1,0:T(8,128)(2,1)S(1)} collective-permute-done((bf16[192,1024]{1,0:T(8,128)(2,1)}, bf16[192,1024]{1,0:T(8,128)(2,1)S(1)}, u32[]{:S(2)}, u32[]{:S(2)}) %collective-permute-start.1) | collective-permute-done | bytes 393248 | tf_op jit(solution)/shard_map/ppermute | solution.py:217
  27.2 0.0 collective-permute-done.4.refs_2_
  27.2 0.0 collective-permute-done.6
  27.2 1.4 %collective-permute-done.3.refs_3_ = bf16[192,1024]{1,0:T(8,128)(2,1)S(1)} collective-permute-done((bf16[192,1024]{1,0:T(8,128)(2,1)S(1)}, bf16[192,1024]{1,0:T(8,128)(2,1)S(1)}, u32[]{:S(2)}, u32[]{:S(2)}) %collective-permute-start.3) | collective-permute-done | bytes 393248 | tf_op jit(solution)/shard_map/ppermute | solution.py:217
  28.6 0.5 collective-permute-start.9
  29.1 1.5 %collective-permute-start.10 = (bf16[192,1024]{1,0:T(8,128)(2,1)S(1)}, bf16[192,1024]{1,0:T(8,128)(2,1)S(1)}, u32[]{:S(2)}, u32[]{:S(2)}) collective-permute-start(bf16[192,1024]{1,0:T(8,128)(2,1)S(1)} %collective-permute-done.1.refs_0_), channel_id=1, source_target_pairs={{0,4},{2,6},{4,0},{6,2},{8,12},{10,14},{12,8},{14,10},{16,20},{18,... | collective-permute-start | bytes 1179656 | tf_op jit(solution)/shard_map/ppermute | solution.py:217
  30.6 0.0 collective-permute-done
  30.7 1.5 %collective-permute-start.8 = (bf16[96,1024]{1,0:T(8,128)(2,1)S(1)}, bf16[96,1024]{1,0:T(8,128)(2,1)S(1)}, u32[]{:S(2)}, u32[]{:S(2)}) collective-permute-start(bf16[96,1024]{1,0:T(8,128)(2,1)S(1)} %slice.272), channel_id=1, source_target_pairs={{0,6},{2,4},{4,2},{6,0},{8,14},{10,12},{12,10},{14,8},{16,22},{18,... | collective-permute-start | bytes 589832 | tf_op jit(solution)/shard_map/ppermute | solution.py:217
  32.2 0.4 collective-permute-start.7
  32.7 0.0 copy-done.4
  32.7 0.0 copy-start
  32.7 1.8 %first_pass.3 = (f32[2,4,192]{2,1,0:T(4,128)S(1)}, f32[1,768]{1,0:T(1,128)S(1)}, bf16[768,1024]{1,0:T(8,128)(2,1)S(1)}) custom-call(bf16[512,1024]{1,0:T(8,128)(2,1)S(1)} %constant_dynamic-update-slice_fusion.cents, bf16[192,1024]{1,0:T(8,128)(2,1)S(1)} %copy-done.4, bf16[192,1024]{1,0:T(8,128)(2,1)S(1)} %collective-permute-done.2.refs_1_, ...), custom_call_target="tpu_custom_call" | custom-call | flops 805306368 | bytes 1572864 | tf_op jit(solution)/shard_map/first_pass/pallas_call | solution.py:98
  34.4 5.4 %collective-permute-done.9.refs_1_ = bf16[192,1024]{1,0:T(8,128)(2,1)S(1)} collective-permute-done((bf16[192,1024]{1,0:T(8,128)(2,1)S(1)}, bf16[192,1024]{1,0:T(8,128)(2,1)S(1)}, u32[]{:S(2)}, u32[]{:S(2)}) %collective-permute-start.9) | collective-permute-done | bytes 393248 | tf_op jit(solution)/shard_map/ppermute | solution.py:217
  39.8 1.0 %first_pass.4 = (f32[2,2,192]{2,1,0:T(2,128)S(1)}, f32[1,384]{1,0:T(1,128)S(1)}, bf16[384,1024]{1,0:T(8,128)(2,1)S(1)}) custom-call(bf16[512,1024]{1,0:T(8,128)(2,1)S(1)} %constant_dynamic-update-slice_fusion.cents, bf16[192,1024]{1,0:T(8,128)(2,1)S(1)} %collective-permute-done.1.refs_0_, bf16[192,1024]{1,0:T(8,128)(2,1)S(1)} %collective-permute-done.9.refs_1_), custom_call_target="tpu_custom_call" | custom-call | flops 402653184 | bytes 786432 | tf_op jit(solution)/shard_map/first_pass/pallas_call | solution.py:98
  40.8 2.1 %collective-permute-done.8.refs_2_ = bf16[96,1024]{1,0:T(8,128)(2,1)S(1)} collective-permute-done((bf16[96,1024]{1,0:T(8,128)(2,1)S(1)}, bf16[96,1024]{1,0:T(8,128)(2,1)S(1)}, u32[]{:S(2)}, u32[]{:S(2)}) %collective-permute-start.8) | collective-permute-done | bytes 196640 | tf_op jit(solution)/shard_map/ppermute | solution.py:217
  42.8 0.0 collective-permute-done.7.refs_1_
  42.8 0.0 collective-permute-done.10.refs_0_
  42.8 0.0 copy-done
  42.9 1.1 %first_pass.5 = (f32[2,2,192]{2,1,0:T(2,128)S(1)}, f32[1,768]{1,0:T(1,128)S(1)}, bf16[768,1024]{1,0:T(8,128)(2,1)S(1)}) custom-call(bf16[512,1024]{1,0:T(8,128)(2,1)S(1)} %constant_dynamic-update-slice_fusion.cents, bf16[192,1024]{1,0:T(8,128)(2,1)S(1)} %collective-permute-done.10.refs_0_, bf16[96,1024]{1,0:T(8,128)(2,1)S(1)} %collective-permute-done.7.refs_1_, ...), custom_call_target="tpu_custom_call" | custom-call | flops 402653184 | bytes 786432 | tf_op jit(solution)/shard_map/first_pass/pallas_call | solution.py:98
  44.1 11.3 %all_to_all.10 = f32[8,2,8,192]{3,2,1,0:T(8,128)S(1)} all-to-all(f32[8,2,8,192]{3,2,1,0:T(8,128)S(1)} %broadcast_in_dim.6), channel_id=1, replica_groups={{0,2,4,6,16,18,20,22},{8,10,12,14,24,26,28,30},{1,3,5,7,17,19,21,23},{9..., dimensions={0} | all-to-all | bytes 196608 | tf_op jit(solution)/shard_map/all_to_all | solution.py:268
  55.6 0.1 reshape.134.refs_0_
  55.7 0.1 reshape.135.refs_1_
  55.7 1.2 %copy-done.1 = bf16[512,1024]{1,0:T(8,128)(2,1)S(1)} copy-done((bf16[512,1024]{1,0:T(8,128)(2,1)S(1)}, bf16[512,1024]{1,0:T(8,128)(2,1)}, u32[]{:S(2)}) %copy-start.1) | copy-done | bytes 1048600
  57.0 2.4 %sums_pass.3 = f32[256,1152]{1,0:T(8,128)S(1)} custom-call(bf16[512,1024]{1,0:T(8,128)(2,1)S(1)} %copy-done.1, f32[2,768]{1,0:T(2,128)S(1)} %reshape.134.refs_0_, f32[2,768]{1,0:T(2,128)S(1)} %reshape.135.refs_1_, f32[1,768]{1,0:T(1,128)S(1)} %get-tuple-element.54.refs_2_.refs_0_, f32[1,768]{1,0:T(1,128)S(1)} %get-tuple-element.55.refs_3_.refs_1_, ...), custom_call_target="tpu_custom_call" | custom-call | flops 1610612736 | bytes 3145728 | tf_op jit(solution)/shard_map/sums_pass/pallas_call | solution.py:141
  59.3 0.0 copy-start.2
  59.4 0.1 collective-permute-start.12
  59.5 0.0 copy-done.3
  59.5 1.1 %copy-done.2 = bf16[512,1024]{1,0:T(8,128)(2,1)S(1)} copy-done((bf16[512,1024]{1,0:T(8,128)(2,1)S(1)}, bf16[512,1024]{1,0:T(8,128)(2,1)}, u32[]{:S(2)}) %copy-start.2) | copy-done | bytes 1048600
  60.6 2.4 %sums_pass.2 = f32[256,1152]{1,0:T(8,128)S(1)} custom-call(bf16[512,1024]{1,0:T(8,128)(2,1)S(1)} %copy-done.2, f32[2,768]{1,0:T(2,128)S(1)} %reshape.134.refs_0_, f32[2,768]{1,0:T(2,128)S(1)} %reshape.135.refs_1_, f32[1,768]{1,0:T(1,128)S(1)} %get-tuple-element.54.refs_2_.refs_0_, f32[1,768]{1,0:T(1,128)S(1)} %get-tuple-element.55.refs_3_.refs_1_, ...), custom_call_target="tpu_custom_call" | custom-call | flops 1610612736 | bytes 3145728 | tf_op jit(solution)/shard_map/sums_pass/pallas_call | solution.py:141
  63.0 0.1 collective-permute-start.11
  63.1 0.0 collective-permute-done.12
  63.1 0.1 slice_add_fusion
  63.2 0.2 collective-permute-start.13
  63.5 9.2 %collective-permute-done.13 = bf16[128,1152]{1,0:T(8,128)(2,1)S(1)} collective-permute-done((bf16[128,1152]{1,0:T(8,128)(2,1)S(1)}, bf16[128,1152]{1,0:T(8,128)(2,1)S(1)}, u32[]{:S(2)}, u32[]{:S(2)}) %collective-permute-start.13) | collective-permute-done | bytes 294944 | tf_op jit(solution)/shard_map/ppermute | solution.py:217
  72.8 0.2 fusion.2
  73.0 0.0 collective-permute-done.11
  73.0 0.1 broadcast_in_dim.8
  73.1 0.1 fusion
  73.2 0.1 slice_reduce_fusion
  73.3 0.9 fusion.32
  74.2 0.0 collective-permute-start.15
  74.3 0.3 collective-permute-start.14
  74.5 1.2 %collective-permute-done.15 = bf16[128,1024]{1,0:T(8,128)(2,1)S(1)} collective-permute-done((bf16[128,1024]{1,0:T(8,128)(2,1)S(1)}, bf16[128,1024]{1,0:T(8,128)(2,1)S(1)}, u32[]{:S(2)}, u32[]{:S(2)}) %collective-permute-start.15) | collective-permute-done | bytes 262176 | tf_op jit(solution)/shard_map/ppermute | solution.py:226
  75.8 1.5 %second_pass.3 = (f32[3,4,192]{2,1,0:T(4,128)S(1)}, f32[3,4,192]{2,1,0:T(4,128)S(1)}) custom-call(bf16[256,1024]{1,0:T(8,128)(2,1)S(1)} %pad_maximum_fusion.cents, f32[1,768]{1,0:T(1,128)S(1)} %get-tuple-element.54.refs_2_.refs_0_, f32[1,768]{1,0:T(1,128)S(1)} %get-tuple-element.55.refs_3_.refs_1_, bf16[768,1024]{1,0:T(8,128)(2,1)S(1)} %get-tuple-element.56.refs_4_.refs_2_, ...), custom_call_target="tpu_custom_call" | custom-call | flops 805306368 | bytes 3145728 | tf_op jit(solution)/shard_map/second_pass/pallas_call | solution.py:182
  77.4 5.6 %collective-permute-done.14.cents = bf16[128,1024]{1,0:T(8,128)(2,1)S(1)} collective-permute-done((bf16[128,1024]{1,0:T(8,128)(2,1)S(1)}, bf16[128,1024]{1,0:T(8,128)(2,1)S(1)}, u32[]{:S(2)}, u32[]{:S(2)}) %collective-permute-start.14) | collective-permute-done | bytes 262176 | tf_op jit(solution)/shard_map/ppermute | solution.py:217
  83.0 0.0 collective-permute-start.16
  83.0 1.2 %second_pass.4 = (f32[3,4,192]{2,1,0:T(4,128)S(1)}, f32[3,4,192]{2,1,0:T(4,128)S(1)}) custom-call(bf16[128,1024]{1,0:T(8,128)(2,1)S(1)} %collective-permute-done.14.cents, f32[1,768]{1,0:T(1,128)S(1)} %get-tuple-element.54.refs_2_.refs_0_, f32[1,768]{1,0:T(1,128)S(1)} %get-tuple-element.55.refs_3_.refs_1_, ...), custom_call_target="tpu_custom_call" | custom-call | flops 402653184 | bytes 3145728 | tf_op jit(solution)/shard_map/second_pass/pallas_call | solution.py:182
  84.2 0.3 collective-permute-done.16.cents
  84.5 1.2 %second_pass.5 = (f32[3,4,192]{2,1,0:T(4,128)S(1)}, f32[3,4,192]{2,1,0:T(4,128)S(1)}) custom-call(bf16[128,1024]{1,0:T(8,128)(2,1)S(1)} %collective-permute-done.16.cents, f32[1,768]{1,0:T(1,128)S(1)} %get-tuple-element.54.refs_2_.refs_0_, f32[1,768]{1,0:T(1,128)S(1)} %get-tuple-element.55.refs_3_.refs_1_, ...), custom_call_target="tpu_custom_call" | custom-call | flops 402653184 | bytes 3145728 | tf_op jit(solution)/shard_map/second_pass/pallas_call | solution.py:182
  85.8 0.1 stack.58
  86.0 9.0 %all_to_all.11 = f32[8,3,192]{2,1,0:T(4,128)S(1)} all-to-all(f32[8,3,192]{2,1,0:T(4,128)S(1)} %copy.14), channel_id=1, replica_groups={{0,2,4,6,16,18,20,22},{8,10,12,14,24,26,28,30},{1,3,5,7,17,19,21,23},{9..., dimensions={0} | all-to-all | bytes 36864 | tf_op jit(solution)/shard_map/all_to_all | solution.py:268
  95.0 0.6 divide_subtract_fusion
  (48 shorter events, 0.9 us)
Async XLA Ops:
  2.8 12.3 %collective-permute-start.2 = (bf16[192,1024]{1,0:T(8,128)(2,1)}, bf16[192,1024]{1,0:T(8,128)(2,1)S(1)}, u32[]{:S(2)}, u32[]{:S(2)}) collective-permute-start(bf16[192,1024]{1,0:T(8,128)(2,1)} %get-tuple-element.35.refs_0_), channel_id=1, source_target_pairs={{0,2},{2,0},{4,6},{6,4},{8,10},{10,8},{12,14},{14,12},{16,18},{18,... | collective-permute-start | bytes 1179656 | tf_op jit(solution)/shard_map/ppermute | solution.py:217
  5.8 13.5 %collective-permute-start.5 = (bf16[128,1024]{1,0:T(8,128)(2,1)}, bf16[128,1024]{1,0:T(8,128)(2,1)S(1)}, u32[]{:S(2)}, u32[]{:S(2)}) collective-permute-start(bf16[128,1024]{1,0:T(8,128)(2,1)} %get-tuple-element.34), channel_id=1, source_target_pairs={{0,8},{2,10},{4,12},{6,14},{8,0},{10,2},{12,4},{14,6},{16,24},{18,... | collective-permute-start | bytes 786440 | tf_op jit(solution)/shard_map/ppermute | solution.py:217
  7.3 19.9 %collective-permute-start.1 = (bf16[192,1024]{1,0:T(8,128)(2,1)}, bf16[192,1024]{1,0:T(8,128)(2,1)S(1)}, u32[]{:S(2)}, u32[]{:S(2)}) collective-permute-start(bf16[192,1024]{1,0:T(8,128)(2,1)} %get-tuple-element.35.refs_0_), channel_id=1, source_target_pairs={{0,16},{2,18},{4,20},{6,22},{8,24},{10,26},{12,28},{14,30},{16,0},... | collective-permute-start | bytes 1179656 | tf_op jit(solution)/shard_map/ppermute | solution.py:217
  9.9 17.3 %collective-permute-start.4 = (bf16[192,1024]{1,0:T(8,128)(2,1)}, bf16[192,1024]{1,0:T(8,128)(2,1)S(1)}, u32[]{:S(2)}, u32[]{:S(2)}) collective-permute-start(bf16[192,1024]{1,0:T(8,128)(2,1)} %get-tuple-element.35.refs_0_), channel_id=1, source_target_pairs={{0,4},{2,6},{4,0},{6,2},{8,12},{10,14},{12,8},{14,10},{16,20},{18,... | collective-permute-start | bytes 1179656 | tf_op jit(solution)/shard_map/ppermute | solution.py:217
  15.1 13.5 %collective-permute-start.3 = (bf16[192,1024]{1,0:T(8,128)(2,1)S(1)}, bf16[192,1024]{1,0:T(8,128)(2,1)S(1)}, u32[]{:S(2)}, u32[]{:S(2)}) collective-permute-start(bf16[192,1024]{1,0:T(8,128)(2,1)S(1)} %collective-permute-done.2.refs_1_), channel_id=1, source_target_pairs={{0,4},{2,6},{4,0},{6,2},{8,12},{10,14},{12,8},{14,10},{16,20},{18,... | collective-permute-start | bytes 1179656 | tf_op jit(solution)/shard_map/ppermute | solution.py:217
  19.2 8.0 %collective-permute-start.6 = (bf16[128,1024]{1,0:T(8,128)(2,1)S(1)}, bf16[128,1024]{1,0:T(8,128)(2,1)S(1)}, u32[]{:S(2)}, u32[]{:S(2)}) collective-permute-start(bf16[128,1024]{1,0:T(8,128)(2,1)S(1)} %collective-permute-done.5), channel_id=1, source_target_pairs={{0,1},{1,0},{2,3},{3,2},{4,5},{5,4},{6,7},{7,6},{8,9},{9,8},{10,11... | collective-permute-start | bytes 786440 | tf_op jit(solution)/shard_map/ppermute | solution.py:226
  19.2 11.4 %collective-permute-start = (bf16[128,1024]{1,0:T(8,128)(2,1)}, bf16[128,1024]{1,0:T(8,128)(2,1)S(1)}, u32[]{:S(2)}, u32[]{:S(2)}) collective-permute-start(bf16[128,1024]{1,0:T(8,128)(2,1)} %get-tuple-element.34), channel_id=1, source_target_pairs={{0,1},{1,0},{2,3},{3,2},{4,5},{5,4},{6,7},{7,6},{8,9},{9,8},{10,11... | collective-permute-start | bytes 786440 | tf_op jit(solution)/shard_map/ppermute | solution.py:226
  20.7 11.9 %copy-start.4 = (bf16[192,1024]{1,0:T(8,128)(2,1)S(1)}, bf16[192,1024]{1,0:T(8,128)(2,1)}, u32[]{:S(2)}) copy-start(bf16[192,1024]{1,0:T(8,128)(2,1)} %get-tuple-element.35.refs_0_) | copy-start | bytes 1179652
  28.6 11.2 %collective-permute-start.9 = (bf16[192,1024]{1,0:T(8,128)(2,1)S(1)}, bf16[192,1024]{1,0:T(8,128)(2,1)S(1)}, u32[]{:S(2)}, u32[]{:S(2)}) collective-permute-start(bf16[192,1024]{1,0:T(8,128)(2,1)S(1)} %collective-permute-done.1.refs_0_), channel_id=1, source_target_pairs={{0,2},{2,0},{4,6},{6,4},{8,10},{10,8},{12,14},{14,12},{16,18},{18,... | collective-permute-start | bytes 1179656 | tf_op jit(solution)/shard_map/ppermute | solution.py:217
  29.1 13.7 %collective-permute-start.10 = (bf16[192,1024]{1,0:T(8,128)(2,1)S(1)}, bf16[192,1024]{1,0:T(8,128)(2,1)S(1)}, u32[]{:S(2)}, u32[]{:S(2)}) collective-permute-start(bf16[192,1024]{1,0:T(8,128)(2,1)S(1)} %collective-permute-done.1.refs_0_), channel_id=1, source_target_pairs={{0,4},{2,6},{4,0},{6,2},{8,12},{10,14},{12,8},{14,10},{16,20},{18,... | collective-permute-start | bytes 1179656 | tf_op jit(solution)/shard_map/ppermute | solution.py:217
  30.7 12.2 %collective-permute-start.8 = (bf16[96,1024]{1,0:T(8,128)(2,1)S(1)}, bf16[96,1024]{1,0:T(8,128)(2,1)S(1)}, u32[]{:S(2)}, u32[]{:S(2)}) collective-permute-start(bf16[96,1024]{1,0:T(8,128)(2,1)S(1)} %slice.272), channel_id=1, source_target_pairs={{0,6},{2,4},{4,2},{6,0},{8,14},{10,12},{12,10},{14,8},{16,22},{18,... | collective-permute-start | bytes 589832 | tf_op jit(solution)/shard_map/ppermute | solution.py:217
  32.2 10.6 %collective-permute-start.7 = (bf16[96,1024]{1,0:T(8,128)(2,1)S(1)}, bf16[96,1024]{1,0:T(8,128)(2,1)S(1)}, u32[]{:S(2)}, u32[]{:S(2)}) collective-permute-start(bf16[96,1024]{1,0:T(8,128)(2,1)S(1)} %slice.271), channel_id=1, source_target_pairs={{0,16},{2,18},{4,20},{6,22},{8,24},{10,26},{12,28},{14,30},{16,0},... | collective-permute-start | bytes 589832 | tf_op jit(solution)/shard_map/ppermute | solution.py:217
  32.7 10.2 %copy-start = (bf16[512,1024]{1,0:T(8,128)(2,1)}, bf16[512,1024]{1,0:T(8,128)(2,1)S(1)}, u32[]{:S(2)}) copy-start(bf16[512,1024]{1,0:T(8,128)(2,1)S(1)} %constant_dynamic-update-slice_fusion.cents) | copy-start | bytes 3145732
  55.7 1.2 %copy-start.1 = (bf16[512,1024]{1,0:T(8,128)(2,1)S(1)}, bf16[512,1024]{1,0:T(8,128)(2,1)}, u32[]{:S(2)}) copy-start(bf16[512,1024]{1,0:T(8,128)(2,1)} %copy-done) | copy-start | bytes 3145732
  57.0 2.5 %copy-start.3 = (f32[128,1024]{1,0:T(8,128)S(1)}, f32[128,1024]{1,0:T(8,128)}, u32[]{:S(2)}) copy-start(f32[128,1024]{1,0:T(8,128)} %refs_6_.1) | copy-start | bytes 1572868
  59.3 1.2 %copy-start.2 = (bf16[512,1024]{1,0:T(8,128)(2,1)S(1)}, bf16[512,1024]{1,0:T(8,128)(2,1)}, u32[]{:S(2)}) copy-start(bf16[512,1024]{1,0:T(8,128)(2,1)} %copy-done) | copy-start | bytes 3145732
  59.4 3.7 %collective-permute-start.12 = (f32[128,1152]{1,0:T(8,128)S(1)}, f32[128,1152]{1,0:T(8,128)S(1)}, u32[]{:S(2)}, u32[]{:S(2)}) collective-permute-start(f32[128,1152]{1,0:T(8,128)S(1)} %slice.377), channel_id=1, source_target_pairs={{0,1},{1,0},{2,3},{3,2},{4,5},{5,4},{6,7},{7,6},{8,9},{9,8},{10,11... | collective-permute-start | bytes 1769480 | tf_op jit(solution)/shard_map/ppermute | solution.py:226
  63.0 10.0 %collective-permute-start.11 = (f32[128,1152]{1,0:T(8,128)S(1)}, f32[128,1152]{1,0:T(8,128)S(1)}, u32[]{:S(2)}, u32[]{:S(2)}) collective-permute-start(f32[128,1152]{1,0:T(8,128)S(1)} %slice.375), channel_id=1, source_target_pairs={{0,1},{1,0},{2,3},{3,2},{4,5},{5,4},{6,7},{7,6},{8,9},{9,8},{10,11... | collective-permute-start | bytes 1769480 | tf_op jit(solution)/shard_map/ppermute | solution.py:226
  63.2 9.5 %collective-permute-start.13 = (bf16[128,1152]{1,0:T(8,128)(2,1)S(1)}, bf16[128,1152]{1,0:T(8,128)(2,1)S(1)}, u32[]{:S(2)}, u32[]{:S(2)}) collective-permute-start(bf16[128,1152]{1,0:T(8,128)(2,1)S(1)} %pad_maximum_fusion.1), channel_id=1, source_target_pairs={{0,8},{2,10},{4,12},{6,14},{8,0},{10,2},{12,4},{14,6},{16,24},{18,... | collective-permute-start | bytes 884744 | tf_op jit(solution)/shard_map/ppermute | solution.py:217
  74.2 1.5 %collective-permute-start.15 = (bf16[128,1024]{1,0:T(8,128)(2,1)S(1)}, bf16[128,1024]{1,0:T(8,128)(2,1)S(1)}, u32[]{:S(2)}, u32[]{:S(2)}) collective-permute-start(bf16[128,1024]{1,0:T(8,128)(2,1)S(1)} %get-tuple-element.68), channel_id=1, source_target_pairs={{0,1},{1,0},{2,3},{3,2},{4,5},{5,4},{6,7},{7,6},{8,9},{9,8},{10,11... | collective-permute-start | bytes 786440 | tf_op jit(solution)/shard_map/ppermute | solution.py:226
  74.3 8.7 %collective-permute-start.14 = (bf16[128,1024]{1,0:T(8,128)(2,1)S(1)}, bf16[128,1024]{1,0:T(8,128)(2,1)S(1)}, u32[]{:S(2)}, u32[]{:S(2)}) collective-permute-start(bf16[128,1024]{1,0:T(8,128)(2,1)S(1)} %get-tuple-element.68), channel_id=1, source_target_pairs={{0,8},{2,10},{4,12},{6,14},{8,0},{10,2},{12,4},{14,6},{16,24},{18,... | collective-permute-start | bytes 786440 | tf_op jit(solution)/shard_map/ppermute | solution.py:217
  83.0 1.5 %collective-permute-start.16 = (bf16[128,1024]{1,0:T(8,128)(2,1)S(1)}, bf16[128,1024]{1,0:T(8,128)(2,1)S(1)}, u32[]{:S(2)}, u32[]{:S(2)}) collective-permute-start(bf16[128,1024]{1,0:T(8,128)(2,1)S(1)} %collective-permute-done.14.cents), channel_id=1, source_target_pairs={{0,1},{1,0},{2,3},{3,2},{4,5},{5,4},{6,7},{7,6},{8,9},{9,8},{10,11... | collective-permute-start | bytes 786440 | tf_op jit(solution)/shard_map/ppermute | solution.py:226

commit v14 on v11

--- a/solution.py
+++ b/solution.py
@@ -201,8 +201,9 @@
     def across(value, bits):
         return lax.ppermute(value, "cent", [(i, i ^ bits) for i in range(n_cent)])
 
-    def gather_cent(value):
-        blocks = [value]
+    def gather_cent(value, cuts=1):
+        cuts = cuts if value.shape[0] % (16 * cuts) == 0 else 1
+        blocks = jnp.split(value, cuts, axis=0)
         bits = 1
         while bits < n_cent:
             blocks = blocks + [across(b, bits) for b in blocks]
@@ -260,7 +261,7 @@
         far_own = flip(near_own, top_bit)
         near = gather_cent(near_own)
         n_near = len(near) * near_own.shape[0]
-        far = gather_cent(far_own)
+        far = gather_cent(far_own, 2)
         chunk[4], chunk[3], chunk[2], far = hold(chunk[4], chunk[3], chunk[2], far)
         chunk[5] = rows_from(chunk[4], 1)
         chunk[6] = rows_from(chunk[4], 2)

time: 93.1 us -> 94.8 us (1.018)
  local copies, waits for them, and re-layouts: 0.6 us -> 5.93 us
  other arithmetic: 5.88 us -> 3.89 us
  waiting for transfers between devices: 34.4 us -> 32.8 us
    unnamed x9 -> x13, local copies, waits for them, and re-layouts: 0.06 us -> 3.77 us
    ppermute x11, waiting for transfers between devices: 34.1 us -> 32 us  [flip(): return lax.ppermute(value, 'dp', [(i, i ^ bits) for i in range(n_dp)])]
    convert_element_type x1 -> x0, other arithmetic: 1.07 us -> none  [on_device(): near_own = gather_near(centroids.astype(jnp.bfloat16))]
    concatenate x1 -> x0, other arithmetic: 1.02 us -> none  [on_device(): piece = jnp.concatenate(near + far, axis=0)]
  transfers between devices with their start and end apart: 17 -> 18, of which waited for: 9 -> 12; matrix products, arithmetic and copies ran while one was open for 3% -> 6% of each run, Pallas kernels for 9% -> 9%
where the time goes in v14:
time: 94.8 us; the launch traced here: 94.5 us
  waiting for transfers between devices  32.8 us (35%)
  blocking collectives  18.9 us (20%)
  starting transfers between devices  18.6 us (20%)
  Pallas kernels  13.4 us (14%)
  local copies, waits for them, and re-layouts  5.93 us (6%)
  other arithmetic  3.89 us (4%)
  between operations  1.09 us (1%)
    ppermute x11, waiting for transfers between devices, flip(): return lax.ppermute(value, 'dp', [(i, i ^ bits) for i in range(n_dp)])  32 us
    all_to_all x2, blocking collectives, exchange(): return lax.all_to_all(value, 'dp', 0, 0, axis_index_groups=groups)  18.9 us
    ppermute x11, starting transfers between devices, flip(): return lax.ppermute(value, 'dp', [(i, i ^ bits) for i in range(n_dp)])  17.4 us
    pallas_call x2, Pallas kernels, sums_pass(): pl.pallas_call(functools.partial(sums_kernel, first, last, n), out_shape=...  5.59 us
    pallas_call x3, Pallas kernels, second_pass(): pl.pallas_call(functools.partial(second_kernel, shard, n), out_shape=tupl...  4.01 us
    unnamed x13, local copies, waits for them, and re-layouts  3.77 us
    pallas_call x3, Pallas kernels, first_pass(): pl.pallas_call(functools.partial(first_kernel, len(chunks), shard), out_s...  3.76 us
  transfers between devices with their start and end apart: 18, of which 12 were waited for; matrix products, arithmetic and copies ran while one was open for 6% of the time, Pallas kernels for 9%

profile of v14, /device:TPU:0, one launch (start us, length us, event | category | flops | bytes accessed | tf_op | source)
XLA Modules:
  0.0 94.5 jit_solution(14944010783387896747)
XLA Ops:
  0.6 0.0 copy-start
  0.6 1.2 %convert_element_type.14.refs_0_ = bf16[192,1024]{1,0:T(8,128)(2,1)S(1)} convert(f32[192,1024]{1,0:T(8,128)} %param.2) | non-fusion elementwise | flops 196608 | bytes 1179648 | tf_op jit(solution)/shard_map/convert_element_type | solution.py:256
  1.9 3.0 %collective-permute-start.2 = (bf16[192,1024]{1,0:T(8,128)(2,1)S(1)}, bf16[192,1024]{1,0:T(8,128)(2,1)S(1)}, u32[]{:S(2)}, u32[]{:S(2)}) collective-permute-start(bf16[192,1024]{1,0:T(8,128)(2,1)S(1)} %convert_element_type.14.refs_0_), channel_id=1, source_target_pairs={{0,2},{2,0},{4,6},{6,4},{8,10},{10,8},{12,14},{14,12},{16,18},{18,... | collective-permute-start | bytes 1179656 | tf_op jit(solution)/shard_map/ppermute | solution.py:193
  4.9 1.6 %collective-permute-start.5 = (bf16[128,1024]{1,0:T(8,128)(2,1)S(1)}, bf16[128,1024]{1,0:T(8,128)(2,1)S(1)}, u32[]{:S(2)}, u32[]{:S(2)}) collective-permute-start(bf16[128,1024]{1,0:T(8,128)(2,1)S(1)} %get-tuple-element.77), channel_id=1, source_target_pairs={{0,8},{2,10},{4,12},{6,14},{8,0},{10,2},{12,4},{14,6},{16,24},{18,... | collective-permute-start | bytes 786440 | tf_op jit(solution)/shard_map/ppermute | solution.py:193
  6.6 0.0 collective-permute-start
  6.6 2.6 %collective-permute-start.1 = (bf16[192,1024]{1,0:T(8,128)(2,1)S(1)}, bf16[192,1024]{1,0:T(8,128)(2,1)S(1)}, u32[]{:S(2)}, u32[]{:S(2)}) collective-permute-start(bf16[192,1024]{1,0:T(8,128)(2,1)S(1)} %convert_element_type.14.refs_0_), channel_id=1, source_target_pairs={{0,16},{2,18},{4,20},{6,22},{8,24},{10,26},{12,28},{14,30},{16,0},... | collective-permute-start | bytes 1179656 | tf_op jit(solution)/shard_map/ppermute | solution.py:193
  9.2 1.5 %collective-permute-start.4 = (bf16[192,1024]{1,0:T(8,128)(2,1)S(1)}, bf16[192,1024]{1,0:T(8,128)(2,1)S(1)}, u32[]{:S(2)}, u32[]{:S(2)}) collective-permute-start(bf16[192,1024]{1,0:T(8,128)(2,1)S(1)} %convert_element_type.14.refs_0_), channel_id=1, source_target_pairs={{0,4},{2,6},{4,0},{6,2},{8,12},{10,14},{12,8},{14,10},{16,20},{18,... | collective-permute-start | bytes 1179656 | tf_op jit(solution)/shard_map/ppermute | solution.py:193
  10.7 3.3 %collective-permute-done.2.refs_1_ = bf16[192,1024]{1,0:T(8,128)(2,1)S(1)} collective-permute-done((bf16[192,1024]{1,0:T(8,128)(2,1)S(1)}, bf16[192,1024]{1,0:T(8,128)(2,1)S(1)}, u32[]{:S(2)}, u32[]{:S(2)}) %collective-permute-start.2) | collective-permute-done | bytes 393248 | tf_op jit(solution)/shard_map/ppermute | solution.py:193
  14.0 1.8 %collective-permute-start.3 = (bf16[192,1024]{1,0:T(8,128)(2,1)S(1)}, bf16[192,1024]{1,0:T(8,128)(2,1)S(1)}, u32[]{:S(2)}, u32[]{:S(2)}) collective-permute-start(bf16[192,1024]{1,0:T(8,128)(2,1)S(1)} %collective-permute-done.2.refs_1_), channel_id=1, source_target_pairs={{0,4},{2,6},{4,0},{6,2},{8,12},{10,14},{12,8},{14,10},{16,20},{18,... | collective-permute-start | bytes 1179656 | tf_op jit(solution)/shard_map/ppermute | solution.py:193
  15.8 1.3 %collective-permute-done.5 = bf16[128,1024]{1,0:T(8,128)(2,1)S(1)} collective-permute-done((bf16[128,1024]{1,0:T(8,128)(2,1)S(1)}, bf16[128,1024]{1,0:T(8,128)(2,1)S(1)}, u32[]{:S(2)}, u32[]{:S(2)}) %collective-permute-start.5) | collective-permute-done | bytes 262176 | tf_op jit(solution)/shard_map/ppermute | solution.py:193
  17.0 0.7 fusion.26
  17.7 0.0 collective-permute-start.6
  17.7 0.0 collective-permute-done
  17.7 0.5 collective-permute-start.7
  18.2 1.0 %constant_dynamic-update-slice_fusion.4 = bf16[512,1024]{1,0:T(8,128)(2,1)S(1)} fusion(bf16[512,1024]{1,0:T(8,128)(2,1)S(1)} %get-tuple-element.76, bf16[128,1024]{1,0:T(8,128)(2,1)} %collective-permute-done), kind=kLoop, calls=%fused_computation.22 | loop fusion | bytes 524288
  19.2 0.2 collective-permute-done.6
  19.4 0.2 collective-permute-done.7
  19.6 7.9 %collective-permute-done.1.refs_0_ = bf16[192,1024]{1,0:T(8,128)(2,1)S(1)} collective-permute-done((bf16[192,1024]{1,0:T(8,128)(2,1)S(1)}, bf16[192,1024]{1,0:T(8,128)(2,1)S(1)}, u32[]{:S(2)}, u32[]{:S(2)}) %collective-permute-start.1) | collective-permute-done | bytes 393248 | tf_op jit(solution)/shard_map/ppermute | solution.py:193
  27.5 0.0 collective-permute-done.4.refs_2_
  27.5 1.4 %collective-permute-done.3.refs_3_ = bf16[192,1024]{1,0:T(8,128)(2,1)S(1)} collective-permute-done((bf16[192,1024]{1,0:T(8,128)(2,1)S(1)}, bf16[192,1024]{1,0:T(8,128)(2,1)S(1)}, u32[]{:S(2)}, u32[]{:S(2)}) %collective-permute-start.3) | collective-permute-done | bytes 393248 | tf_op jit(solution)/shard_map/ppermute | solution.py:193
  28.8 0.5 collective-permute-start.10
  29.4 1.6 %collective-permute-start.11 = (bf16[192,1024]{1,0:T(8,128)(2,1)S(1)}, bf16[192,1024]{1,0:T(8,128)(2,1)S(1)}, u32[]{:S(2)}, u32[]{:S(2)}) collective-permute-start(bf16[192,1024]{1,0:T(8,128)(2,1)S(1)} %collective-permute-done.1.refs_0_), channel_id=1, source_target_pairs={{0,4},{2,6},{4,0},{6,2},{8,12},{10,14},{12,8},{14,10},{16,20},{18,... | collective-permute-start | bytes 1179656 | tf_op jit(solution)/shard_map/ppermute | solution.py:193
  31.0 1.4 %collective-permute-start.9 = (bf16[96,1024]{1,0:T(8,128)(2,1)S(1)}, bf16[96,1024]{1,0:T(8,128)(2,1)S(1)}, u32[]{:S(2)}, u32[]{:S(2)}) collective-permute-start(bf16[96,1024]{1,0:T(8,128)(2,1)S(1)} %slice.326), channel_id=1, source_target_pairs={{0,6},{2,4},{4,2},{6,0},{8,14},{10,12},{12,10},{14,8},{16,22},{18,... | collective-permute-start | bytes 589832 | tf_op jit(solution)/shard_map/ppermute | solution.py:193
  32.4 0.4 collective-permute-start.8
  32.8 0.9 constant_dynamic-update-slice_fusion.3
  33.8 0.9 constant_dynamic-update-slice_fusion.2
  34.7 0.9 constant_dynamic-update-slice_fusion.1
  35.6 0.9 constant_dynamic-update-slice_fusion.cents
  36.5 1.8 %first_pass.3 = (f32[2,4,192]{2,1,0:T(4,128)S(1)}, f32[1,768]{1,0:T(1,128)S(1)}, bf16[768,1024]{1,0:T(8,128)(2,1)S(1)}) custom-call(bf16[512,1024]{1,0:T(8,128)(2,1)S(1)} %constant_dynamic-update-slice_fusion.cents, bf16[192,1024]{1,0:T(8,128)(2,1)S(1)} %convert_element_type.14.refs_0_, bf16[192,1024]{1,0:T(8,128)(2,1)S(1)} %collective-permute-done.2.refs_1_, ...), custom_call_target="tpu_custom_call" | custom-call | flops 805306368 | bytes 1572864 | tf_op jit(solution)/shard_map/first_pass/pallas_call | solution.py:69
  38.3 2.6 %collective-permute-done.10.refs_1_ = bf16[192,1024]{1,0:T(8,128)(2,1)S(1)} collective-permute-done((bf16[192,1024]{1,0:T(8,128)(2,1)S(1)}, bf16[192,1024]{1,0:T(8,128)(2,1)S(1)}, u32[]{:S(2)}, u32[]{:S(2)}) %collective-permute-start.10) | collective-permute-done | bytes 393248 | tf_op jit(solution)/shard_map/ppermute | solution.py:193
  40.9 1.0 %first_pass.4 = (f32[2,2,192]{2,1,0:T(2,128)S(1)}, f32[1,384]{1,0:T(1,128)S(1)}, bf16[384,1024]{1,0:T(8,128)(2,1)S(1)}) custom-call(bf16[512,1024]{1,0:T(8,128)(2,1)S(1)} %constant_dynamic-update-slice_fusion.cents, bf16[192,1024]{1,0:T(8,128)(2,1)S(1)} %collective-permute-done.1.refs_0_, bf16[192,1024]{1,0:T(8,128)(2,1)S(1)} %collective-permute-done.10.refs_1_), custom_call_target="tpu_custom_call" | custom-call | flops 402653184 | bytes 786432 | tf_op jit(solution)/shard_map/first_pass/pallas_call | solution.py:69
  41.9 2.5 %collective-permute-done.9.refs_2_ = bf16[96,1024]{1,0:T(8,128)(2,1)S(1)} collective-permute-done((bf16[96,1024]{1,0:T(8,128)(2,1)S(1)}, bf16[96,1024]{1,0:T(8,128)(2,1)S(1)}, u32[]{:S(2)}, u32[]{:S(2)}) %collective-permute-start.9) | collective-permute-done | bytes 196640 | tf_op jit(solution)/shard_map/ppermute | solution.py:193
  44.4 0.0 collective-permute-done.8.refs_1_
  44.4 0.0 collective-permute-done.11.refs_0_
  44.4 1.0 %first_pass.5 = (f32[2,2,192]{2,1,0:T(2,128)S(1)}, f32[1,384]{1,0:T(1,128)S(1)}, bf16[384,1024]{1,0:T(8,128)(2,1)S(1)}) custom-call(bf16[512,1024]{1,0:T(8,128)(2,1)S(1)} %constant_dynamic-update-slice_fusion.cents, bf16[192,1024]{1,0:T(8,128)(2,1)S(1)} %collective-permute-done.11.refs_0_, bf16[96,1024]{1,0:T(8,128)(2,1)S(1)} %collective-permute-done.8.refs_1_, ...), custom_call_target="tpu_custom_call" | custom-call | flops 402653184 | bytes 786432 | tf_op jit(solution)/shard_map/first_pass/pallas_call | solution.py:69
  45.7 9.9 %all_to_all.10 = f32[8,2,8,192]{3,2,1,0:T(8,128)S(1)} all-to-all(f32[8,2,8,192]{3,2,1,0:T(8,128)S(1)} %broadcast_in_dim.6), channel_id=1, replica_groups={{0,2,4,6,16,18,20,22},{8,10,12,14,24,26,28,30},{1,3,5,7,17,19,21,23},{9..., dimensions={0} | all-to-all | bytes 196608 | tf_op jit(solution)/shard_map/all_to_all | solution.py:245
  55.9 0.1 pad_maximum_fusion.8
  56.0 0.1 pad_maximum_fusion.7.refs_0_
  56.1 2.8 %sums_pass.3 = f32[256,1152]{1,0:T(8,128)S(1)} custom-call(bf16[512,1024]{1,0:T(8,128)(2,1)S(1)} %constant_dynamic-update-slice_fusion.cents, f32[2,768]{1,0:T(2,128)S(1)} %pad_maximum_fusion.7.refs_0_, f32[2,384]{1,0:T(2,128)S(1)} %get-tuple-element.121.refs_1_, f32[2,384]{1,0:T(2,128)S(1)} %get-tuple-element.122.refs_2_, ...), custom_call_target="tpu_custom_call" | custom-call | flops 1610612736 | bytes 3145728 | tf_op jit(solution)/shard_map/sums_pass/pallas_call | solution.py:112
  58.9 0.1 collective-permute-start.13
  59.0 2.8 %sums_pass.2 = f32[256,1152]{1,0:T(8,128)S(1)} custom-call(bf16[512,1024]{1,0:T(8,128)(2,1)S(1)} %constant_dynamic-update-slice_fusion.cents, f32[2,768]{1,0:T(2,128)S(1)} %pad_maximum_fusion.7.refs_0_, f32[2,384]{1,0:T(2,128)S(1)} %get-tuple-element.121.refs_1_, f32[2,384]{1,0:T(2,128)S(1)} %get-tuple-element.122.refs_2_, ...), custom_call_target="tpu_custom_call" | custom-call | flops 1610612736 | bytes 3145728 | tf_op jit(solution)/shard_map/sums_pass/pallas_call | solution.py:112
  61.9 0.6 collective-permute-start.12
  62.4 0.0 collective-permute-done.13
  62.4 0.1 slice_add_fusion
  62.6 1.5 %collective-permute-start.14 = (bf16[128,1152]{1,0:T(8,128)(2,1)S(1)}, bf16[128,1152]{1,0:T(8,128)(2,1)S(1)}, u32[]{:S(2)}, u32[]{:S(2)}) collective-permute-start(bf16[128,1152]{1,0:T(8,128)(2,1)S(1)} %pad_maximum_fusion.1), channel_id=1, source_target_pairs={{0,8},{2,10},{4,12},{6,14},{8,0},{10,2},{12,4},{14,6},{16,24},{18,... | collective-permute-start | bytes 884744 | tf_op jit(solution)/shard_map/ppermute | solution.py:193
  64.1 7.5 %collective-permute-done.14 = bf16[128,1152]{1,0:T(8,128)(2,1)S(1)} collective-permute-done((bf16[128,1152]{1,0:T(8,128)(2,1)S(1)}, bf16[128,1152]{1,0:T(8,128)(2,1)S(1)}, u32[]{:S(2)}, u32[]{:S(2)}) %collective-permute-start.14) | collective-permute-done | bytes 294944 | tf_op jit(solution)/shard_map/ppermute | solution.py:193
  71.7 0.2 fusion.2
  71.9 0.0 collective-permute-done.12
  71.9 0.1 broadcast_in_dim.8
  72.0 0.1 fusion
  72.1 0.1 slice_reduce_fusion
  72.2 0.9 fusion.25
  73.1 0.0 collective-permute-start.16
  73.1 1.4 %collective-permute-start.15 = (bf16[128,1024]{1,0:T(8,128)(2,1)S(1)}, bf16[128,1024]{1,0:T(8,128)(2,1)S(1)}, u32[]{:S(2)}, u32[]{:S(2)}) collective-permute-start(bf16[128,1024]{1,0:T(8,128)(2,1)S(1)} %get-tuple-element.74), channel_id=1, source_target_pairs={{0,8},{2,10},{4,12},{6,14},{8,0},{10,2},{12,4},{14,6},{16,24},{18,... | collective-permute-start | bytes 786440 | tf_op jit(solution)/shard_map/ppermute | solution.py:193
  74.6 0.1 collective-permute-done.16
  74.7 1.6 %second_pass.3 = (f32[3,4,192]{2,1,0:T(4,128)S(1)}, f32[3,2,192]{2,1,0:T(2,128)S(1)}, f32[3,2,192]{2,1,0:T(2,128)S(1)}) custom-call(bf16[256,1024]{1,0:T(8,128)(2,1)S(1)} %pad_maximum_fusion.cents, f32[1,768]{1,0:T(1,128)S(1)} %get-tuple-element.55.refs_3_.refs_0_, f32[1,384]{1,0:T(1,128)S(1)} %get-tuple-element.56.refs_4_.refs_1_, ...), custom_call_target="tpu_custom_call" | custom-call | flops 805306368 | bytes 3145728 | tf_op jit(solution)/shard_map/second_pass/pallas_call | solution.py:153
  76.3 5.5 %collective-permute-done.15.cents = bf16[128,1024]{1,0:T(8,128)(2,1)S(1)} collective-permute-done((bf16[128,1024]{1,0:T(8,128)(2,1)S(1)}, bf16[128,1024]{1,0:T(8,128)(2,1)S(1)}, u32[]{:S(2)}, u32[]{:S(2)}) %collective-permute-start.15) | collective-permute-done | bytes 262176 | tf_op jit(solution)/shard_map/ppermute | solution.py:193
  81.9 0.0 collective-permute-start.17
  81.9 1.2 %second_pass.4 = (f32[3,4,192]{2,1,0:T(4,128)S(1)}, f32[3,2,192]{2,1,0:T(2,128)S(1)}, f32[3,2,192]{2,1,0:T(2,128)S(1)}) custom-call(bf16[128,1024]{1,0:T(8,128)(2,1)S(1)} %collective-permute-done.15.cents, f32[1,768]{1,0:T(1,128)S(1)} %get-tuple-element.55.refs_3_.refs_0_, f32[1,384]{1,0:T(1,128)S(1)} %get-tuple-element.56.refs_4_.refs_1_, ...), custom_call_target="tpu_custom_call" | custom-call | flops 402653184 | bytes 3145728 | tf_op jit(solution)/shard_map/second_pass/pallas_call | solution.py:153
  83.1 0.3 collective-permute-done.17.cents
  83.4 1.2 %second_pass.5 = (f32[3,4,192]{2,1,0:T(4,128)S(1)}, f32[3,2,192]{2,1,0:T(2,128)S(1)}, f32[3,2,192]{2,1,0:T(2,128)S(1)}) custom-call(bf16[128,1024]{1,0:T(8,128)(2,1)S(1)} %collective-permute-done.17.cents, f32[1,768]{1,0:T(1,128)S(1)} %get-tuple-element.55.refs_3_.refs_0_, f32[1,384]{1,0:T(1,128)S(1)} %get-tuple-element.56.refs_4_.refs_1_, ...), custom_call_target="tpu_custom_call" | custom-call | flops 402653184 | bytes 3145728 | tf_op jit(solution)/shard_map/second_pass/pallas_call | solution.py:153
  84.7 0.1 stack.78
  84.9 9.0 %all_to_all.11 = f32[8,3,192]{2,1,0:T(4,128)S(1)} all-to-all(f32[8,3,192]{2,1,0:T(4,128)S(1)} %copy.74), channel_id=1, replica_groups={{0,2,4,6,16,18,20,22},{8,10,12,14,24,26,28,30},{1,3,5,7,17,19,21,23},{9..., dimensions={0} | all-to-all | bytes 36864 | tf_op jit(solution)/shard_map/all_to_all | solution.py:245
  93.9 0.6 divide_subtract_fusion
  (63 shorter events, 1.0 us)
Async XLA Ops:
  0.6 4.3 %copy-start = (f32[128,1024]{1,0:T(8,128)S(1)}, f32[128,1024]{1,0:T(8,128)}, u32[]{:S(2)}) copy-start(f32[128,1024]{1,0:T(8,128)} %refs_9_.1) | copy-start | bytes 1572868
  1.9 12.1 %collective-permute-start.2 = (bf16[192,1024]{1,0:T(8,128)(2,1)S(1)}, bf16[192,1024]{1,0:T(8,128)(2,1)S(1)}, u32[]{:S(2)}, u32[]{:S(2)}) collective-permute-start(bf16[192,1024]{1,0:T(8,128)(2,1)S(1)} %convert_element_type.14.refs_0_), channel_id=1, source_target_pairs={{0,2},{2,0},{4,6},{6,4},{8,10},{10,8},{12,14},{14,12},{16,18},{18,... | collective-permute-start | bytes 1179656 | tf_op jit(solution)/shard_map/ppermute | solution.py:193
  4.9 12.1 %collective-permute-start.5 = (bf16[128,1024]{1,0:T(8,128)(2,1)S(1)}, bf16[128,1024]{1,0:T(8,128)(2,1)S(1)}, u32[]{:S(2)}, u32[]{:S(2)}) collective-permute-start(bf16[128,1024]{1,0:T(8,128)(2,1)S(1)} %get-tuple-element.77), channel_id=1, source_target_pairs={{0,8},{2,10},{4,12},{6,14},{8,0},{10,2},{12,4},{14,6},{16,24},{18,... | collective-permute-start | bytes 786440 | tf_op jit(solution)/shard_map/ppermute | solution.py:193
  6.6 11.2 %collective-permute-start = (bf16[128,1024]{1,0:T(8,128)(2,1)S(1)}, bf16[128,1024]{1,0:T(8,128)(2,1)}, u32[]{:S(2)}, u32[]{:S(2)}) collective-permute-start(bf16[128,1024]{1,0:T(8,128)(2,1)S(1)} %get-tuple-element.77), channel_id=1, source_target_pairs={{0,1},{1,0},{2,3},{3,2},{4,5},{5,4},{6,7},{7,6},{8,9},{9,8},{10,11... | collective-permute-start | bytes 786440 | tf_op jit(solution)/shard_map/ppermute | solution.py:202
  6.6 20.9 %collective-permute-start.1 = (bf16[192,1024]{1,0:T(8,128)(2,1)S(1)}, bf16[192,1024]{1,0:T(8,128)(2,1)S(1)}, u32[]{:S(2)}, u32[]{:S(2)}) collective-permute-start(bf16[192,1024]{1,0:T(8,128)(2,1)S(1)} %convert_element_type.14.refs_0_), channel_id=1, source_target_pairs={{0,16},{2,18},{4,20},{6,22},{8,24},{10,26},{12,28},{14,30},{16,0},... | collective-permute-start | bytes 1179656 | tf_op jit(solution)/shard_map/ppermute | solution.py:193
  9.2 18.3 %collective-permute-start.4 = (bf16[192,1024]{1,0:T(8,128)(2,1)S(1)}, bf16[192,1024]{1,0:T(8,128)(2,1)S(1)}, u32[]{:S(2)}, u32[]{:S(2)}) collective-permute-start(bf16[192,1024]{1,0:T(8,128)(2,1)S(1)} %convert_element_type.14.refs_0_), channel_id=1, source_target_pairs={{0,4},{2,6},{4,0},{6,2},{8,12},{10,14},{12,8},{14,10},{16,20},{18,... | collective-permute-start | bytes 1179656 | tf_op jit(solution)/shard_map/ppermute | solution.py:193
  14.0 14.8 %collective-permute-start.3 = (bf16[192,1024]{1,0:T(8,128)(2,1)S(1)}, bf16[192,1024]{1,0:T(8,128)(2,1)S(1)}, u32[]{:S(2)}, u32[]{:S(2)}) collective-permute-start(bf16[192,1024]{1,0:T(8,128)(2,1)S(1)} %collective-permute-done.2.refs_1_), channel_id=1, source_target_pairs={{0,4},{2,6},{4,0},{6,2},{8,12},{10,14},{12,8},{14,10},{16,20},{18,... | collective-permute-start | bytes 1179656 | tf_op jit(solution)/shard_map/ppermute | solution.py:193
  17.7 1.7 %collective-permute-start.6 = (bf16[64,1024]{1,0:T(8,128)(2,1)}, bf16[64,1024]{1,0:T(8,128)(2,1)}, u32[]{:S(2)}, u32[]{:S(2)}) collective-permute-start(bf16[64,1024]{1,0:T(8,128)(2,1)} %get-tuple-element.37), channel_id=1, source_target_pairs={{0,1},{1,0},{2,3},{3,2},{4,5},{5,4},{6,7},{7,6},{8,9},{9,8},{10,11... | collective-permute-start | bytes 393224 | tf_op jit(solution)/shard_map/ppermute | solution.py:202
  17.7 1.9 %collective-permute-start.7 = (bf16[64,1024]{1,0:T(8,128)(2,1)}, bf16[64,1024]{1,0:T(8,128)(2,1)}, u32[]{:S(2)}, u32[]{:S(2)}) collective-permute-start(bf16[64,1024]{1,0:T(8,128)(2,1)} %get-tuple-element.38), channel_id=1, source_target_pairs={{0,1},{1,0},{2,3},{3,2},{4,5},{5,4},{6,7},{7,6},{8,9},{9,8},{10,11... | collective-permute-start | bytes 393224 | tf_op jit(solution)/shard_map/ppermute | solution.py:202
  28.8 12.1 %collective-permute-start.10 = (bf16[192,1024]{1,0:T(8,128)(2,1)S(1)}, bf16[192,1024]{1,0:T(8,128)(2,1)S(1)}, u32[]{:S(2)}, u32[]{:S(2)}) collective-permute-start(bf16[192,1024]{1,0:T(8,128)(2,1)S(1)} %collective-permute-done.1.refs_0_), channel_id=1, source_target_pairs={{0,2},{2,0},{4,6},{6,4},{8,10},{10,8},{12,14},{14,12},{16,18},{18,... | collective-permute-start | bytes 1179656 | tf_op jit(solution)/shard_map/ppermute | solution.py:193
  29.4 15.1 %collective-permute-start.11 = (bf16[192,1024]{1,0:T(8,128)(2,1)S(1)}, bf16[192,1024]{1,0:T(8,128)(2,1)S(1)}, u32[]{:S(2)}, u32[]{:S(2)}) collective-permute-start(bf16[192,1024]{1,0:T(8,128)(2,1)S(1)} %collective-permute-done.1.refs_0_), channel_id=1, source_target_pairs={{0,4},{2,6},{4,0},{6,2},{8,12},{10,14},{12,8},{14,10},{16,20},{18,... | collective-permute-start | bytes 1179656 | tf_op jit(solution)/shard_map/ppermute | solution.py:193
  31.0 13.5 %collective-permute-start.9 = (bf16[96,1024]{1,0:T(8,128)(2,1)S(1)}, bf16[96,1024]{1,0:T(8,128)(2,1)S(1)}, u32[]{:S(2)}, u32[]{:S(2)}) collective-permute-start(bf16[96,1024]{1,0:T(8,128)(2,1)S(1)} %slice.326), channel_id=1, source_target_pairs={{0,6},{2,4},{4,2},{6,0},{8,14},{10,12},{12,10},{14,8},{16,22},{18,... | collective-permute-start | bytes 589832 | tf_op jit(solution)/shard_map/ppermute | solution.py:193
  32.4 12.0 %collective-permute-start.8 = (bf16[96,1024]{1,0:T(8,128)(2,1)S(1)}, bf16[96,1024]{1,0:T(8,128)(2,1)S(1)}, u32[]{:S(2)}, u32[]{:S(2)}) collective-permute-start(bf16[96,1024]{1,0:T(8,128)(2,1)S(1)} %slice.325), channel_id=1, source_target_pairs={{0,16},{2,18},{4,20},{6,22},{8,24},{10,26},{12,28},{14,30},{16,0},... | collective-permute-start | bytes 589832 | tf_op jit(solution)/shard_map/ppermute | solution.py:193
  58.9 3.5 %collective-permute-start.13 = (f32[128,1152]{1,0:T(8,128)S(1)}, f32[128,1152]{1,0:T(8,128)S(1)}, u32[]{:S(2)}, u32[]{:S(2)}) collective-permute-start(f32[128,1152]{1,0:T(8,128)S(1)} %slice.451), channel_id=1, source_target_pairs={{0,1},{1,0},{2,3},{3,2},{4,5},{5,4},{6,7},{7,6},{8,9},{9,8},{10,11... | collective-permute-start | bytes 1769480 | tf_op jit(solution)/shard_map/ppermute | solution.py:202
  61.9 10.0 %collective-permute-start.12 = (f32[128,1152]{1,0:T(8,128)S(1)}, f32[128,1152]{1,0:T(8,128)S(1)}, u32[]{:S(2)}, u32[]{:S(2)}) collective-permute-start(f32[128,1152]{1,0:T(8,128)S(1)} %slice.449), channel_id=1, source_target_pairs={{0,1},{1,0},{2,3},{3,2},{4,5},{5,4},{6,7},{7,6},{8,9},{9,8},{10,11... | collective-permute-start | bytes 1769480 | tf_op jit(solution)/shard_map/ppermute | solution.py:202
  62.6 9.0 %collective-permute-start.14 = (bf16[128,1152]{1,0:T(8,128)(2,1)S(1)}, bf16[128,1152]{1,0:T(8,128)(2,1)S(1)}, u32[]{:S(2)}, u32[]{:S(2)}) collective-permute-start(bf16[128,1152]{1,0:T(8,128)(2,1)S(1)} %pad_maximum_fusion.1), channel_id=1, source_target_pairs={{0,8},{2,10},{4,12},{6,14},{8,0},{10,2},{12,4},{14,6},{16,24},{18,... | collective-permute-start | bytes 884744 | tf_op jit(solution)/shard_map/ppermute | solution.py:193
  73.1 1.5 %collective-permute-start.16 = (bf16[128,1024]{1,0:T(8,128)(2,1)S(1)}, bf16[128,1024]{1,0:T(8,128)(2,1)S(1)}, u32[]{:S(2)}, u32[]{:S(2)}) collective-permute-start(bf16[128,1024]{1,0:T(8,128)(2,1)S(1)} %get-tuple-element.74), channel_id=1, source_target_pairs={{0,1},{1,0},{2,3},{3,2},{4,5},{5,4},{6,7},{7,6},{8,9},{9,8},{10,11... | collective-permute-start | bytes 786440 | tf_op jit(solution)/shard_map/ppermute | solution.py:202
  73.1 8.7 %collective-permute-start.15 = (bf16[128,1024]{1,0:T(8,128)(2,1)S(1)}, bf16[128,1024]{1,0:T(8,128)(2,1)S(1)}, u32[]{:S(2)}, u32[]{:S(2)}) collective-permute-start(bf16[128,1024]{1,0:T(8,128)(2,1)S(1)} %get-tuple-element.74), channel_id=1, source_target_pairs={{0,8},{2,10},{4,12},{6,14},{8,0},{10,2},{12,4},{14,6},{16,24},{18,... | collective-permute-start | bytes 786440 | tf_op jit(solution)/shard_map/ppermute | solution.py:193
  81.9 1.5 %collective-permute-start.17 = (bf16[128,1024]{1,0:T(8,128)(2,1)S(1)}, bf16[128,1024]{1,0:T(8,128)(2,1)S(1)}, u32[]{:S(2)}, u32[]{:S(2)}) collective-permute-start(bf16[128,1024]{1,0:T(8,128)(2,1)S(1)} %collective-permute-done.15.cents), channel_id=1, source_target_pairs={{0,1},{1,0},{2,3},{3,2},{4,5},{5,4},{6,7},{7,6},{8,9},{9,8},{10,11... | collective-permute-start | bytes 786440 | tf_op jit(solution)/shard_map/ppermute | solution.py:202

commit v15 on v11

--- a/solution.py
+++ b/solution.py
@@ -209,11 +209,14 @@
             bits *= 2
         return blocks
 
-    def scatter_cent(value):
+    def scatter_cent(value, other=None):
         bits = n_cent // 2
         while bits:
             half = value.shape[0] // 2
-            value = value[:half] + across(value[half:], bits)
+            if other is not None:
+                value, other = value + across(other, bits), None
+            else:
+                value = value[:half] + across(value[half:], bits)
             bits //= 2
         return value
 
@@ -283,8 +286,12 @@
         coarse = lax.reduce_precision(count, 8, 7)
         lane = lax.broadcasted_iota(jnp.int32, count.shape, 1)
         far = jnp.concatenate([far[:, :width], jnp.where(lane < 64, coarse, count - coarse)], axis=1)
-        far = flip(far.astype(jnp.bfloat16), top_bit).astype(jnp.float32)
-        near = scatter_cent(sums_pass(piece, final, row_sqs, rows, 0, n_near, [centroids]))
+        far = far.astype(jnp.bfloat16)
+        n_half = n_near // 2
+        other = sums_pass(piece, final, row_sqs, rows, n_half, n_near)
+        near = sums_pass(piece, hold(final, far)[0], row_sqs, rows, 0, n_half, [centroids])
+        near = scatter_cent(near, other)
+        far = flip(far, top_bit).astype(jnp.float32)
         counts = far[:, width : width + 1] + far[:, width + 64 : width + 65]
         far = jnp.concatenate([far[:, :width], jnp.broadcast_to(counts, count.shape)], axis=1)
         sums = scatter_near(near + far)

time: 93.1 us -> 92.5 us (level)
  Pallas kernels: 13.3 us -> 15.1 us
  waiting for transfers between devices: 34.4 us -> 33.1 us
    pallas_call x2 -> x3, Pallas kernels: 5.56 us -> 7.31 us  [sums_pass(): pl.pallas_call(functools.partial(sums_kernel, first, last, n), out_shape=...]
    ppermute x11, waiting for transfers between devices: 34.1 us -> 32.7 us  [flip(): return lax.ppermute(value, 'dp', [(i, i ^ bits) for i in range(n_dp)])]
    concatenate x1, other arithmetic: 1.02 us -> 0.07 us  [on_device(): piece = jnp.concatenate(near + far, axis=0)]
  transfers between devices with their start and end apart: 17 -> 17, of which waited for: 9 -> 9; matrix products, arithmetic and copies ran while one was open for 3% -> 2% of each run, Pallas kernels for 9% -> 11%
where the time goes in v15:
time: 92.5 us; the launch traced here: 92.2 us
  waiting for transfers between devices  33.1 us (36%)
  blocking collectives  18.8 us (20%)
  starting transfers between devices  18.7 us (20%)
  Pallas kernels  15.1 us (16%)
  other arithmetic  4.97 us (5%)
  between operations  1.06 us (1%)
    ppermute x11, waiting for transfers between devices, flip(): return lax.ppermute(value, 'dp', [(i, i ^ bits) for i in range(n_dp)])  32.7 us
    all_to_all x2, blocking collectives, exchange(): return lax.all_to_all(value, 'dp', 0, 0, axis_index_groups=groups)  18.8 us
    ppermute x11, starting transfers between devices, flip(): return lax.ppermute(value, 'dp', [(i, i ^ bits) for i in range(n_dp)])  17.6 us
    pallas_call x3, Pallas kernels, sums_pass(): pl.pallas_call(functools.partial(sums_kernel, first, last, n), out_shape=...  7.31 us
    pallas_call x3, Pallas kernels, second_pass(): pl.pallas_call(functools.partial(second_kernel, shard, n), out_shape=tupl...  4 us
    pallas_call x3, Pallas kernels, first_pass(): pl.pallas_call(functools.partial(first_kernel, len(chunks), shard), out_s...  3.77 us
  transfers between devices with their start and end apart: 17, of which 9 were waited for; matrix products, arithmetic and copies ran while one was open for 2% of the time, Pallas kernels for 11%

profile of v15, /device:TPU:0, one launch (start us, length us, event | category | flops | bytes accessed | tf_op | source)
XLA Modules:
  0.0 92.2 jit_solution(14642501919785431394)
XLA Ops:
  0.6 1.2 %convert_element_type.14.refs_0_ = bf16[192,1024]{1,0:T(8,128)(2,1)S(1)} convert(f32[192,1024]{1,0:T(8,128)} %param.2) | non-fusion elementwise | flops 196608 | bytes 1179648 | tf_op jit(solution)/shard_map/convert_element_type | solution.py:258
  1.8 3.0 %collective-permute-start.2 = (bf16[192,1024]{1,0:T(8,128)(2,1)S(1)}, bf16[192,1024]{1,0:T(8,128)(2,1)S(1)}, u32[]{:S(2)}, u32[]{:S(2)}) collective-permute-start(bf16[192,1024]{1,0:T(8,128)(2,1)S(1)} %convert_element_type.14.refs_0_), channel_id=1, source_target_pairs={{0,2},{2,0},{4,6},{6,4},{8,10},{10,8},{12,14},{14,12},{16,18},{18,... | collective-permute-start | bytes 1179656 | tf_op jit(solution)/shard_map/ppermute | solution.py:193
  4.8 1.1 %convert_element_type.13 = bf16[128,1024]{1,0:T(8,128)(2,1)S(1)} convert(f32[128,1024]{1,0:T(8,128)} %refs_9_.1) | non-fusion elementwise | flops 131072 | bytes 786432 | tf_op jit(solution)/shard_map/convert_element_type | solution.py:262
  5.9 1.6 %collective-permute-start.5 = (bf16[128,1024]{1,0:T(8,128)(2,1)S(1)}, bf16[128,1024]{1,0:T(8,128)(2,1)S(1)}, u32[]{:S(2)}, u32[]{:S(2)}) collective-permute-start(bf16[128,1024]{1,0:T(8,128)(2,1)S(1)} %convert_element_type.13), channel_id=1, source_target_pairs={{0,8},{2,10},{4,12},{6,14},{8,0},{10,2},{12,4},{14,6},{16,24},{18,... | collective-permute-start | bytes 786440 | tf_op jit(solution)/shard_map/ppermute | solution.py:193
  7.5 2.6 %collective-permute-start.1 = (bf16[192,1024]{1,0:T(8,128)(2,1)S(1)}, bf16[192,1024]{1,0:T(8,128)(2,1)S(1)}, u32[]{:S(2)}, u32[]{:S(2)}) collective-permute-start(bf16[192,1024]{1,0:T(8,128)(2,1)S(1)} %convert_element_type.14.refs_0_), channel_id=1, source_target_pairs={{0,16},{2,18},{4,20},{6,22},{8,24},{10,26},{12,28},{14,30},{16,0},... | collective-permute-start | bytes 1179656 | tf_op jit(solution)/shard_map/ppermute | solution.py:193
  10.1 1.5 %collective-permute-start.4 = (bf16[192,1024]{1,0:T(8,128)(2,1)S(1)}, bf16[192,1024]{1,0:T(8,128)(2,1)S(1)}, u32[]{:S(2)}, u32[]{:S(2)}) collective-permute-start(bf16[192,1024]{1,0:T(8,128)(2,1)S(1)} %convert_element_type.14.refs_0_), channel_id=1, source_target_pairs={{0,4},{2,6},{4,0},{6,2},{8,12},{10,14},{12,8},{14,10},{16,20},{18,... | collective-permute-start | bytes 1179656 | tf_op jit(solution)/shard_map/ppermute | solution.py:193
  11.7 2.3 %collective-permute-done.2.refs_1_ = bf16[192,1024]{1,0:T(8,128)(2,1)S(1)} collective-permute-done((bf16[192,1024]{1,0:T(8,128)(2,1)S(1)}, bf16[192,1024]{1,0:T(8,128)(2,1)S(1)}, u32[]{:S(2)}, u32[]{:S(2)}) %collective-permute-start.2) | collective-permute-done | bytes 393248 | tf_op jit(solution)/shard_map/ppermute | solution.py:193
  13.9 1.8 %collective-permute-start.3 = (bf16[192,1024]{1,0:T(8,128)(2,1)S(1)}, bf16[192,1024]{1,0:T(8,128)(2,1)S(1)}, u32[]{:S(2)}, u32[]{:S(2)}) collective-permute-start(bf16[192,1024]{1,0:T(8,128)(2,1)S(1)} %collective-permute-done.2.refs_1_), channel_id=1, source_target_pairs={{0,4},{2,6},{4,0},{6,2},{8,12},{10,14},{12,8},{14,10},{16,20},{18,... | collective-permute-start | bytes 1179656 | tf_op jit(solution)/shard_map/ppermute | solution.py:193
  15.7 3.5 %collective-permute-done.5 = bf16[128,1024]{1,0:T(8,128)(2,1)S(1)} collective-permute-done((bf16[128,1024]{1,0:T(8,128)(2,1)S(1)}, bf16[128,1024]{1,0:T(8,128)(2,1)S(1)}, u32[]{:S(2)}, u32[]{:S(2)}) %collective-permute-start.5) | collective-permute-done | bytes 262176 | tf_op jit(solution)/shard_map/ppermute | solution.py:193
  19.2 0.0 collective-permute-start.6
  19.2 0.5 collective-permute-start
  19.7 7.5 %collective-permute-done.1.refs_0_ = bf16[192,1024]{1,0:T(8,128)(2,1)S(1)} collective-permute-done((bf16[192,1024]{1,0:T(8,128)(2,1)S(1)}, bf16[192,1024]{1,0:T(8,128)(2,1)S(1)}, u32[]{:S(2)}, u32[]{:S(2)}) %collective-permute-start.1) | collective-permute-done | bytes 393248 | tf_op jit(solution)/shard_map/ppermute | solution.py:193
  27.2 0.0 collective-permute-done.4.refs_2_
  27.2 0.0 collective-permute-done.6
  27.2 1.4 %collective-permute-done.3.refs_3_ = bf16[192,1024]{1,0:T(8,128)(2,1)S(1)} collective-permute-done((bf16[192,1024]{1,0:T(8,128)(2,1)S(1)}, bf16[192,1024]{1,0:T(8,128)(2,1)S(1)}, u32[]{:S(2)}, u32[]{:S(2)}) %collective-permute-start.3) | collective-permute-done | bytes 393248 | tf_op jit(solution)/shard_map/ppermute | solution.py:193
  28.6 0.5 collective-permute-start.9
  29.1 1.6 %collective-permute-start.10 = (bf16[192,1024]{1,0:T(8,128)(2,1)S(1)}, bf16[192,1024]{1,0:T(8,128)(2,1)S(1)}, u32[]{:S(2)}, u32[]{:S(2)}) collective-permute-start(bf16[192,1024]{1,0:T(8,128)(2,1)S(1)} %collective-permute-done.1.refs_0_), channel_id=1, source_target_pairs={{0,4},{2,6},{4,0},{6,2},{8,12},{10,14},{12,8},{14,10},{16,20},{18,... | collective-permute-start | bytes 1179656 | tf_op jit(solution)/shard_map/ppermute | solution.py:193
  30.7 0.4 collective-permute-start.7
  31.1 1.4 %collective-permute-start.8 = (bf16[96,1024]{1,0:T(8,128)(2,1)S(1)}, bf16[96,1024]{1,0:T(8,128)(2,1)S(1)}, u32[]{:S(2)}, u32[]{:S(2)}) collective-permute-start(bf16[96,1024]{1,0:T(8,128)(2,1)S(1)} %slice.320), channel_id=1, source_target_pairs={{0,6},{2,4},{4,2},{6,0},{8,14},{10,12},{12,10},{14,8},{16,22},{18,... | collective-permute-start | bytes 589832 | tf_op jit(solution)/shard_map/ppermute | solution.py:193
  32.6 0.0 collective-permute-done
  32.6 0.1 pad_maximum_fusion.cents
  32.6 1.8 %first_pass.3 = (f32[2,4,192]{2,1,0:T(4,128)S(1)}, f32[1,768]{1,0:T(1,128)S(1)}, bf16[768,1024]{1,0:T(8,128)(2,1)S(1)}) custom-call(bf16[512,1024]{1,0:T(8,128)(2,1)S(1)} %pad_maximum_fusion.cents, bf16[192,1024]{1,0:T(8,128)(2,1)S(1)} %convert_element_type.14.refs_0_, bf16[192,1024]{1,0:T(8,128)(2,1)S(1)} %collective-permute-done.2.refs_1_, ...), custom_call_target="tpu_custom_call" | custom-call | flops 805306368 | bytes 1572864 | tf_op jit(solution)/shard_map/first_pass/pallas_call | solution.py:69
  34.4 5.4 %collective-permute-done.9.refs_1_ = bf16[192,1024]{1,0:T(8,128)(2,1)S(1)} collective-permute-done((bf16[192,1024]{1,0:T(8,128)(2,1)S(1)}, bf16[192,1024]{1,0:T(8,128)(2,1)S(1)}, u32[]{:S(2)}, u32[]{:S(2)}) %collective-permute-start.9) | collective-permute-done | bytes 393248 | tf_op jit(solution)/shard_map/ppermute | solution.py:193
  39.8 1.0 %first_pass.4 = (f32[2,2,192]{2,1,0:T(2,128)S(1)}, f32[1,384]{1,0:T(1,128)S(1)}, bf16[384,1024]{1,0:T(8,128)(2,1)S(1)}) custom-call(bf16[512,1024]{1,0:T(8,128)(2,1)S(1)} %pad_maximum_fusion.cents, bf16[192,1024]{1,0:T(8,128)(2,1)S(1)} %collective-permute-done.1.refs_0_, bf16[192,1024]{1,0:T(8,128)(2,1)S(1)} %collective-permute-done.9.refs_1_), custom_call_target="tpu_custom_call" | custom-call | flops 402653184 | bytes 786432 | tf_op jit(solution)/shard_map/first_pass/pallas_call | solution.py:69
  40.8 0.0 collective-permute-done.7.refs_1_
  40.8 2.1 %collective-permute-done.8.refs_2_ = bf16[96,1024]{1,0:T(8,128)(2,1)S(1)} collective-permute-done((bf16[96,1024]{1,0:T(8,128)(2,1)S(1)}, bf16[96,1024]{1,0:T(8,128)(2,1)S(1)}, u32[]{:S(2)}, u32[]{:S(2)}) %collective-permute-start.8) | collective-permute-done | bytes 196640 | tf_op jit(solution)/shard_map/ppermute | solution.py:193
  42.9 0.0 collective-permute-done.10.refs_0_
  42.9 1.0 %first_pass.5 = (f32[2,2,192]{2,1,0:T(2,128)S(1)}, f32[1,384]{1,0:T(1,128)S(1)}, bf16[384,1024]{1,0:T(8,128)(2,1)S(1)}) custom-call(bf16[512,1024]{1,0:T(8,128)(2,1)S(1)} %pad_maximum_fusion.cents, bf16[192,1024]{1,0:T(8,128)(2,1)S(1)} %collective-permute-done.10.refs_0_, bf16[96,1024]{1,0:T(8,128)(2,1)S(1)} %collective-permute-done.7.refs_1_, ...), custom_call_target="tpu_custom_call" | custom-call | flops 402653184 | bytes 786432 | tf_op jit(solution)/shard_map/first_pass/pallas_call | solution.py:69
  44.1 9.8 %all_to_all.10 = f32[8,2,8,192]{3,2,1,0:T(8,128)S(1)} all-to-all(f32[8,2,8,192]{3,2,1,0:T(8,128)S(1)} %broadcast_in_dim.6), channel_id=1, replica_groups={{0,2,4,6,16,18,20,22},{8,10,12,14,24,26,28,30},{1,3,5,7,17,19,21,23},{9..., dimensions={0} | all-to-all | bytes 196608 | tf_op jit(solution)/shard_map/all_to_all | solution.py:247
  54.2 0.1 pad_maximum_fusion.8.refs_0_
  54.3 0.1 pad_maximum_fusion.9
  54.4 2.8 %sums_pass.3 = f32[256,1152]{1,0:T(8,128)S(1)} custom-call(bf16[512,1024]{1,0:T(8,128)(2,1)S(1)} %pad_maximum_fusion.cents, f32[2,768]{1,0:T(2,128)S(1)} %pad_maximum_fusion.8.refs_0_, f32[2,384]{1,0:T(2,128)S(1)} %get-tuple-element.61.refs_1_, f32[2,384]{1,0:T(2,128)S(1)} %get-tuple-element.62.refs_2_, f32[1,768]{1,0:T(1,128)S(1)} %get-tuple-element.54.refs_3_.refs_0_, ...), custom_call_target="tpu_custom_call" | custom-call | flops 1610612736 | bytes 3145728 | tf_op jit(solution)/shard_map/sums_pass/pallas_call | solution.py:112
  57.2 0.1 collective-permute-start.11
  57.3 2.3 %sums_pass.5 = f32[128,1152]{1,0:T(8,128)S(1)} custom-call(bf16[512,1024]{1,0:T(8,128)(2,1)S(1)} %pad_maximum_fusion.cents, f32[2,768]{1,0:T(2,128)S(1)} %pad_maximum_fusion.8.refs_0_, f32[2,384]{1,0:T(2,128)S(1)} %get-tuple-element.61.refs_1_, f32[2,384]{1,0:T(2,128)S(1)} %get-tuple-element.62.refs_2_, f32[1,768]{1,0:T(1,128)S(1)} %get-tuple-element.54.refs_3_.refs_0_, ...), custom_call_target="tpu_custom_call" | custom-call | flops 805306368 | bytes 3145728 | tf_op jit(solution)/shard_map/sums_pass/pallas_call | solution.py:112
  59.6 0.0 copy-start
  59.6 0.6 collective-permute-start.12
  60.2 0.0 collective-permute-done.11
  60.2 0.1 slice_add_fusion
  60.3 1.6 %collective-permute-start.13 = (bf16[128,1152]{1,0:T(8,128)(2,1)S(1)}, bf16[128,1152]{1,0:T(8,128)(2,1)S(1)}, u32[]{:S(2)}, u32[]{:S(2)}) collective-permute-start(bf16[128,1152]{1,0:T(8,128)(2,1)S(1)} %pad_maximum_fusion.2), channel_id=1, source_target_pairs={{0,8},{2,10},{4,12},{6,14},{8,0},{10,2},{12,4},{14,6},{16,24},{18,... | collective-permute-start | bytes 884744 | tf_op jit(solution)/shard_map/ppermute | solution.py:193
  61.9 0.0 copy-done
  61.9 2.3 %sums_pass.4 = f32[128,1152]{1,0:T(8,128)S(1)} custom-call(bf16[512,1024]{1,0:T(8,128)(2,1)S(1)} %pad_maximum_fusion.cents, f32[2,768]{1,0:T(2,128)S(1)} %pad_maximum_fusion.8.refs_0_, f32[2,384]{1,0:T(2,128)S(1)} %get-tuple-element.61.refs_1_, f32[2,384]{1,0:T(2,128)S(1)} %get-tuple-element.62.refs_2_, f32[1,768]{1,0:T(1,128)S(1)} %get-tuple-element.54.refs_3_.refs_0_, ...), custom_call_target="tpu_custom_call" | custom-call | flops 805306368 | bytes 3145728 | tf_op jit(solution)/shard_map/sums_pass/pallas_call | solution.py:112
  64.2 5.1 %collective-permute-done.13 = bf16[128,1152]{1,0:T(8,128)(2,1)S(1)} collective-permute-done((bf16[128,1152]{1,0:T(8,128)(2,1)S(1)}, bf16[128,1152]{1,0:T(8,128)(2,1)S(1)}, u32[]{:S(2)}, u32[]{:S(2)}) %collective-permute-start.13) | collective-permute-done | bytes 294944 | tf_op jit(solution)/shard_map/ppermute | solution.py:193
  69.4 0.2 fusion.1
  69.6 0.0 collective-permute-done.12
  69.6 0.1 broadcast_in_dim.8
  69.7 0.1 maximum_add_fusion
  69.8 0.1 slice_reduce_fusion
  69.9 0.9 %fusion.24 = (bf16[128,1024]{1,0:T(8,128)(2,1)S(1)}, f32[128,1024]{1,0:T(8,128)}) fusion(f32[128]{0:T(128)S(1)} %slice_reduce_fusion, f32[128,1152]{1,0:T(8,128)S(1)} %maximum_add_fusion), kind=kLoop, calls=%fused_computation.109 | loop fusion | flops 262144 | bytes 1311232 | tf_op jit(solution)/shard_map/convert_element_type | solution.py:299
  70.9 0.0 collective-permute-start.15
  70.9 1.5 %collective-permute-start.14 = (bf16[128,1024]{1,0:T(8,128)(2,1)S(1)}, bf16[128,1024]{1,0:T(8,128)(2,1)S(1)}, u32[]{:S(2)}, u32[]{:S(2)}) collective-permute-start(bf16[128,1024]{1,0:T(8,128)(2,1)S(1)} %get-tuple-element.76), channel_id=1, source_target_pairs={{0,8},{2,10},{4,12},{6,14},{8,0},{10,2},{12,4},{14,6},{16,24},{18,... | collective-permute-start | bytes 786440 | tf_op jit(solution)/shard_map/ppermute | solution.py:193
  72.4 0.0 collective-permute-done.15
  72.5 1.6 %second_pass.3 = (f32[3,4,192]{2,1,0:T(4,128)S(1)}, f32[3,2,192]{2,1,0:T(2,128)S(1)}, f32[3,2,192]{2,1,0:T(2,128)S(1)}) custom-call(bf16[256,1024]{1,0:T(8,128)(2,1)S(1)} %pad_maximum_fusion.1.cents, f32[1,768]{1,0:T(1,128)S(1)} %get-tuple-element.54.refs_3_.refs_0_, f32[1,384]{1,0:T(1,128)S(1)} %get-tuple-element.55.refs_4_.refs_1_, ...), custom_call_target="tpu_custom_call" | custom-call | flops 805306368 | bytes 3145728 | tf_op jit(solution)/shard_map/second_pass/pallas_call | solution.py:153
  74.1 5.5 %collective-permute-done.14.cents = bf16[128,1024]{1,0:T(8,128)(2,1)S(1)} collective-permute-done((bf16[128,1024]{1,0:T(8,128)(2,1)S(1)}, bf16[128,1024]{1,0:T(8,128)(2,1)S(1)}, u32[]{:S(2)}, u32[]{:S(2)}) %collective-permute-start.14) | collective-permute-done | bytes 262176 | tf_op jit(solution)/shard_map/ppermute | solution.py:193
  79.6 0.0 collective-permute-start.16
  79.6 1.2 %second_pass.4 = (f32[3,4,192]{2,1,0:T(4,128)S(1)}, f32[3,2,192]{2,1,0:T(2,128)S(1)}, f32[3,2,192]{2,1,0:T(2,128)S(1)}) custom-call(bf16[128,1024]{1,0:T(8,128)(2,1)S(1)} %collective-permute-done.14.cents, f32[1,768]{1,0:T(1,128)S(1)} %get-tuple-element.54.refs_3_.refs_0_, f32[1,384]{1,0:T(1,128)S(1)} %get-tuple-element.55.refs_4_.refs_1_, ...), custom_call_target="tpu_custom_call" | custom-call | flops 402653184 | bytes 3145728 | tf_op jit(solution)/shard_map/second_pass/pallas_call | solution.py:153
  80.8 0.3 collective-permute-done.16.cents
  81.1 1.2 %second_pass.5 = (f32[3,4,192]{2,1,0:T(4,128)S(1)}, f32[3,2,192]{2,1,0:T(2,128)S(1)}, f32[3,2,192]{2,1,0:T(2,128)S(1)}) custom-call(bf16[128,1024]{1,0:T(8,128)(2,1)S(1)} %collective-permute-done.16.cents, f32[1,768]{1,0:T(1,128)S(1)} %get-tuple-element.54.refs_3_.refs_0_, f32[1,384]{1,0:T(1,128)S(1)} %get-tuple-element.55.refs_4_.refs_1_, ...), custom_call_target="tpu_custom_call" | custom-call | flops 402653184 | bytes 3145728 | tf_op jit(solution)/shard_map/second_pass/pallas_call | solution.py:153
  82.4 0.1 stack.78
  82.6 9.0 %all_to_all.11 = f32[8,3,192]{2,1,0:T(4,128)S(1)} all-to-all(f32[8,3,192]{2,1,0:T(4,128)S(1)} %copy.74), channel_id=1, replica_groups={{0,2,4,6,16,18,20,22},{8,10,12,14,24,26,28,30},{1,3,5,7,17,19,21,23},{9..., dimensions={0} | all-to-all | bytes 36864 | tf_op jit(solution)/shard_map/all_to_all | solution.py:247
  91.7 0.6 divide_subtract_fusion
  (60 shorter events, 0.9 us)
Async XLA Ops:
  1.8 12.1 %collective-permute-start.2 = (bf16[192,1024]{1,0:T(8,128)(2,1)S(1)}, bf16[192,1024]{1,0:T(8,128)(2,1)S(1)}, u32[]{:S(2)}, u32[]{:S(2)}) collective-permute-start(bf16[192,1024]{1,0:T(8,128)(2,1)S(1)} %convert_element_type.14.refs_0_), channel_id=1, source_target_pairs={{0,2},{2,0},{4,6},{6,4},{8,10},{10,8},{12,14},{14,12},{16,18},{18,... | collective-permute-start | bytes 1179656 | tf_op jit(solution)/shard_map/ppermute | solution.py:193
  5.9 13.3 %collective-permute-start.5 = (bf16[128,1024]{1,0:T(8,128)(2,1)S(1)}, bf16[128,1024]{1,0:T(8,128)(2,1)S(1)}, u32[]{:S(2)}, u32[]{:S(2)}) collective-permute-start(bf16[128,1024]{1,0:T(8,128)(2,1)S(1)} %convert_element_type.13), channel_id=1, source_target_pairs={{0,8},{2,10},{4,12},{6,14},{8,0},{10,2},{12,4},{14,6},{16,24},{18,... | collective-permute-start | bytes 786440 | tf_op jit(solution)/shard_map/ppermute | solution.py:193
  7.5 19.7 %collective-permute-start.1 = (bf16[192,1024]{1,0:T(8,128)(2,1)S(1)}, bf16[192,1024]{1,0:T(8,128)(2,1)S(1)}, u32[]{:S(2)}, u32[]{:S(2)}) collective-permute-start(bf16[192,1024]{1,0:T(8,128)(2,1)S(1)} %convert_element_type.14.refs_0_), channel_id=1, source_target_pairs={{0,16},{2,18},{4,20},{6,22},{8,24},{10,26},{12,28},{14,30},{16,0},... | collective-permute-start | bytes 1179656 | tf_op jit(solution)/shard_map/ppermute | solution.py:193
  10.1 17.1 %collective-permute-start.4 = (bf16[192,1024]{1,0:T(8,128)(2,1)S(1)}, bf16[192,1024]{1,0:T(8,128)(2,1)S(1)}, u32[]{:S(2)}, u32[]{:S(2)}) collective-permute-start(bf16[192,1024]{1,0:T(8,128)(2,1)S(1)} %convert_element_type.14.refs_0_), channel_id=1, source_target_pairs={{0,4},{2,6},{4,0},{6,2},{8,12},{10,14},{12,8},{14,10},{16,20},{18,... | collective-permute-start | bytes 1179656 | tf_op jit(solution)/shard_map/ppermute | solution.py:193
  13.9 14.6 %collective-permute-start.3 = (bf16[192,1024]{1,0:T(8,128)(2,1)S(1)}, bf16[192,1024]{1,0:T(8,128)(2,1)S(1)}, u32[]{:S(2)}, u32[]{:S(2)}) collective-permute-start(bf16[192,1024]{1,0:T(8,128)(2,1)S(1)} %collective-permute-done.2.refs_1_), channel_id=1, source_target_pairs={{0,4},{2,6},{4,0},{6,2},{8,12},{10,14},{12,8},{14,10},{16,20},{18,... | collective-permute-start | bytes 1179656 | tf_op jit(solution)/shard_map/ppermute | solution.py:193
  19.2 8.0 %collective-permute-start.6 = (bf16[128,1024]{1,0:T(8,128)(2,1)S(1)}, bf16[128,1024]{1,0:T(8,128)(2,1)S(1)}, u32[]{:S(2)}, u32[]{:S(2)}) collective-permute-start(bf16[128,1024]{1,0:T(8,128)(2,1)S(1)} %collective-permute-done.5), channel_id=1, source_target_pairs={{0,1},{1,0},{2,3},{3,2},{4,5},{5,4},{6,7},{7,6},{8,9},{9,8},{10,11... | collective-permute-start | bytes 786440 | tf_op jit(solution)/shard_map/ppermute | solution.py:202
  19.2 13.3 %collective-permute-start = (bf16[128,1024]{1,0:T(8,128)(2,1)S(1)}, bf16[128,1024]{1,0:T(8,128)(2,1)S(1)}, u32[]{:S(2)}, u32[]{:S(2)}) collective-permute-start(bf16[128,1024]{1,0:T(8,128)(2,1)S(1)} %convert_element_type.13), channel_id=1, source_target_pairs={{0,1},{1,0},{2,3},{3,2},{4,5},{5,4},{6,7},{7,6},{8,9},{9,8},{10,11... | collective-permute-start | bytes 786440 | tf_op jit(solution)/shard_map/ppermute | solution.py:202
  28.6 11.2 %collective-permute-start.9 = (bf16[192,1024]{1,0:T(8,128)(2,1)S(1)}, bf16[192,1024]{1,0:T(8,128)(2,1)S(1)}, u32[]{:S(2)}, u32[]{:S(2)}) collective-permute-start(bf16[192,1024]{1,0:T(8,128)(2,1)S(1)} %collective-permute-done.1.refs_0_), channel_id=1, source_target_pairs={{0,2},{2,0},{4,6},{6,4},{8,10},{10,8},{12,14},{14,12},{16,18},{18,... | collective-permute-start | bytes 1179656 | tf_op jit(solution)/shard_map/ppermute | solution.py:193
  29.1 13.8 %collective-permute-start.10 = (bf16[192,1024]{1,0:T(8,128)(2,1)S(1)}, bf16[192,1024]{1,0:T(8,128)(2,1)S(1)}, u32[]{:S(2)}, u32[]{:S(2)}) collective-permute-start(bf16[192,1024]{1,0:T(8,128)(2,1)S(1)} %collective-permute-done.1.refs_0_), channel_id=1, source_target_pairs={{0,4},{2,6},{4,0},{6,2},{8,12},{10,14},{12,8},{14,10},{16,20},{18,... | collective-permute-start | bytes 1179656 | tf_op jit(solution)/shard_map/ppermute | solution.py:193
  30.7 10.1 %collective-permute-start.7 = (bf16[96,1024]{1,0:T(8,128)(2,1)S(1)}, bf16[96,1024]{1,0:T(8,128)(2,1)S(1)}, u32[]{:S(2)}, u32[]{:S(2)}) collective-permute-start(bf16[96,1024]{1,0:T(8,128)(2,1)S(1)} %slice.319), channel_id=1, source_target_pairs={{0,16},{2,18},{4,20},{6,22},{8,24},{10,26},{12,28},{14,30},{16,0},... | collective-permute-start | bytes 589832 | tf_op jit(solution)/shard_map/ppermute | solution.py:193
  31.1 11.7 %collective-permute-start.8 = (bf16[96,1024]{1,0:T(8,128)(2,1)S(1)}, bf16[96,1024]{1,0:T(8,128)(2,1)S(1)}, u32[]{:S(2)}, u32[]{:S(2)}) collective-permute-start(bf16[96,1024]{1,0:T(8,128)(2,1)S(1)} %slice.320), channel_id=1, source_target_pairs={{0,6},{2,4},{4,2},{6,0},{8,14},{10,12},{12,10},{14,8},{16,22},{18,... | collective-permute-start | bytes 589832 | tf_op jit(solution)/shard_map/ppermute | solution.py:193
  57.2 2.9 %collective-permute-start.11 = (f32[128,1152]{1,0:T(8,128)S(1)}, f32[128,1152]{1,0:T(8,128)S(1)}, u32[]{:S(2)}, u32[]{:S(2)}) collective-permute-start(f32[128,1152]{1,0:T(8,128)S(1)} %slice.441), channel_id=1, source_target_pairs={{0,1},{1,0},{2,3},{3,2},{4,5},{5,4},{6,7},{7,6},{8,9},{9,8},{10,11... | collective-permute-start | bytes 1769480 | tf_op jit(solution)/shard_map/ppermute | solution.py:202
  59.6 2.3 %copy-start = (f32[128,1024]{1,0:T(8,128)S(1)}, f32[128,1024]{1,0:T(8,128)}, u32[]{:S(2)}) copy-start(f32[128,1024]{1,0:T(8,128)} %refs_9_.1) | copy-start | bytes 1572868
  59.6 10.0 %collective-permute-start.12 = (f32[128,1152]{1,0:T(8,128)S(1)}, f32[128,1152]{1,0:T(8,128)S(1)}, u32[]{:S(2)}, u32[]{:S(2)}) collective-permute-start(f32[128,1152]{1,0:T(8,128)S(1)} %sums_pass.5), channel_id=1, source_target_pairs={{0,1},{1,0},{2,3},{3,2},{4,5},{5,4},{6,7},{7,6},{8,9},{9,8},{10,11... | collective-permute-start | bytes 1769480 | tf_op jit(solution)/shard_map/ppermute | solution.py:202
  60.3 9.0 %collective-permute-start.13 = (bf16[128,1152]{1,0:T(8,128)(2,1)S(1)}, bf16[128,1152]{1,0:T(8,128)(2,1)S(1)}, u32[]{:S(2)}, u32[]{:S(2)}) collective-permute-start(bf16[128,1152]{1,0:T(8,128)(2,1)S(1)} %pad_maximum_fusion.2), channel_id=1, source_target_pairs={{0,8},{2,10},{4,12},{6,14},{8,0},{10,2},{12,4},{14,6},{16,24},{18,... | collective-permute-start | bytes 884744 | tf_op jit(solution)/shard_map/ppermute | solution.py:193
  70.9 1.5 %collective-permute-start.15 = (bf16[128,1024]{1,0:T(8,128)(2,1)S(1)}, bf16[128,1024]{1,0:T(8,128)(2,1)S(1)}, u32[]{:S(2)}, u32[]{:S(2)}) collective-permute-start(bf16[128,1024]{1,0:T(8,128)(2,1)S(1)} %get-tuple-element.76), channel_id=1, source_target_pairs={{0,1},{1,0},{2,3},{3,2},{4,5},{5,4},{6,7},{7,6},{8,9},{9,8},{10,11... | collective-permute-start | bytes 786440 | tf_op jit(solution)/shard_map/ppermute | solution.py:202
  70.9 8.7 %collective-permute-start.14 = (bf16[128,1024]{1,0:T(8,128)(2,1)S(1)}, bf16[128,1024]{1,0:T(8,128)(2,1)S(1)}, u32[]{:S(2)}, u32[]{:S(2)}) collective-permute-start(bf16[128,1024]{1,0:T(8,128)(2,1)S(1)} %get-tuple-element.76), channel_id=1, source_target_pairs={{0,8},{2,10},{4,12},{6,14},{8,0},{10,2},{12,4},{14,6},{16,24},{18,... | collective-permute-start | bytes 786440 | tf_op jit(solution)/shard_map/ppermute | solution.py:193
  79.6 1.5 %collective-permute-start.16 = (bf16[128,1024]{1,0:T(8,128)(2,1)S(1)}, bf16[128,1024]{1,0:T(8,128)(2,1)S(1)}, u32[]{:S(2)}, u32[]{:S(2)}) collective-permute-start(bf16[128,1024]{1,0:T(8,128)(2,1)S(1)} %collective-permute-done.14.cents), channel_id=1, source_target_pairs={{0,1},{1,0},{2,3},{3,2},{4,5},{5,4},{6,7},{7,6},{8,9},{9,8},{10,11... | collective-permute-start | bytes 786440 | tf_op jit(solution)/shard_map/ppermute | solution.py:202

commit v16 on v15

--- a/solution.py
+++ b/solution.py
@@ -281,16 +281,17 @@
         stats = by_position(jnp.stack([top, total]))
         final = [jnp.concatenate([stats[:, b] for b in bits], axis=1) for bits in GROUPS]
 
-        far = scatter_cent(sums_pass(piece, final, row_sqs, rows, n_near, 2 * n_near))
+        n_half = n_near // 2
+        far_other = sums_pass(piece, final, row_sqs, rows, n_near + n_half, 2 * n_near)
+        middle = sums_pass(piece, final, row_sqs, rows, n_half, n_near + n_half)
+        far = scatter_cent(middle[n_half:], far_other)
         count = far[:, width:]
         coarse = lax.reduce_precision(count, 8, 7)
         lane = lax.broadcasted_iota(jnp.int32, count.shape, 1)
         far = jnp.concatenate([far[:, :width], jnp.where(lane < 64, coarse, count - coarse)], axis=1)
         far = far.astype(jnp.bfloat16)
-        n_half = n_near // 2
-        other = sums_pass(piece, final, row_sqs, rows, n_half, n_near)
         near = sums_pass(piece, hold(final, far)[0], row_sqs, rows, 0, n_half, [centroids])
-        near = scatter_cent(near, other)
+        near = scatter_cent(near, middle[:n_half])
         far = flip(far, top_bit).astype(jnp.float32)
         counts = far[:, width : width + 1] + far[:, width + 64 : width + 65]
         far = jnp.concatenate([far[:, :width], jnp.broadcast_to(counts, count.shape)], axis=1)

time: 92.5 us -> 92.5 us (level)
  waiting for transfers between devices: 33.1 us -> 32.1 us
  other arithmetic: 4.97 us -> 5.92 us
    concatenate x1, other arithmetic: 0.07 us -> 1.02 us  [on_device(): piece = jnp.concatenate(near + far, axis=0)]
    ppermute x11, waiting for transfers between devices: 32.7 us -> 31.8 us  [flip(): return lax.ppermute(value, 'dp', [(i, i ^ bits) for i in range(n_dp)])]
  transfers between devices with their start and end apart: 17 -> 17, of which waited for: 9 -> 9; matrix products, arithmetic and copies ran while one was open for 2% -> 3% of each run, Pallas kernels for 11% -> 12%
where the time goes in v16:
time: 92.5 us; the launch traced here: 92.2 us
  waiting for transfers between devices  32.1 us (35%)
  blocking collectives  18.8 us (20%)
  starting transfers between devices  18.7 us (20%)
  Pallas kernels  15.1 us (16%)
  other arithmetic  5.92 us (6%)
  between operations  1.07 us (1%)
    ppermute x11, waiting for transfers between devices, flip(): return lax.ppermute(value, 'dp', [(i, i ^ bits) for i in range(n_dp)])  31.8 us
    all_to_all x2, blocking collectives, exchange(): return lax.all_to_all(value, 'dp', 0, 0, axis_index_groups=groups)  18.8 us
    ppermute x11, starting transfers between devices, flip(): return lax.ppermute(value, 'dp', [(i, i ^ bits) for i in range(n_dp)])  17.6 us
    pallas_call x3, Pallas kernels, sums_pass(): pl.pallas_call(functools.partial(sums_kernel, first, last, n), out_shape=...  7.32 us
    pallas_call x3, Pallas kernels, second_pass(): pl.pallas_call(functools.partial(second_kernel, shard, n), out_shape=tupl...  4 us
    pallas_call x3, Pallas kernels, first_pass(): pl.pallas_call(functools.partial(first_kernel, len(chunks), shard), out_s...  3.77 us
  transfers between devices with their start and end apart: 17, of which 9 were waited for; matrix products, arithmetic and copies ran while one was open for 3% of the time, Pallas kernels for 12%

profile of v16, /device:TPU:0, one launch (start us, length us, event | category | flops | bytes accessed | tf_op | source)
XLA Modules:
  0.0 92.2 jit_solution(9900573924430586856)
XLA Ops:
  0.6 1.2 %convert_element_type.14.refs_0_ = bf16[192,1024]{1,0:T(8,128)(2,1)S(1)} convert(f32[192,1024]{1,0:T(8,128)} %param.2) | non-fusion elementwise | flops 196608 | bytes 1179648 | tf_op jit(solution)/shard_map/convert_element_type | solution.py:258
  1.8 3.0 %collective-permute-start.2 = (bf16[192,1024]{1,0:T(8,128)(2,1)S(1)}, bf16[192,1024]{1,0:T(8,128)(2,1)S(1)}, u32[]{:S(2)}, u32[]{:S(2)}) collective-permute-start(bf16[192,1024]{1,0:T(8,128)(2,1)S(1)} %convert_element_type.14.refs_0_), channel_id=1, source_target_pairs={{0,2},{2,0},{4,6},{6,4},{8,10},{10,8},{12,14},{14,12},{16,18},{18,... | collective-permute-start | bytes 1179656 | tf_op jit(solution)/shard_map/ppermute | solution.py:193
  4.8 1.1 %convert_element_type.13 = bf16[128,1024]{1,0:T(8,128)(2,1)S(1)} convert(f32[128,1024]{1,0:T(8,128)} %refs_9_.1) | non-fusion elementwise | flops 131072 | bytes 786432 | tf_op jit(solution)/shard_map/convert_element_type | solution.py:262
  5.9 1.6 %collective-permute-start.5 = (bf16[128,1024]{1,0:T(8,128)(2,1)S(1)}, bf16[128,1024]{1,0:T(8,128)(2,1)S(1)}, u32[]{:S(2)}, u32[]{:S(2)}) collective-permute-start(bf16[128,1024]{1,0:T(8,128)(2,1)S(1)} %convert_element_type.13), channel_id=1, source_target_pairs={{0,8},{2,10},{4,12},{6,14},{8,0},{10,2},{12,4},{14,6},{16,24},{18,... | collective-permute-start | bytes 786440 | tf_op jit(solution)/shard_map/ppermute | solution.py:193
  7.5 2.6 %collective-permute-start.1 = (bf16[192,1024]{1,0:T(8,128)(2,1)S(1)}, bf16[192,1024]{1,0:T(8,128)(2,1)S(1)}, u32[]{:S(2)}, u32[]{:S(2)}) collective-permute-start(bf16[192,1024]{1,0:T(8,128)(2,1)S(1)} %convert_element_type.14.refs_0_), channel_id=1, source_target_pairs={{0,16},{2,18},{4,20},{6,22},{8,24},{10,26},{12,28},{14,30},{16,0},... | collective-permute-start | bytes 1179656 | tf_op jit(solution)/shard_map/ppermute | solution.py:193
  10.1 1.5 %collective-permute-start.4 = (bf16[192,1024]{1,0:T(8,128)(2,1)S(1)}, bf16[192,1024]{1,0:T(8,128)(2,1)S(1)}, u32[]{:S(2)}, u32[]{:S(2)}) collective-permute-start(bf16[192,1024]{1,0:T(8,128)(2,1)S(1)} %convert_element_type.14.refs_0_), channel_id=1, source_target_pairs={{0,4},{2,6},{4,0},{6,2},{8,12},{10,14},{12,8},{14,10},{16,20},{18,... | collective-permute-start | bytes 1179656 | tf_op jit(solution)/shard_map/ppermute | solution.py:193
  11.7 2.3 %collective-permute-done.2.refs_1_ = bf16[192,1024]{1,0:T(8,128)(2,1)S(1)} collective-permute-done((bf16[192,1024]{1,0:T(8,128)(2,1)S(1)}, bf16[192,1024]{1,0:T(8,128)(2,1)S(1)}, u32[]{:S(2)}, u32[]{:S(2)}) %collective-permute-start.2) | collective-permute-done | bytes 393248 | tf_op jit(solution)/shard_map/ppermute | solution.py:193
  13.9 1.8 %collective-permute-start.3 = (bf16[192,1024]{1,0:T(8,128)(2,1)S(1)}, bf16[192,1024]{1,0:T(8,128)(2,1)S(1)}, u32[]{:S(2)}, u32[]{:S(2)}) collective-permute-start(bf16[192,1024]{1,0:T(8,128)(2,1)S(1)} %collective-permute-done.2.refs_1_), channel_id=1, source_target_pairs={{0,4},{2,6},{4,0},{6,2},{8,12},{10,14},{12,8},{14,10},{16,20},{18,... | collective-permute-start | bytes 1179656 | tf_op jit(solution)/shard_map/ppermute | solution.py:193
  15.7 3.5 %collective-permute-done.5 = bf16[128,1024]{1,0:T(8,128)(2,1)S(1)} collective-permute-done((bf16[128,1024]{1,0:T(8,128)(2,1)S(1)}, bf16[128,1024]{1,0:T(8,128)(2,1)S(1)}, u32[]{:S(2)}, u32[]{:S(2)}) %collective-permute-start.5) | collective-permute-done | bytes 262176 | tf_op jit(solution)/shard_map/ppermute | solution.py:193
  19.2 0.0 collective-permute-start.6
  19.2 0.5 collective-permute-start
  19.7 7.5 %collective-permute-done.1.refs_0_ = bf16[192,1024]{1,0:T(8,128)(2,1)S(1)} collective-permute-done((bf16[192,1024]{1,0:T(8,128)(2,1)S(1)}, bf16[192,1024]{1,0:T(8,128)(2,1)S(1)}, u32[]{:S(2)}, u32[]{:S(2)}) %collective-permute-start.1) | collective-permute-done | bytes 393248 | tf_op jit(solution)/shard_map/ppermute | solution.py:193
  27.2 0.0 collective-permute-done.4.refs_2_
  27.2 0.0 collective-permute-done.6
  27.2 1.4 %collective-permute-done.3.refs_3_ = bf16[192,1024]{1,0:T(8,128)(2,1)S(1)} collective-permute-done((bf16[192,1024]{1,0:T(8,128)(2,1)S(1)}, bf16[192,1024]{1,0:T(8,128)(2,1)S(1)}, u32[]{:S(2)}, u32[]{:S(2)}) %collective-permute-start.3) | collective-permute-done | bytes 393248 | tf_op jit(solution)/shard_map/ppermute | solution.py:193
  28.6 0.5 collective-permute-start.9
  29.1 1.5 %collective-permute-start.10 = (bf16[192,1024]{1,0:T(8,128)(2,1)S(1)}, bf16[192,1024]{1,0:T(8,128)(2,1)S(1)}, u32[]{:S(2)}, u32[]{:S(2)}) collective-permute-start(bf16[192,1024]{1,0:T(8,128)(2,1)S(1)} %collective-permute-done.1.refs_0_), channel_id=1, source_target_pairs={{0,4},{2,6},{4,0},{6,2},{8,12},{10,14},{12,8},{14,10},{16,20},{18,... | collective-permute-start | bytes 1179656 | tf_op jit(solution)/shard_map/ppermute | solution.py:193
  30.6 1.5 %collective-permute-start.8 = (bf16[96,1024]{1,0:T(8,128)(2,1)S(1)}, bf16[96,1024]{1,0:T(8,128)(2,1)S(1)}, u32[]{:S(2)}, u32[]{:S(2)}) collective-permute-start(bf16[96,1024]{1,0:T(8,128)(2,1)S(1)} %slice.320), channel_id=1, source_target_pairs={{0,6},{2,4},{4,2},{6,0},{8,14},{10,12},{12,10},{14,8},{16,22},{18,... | collective-permute-start | bytes 589832 | tf_op jit(solution)/shard_map/ppermute | solution.py:193
  32.2 0.4 collective-permute-start.7
  32.6 0.0 collective-permute-done
  32.6 1.0 %pad_maximum_fusion.cents = bf16[512,1024]{1,0:T(8,128)(2,1)S(1)} fusion(bf16[128,1024]{1,0:T(8,128)(2,1)S(1)} %collective-permute-done.6, bf16[128,1024]{1,0:T(8,128)(2,1)S(1)} %collective-permute-done.5, bf16[128,1024]{1,0:T(8,128)(2,1)} %collective-permute-done, bf16[128,1024]{1,0:T(8,128)(2,1)S(1)} %convert_element_type.13), kind=kLoop, calls=%fused_computation | loop fusion | flops 4194304 | bytes 2097152 | tf_op jit(solution)/shard_map/concatenate | solution.py:271
  33.6 1.8 %first_pass.3 = (f32[2,4,192]{2,1,0:T(4,128)S(1)}, f32[1,768]{1,0:T(1,128)S(1)}, bf16[768,1024]{1,0:T(8,128)(2,1)S(1)}) custom-call(bf16[512,1024]{1,0:T(8,128)(2,1)S(1)} %pad_maximum_fusion.cents, bf16[192,1024]{1,0:T(8,128)(2,1)S(1)} %convert_element_type.14.refs_0_, bf16[192,1024]{1,0:T(8,128)(2,1)S(1)} %collective-permute-done.2.refs_1_, ...), custom_call_target="tpu_custom_call" | custom-call | flops 805306368 | bytes 1572864 | tf_op jit(solution)/shard_map/first_pass/pallas_call | solution.py:69
  35.3 4.4 %collective-permute-done.9.refs_1_ = bf16[192,1024]{1,0:T(8,128)(2,1)S(1)} collective-permute-done((bf16[192,1024]{1,0:T(8,128)(2,1)S(1)}, bf16[192,1024]{1,0:T(8,128)(2,1)S(1)}, u32[]{:S(2)}, u32[]{:S(2)}) %collective-permute-start.9) | collective-permute-done | bytes 393248 | tf_op jit(solution)/shard_map/ppermute | solution.py:193
  39.8 1.0 %first_pass.4 = (f32[2,2,192]{2,1,0:T(2,128)S(1)}, f32[1,384]{1,0:T(1,128)S(1)}, bf16[384,1024]{1,0:T(8,128)(2,1)S(1)}) custom-call(bf16[512,1024]{1,0:T(8,128)(2,1)S(1)} %pad_maximum_fusion.cents, bf16[192,1024]{1,0:T(8,128)(2,1)S(1)} %collective-permute-done.1.refs_0_, bf16[192,1024]{1,0:T(8,128)(2,1)S(1)} %collective-permute-done.9.refs_1_), custom_call_target="tpu_custom_call" | custom-call | flops 402653184 | bytes 786432 | tf_op jit(solution)/shard_map/first_pass/pallas_call | solution.py:69
  40.8 2.1 %collective-permute-done.8.refs_2_ = bf16[96,1024]{1,0:T(8,128)(2,1)S(1)} collective-permute-done((bf16[96,1024]{1,0:T(8,128)(2,1)S(1)}, bf16[96,1024]{1,0:T(8,128)(2,1)S(1)}, u32[]{:S(2)}, u32[]{:S(2)}) %collective-permute-start.8) | collective-permute-done | bytes 196640 | tf_op jit(solution)/shard_map/ppermute | solution.py:193
  42.8 0.0 collective-permute-done.7.refs_1_
  42.8 0.0 collective-permute-done.10.refs_0_
  42.8 1.0 %first_pass.5 = (f32[2,2,192]{2,1,0:T(2,128)S(1)}, f32[1,384]{1,0:T(1,128)S(1)}, bf16[384,1024]{1,0:T(8,128)(2,1)S(1)}) custom-call(bf16[512,1024]{1,0:T(8,128)(2,1)S(1)} %pad_maximum_fusion.cents, bf16[192,1024]{1,0:T(8,128)(2,1)S(1)} %collective-permute-done.10.refs_0_, bf16[96,1024]{1,0:T(8,128)(2,1)S(1)} %collective-permute-done.7.refs_1_, ...), custom_call_target="tpu_custom_call" | custom-call | flops 402653184 | bytes 786432 | tf_op jit(solution)/shard_map/first_pass/pallas_call | solution.py:69
  44.1 9.8 %all_to_all.10 = f32[8,2,8,192]{3,2,1,0:T(8,128)S(1)} all-to-all(f32[8,2,8,192]{3,2,1,0:T(8,128)S(1)} %broadcast_in_dim.6), channel_id=1, replica_groups={{0,2,4,6,16,18,20,22},{8,10,12,14,24,26,28,30},{1,3,5,7,17,19,21,23},{9..., dimensions={0} | all-to-all | bytes 196608 | tf_op jit(solution)/shard_map/all_to_all | solution.py:247
  54.3 0.1 pad_maximum_fusion.9
  54.3 0.1 pad_maximum_fusion.8.refs_0_
  54.4 2.3 %sums_pass.4 = f32[128,1152]{1,0:T(8,128)S(1)} custom-call(bf16[512,1024]{1,0:T(8,128)(2,1)S(1)} %pad_maximum_fusion.cents, f32[2,768]{1,0:T(2,128)S(1)} %pad_maximum_fusion.8.refs_0_, f32[2,384]{1,0:T(2,128)S(1)} %get-tuple-element.61.refs_1_, f32[2,384]{1,0:T(2,128)S(1)} %get-tuple-element.62.refs_2_, f32[1,768]{1,0:T(1,128)S(1)} %get-tuple-element.54.refs_3_.refs_0_, ...), custom_call_target="tpu_custom_call" | custom-call | flops 805306368 | bytes 3145728 | tf_op jit(solution)/shard_map/sums_pass/pallas_call | solution.py:112
  56.7 0.1 collective-permute-start.11
  56.8 2.8 %sums_pass.3 = f32[256,1152]{1,0:T(8,128)S(1)} custom-call(bf16[512,1024]{1,0:T(8,128)(2,1)S(1)} %pad_maximum_fusion.cents, f32[2,768]{1,0:T(2,128)S(1)} %pad_maximum_fusion.8.refs_0_, f32[2,384]{1,0:T(2,128)S(1)} %get-tuple-element.61.refs_1_, f32[2,384]{1,0:T(2,128)S(1)} %get-tuple-element.62.refs_2_, f32[1,768]{1,0:T(1,128)S(1)} %get-tuple-element.54.refs_3_.refs_0_, ...), custom_call_target="tpu_custom_call" | custom-call | flops 1610612736 | bytes 3145728 | tf_op jit(solution)/shard_map/sums_pass/pallas_call | solution.py:112
  59.6 0.0 copy-start
  59.6 0.0 collective-permute-done.11
  59.6 0.1 fusion.25
  59.7 0.6 collective-permute-start.12
  60.3 1.6 %collective-permute-start.13 = (bf16[128,1152]{1,0:T(8,128)(2,1)S(1)}, bf16[128,1152]{1,0:T(8,128)(2,1)S(1)}, u32[]{:S(2)}, u32[]{:S(2)}) collective-permute-start(bf16[128,1152]{1,0:T(8,128)(2,1)S(1)} %pad_maximum_fusion.2), channel_id=1, source_target_pairs={{0,8},{2,10},{4,12},{6,14},{8,0},{10,2},{12,4},{14,6},{16,24},{18,... | collective-permute-start | bytes 884744 | tf_op jit(solution)/shard_map/ppermute | solution.py:193
  61.9 0.0 copy-done
  61.9 2.3 %sums_pass.5 = f32[128,1152]{1,0:T(8,128)S(1)} custom-call(bf16[512,1024]{1,0:T(8,128)(2,1)S(1)} %pad_maximum_fusion.cents, f32[2,768]{1,0:T(2,128)S(1)} %pad_maximum_fusion.8.refs_0_, f32[2,384]{1,0:T(2,128)S(1)} %get-tuple-element.61.refs_1_, f32[2,384]{1,0:T(2,128)S(1)} %get-tuple-element.62.refs_2_, f32[1,768]{1,0:T(1,128)S(1)} %get-tuple-element.54.refs_3_.refs_0_, ...), custom_call_target="tpu_custom_call" | custom-call | flops 805306368 | bytes 3145728 | tf_op jit(solution)/shard_map/sums_pass/pallas_call | solution.py:112
  64.2 5.1 %collective-permute-done.13 = bf16[128,1152]{1,0:T(8,128)(2,1)S(1)} collective-permute-done((bf16[128,1152]{1,0:T(8,128)(2,1)S(1)}, bf16[128,1152]{1,0:T(8,128)(2,1)S(1)}, u32[]{:S(2)}, u32[]{:S(2)}) %collective-permute-start.13) | collective-permute-done | bytes 294944 | tf_op jit(solution)/shard_map/ppermute | solution.py:193
  69.4 0.2 fusion.1
  69.6 0.0 collective-permute-done.12
  69.6 0.1 broadcast_in_dim.8
  69.7 0.1 maximum_add_fusion
  69.8 0.1 slice_reduce_fusion
  69.9 0.9 %fusion.24 = (bf16[128,1024]{1,0:T(8,128)(2,1)S(1)}, f32[128,1024]{1,0:T(8,128)}) fusion(f32[128]{0:T(128)S(1)} %slice_reduce_fusion, f32[128,1152]{1,0:T(8,128)S(1)} %maximum_add_fusion), kind=kLoop, calls=%fused_computation.109 | loop fusion | flops 262144 | bytes 1311232 | tf_op jit(solution)/shard_map/convert_element_type | solution.py:300
  70.9 0.0 collective-permute-start.15
  70.9 1.5 %collective-permute-start.14 = (bf16[128,1024]{1,0:T(8,128)(2,1)S(1)}, bf16[128,1024]{1,0:T(8,128)(2,1)S(1)}, u32[]{:S(2)}, u32[]{:S(2)}) collective-permute-start(bf16[128,1024]{1,0:T(8,128)(2,1)S(1)} %get-tuple-element.76), channel_id=1, source_target_pairs={{0,8},{2,10},{4,12},{6,14},{8,0},{10,2},{12,4},{14,6},{16,24},{18,... | collective-permute-start | bytes 786440 | tf_op jit(solution)/shard_map/ppermute | solution.py:193
  72.4 0.0 collective-permute-done.15
  72.4 1.6 %second_pass.3 = (f32[3,4,192]{2,1,0:T(4,128)S(1)}, f32[3,2,192]{2,1,0:T(2,128)S(1)}, f32[3,2,192]{2,1,0:T(2,128)S(1)}) custom-call(bf16[256,1024]{1,0:T(8,128)(2,1)S(1)} %pad_maximum_fusion.1.cents, f32[1,768]{1,0:T(1,128)S(1)} %get-tuple-element.54.refs_3_.refs_0_, f32[1,384]{1,0:T(1,128)S(1)} %get-tuple-element.55.refs_4_.refs_1_, ...), custom_call_target="tpu_custom_call" | custom-call | flops 805306368 | bytes 3145728 | tf_op jit(solution)/shard_map/second_pass/pallas_call | solution.py:153
  74.1 5.5 %collective-permute-done.14.cents = bf16[128,1024]{1,0:T(8,128)(2,1)S(1)} collective-permute-done((bf16[128,1024]{1,0:T(8,128)(2,1)S(1)}, bf16[128,1024]{1,0:T(8,128)(2,1)S(1)}, u32[]{:S(2)}, u32[]{:S(2)}) %collective-permute-start.14) | collective-permute-done | bytes 262176 | tf_op jit(solution)/shard_map/ppermute | solution.py:193
  79.6 0.0 collective-permute-start.16
  79.6 1.2 %second_pass.4 = (f32[3,4,192]{2,1,0:T(4,128)S(1)}, f32[3,2,192]{2,1,0:T(2,128)S(1)}, f32[3,2,192]{2,1,0:T(2,128)S(1)}) custom-call(bf16[128,1024]{1,0:T(8,128)(2,1)S(1)} %collective-permute-done.14.cents, f32[1,768]{1,0:T(1,128)S(1)} %get-tuple-element.54.refs_3_.refs_0_, f32[1,384]{1,0:T(1,128)S(1)} %get-tuple-element.55.refs_4_.refs_1_, ...), custom_call_target="tpu_custom_call" | custom-call | flops 402653184 | bytes 3145728 | tf_op jit(solution)/shard_map/second_pass/pallas_call | solution.py:153
  80.8 0.3 collective-permute-done.16.cents
  81.1 1.2 %second_pass.5 = (f32[3,4,192]{2,1,0:T(4,128)S(1)}, f32[3,2,192]{2,1,0:T(2,128)S(1)}, f32[3,2,192]{2,1,0:T(2,128)S(1)}) custom-call(bf16[128,1024]{1,0:T(8,128)(2,1)S(1)} %collective-permute-done.16.cents, f32[1,768]{1,0:T(1,128)S(1)} %get-tuple-element.54.refs_3_.refs_0_, f32[1,384]{1,0:T(1,128)S(1)} %get-tuple-element.55.refs_4_.refs_1_, ...), custom_call_target="tpu_custom_call" | custom-call | flops 402653184 | bytes 3145728 | tf_op jit(solution)/shard_map/second_pass/pallas_call | solution.py:153
  82.4 0.1 stack.78
  82.6 9.0 %all_to_all.11 = f32[8,3,192]{2,1,0:T(4,128)S(1)} all-to-all(f32[8,3,192]{2,1,0:T(4,128)S(1)} %copy.74), channel_id=1, replica_groups={{0,2,4,6,16,18,20,22},{8,10,12,14,24,26,28,30},{1,3,5,7,17,19,21,23},{9..., dimensions={0} | all-to-all | bytes 36864 | tf_op jit(solution)/shard_map/all_to_all | solution.py:247
  91.6 0.6 divide_subtract_fusion
  (59 shorter events, 0.9 us)
Async XLA Ops:
  1.8 12.1 %collective-permute-start.2 = (bf16[192,1024]{1,0:T(8,128)(2,1)S(1)}, bf16[192,1024]{1,0:T(8,128)(2,1)S(1)}, u32[]{:S(2)}, u32[]{:S(2)}) collective-permute-start(bf16[192,1024]{1,0:T(8,128)(2,1)S(1)} %convert_element_type.14.refs_0_), channel_id=1, source_target_pairs={{0,2},{2,0},{4,6},{6,4},{8,10},{10,8},{12,14},{14,12},{16,18},{18,... | collective-permute-start | bytes 1179656 | tf_op jit(solution)/shard_map/ppermute | solution.py:193
  5.9 13.3 %collective-permute-start.5 = (bf16[128,1024]{1,0:T(8,128)(2,1)S(1)}, bf16[128,1024]{1,0:T(8,128)(2,1)S(1)}, u32[]{:S(2)}, u32[]{:S(2)}) collective-permute-start(bf16[128,1024]{1,0:T(8,128)(2,1)S(1)} %convert_element_type.13), channel_id=1, source_target_pairs={{0,8},{2,10},{4,12},{6,14},{8,0},{10,2},{12,4},{14,6},{16,24},{18,... | collective-permute-start | bytes 786440 | tf_op jit(solution)/shard_map/ppermute | solution.py:193
  7.5 19.7 %collective-permute-start.1 = (bf16[192,1024]{1,0:T(8,128)(2,1)S(1)}, bf16[192,1024]{1,0:T(8,128)(2,1)S(1)}, u32[]{:S(2)}, u32[]{:S(2)}) collective-permute-start(bf16[192,1024]{1,0:T(8,128)(2,1)S(1)} %convert_element_type.14.refs_0_), channel_id=1, source_target_pairs={{0,16},{2,18},{4,20},{6,22},{8,24},{10,26},{12,28},{14,30},{16,0},... | collective-permute-start | bytes 1179656 | tf_op jit(solution)/shard_map/ppermute | solution.py:193
  10.1 17.1 %collective-permute-start.4 = (bf16[192,1024]{1,0:T(8,128)(2,1)S(1)}, bf16[192,1024]{1,0:T(8,128)(2,1)S(1)}, u32[]{:S(2)}, u32[]{:S(2)}) collective-permute-start(bf16[192,1024]{1,0:T(8,128)(2,1)S(1)} %convert_element_type.14.refs_0_), channel_id=1, source_target_pairs={{0,4},{2,6},{4,0},{6,2},{8,12},{10,14},{12,8},{14,10},{16,20},{18,... | collective-permute-start | bytes 1179656 | tf_op jit(solution)/shard_map/ppermute | solution.py:193
  13.9 14.6 %collective-permute-start.3 = (bf16[192,1024]{1,0:T(8,128)(2,1)S(1)}, bf16[192,1024]{1,0:T(8,128)(2,1)S(1)}, u32[]{:S(2)}, u32[]{:S(2)}) collective-permute-start(bf16[192,1024]{1,0:T(8,128)(2,1)S(1)} %collective-permute-done.2.refs_1_), channel_id=1, source_target_pairs={{0,4},{2,6},{4,0},{6,2},{8,12},{10,14},{12,8},{14,10},{16,20},{18,... | collective-permute-start | bytes 1179656 | tf_op jit(solution)/shard_map/ppermute | solution.py:193
  19.2 8.0 %collective-permute-start.6 = (bf16[128,1024]{1,0:T(8,128)(2,1)S(1)}, bf16[128,1024]{1,0:T(8,128)(2,1)S(1)}, u32[]{:S(2)}, u32[]{:S(2)}) collective-permute-start(bf16[128,1024]{1,0:T(8,128)(2,1)S(1)} %collective-permute-done.5), channel_id=1, source_target_pairs={{0,1},{1,0},{2,3},{3,2},{4,5},{5,4},{6,7},{7,6},{8,9},{9,8},{10,11... | collective-permute-start | bytes 786440 | tf_op jit(solution)/shard_map/ppermute | solution.py:202
  19.2 13.3 %collective-permute-start = (bf16[128,1024]{1,0:T(8,128)(2,1)S(1)}, bf16[128,1024]{1,0:T(8,128)(2,1)}, u32[]{:S(2)}, u32[]{:S(2)}) collective-permute-start(bf16[128,1024]{1,0:T(8,128)(2,1)S(1)} %convert_element_type.13), channel_id=1, source_target_pairs={{0,1},{1,0},{2,3},{3,2},{4,5},{5,4},{6,7},{7,6},{8,9},{9,8},{10,11... | collective-permute-start | bytes 786440 | tf_op jit(solution)/shard_map/ppermute | solution.py:202
  28.6 11.2 %collective-permute-start.9 = (bf16[192,1024]{1,0:T(8,128)(2,1)S(1)}, bf16[192,1024]{1,0:T(8,128)(2,1)S(1)}, u32[]{:S(2)}, u32[]{:S(2)}) collective-permute-start(bf16[192,1024]{1,0:T(8,128)(2,1)S(1)} %collective-permute-done.1.refs_0_), channel_id=1, source_target_pairs={{0,2},{2,0},{4,6},{6,4},{8,10},{10,8},{12,14},{14,12},{16,18},{18,... | collective-permute-start | bytes 1179656 | tf_op jit(solution)/shard_map/ppermute | solution.py:193
  29.1 13.7 %collective-permute-start.10 = (bf16[192,1024]{1,0:T(8,128)(2,1)S(1)}, bf16[192,1024]{1,0:T(8,128)(2,1)S(1)}, u32[]{:S(2)}, u32[]{:S(2)}) collective-permute-start(bf16[192,1024]{1,0:T(8,128)(2,1)S(1)} %collective-permute-done.1.refs_0_), channel_id=1, source_target_pairs={{0,4},{2,6},{4,0},{6,2},{8,12},{10,14},{12,8},{14,10},{16,20},{18,... | collective-permute-start | bytes 1179656 | tf_op jit(solution)/shard_map/ppermute | solution.py:193
  30.6 12.2 %collective-permute-start.8 = (bf16[96,1024]{1,0:T(8,128)(2,1)S(1)}, bf16[96,1024]{1,0:T(8,128)(2,1)S(1)}, u32[]{:S(2)}, u32[]{:S(2)}) collective-permute-start(bf16[96,1024]{1,0:T(8,128)(2,1)S(1)} %slice.320), channel_id=1, source_target_pairs={{0,6},{2,4},{4,2},{6,0},{8,14},{10,12},{12,10},{14,8},{16,22},{18,... | collective-permute-start | bytes 589832 | tf_op jit(solution)/shard_map/ppermute | solution.py:193
  32.2 10.7 %collective-permute-start.7 = (bf16[96,1024]{1,0:T(8,128)(2,1)S(1)}, bf16[96,1024]{1,0:T(8,128)(2,1)S(1)}, u32[]{:S(2)}, u32[]{:S(2)}) collective-permute-start(bf16[96,1024]{1,0:T(8,128)(2,1)S(1)} %slice.319), channel_id=1, source_target_pairs={{0,16},{2,18},{4,20},{6,22},{8,24},{10,26},{12,28},{14,30},{16,0},... | collective-permute-start | bytes 589832 | tf_op jit(solution)/shard_map/ppermute | solution.py:193
  56.7 2.9 %collective-permute-start.11 = (f32[128,1152]{1,0:T(8,128)S(1)}, f32[128,1152]{1,0:T(8,128)S(1)}, u32[]{:S(2)}, u32[]{:S(2)}) collective-permute-start(f32[128,1152]{1,0:T(8,128)S(1)} %sums_pass.4), channel_id=1, source_target_pairs={{0,1},{1,0},{2,3},{3,2},{4,5},{5,4},{6,7},{7,6},{8,9},{9,8},{10,11... | collective-permute-start | bytes 1769480 | tf_op jit(solution)/shard_map/ppermute | solution.py:202
  59.6 2.3 %copy-start = (f32[128,1024]{1,0:T(8,128)S(1)}, f32[128,1024]{1,0:T(8,128)}, u32[]{:S(2)}) copy-start(f32[128,1024]{1,0:T(8,128)} %refs_9_.1) | copy-start | bytes 1572868
  59.7 9.9 %collective-permute-start.12 = (f32[128,1152]{1,0:T(8,128)S(1)}, f32[128,1152]{1,0:T(8,128)S(1)}, u32[]{:S(2)}, u32[]{:S(2)}) collective-permute-start(f32[128,1152]{1,0:T(8,128)S(1)} %get-tuple-element.78), channel_id=1, source_target_pairs={{0,1},{1,0},{2,3},{3,2},{4,5},{5,4},{6,7},{7,6},{8,9},{9,8},{10,11... | collective-permute-start | bytes 1769480 | tf_op jit(solution)/shard_map/ppermute | solution.py:202
  60.3 9.0 %collective-permute-start.13 = (bf16[128,1152]{1,0:T(8,128)(2,1)S(1)}, bf16[128,1152]{1,0:T(8,128)(2,1)S(1)}, u32[]{:S(2)}, u32[]{:S(2)}) collective-permute-start(bf16[128,1152]{1,0:T(8,128)(2,1)S(1)} %pad_maximum_fusion.2), channel_id=1, source_target_pairs={{0,8},{2,10},{4,12},{6,14},{8,0},{10,2},{12,4},{14,6},{16,24},{18,... | collective-permute-start | bytes 884744 | tf_op jit(solution)/shard_map/ppermute | solution.py:193
  70.9 1.5 %collective-permute-start.15 = (bf16[128,1024]{1,0:T(8,128)(2,1)S(1)}, bf16[128,1024]{1,0:T(8,128)(2,1)S(1)}, u32[]{:S(2)}, u32[]{:S(2)}) collective-permute-start(bf16[128,1024]{1,0:T(8,128)(2,1)S(1)} %get-tuple-element.76), channel_id=1, source_target_pairs={{0,1},{1,0},{2,3},{3,2},{4,5},{5,4},{6,7},{7,6},{8,9},{9,8},{10,11... | collective-permute-start | bytes 786440 | tf_op jit(solution)/shard_map/ppermute | solution.py:202
  70.9 8.7 %collective-permute-start.14 = (bf16[128,1024]{1,0:T(8,128)(2,1)S(1)}, bf16[128,1024]{1,0:T(8,128)(2,1)S(1)}, u32[]{:S(2)}, u32[]{:S(2)}) collective-permute-start(bf16[128,1024]{1,0:T(8,128)(2,1)S(1)} %get-tuple-element.76), channel_id=1, source_target_pairs={{0,8},{2,10},{4,12},{6,14},{8,0},{10,2},{12,4},{14,6},{16,24},{18,... | collective-permute-start | bytes 786440 | tf_op jit(solution)/shard_map/ppermute | solution.py:193
  79.6 1.5 %collective-permute-start.16 = (bf16[128,1024]{1,0:T(8,128)(2,1)S(1)}, bf16[128,1024]{1,0:T(8,128)(2,1)S(1)}, u32[]{:S(2)}, u32[]{:S(2)}) collective-permute-start(bf16[128,1024]{1,0:T(8,128)(2,1)S(1)} %collective-permute-done.14.cents), channel_id=1, source_target_pairs={{0,1},{1,0},{2,3},{3,2},{4,5},{5,4},{6,7},{7,6},{8,9},{9,8},{10,11... | collective-permute-start | bytes 786440 | tf_op jit(solution)/shard_map/ppermute | solution.py:202

commit v17 on v15

--- a/solution.py
+++ b/solution.py
@@ -295,8 +295,10 @@
         counts = far[:, width : width + 1] + far[:, width + 64 : width + 65]
         far = jnp.concatenate([far[:, :width], jnp.broadcast_to(counts, count.shape)], axis=1)
         sums = scatter_near(near + far)
+        rounded = (sums[:, :width] / sums[:, width : width + 1]).astype(jnp.bfloat16)
+        sums = hold(sums, rounded)[0]
         updated = sums[:, :width] / sums[:, width : width + 1]
-        near_own = gather_near(updated.astype(jnp.bfloat16))
+        near_own = gather_near(rounded)
         far_own = flip(near_own, top_bit)
         stats = second_pass(jnp.concatenate(gather_cent(near_own), axis=0), row_sqs, rows, shard)
         far_own, stats = hold(far_own, stats)

time: 92.5 us -> 93.3 us (level)
  blocking collectives: 18.8 us -> 9.81 us
  waiting for transfers between devices: 33.1 us -> 38.5 us
  starting transfers between devices: 18.7 us -> 22.2 us
    all_to_all x2 -> x1, blocking collectives: 18.8 us -> 9.81 us  [exchange(): return lax.all_to_all(value, 'dp', 0, 0, axis_index_groups=groups)]
    all_to_all x0 -> x1, waiting for transfers between devices: none -> 5.63 us  [exchange(): return lax.all_to_all(value, 'dp', 0, 0, axis_index_groups=groups)]
    all_to_all x0 -> x1, starting transfers between devices: none -> 3.33 us  [exchange(): return lax.all_to_all(value, 'dp', 0, 0, axis_index_groups=groups)]
  transfers between devices with their start and end apart: 17 -> 18, of which waited for: 9 -> 10; matrix products, arithmetic and copies ran while one was open for 2% -> 3% of each run, Pallas kernels for 11% -> 11%
where the time goes in v17:
time: 93.3 us; the launch traced here: 93 us
  waiting for transfers between devices  38.5 us (41%)
  starting transfers between devices  22.2 us (24%)
  Pallas kernels  15.1 us (16%)
  blocking collectives  9.81 us (11%)
  other arithmetic  5.04 us (5%)
  local copies, waits for them, and re-layouts  1.27 us (1%)
  between operations  1.08 us (1%)
    ppermute x11, waiting for transfers between devices, flip(): return lax.ppermute(value, 'dp', [(i, i ^ bits) for i in range(n_dp)])  32.7 us
    ppermute x11, starting transfers between devices, flip(): return lax.ppermute(value, 'dp', [(i, i ^ bits) for i in range(n_dp)])  17.6 us
    all_to_all x1, blocking collectives, exchange(): return lax.all_to_all(value, 'dp', 0, 0, axis_index_groups=groups)  9.81 us
    pallas_call x3, Pallas kernels, sums_pass(): pl.pallas_call(functools.partial(sums_kernel, first, last, n), out_shape=...  7.31 us
    all_to_all x1, waiting for transfers between devices, exchange(): return lax.all_to_all(value, 'dp', 0, 0, axis_index_groups=groups)  5.63 us
    pallas_call x3, Pallas kernels, second_pass(): pl.pallas_call(functools.partial(second_kernel, shard, n), out_shape=tupl...  4.02 us
    pallas_call x3, Pallas kernels, first_pass(): pl.pallas_call(functools.partial(first_kernel, len(chunks), shard), out_s...  3.77 us
    all_to_all x1, starting transfers between devices, exchange(): return lax.all_to_all(value, 'dp', 0, 0, axis_index_groups=groups)  3.33 us
  transfers between devices with their start and end apart: 18, of which 10 were waited for; matrix products, arithmetic and copies ran while one was open for 3% of the time, Pallas kernels for 11%

profile of v17, /device:TPU:0, one launch (start us, length us, event | category | flops | bytes accessed | tf_op | source)
XLA Modules:
  0.0 93.0 jit_solution(3699062016181165468)
XLA Ops:
  0.6 1.2 %convert_element_type.14.refs_0_ = bf16[192,1024]{1,0:T(8,128)(2,1)S(1)} convert(f32[192,1024]{1,0:T(8,128)} %param.2) | non-fusion elementwise | flops 196608 | bytes 1179648 | tf_op jit(solution)/shard_map/convert_element_type | solution.py:258
  1.8 3.0 %collective-permute-start.2 = (bf16[192,1024]{1,0:T(8,128)(2,1)S(1)}, bf16[192,1024]{1,0:T(8,128)(2,1)S(1)}, u32[]{:S(2)}, u32[]{:S(2)}) collective-permute-start(bf16[192,1024]{1,0:T(8,128)(2,1)S(1)} %convert_element_type.14.refs_0_), channel_id=1, source_target_pairs={{0,2},{2,0},{4,6},{6,4},{8,10},{10,8},{12,14},{14,12},{16,18},{18,... | collective-permute-start | bytes 1179656 | tf_op jit(solution)/shard_map/ppermute | solution.py:193
  4.8 1.1 %convert_element_type.13 = bf16[128,1024]{1,0:T(8,128)(2,1)S(1)} convert(f32[128,1024]{1,0:T(8,128)} %refs_9_.1) | non-fusion elementwise | flops 131072 | bytes 786432 | tf_op jit(solution)/shard_map/convert_element_type | solution.py:262
  5.9 1.6 %collective-permute-start.5 = (bf16[128,1024]{1,0:T(8,128)(2,1)S(1)}, bf16[128,1024]{1,0:T(8,128)(2,1)S(1)}, u32[]{:S(2)}, u32[]{:S(2)}) collective-permute-start(bf16[128,1024]{1,0:T(8,128)(2,1)S(1)} %convert_element_type.13), channel_id=1, source_target_pairs={{0,8},{2,10},{4,12},{6,14},{8,0},{10,2},{12,4},{14,6},{16,24},{18,... | collective-permute-start | bytes 786440 | tf_op jit(solution)/shard_map/ppermute | solution.py:193
  7.5 2.6 %collective-permute-start.1 = (bf16[192,1024]{1,0:T(8,128)(2,1)S(1)}, bf16[192,1024]{1,0:T(8,128)(2,1)S(1)}, u32[]{:S(2)}, u32[]{:S(2)}) collective-permute-start(bf16[192,1024]{1,0:T(8,128)(2,1)S(1)} %convert_element_type.14.refs_0_), channel_id=1, source_target_pairs={{0,16},{2,18},{4,20},{6,22},{8,24},{10,26},{12,28},{14,30},{16,0},... | collective-permute-start | bytes 1179656 | tf_op jit(solution)/shard_map/ppermute | solution.py:193
  10.1 1.5 %collective-permute-start.4 = (bf16[192,1024]{1,0:T(8,128)(2,1)S(1)}, bf16[192,1024]{1,0:T(8,128)(2,1)S(1)}, u32[]{:S(2)}, u32[]{:S(2)}) collective-permute-start(bf16[192,1024]{1,0:T(8,128)(2,1)S(1)} %convert_element_type.14.refs_0_), channel_id=1, source_target_pairs={{0,4},{2,6},{4,0},{6,2},{8,12},{10,14},{12,8},{14,10},{16,20},{18,... | collective-permute-start | bytes 1179656 | tf_op jit(solution)/shard_map/ppermute | solution.py:193
  11.7 2.3 %collective-permute-done.2.refs_1_ = bf16[192,1024]{1,0:T(8,128)(2,1)S(1)} collective-permute-done((bf16[192,1024]{1,0:T(8,128)(2,1)S(1)}, bf16[192,1024]{1,0:T(8,128)(2,1)S(1)}, u32[]{:S(2)}, u32[]{:S(2)}) %collective-permute-start.2) | collective-permute-done | bytes 393248 | tf_op jit(solution)/shard_map/ppermute | solution.py:193
  13.9 1.8 %collective-permute-start.3 = (bf16[192,1024]{1,0:T(8,128)(2,1)S(1)}, bf16[192,1024]{1,0:T(8,128)(2,1)S(1)}, u32[]{:S(2)}, u32[]{:S(2)}) collective-permute-start(bf16[192,1024]{1,0:T(8,128)(2,1)S(1)} %collective-permute-done.2.refs_1_), channel_id=1, source_target_pairs={{0,4},{2,6},{4,0},{6,2},{8,12},{10,14},{12,8},{14,10},{16,20},{18,... | collective-permute-start | bytes 1179656 | tf_op jit(solution)/shard_map/ppermute | solution.py:193
  15.7 3.5 %collective-permute-done.5 = bf16[128,1024]{1,0:T(8,128)(2,1)S(1)} collective-permute-done((bf16[128,1024]{1,0:T(8,128)(2,1)S(1)}, bf16[128,1024]{1,0:T(8,128)(2,1)S(1)}, u32[]{:S(2)}, u32[]{:S(2)}) %collective-permute-start.5) | collective-permute-done | bytes 262176 | tf_op jit(solution)/shard_map/ppermute | solution.py:193
  19.2 0.0 collective-permute-start.6
  19.2 0.5 collective-permute-start
  19.7 7.5 %collective-permute-done.1.refs_0_ = bf16[192,1024]{1,0:T(8,128)(2,1)S(1)} collective-permute-done((bf16[192,1024]{1,0:T(8,128)(2,1)S(1)}, bf16[192,1024]{1,0:T(8,128)(2,1)S(1)}, u32[]{:S(2)}, u32[]{:S(2)}) %collective-permute-start.1) | collective-permute-done | bytes 393248 | tf_op jit(solution)/shard_map/ppermute | solution.py:193
  27.2 0.0 collective-permute-done.4.refs_2_
  27.2 0.0 collective-permute-done.6
  27.2 1.4 %collective-permute-done.3.refs_3_ = bf16[192,1024]{1,0:T(8,128)(2,1)S(1)} collective-permute-done((bf16[192,1024]{1,0:T(8,128)(2,1)S(1)}, bf16[192,1024]{1,0:T(8,128)(2,1)S(1)}, u32[]{:S(2)}, u32[]{:S(2)}) %collective-permute-start.3) | collective-permute-done | bytes 393248 | tf_op jit(solution)/shard_map/ppermute | solution.py:193
  28.6 0.5 collective-permute-start.9
  29.1 1.6 %collective-permute-start.10 = (bf16[192,1024]{1,0:T(8,128)(2,1)S(1)}, bf16[192,1024]{1,0:T(8,128)(2,1)S(1)}, u32[]{:S(2)}, u32[]{:S(2)}) collective-permute-start(bf16[192,1024]{1,0:T(8,128)(2,1)S(1)} %collective-permute-done.1.refs_0_), channel_id=1, source_target_pairs={{0,4},{2,6},{4,0},{6,2},{8,12},{10,14},{12,8},{14,10},{16,20},{18,... | collective-permute-start | bytes 1179656 | tf_op jit(solution)/shard_map/ppermute | solution.py:193
  30.7 0.4 collective-permute-start.7
  31.1 1.4 %collective-permute-start.8 = (bf16[96,1024]{1,0:T(8,128)(2,1)S(1)}, bf16[96,1024]{1,0:T(8,128)(2,1)S(1)}, u32[]{:S(2)}, u32[]{:S(2)}) collective-permute-start(bf16[96,1024]{1,0:T(8,128)(2,1)S(1)} %slice.326), channel_id=1, source_target_pairs={{0,6},{2,4},{4,2},{6,0},{8,14},{10,12},{12,10},{14,8},{16,22},{18,... | collective-permute-start | bytes 589832 | tf_op jit(solution)/shard_map/ppermute | solution.py:193
  32.6 0.0 collective-permute-done
  32.6 0.1 pad_maximum_fusion.cents
  32.6 1.8 %first_pass.3 = (f32[2,4,192]{2,1,0:T(4,128)S(1)}, f32[1,768]{1,0:T(1,128)S(1)}, bf16[768,1024]{1,0:T(8,128)(2,1)S(1)}) custom-call(bf16[512,1024]{1,0:T(8,128)(2,1)S(1)} %pad_maximum_fusion.cents, bf16[192,1024]{1,0:T(8,128)(2,1)S(1)} %convert_element_type.14.refs_0_, bf16[192,1024]{1,0:T(8,128)(2,1)S(1)} %collective-permute-done.2.refs_1_, ...), custom_call_target="tpu_custom_call" | custom-call | flops 805306368 | bytes 1572864 | tf_op jit(solution)/shard_map/first_pass/pallas_call | solution.py:69
  34.4 5.4 %collective-permute-done.9.refs_1_ = bf16[192,1024]{1,0:T(8,128)(2,1)S(1)} collective-permute-done((bf16[192,1024]{1,0:T(8,128)(2,1)S(1)}, bf16[192,1024]{1,0:T(8,128)(2,1)S(1)}, u32[]{:S(2)}, u32[]{:S(2)}) %collective-permute-start.9) | collective-permute-done | bytes 393248 | tf_op jit(solution)/shard_map/ppermute | solution.py:193
  39.8 1.0 %first_pass.4 = (f32[2,2,192]{2,1,0:T(2,128)S(1)}, f32[1,384]{1,0:T(1,128)S(1)}, bf16[384,1024]{1,0:T(8,128)(2,1)S(1)}) custom-call(bf16[512,1024]{1,0:T(8,128)(2,1)S(1)} %pad_maximum_fusion.cents, bf16[192,1024]{1,0:T(8,128)(2,1)S(1)} %collective-permute-done.1.refs_0_, bf16[192,1024]{1,0:T(8,128)(2,1)S(1)} %collective-permute-done.9.refs_1_), custom_call_target="tpu_custom_call" | custom-call | flops 402653184 | bytes 786432 | tf_op jit(solution)/shard_map/first_pass/pallas_call | solution.py:69
  40.8 0.0 collective-permute-done.7.refs_1_
  40.8 2.1 %collective-permute-done.8.refs_2_ = bf16[96,1024]{1,0:T(8,128)(2,1)S(1)} collective-permute-done((bf16[96,1024]{1,0:T(8,128)(2,1)S(1)}, bf16[96,1024]{1,0:T(8,128)(2,1)S(1)}, u32[]{:S(2)}, u32[]{:S(2)}) %collective-permute-start.8) | collective-permute-done | bytes 196640 | tf_op jit(solution)/shard_map/ppermute | solution.py:193
  42.9 0.0 collective-permute-done.10.refs_0_
  42.9 1.0 %first_pass.5 = (f32[2,2,192]{2,1,0:T(2,128)S(1)}, f32[1,384]{1,0:T(1,128)S(1)}, bf16[384,1024]{1,0:T(8,128)(2,1)S(1)}) custom-call(bf16[512,1024]{1,0:T(8,128)(2,1)S(1)} %pad_maximum_fusion.cents, bf16[192,1024]{1,0:T(8,128)(2,1)S(1)} %collective-permute-done.10.refs_0_, bf16[96,1024]{1,0:T(8,128)(2,1)S(1)} %collective-permute-done.7.refs_1_, ...), custom_call_target="tpu_custom_call" | custom-call | flops 402653184 | bytes 786432 | tf_op jit(solution)/shard_map/first_pass/pallas_call | solution.py:69
  44.1 9.8 %all_to_all.10 = f32[8,2,8,192]{3,2,1,0:T(8,128)S(1)} all-to-all(f32[8,2,8,192]{3,2,1,0:T(8,128)S(1)} %broadcast_in_dim.6), channel_id=1, replica_groups={{0,2,4,6,16,18,20,22},{8,10,12,14,24,26,28,30},{1,3,5,7,17,19,21,23},{9..., dimensions={0} | all-to-all | bytes 196608 | tf_op jit(solution)/shard_map/all_to_all | solution.py:247
  54.2 0.1 pad_maximum_fusion.8.refs_0_
  54.3 0.1 pad_maximum_fusion.9
  54.4 2.8 %sums_pass.3 = f32[256,1152]{1,0:T(8,128)S(1)} custom-call(bf16[512,1024]{1,0:T(8,128)(2,1)S(1)} %pad_maximum_fusion.cents, f32[2,768]{1,0:T(2,128)S(1)} %pad_maximum_fusion.8.refs_0_, f32[2,384]{1,0:T(2,128)S(1)} %get-tuple-element.62.refs_1_, f32[2,384]{1,0:T(2,128)S(1)} %get-tuple-element.63.refs_2_, f32[1,768]{1,0:T(1,128)S(1)} %get-tuple-element.55.refs_3_.refs_0_, ...), custom_call_target="tpu_custom_call" | custom-call | flops 1610612736 | bytes 3145728 | tf_op jit(solution)/shard_map/sums_pass/pallas_call | solution.py:112
  57.2 0.1 collective-permute-start.11
  57.3 2.3 %sums_pass.5 = f32[128,1152]{1,0:T(8,128)S(1)} custom-call(bf16[512,1024]{1,0:T(8,128)(2,1)S(1)} %pad_maximum_fusion.cents, f32[2,768]{1,0:T(2,128)S(1)} %pad_maximum_fusion.8.refs_0_, f32[2,384]{1,0:T(2,128)S(1)} %get-tuple-element.62.refs_1_, f32[2,384]{1,0:T(2,128)S(1)} %get-tuple-element.63.refs_2_, f32[1,768]{1,0:T(1,128)S(1)} %get-tuple-element.55.refs_3_.refs_0_, ...), custom_call_target="tpu_custom_call" | custom-call | flops 805306368 | bytes 3145728 | tf_op jit(solution)/shard_map/sums_pass/pallas_call | solution.py:112
  59.6 0.0 copy-start
  59.6 0.6 collective-permute-start.12
  60.2 0.0 collective-permute-done.11
  60.2 0.1 slice_add_fusion
  60.3 1.6 %collective-permute-start.13 = (bf16[128,1152]{1,0:T(8,128)(2,1)S(1)}, bf16[128,1152]{1,0:T(8,128)(2,1)S(1)}, u32[]{:S(2)}, u32[]{:S(2)}) collective-permute-start(bf16[128,1152]{1,0:T(8,128)(2,1)S(1)} %pad_maximum_fusion.2), channel_id=1, source_target_pairs={{0,8},{2,10},{4,12},{6,14},{8,0},{10,2},{12,4},{14,6},{16,24},{18,... | collective-permute-start | bytes 884744 | tf_op jit(solution)/shard_map/ppermute | solution.py:193
  61.9 0.0 copy-done
  61.9 2.3 %sums_pass.4 = f32[128,1152]{1,0:T(8,128)S(1)} custom-call(bf16[512,1024]{1,0:T(8,128)(2,1)S(1)} %pad_maximum_fusion.cents, f32[2,768]{1,0:T(2,128)S(1)} %pad_maximum_fusion.8.refs_0_, f32[2,384]{1,0:T(2,128)S(1)} %get-tuple-element.62.refs_1_, f32[2,384]{1,0:T(2,128)S(1)} %get-tuple-element.63.refs_2_, f32[1,768]{1,0:T(1,128)S(1)} %get-tuple-element.55.refs_3_.refs_0_, ...), custom_call_target="tpu_custom_call" | custom-call | flops 805306368 | bytes 3145728 | tf_op jit(solution)/shard_map/sums_pass/pallas_call | solution.py:112
  64.2 5.1 %collective-permute-done.13 = bf16[128,1152]{1,0:T(8,128)(2,1)S(1)} collective-permute-done((bf16[128,1152]{1,0:T(8,128)(2,1)S(1)}, bf16[128,1152]{1,0:T(8,128)(2,1)S(1)}, u32[]{:S(2)}, u32[]{:S(2)}) %collective-permute-start.13) | collective-permute-done | bytes 294944 | tf_op jit(solution)/shard_map/ppermute | solution.py:193
  69.4 0.2 fusion.2
  69.6 0.0 collective-permute-done.12
  69.6 0.1 broadcast_in_dim.8
  69.7 0.1 maximum_add_fusion
  69.8 0.1 slice_reduce_fusion
  69.9 0.1 fusion
  70.1 0.1 collective-permute-start.15
  70.1 1.6 %collective-permute-start.14 = (bf16[128,1024]{1,0:T(8,128)(2,1)S(1)}, bf16[128,1024]{1,0:T(8,128)(2,1)S(1)}, u32[]{:S(2)}, u32[]{:S(2)}) collective-permute-start(bf16[128,1024]{1,0:T(8,128)(2,1)S(1)} %fusion), channel_id=1, source_target_pairs={{0,8},{2,10},{4,12},{6,14},{8,0},{10,2},{12,4},{14,6},{16,24},{18,... | collective-permute-start | bytes 786440 | tf_op jit(solution)/shard_map/ppermute | solution.py:193
  71.7 0.0 collective-permute-done.15
  71.8 1.6 %second_pass.3 = (f32[3,4,192]{2,1,0:T(4,128)S(1)}, f32[3,2,192]{2,1,0:T(2,128)S(1)}, f32[3,2,192]{2,1,0:T(2,128)S(1)}) custom-call(bf16[256,1024]{1,0:T(8,128)(2,1)S(1)} %pad_maximum_fusion.1.cents, f32[1,768]{1,0:T(1,128)S(1)} %get-tuple-element.55.refs_3_.refs_0_, f32[1,384]{1,0:T(1,128)S(1)} %get-tuple-element.56.refs_4_.refs_1_, ...), custom_call_target="tpu_custom_call" | custom-call | flops 805306368 | bytes 3145728 | tf_op jit(solution)/shard_map/second_pass/pallas_call | solution.py:153
  73.4 5.5 %collective-permute-done.14.cents = bf16[128,1024]{1,0:T(8,128)(2,1)S(1)} collective-permute-done((bf16[128,1024]{1,0:T(8,128)(2,1)S(1)}, bf16[128,1024]{1,0:T(8,128)(2,1)S(1)}, u32[]{:S(2)}, u32[]{:S(2)}) %collective-permute-start.14) | collective-permute-done | bytes 262176 | tf_op jit(solution)/shard_map/ppermute | solution.py:193
  78.9 0.0 collective-permute-start.16
  78.9 0.1 slice_reduce_fusion.1
  79.0 1.2 %second_pass.4 = (f32[3,4,192]{2,1,0:T(4,128)S(1)}, f32[3,2,192]{2,1,0:T(2,128)S(1)}, f32[3,2,192]{2,1,0:T(2,128)S(1)}) custom-call(bf16[128,1024]{1,0:T(8,128)(2,1)S(1)} %collective-permute-done.14.cents, f32[1,768]{1,0:T(1,128)S(1)} %get-tuple-element.55.refs_3_.refs_0_, f32[1,384]{1,0:T(1,128)S(1)} %get-tuple-element.56.refs_4_.refs_1_, ...), custom_call_target="tpu_custom_call" | custom-call | flops 402653184 | bytes 3145728 | tf_op jit(solution)/shard_map/second_pass/pallas_call | solution.py:153
  80.2 0.2 collective-permute-done.16.cents
  80.4 1.2 %second_pass.5 = (f32[3,4,192]{2,1,0:T(4,128)S(1)}, f32[3,2,192]{2,1,0:T(2,128)S(1)}, f32[3,2,192]{2,1,0:T(2,128)S(1)}) custom-call(bf16[128,1024]{1,0:T(8,128)(2,1)S(1)} %collective-permute-done.16.cents, f32[1,768]{1,0:T(1,128)S(1)} %get-tuple-element.55.refs_3_.refs_0_, f32[1,384]{1,0:T(1,128)S(1)} %get-tuple-element.56.refs_4_.refs_1_, ...), custom_call_target="tpu_custom_call" | custom-call | flops 402653184 | bytes 3145728 | tf_op jit(solution)/shard_map/second_pass/pallas_call | solution.py:153
  81.7 0.1 stack.78
  81.9 0.6 copy.74
  82.5 3.3 %all-to-all-start.1 = ((f32[8,3,192]{2,1,0:T(4,128)}), f32[8,3,192]{2,1,0:T(4,128)S(1)}, u32[]{:S(2)}, u32[]{:S(2)}) async-start(f32[8,3,192]{2,1,0:T(4,128)} %copy.74), calls=%async_computation.1 | async-start | bytes 65536 | tf_op jit(solution)/shard_map/all_to_all | solution.py:247
  85.8 0.9 slice_divide_fusion.1
  86.7 5.6 %all-to-all-done.1 = f32[8,3,192]{2,1,0:T(4,128)S(1)} async-done(((f32[8,3,192]{2,1,0:T(4,128)}), f32[8,3,192]{2,1,0:T(4,128)S(1)}, u32[]{:S(2)}, u32[]{:S(2)}) %all-to-all-start.1) | async-done | bytes 18464 | tf_op jit(solution)/shard_map/all_to_all | solution.py:247
  92.4 0.6 divide_subtract_fusion
  (59 shorter events, 0.9 us)
Async XLA Ops:
  1.8 12.1 %collective-permute-start.2 = (bf16[192,1024]{1,0:T(8,128)(2,1)S(1)}, bf16[192,1024]{1,0:T(8,128)(2,1)S(1)}, u32[]{:S(2)}, u32[]{:S(2)}) collective-permute-start(bf16[192,1024]{1,0:T(8,128)(2,1)S(1)} %convert_element_type.14.refs_0_), channel_id=1, source_target_pairs={{0,2},{2,0},{4,6},{6,4},{8,10},{10,8},{12,14},{14,12},{16,18},{18,... | collective-permute-start | bytes 1179656 | tf_op jit(solution)/shard_map/ppermute | solution.py:193
  5.9 13.3 %collective-permute-start.5 = (bf16[128,1024]{1,0:T(8,128)(2,1)S(1)}, bf16[128,1024]{1,0:T(8,128)(2,1)S(1)}, u32[]{:S(2)}, u32[]{:S(2)}) collective-permute-start(bf16[128,1024]{1,0:T(8,128)(2,1)S(1)} %convert_element_type.13), channel_id=1, source_target_pairs={{0,8},{2,10},{4,12},{6,14},{8,0},{10,2},{12,4},{14,6},{16,24},{18,... | collective-permute-start | bytes 786440 | tf_op jit(solution)/shard_map/ppermute | solution.py:193
  7.5 19.7 %collective-permute-start.1 = (bf16[192,1024]{1,0:T(8,128)(2,1)S(1)}, bf16[192,1024]{1,0:T(8,128)(2,1)S(1)}, u32[]{:S(2)}, u32[]{:S(2)}) collective-permute-start(bf16[192,1024]{1,0:T(8,128)(2,1)S(1)} %convert_element_type.14.refs_0_), channel_id=1, source_target_pairs={{0,16},{2,18},{4,20},{6,22},{8,24},{10,26},{12,28},{14,30},{16,0},... | collective-permute-start | bytes 1179656 | tf_op jit(solution)/shard_map/ppermute | solution.py:193
  10.1 17.1 %collective-permute-start.4 = (bf16[192,1024]{1,0:T(8,128)(2,1)S(1)}, bf16[192,1024]{1,0:T(8,128)(2,1)S(1)}, u32[]{:S(2)}, u32[]{:S(2)}) collective-permute-start(bf16[192,1024]{1,0:T(8,128)(2,1)S(1)} %convert_element_type.14.refs_0_), channel_id=1, source_target_pairs={{0,4},{2,6},{4,0},{6,2},{8,12},{10,14},{12,8},{14,10},{16,20},{18,... | collective-permute-start | bytes 1179656 | tf_op jit(solution)/shard_map/ppermute | solution.py:193
  13.9 14.6 %collective-permute-start.3 = (bf16[192,1024]{1,0:T(8,128)(2,1)S(1)}, bf16[192,1024]{1,0:T(8,128)(2,1)S(1)}, u32[]{:S(2)}, u32[]{:S(2)}) collective-permute-start(bf16[192,1024]{1,0:T(8,128)(2,1)S(1)} %collective-permute-done.2.refs_1_), channel_id=1, source_target_pairs={{0,4},{2,6},{4,0},{6,2},{8,12},{10,14},{12,8},{14,10},{16,20},{18,... | collective-permute-start | bytes 1179656 | tf_op jit(solution)/shard_map/ppermute | solution.py:193
  19.2 8.0 %collective-permute-start.6 = (bf16[128,1024]{1,0:T(8,128)(2,1)S(1)}, bf16[128,1024]{1,0:T(8,128)(2,1)S(1)}, u32[]{:S(2)}, u32[]{:S(2)}) collective-permute-start(bf16[128,1024]{1,0:T(8,128)(2,1)S(1)} %collective-permute-done.5), channel_id=1, source_target_pairs={{0,1},{1,0},{2,3},{3,2},{4,5},{5,4},{6,7},{7,6},{8,9},{9,8},{10,11... | collective-permute-start | bytes 786440 | tf_op jit(solution)/shard_map/ppermute | solution.py:202
  19.2 13.3 %collective-permute-start = (bf16[128,1024]{1,0:T(8,128)(2,1)S(1)}, bf16[128,1024]{1,0:T(8,128)(2,1)S(1)}, u32[]{:S(2)}, u32[]{:S(2)}) collective-permute-start(bf16[128,1024]{1,0:T(8,128)(2,1)S(1)} %convert_element_type.13), channel_id=1, source_target_pairs={{0,1},{1,0},{2,3},{3,2},{4,5},{5,4},{6,7},{7,6},{8,9},{9,8},{10,11... | collective-permute-start | bytes 786440 | tf_op jit(solution)/shard_map/ppermute | solution.py:202
  28.6 11.2 %collective-permute-start.9 = (bf16[192,1024]{1,0:T(8,128)(2,1)S(1)}, bf16[192,1024]{1,0:T(8,128)(2,1)S(1)}, u32[]{:S(2)}, u32[]{:S(2)}) collective-permute-start(bf16[192,1024]{1,0:T(8,128)(2,1)S(1)} %collective-permute-done.1.refs_0_), channel_id=1, source_target_pairs={{0,2},{2,0},{4,6},{6,4},{8,10},{10,8},{12,14},{14,12},{16,18},{18,... | collective-permute-start | bytes 1179656 | tf_op jit(solution)/shard_map/ppermute | solution.py:193
  29.1 13.8 %collective-permute-start.10 = (bf16[192,1024]{1,0:T(8,128)(2,1)S(1)}, bf16[192,1024]{1,0:T(8,128)(2,1)S(1)}, u32[]{:S(2)}, u32[]{:S(2)}) collective-permute-start(bf16[192,1024]{1,0:T(8,128)(2,1)S(1)} %collective-permute-done.1.refs_0_), channel_id=1, source_target_pairs={{0,4},{2,6},{4,0},{6,2},{8,12},{10,14},{12,8},{14,10},{16,20},{18,... | collective-permute-start | bytes 1179656 | tf_op jit(solution)/shard_map/ppermute | solution.py:193
  30.7 10.1 %collective-permute-start.7 = (bf16[96,1024]{1,0:T(8,128)(2,1)S(1)}, bf16[96,1024]{1,0:T(8,128)(2,1)S(1)}, u32[]{:S(2)}, u32[]{:S(2)}) collective-permute-start(bf16[96,1024]{1,0:T(8,128)(2,1)S(1)} %slice.325), channel_id=1, source_target_pairs={{0,16},{2,18},{4,20},{6,22},{8,24},{10,26},{12,28},{14,30},{16,0},... | collective-permute-start | bytes 589832 | tf_op jit(solution)/shard_map/ppermute | solution.py:193
  31.1 11.7 %collective-permute-start.8 = (bf16[96,1024]{1,0:T(8,128)(2,1)S(1)}, bf16[96,1024]{1,0:T(8,128)(2,1)S(1)}, u32[]{:S(2)}, u32[]{:S(2)}) collective-permute-start(bf16[96,1024]{1,0:T(8,128)(2,1)S(1)} %slice.326), channel_id=1, source_target_pairs={{0,6},{2,4},{4,2},{6,0},{8,14},{10,12},{12,10},{14,8},{16,22},{18,... | collective-permute-start | bytes 589832 | tf_op jit(solution)/shard_map/ppermute | solution.py:193
  57.2 2.9 %collective-permute-start.11 = (f32[128,1152]{1,0:T(8,128)S(1)}, f32[128,1152]{1,0:T(8,128)S(1)}, u32[]{:S(2)}, u32[]{:S(2)}) collective-permute-start(f32[128,1152]{1,0:T(8,128)S(1)} %slice.449), channel_id=1, source_target_pairs={{0,1},{1,0},{2,3},{3,2},{4,5},{5,4},{6,7},{7,6},{8,9},{9,8},{10,11... | collective-permute-start | bytes 1769480 | tf_op jit(solution)/shard_map/ppermute | solution.py:202
  59.6 2.3 %copy-start = (f32[128,1024]{1,0:T(8,128)S(1)}, f32[128,1024]{1,0:T(8,128)}, u32[]{:S(2)}) copy-start(f32[128,1024]{1,0:T(8,128)} %refs_9_.1) | copy-start | bytes 1572868
  59.6 10.0 %collective-permute-start.12 = (f32[128,1152]{1,0:T(8,128)S(1)}, f32[128,1152]{1,0:T(8,128)S(1)}, u32[]{:S(2)}, u32[]{:S(2)}) collective-permute-start(f32[128,1152]{1,0:T(8,128)S(1)} %sums_pass.5), channel_id=1, source_target_pairs={{0,1},{1,0},{2,3},{3,2},{4,5},{5,4},{6,7},{7,6},{8,9},{9,8},{10,11... | collective-permute-start | bytes 1769480 | tf_op jit(solution)/shard_map/ppermute | solution.py:202
  60.3 9.0 %collective-permute-start.13 = (bf16[128,1152]{1,0:T(8,128)(2,1)S(1)}, bf16[128,1152]{1,0:T(8,128)(2,1)S(1)}, u32[]{:S(2)}, u32[]{:S(2)}) collective-permute-start(bf16[128,1152]{1,0:T(8,128)(2,1)S(1)} %pad_maximum_fusion.2), channel_id=1, source_target_pairs={{0,8},{2,10},{4,12},{6,14},{8,0},{10,2},{12,4},{14,6},{16,24},{18,... | collective-permute-start | bytes 884744 | tf_op jit(solution)/shard_map/ppermute | solution.py:193
  70.1 1.7 %collective-permute-start.15 = (bf16[128,1024]{1,0:T(8,128)(2,1)S(1)}, bf16[128,1024]{1,0:T(8,128)(2,1)S(1)}, u32[]{:S(2)}, u32[]{:S(2)}) collective-permute-start(bf16[128,1024]{1,0:T(8,128)(2,1)S(1)} %fusion), channel_id=1, source_target_pairs={{0,1},{1,0},{2,3},{3,2},{4,5},{5,4},{6,7},{7,6},{8,9},{9,8},{10,11... | collective-permute-start | bytes 786440 | tf_op jit(solution)/shard_map/ppermute | solution.py:202
  70.1 8.7 %collective-permute-start.14 = (bf16[128,1024]{1,0:T(8,128)(2,1)S(1)}, bf16[128,1024]{1,0:T(8,128)(2,1)S(1)}, u32[]{:S(2)}, u32[]{:S(2)}) collective-permute-start(bf16[128,1024]{1,0:T(8,128)(2,1)S(1)} %fusion), channel_id=1, source_target_pairs={{0,8},{2,10},{4,12},{6,14},{8,0},{10,2},{12,4},{14,6},{16,24},{18,... | collective-permute-start | bytes 786440 | tf_op jit(solution)/shard_map/ppermute | solution.py:193
  78.9 1.5 %collective-permute-start.16 = (bf16[128,1024]{1,0:T(8,128)(2,1)S(1)}, bf16[128,1024]{1,0:T(8,128)(2,1)S(1)}, u32[]{:S(2)}, u32[]{:S(2)}) collective-permute-start(bf16[128,1024]{1,0:T(8,128)(2,1)S(1)} %collective-permute-done.14.cents), channel_id=1, source_target_pairs={{0,1},{1,0},{2,3},{3,2},{4,5},{5,4},{6,7},{7,6},{8,9},{9,8},{10,11... | collective-permute-start | bytes 786440 | tf_op jit(solution)/shard_map/ppermute | solution.py:202
  82.5 9.9 %all-to-all-start.1 = ((f32[8,3,192]{2,1,0:T(4,128)}), f32[8,3,192]{2,1,0:T(4,128)S(1)}, u32[]{:S(2)}, u32[]{:S(2)}) async-start(f32[8,3,192]{2,1,0:T(4,128)} %copy.74), calls=%async_computation.1 | async-start | bytes 65536 | tf_op jit(solution)/shard_map/all_to_all | solution.py:247

commit v18 on v17

--- a/solution.py
+++ b/solution.py
@@ -301,7 +301,7 @@
         near_own = gather_near(rounded)
         far_own = flip(near_own, top_bit)
         stats = second_pass(jnp.concatenate(gather_cent(near_own), axis=0), row_sqs, rows, shard)
-        far_own, stats = hold(far_own, stats)
+        far_own, stats, updated = hold(far_own, stats, updated)
         far = gather_cent(far_own)
         stats = merge(stats, second_pass(far_own, row_sqs, rows, shard))
         stats = merge(stats, second_pass(jnp.concatenate(far[1:], axis=0), row_sqs, rows, shard))

time: 93.3 us -> 90.8 us (0.973)
  blocking collectives: 9.81 us -> 19.1 us
  waiting for transfers between devices: 38.5 us -> 30.7 us
  starting transfers between devices: 22.2 us -> 18.8 us
    all_to_all x1 -> x2, blocking collectives: 9.81 us -> 19.1 us  [exchange(): return lax.all_to_all(value, 'dp', 0, 0, axis_index_groups=groups)]
    all_to_all x1 -> x0, waiting for transfers between devices: 5.63 us -> none  [exchange(): return lax.all_to_all(value, 'dp', 0, 0, axis_index_groups=groups)]
    all_to_all x1 -> x0, starting transfers between devices: 3.33 us -> none  [exchange(): return lax.all_to_all(value, 'dp', 0, 0, axis_index_groups=groups)]
    ppermute x11, waiting for transfers between devices: 32.7 us -> 29.9 us  [flip(): return lax.ppermute(value, 'dp', [(i, i ^ bits) for i in range(n_dp)])]
  transfers between devices with their start and end apart: 18 -> 17, of which waited for: 10 -> 10; matrix products, arithmetic and copies ran while one was open for 3% -> 3% of each run, Pallas kernels for 11% -> 11%
where the time goes in v18:
time: 90.8 us; the launch traced here: 90.5 us
  waiting for transfers between devices  30.7 us (34%)
  blocking collectives  19.1 us (21%)
  starting transfers between devices  18.8 us (21%)
  Pallas kernels  15.1 us (17%)
  other arithmetic  5.02 us (6%)
  between operations  1.07 us (1%)
    ppermute x11, waiting for transfers between devices, flip(): return lax.ppermute(value, 'dp', [(i, i ^ bits) for i in range(n_dp)])  29.9 us
    all_to_all x2, blocking collectives, exchange(): return lax.all_to_all(value, 'dp', 0, 0, axis_index_groups=groups)  19.1 us
    ppermute x11, starting transfers between devices, flip(): return lax.ppermute(value, 'dp', [(i, i ^ bits) for i in range(n_dp)])  17.6 us
    pallas_call x3, Pallas kernels, sums_pass(): pl.pallas_call(functools.partial(sums_kernel, first, last, n), out_shape=...  7.31 us
    pallas_call x3, Pallas kernels, second_pass(): pl.pallas_call(functools.partial(second_kernel, shard, n), out_shape=tupl...  4.01 us
    pallas_call x3, Pallas kernels, first_pass(): pl.pallas_call(functools.partial(first_kernel, len(chunks), shard), out_s...  3.77 us
  transfers between devices with their start and end apart: 17, of which 10 were waited for; matrix products, arithmetic and copies ran while one was open for 3% of the time, Pallas kernels for 11%

profile of v18, /device:TPU:0, one launch (start us, length us, event | category | flops | bytes accessed | tf_op | source)
XLA Modules:
  0.0 90.5 jit_solution(8503429854505216310)
XLA Ops:
  0.6 1.2 %convert_element_type.14.refs_0_ = bf16[192,1024]{1,0:T(8,128)(2,1)S(1)} convert(f32[192,1024]{1,0:T(8,128)} %param.2) | non-fusion elementwise | flops 196608 | bytes 1179648 | tf_op jit(solution)/shard_map/convert_element_type | solution.py:258
  1.8 3.0 %collective-permute-start.2 = (bf16[192,1024]{1,0:T(8,128)(2,1)S(1)}, bf16[192,1024]{1,0:T(8,128)(2,1)S(1)}, u32[]{:S(2)}, u32[]{:S(2)}) collective-permute-start(bf16[192,1024]{1,0:T(8,128)(2,1)S(1)} %convert_element_type.14.refs_0_), channel_id=1, source_target_pairs={{0,2},{2,0},{4,6},{6,4},{8,10},{10,8},{12,14},{14,12},{16,18},{18,... | collective-permute-start | bytes 1179656 | tf_op jit(solution)/shard_map/ppermute | solution.py:193
  4.8 1.1 %convert_element_type.13 = bf16[128,1024]{1,0:T(8,128)(2,1)S(1)} convert(f32[128,1024]{1,0:T(8,128)} %refs_9_.1) | non-fusion elementwise | flops 131072 | bytes 786432 | tf_op jit(solution)/shard_map/convert_element_type | solution.py:262
  5.9 1.6 %collective-permute-start.5 = (bf16[128,1024]{1,0:T(8,128)(2,1)S(1)}, bf16[128,1024]{1,0:T(8,128)(2,1)S(1)}, u32[]{:S(2)}, u32[]{:S(2)}) collective-permute-start(bf16[128,1024]{1,0:T(8,128)(2,1)S(1)} %convert_element_type.13), channel_id=1, source_target_pairs={{0,8},{2,10},{4,12},{6,14},{8,0},{10,2},{12,4},{14,6},{16,24},{18,... | collective-permute-start | bytes 786440 | tf_op jit(solution)/shard_map/ppermute | solution.py:193
  7.5 2.6 %collective-permute-start.1 = (bf16[192,1024]{1,0:T(8,128)(2,1)S(1)}, bf16[192,1024]{1,0:T(8,128)(2,1)S(1)}, u32[]{:S(2)}, u32[]{:S(2)}) collective-permute-start(bf16[192,1024]{1,0:T(8,128)(2,1)S(1)} %convert_element_type.14.refs_0_), channel_id=1, source_target_pairs={{0,16},{2,18},{4,20},{6,22},{8,24},{10,26},{12,28},{14,30},{16,0},... | collective-permute-start | bytes 1179656 | tf_op jit(solution)/shard_map/ppermute | solution.py:193
  10.1 1.5 %collective-permute-start.4 = (bf16[192,1024]{1,0:T(8,128)(2,1)S(1)}, bf16[192,1024]{1,0:T(8,128)(2,1)S(1)}, u32[]{:S(2)}, u32[]{:S(2)}) collective-permute-start(bf16[192,1024]{1,0:T(8,128)(2,1)S(1)} %convert_element_type.14.refs_0_), channel_id=1, source_target_pairs={{0,4},{2,6},{4,0},{6,2},{8,12},{10,14},{12,8},{14,10},{16,20},{18,... | collective-permute-start | bytes 1179656 | tf_op jit(solution)/shard_map/ppermute | solution.py:193
  11.7 2.3 %collective-permute-done.2.refs_1_ = bf16[192,1024]{1,0:T(8,128)(2,1)S(1)} collective-permute-done((bf16[192,1024]{1,0:T(8,128)(2,1)S(1)}, bf16[192,1024]{1,0:T(8,128)(2,1)S(1)}, u32[]{:S(2)}, u32[]{:S(2)}) %collective-permute-start.2) | collective-permute-done | bytes 393248 | tf_op jit(solution)/shard_map/ppermute | solution.py:193
  13.9 1.8 %collective-permute-start.3 = (bf16[192,1024]{1,0:T(8,128)(2,1)S(1)}, bf16[192,1024]{1,0:T(8,128)(2,1)S(1)}, u32[]{:S(2)}, u32[]{:S(2)}) collective-permute-start(bf16[192,1024]{1,0:T(8,128)(2,1)S(1)} %collective-permute-done.2.refs_1_), channel_id=1, source_target_pairs={{0,4},{2,6},{4,0},{6,2},{8,12},{10,14},{12,8},{14,10},{16,20},{18,... | collective-permute-start | bytes 1179656 | tf_op jit(solution)/shard_map/ppermute | solution.py:193
  15.7 3.5 %collective-permute-done.5 = bf16[128,1024]{1,0:T(8,128)(2,1)S(1)} collective-permute-done((bf16[128,1024]{1,0:T(8,128)(2,1)S(1)}, bf16[128,1024]{1,0:T(8,128)(2,1)S(1)}, u32[]{:S(2)}, u32[]{:S(2)}) %collective-permute-start.5) | collective-permute-done | bytes 262176 | tf_op jit(solution)/shard_map/ppermute | solution.py:193
  19.2 0.0 collective-permute-start.6
  19.2 0.5 collective-permute-start
  19.7 7.5 %collective-permute-done.1.refs_0_ = bf16[192,1024]{1,0:T(8,128)(2,1)S(1)} collective-permute-done((bf16[192,1024]{1,0:T(8,128)(2,1)S(1)}, bf16[192,1024]{1,0:T(8,128)(2,1)S(1)}, u32[]{:S(2)}, u32[]{:S(2)}) %collective-permute-start.1) | collective-permute-done | bytes 393248 | tf_op jit(solution)/shard_map/ppermute | solution.py:193
  27.2 0.0 collective-permute-done.4.refs_2_
  27.2 0.0 collective-permute-done.6
  27.2 1.4 %collective-permute-done.3.refs_3_ = bf16[192,1024]{1,0:T(8,128)(2,1)S(1)} collective-permute-done((bf16[192,1024]{1,0:T(8,128)(2,1)S(1)}, bf16[192,1024]{1,0:T(8,128)(2,1)S(1)}, u32[]{:S(2)}, u32[]{:S(2)}) %collective-permute-start.3) | collective-permute-done | bytes 393248 | tf_op jit(solution)/shard_map/ppermute | solution.py:193
  28.6 0.5 collective-permute-start.9
  29.1 1.6 %collective-permute-start.10 = (bf16[192,1024]{1,0:T(8,128)(2,1)S(1)}, bf16[192,1024]{1,0:T(8,128)(2,1)S(1)}, u32[]{:S(2)}, u32[]{:S(2)}) collective-permute-start(bf16[192,1024]{1,0:T(8,128)(2,1)S(1)} %collective-permute-done.1.refs_0_), channel_id=1, source_target_pairs={{0,4},{2,6},{4,0},{6,2},{8,12},{10,14},{12,8},{14,10},{16,20},{18,... | collective-permute-start | bytes 1179656 | tf_op jit(solution)/shard_map/ppermute | solution.py:193
  30.7 0.4 collective-permute-start.7
  31.1 1.4 %collective-permute-start.8 = (bf16[96,1024]{1,0:T(8,128)(2,1)S(1)}, bf16[96,1024]{1,0:T(8,128)(2,1)S(1)}, u32[]{:S(2)}, u32[]{:S(2)}) collective-permute-start(bf16[96,1024]{1,0:T(8,128)(2,1)S(1)} %slice.326), channel_id=1, source_target_pairs={{0,6},{2,4},{4,2},{6,0},{8,14},{10,12},{12,10},{14,8},{16,22},{18,... | collective-permute-start | bytes 589832 | tf_op jit(solution)/shard_map/ppermute | solution.py:193
  32.6 0.0 collective-permute-done
  32.6 0.1 pad_maximum_fusion.cents
  32.6 1.8 %first_pass.3 = (f32[2,4,192]{2,1,0:T(4,128)S(1)}, f32[1,768]{1,0:T(1,128)S(1)}, bf16[768,1024]{1,0:T(8,128)(2,1)S(1)}) custom-call(bf16[512,1024]{1,0:T(8,128)(2,1)S(1)} %pad_maximum_fusion.cents, bf16[192,1024]{1,0:T(8,128)(2,1)S(1)} %convert_element_type.14.refs_0_, bf16[192,1024]{1,0:T(8,128)(2,1)S(1)} %collective-permute-done.2.refs_1_, ...), custom_call_target="tpu_custom_call" | custom-call | flops 805306368 | bytes 1572864 | tf_op jit(solution)/shard_map/first_pass/pallas_call | solution.py:69
  34.4 5.4 %collective-permute-done.9.refs_1_ = bf16[192,1024]{1,0:T(8,128)(2,1)S(1)} collective-permute-done((bf16[192,1024]{1,0:T(8,128)(2,1)S(1)}, bf16[192,1024]{1,0:T(8,128)(2,1)S(1)}, u32[]{:S(2)}, u32[]{:S(2)}) %collective-permute-start.9) | collective-permute-done | bytes 393248 | tf_op jit(solution)/shard_map/ppermute | solution.py:193
  39.8 1.0 %first_pass.4 = (f32[2,2,192]{2,1,0:T(2,128)S(1)}, f32[1,384]{1,0:T(1,128)S(1)}, bf16[384,1024]{1,0:T(8,128)(2,1)S(1)}) custom-call(bf16[512,1024]{1,0:T(8,128)(2,1)S(1)} %pad_maximum_fusion.cents, bf16[192,1024]{1,0:T(8,128)(2,1)S(1)} %collective-permute-done.1.refs_0_, bf16[192,1024]{1,0:T(8,128)(2,1)S(1)} %collective-permute-done.9.refs_1_), custom_call_target="tpu_custom_call" | custom-call | flops 402653184 | bytes 786432 | tf_op jit(solution)/shard_map/first_pass/pallas_call | solution.py:69
  40.8 0.0 collective-permute-done.7.refs_1_
  40.8 2.1 %collective-permute-done.8.refs_2_ = bf16[96,1024]{1,0:T(8,128)(2,1)S(1)} collective-permute-done((bf16[96,1024]{1,0:T(8,128)(2,1)S(1)}, bf16[96,1024]{1,0:T(8,128)(2,1)S(1)}, u32[]{:S(2)}, u32[]{:S(2)}) %collective-permute-start.8) | collective-permute-done | bytes 196640 | tf_op jit(solution)/shard_map/ppermute | solution.py:193
  42.9 0.0 collective-permute-done.10.refs_0_
  42.9 1.0 %first_pass.5 = (f32[2,2,192]{2,1,0:T(2,128)S(1)}, f32[1,384]{1,0:T(1,128)S(1)}, bf16[384,1024]{1,0:T(8,128)(2,1)S(1)}) custom-call(bf16[512,1024]{1,0:T(8,128)(2,1)S(1)} %pad_maximum_fusion.cents, bf16[192,1024]{1,0:T(8,128)(2,1)S(1)} %collective-permute-done.10.refs_0_, bf16[96,1024]{1,0:T(8,128)(2,1)S(1)} %collective-permute-done.7.refs_1_, ...), custom_call_target="tpu_custom_call" | custom-call | flops 402653184 | bytes 786432 | tf_op jit(solution)/shard_map/first_pass/pallas_call | solution.py:69
  44.1 9.8 %all_to_all.10 = f32[8,2,8,192]{3,2,1,0:T(8,128)S(1)} all-to-all(f32[8,2,8,192]{3,2,1,0:T(8,128)S(1)} %broadcast_in_dim.6), channel_id=1, replica_groups={{0,2,4,6,16,18,20,22},{8,10,12,14,24,26,28,30},{1,3,5,7,17,19,21,23},{9..., dimensions={0} | all-to-all | bytes 196608 | tf_op jit(solution)/shard_map/all_to_all | solution.py:247
  54.2 0.1 pad_maximum_fusion.8.refs_0_
  54.3 0.1 pad_maximum_fusion.9
  54.4 2.8 %sums_pass.3 = f32[256,1152]{1,0:T(8,128)S(1)} custom-call(bf16[512,1024]{1,0:T(8,128)(2,1)S(1)} %pad_maximum_fusion.cents, f32[2,768]{1,0:T(2,128)S(1)} %pad_maximum_fusion.8.refs_0_, f32[2,384]{1,0:T(2,128)S(1)} %get-tuple-element.63.refs_1_, f32[2,384]{1,0:T(2,128)S(1)} %get-tuple-element.64.refs_2_, f32[1,768]{1,0:T(1,128)S(1)} %get-tuple-element.56.refs_3_.refs_0_, ...), custom_call_target="tpu_custom_call" | custom-call | flops 1610612736 | bytes 3145728 | tf_op jit(solution)/shard_map/sums_pass/pallas_call | solution.py:112
  57.2 0.1 collective-permute-start.11
  57.3 2.3 %sums_pass.5 = f32[128,1152]{1,0:T(8,128)S(1)} custom-call(bf16[512,1024]{1,0:T(8,128)(2,1)S(1)} %pad_maximum_fusion.cents, f32[2,768]{1,0:T(2,128)S(1)} %pad_maximum_fusion.8.refs_0_, f32[2,384]{1,0:T(2,128)S(1)} %get-tuple-element.63.refs_1_, f32[2,384]{1,0:T(2,128)S(1)} %get-tuple-element.64.refs_2_, f32[1,768]{1,0:T(1,128)S(1)} %get-tuple-element.56.refs_3_.refs_0_, ...), custom_call_target="tpu_custom_call" | custom-call | flops 805306368 | bytes 3145728 | tf_op jit(solution)/shard_map/sums_pass/pallas_call | solution.py:112
  59.6 0.0 copy-start
  59.6 0.6 collective-permute-start.12
  60.2 0.0 collective-permute-done.11
  60.2 0.1 slice_add_fusion
  60.3 1.6 %collective-permute-start.13 = (bf16[128,1152]{1,0:T(8,128)(2,1)S(1)}, bf16[128,1152]{1,0:T(8,128)(2,1)S(1)}, u32[]{:S(2)}, u32[]{:S(2)}) collective-permute-start(bf16[128,1152]{1,0:T(8,128)(2,1)S(1)} %pad_maximum_fusion.2), channel_id=1, source_target_pairs={{0,8},{2,10},{4,12},{6,14},{8,0},{10,2},{12,4},{14,6},{16,24},{18,... | collective-permute-start | bytes 884744 | tf_op jit(solution)/shard_map/ppermute | solution.py:193
  61.9 0.0 copy-done
  61.9 2.3 %sums_pass.4 = f32[128,1152]{1,0:T(8,128)S(1)} custom-call(bf16[512,1024]{1,0:T(8,128)(2,1)S(1)} %pad_maximum_fusion.cents, f32[2,768]{1,0:T(2,128)S(1)} %pad_maximum_fusion.8.refs_0_, f32[2,384]{1,0:T(2,128)S(1)} %get-tuple-element.63.refs_1_, f32[2,384]{1,0:T(2,128)S(1)} %get-tuple-element.64.refs_2_, f32[1,768]{1,0:T(1,128)S(1)} %get-tuple-element.56.refs_3_.refs_0_, ...), custom_call_target="tpu_custom_call" | custom-call | flops 805306368 | bytes 3145728 | tf_op jit(solution)/shard_map/sums_pass/pallas_call | solution.py:112
  64.2 5.1 %collective-permute-done.13 = bf16[128,1152]{1,0:T(8,128)(2,1)S(1)} collective-permute-done((bf16[128,1152]{1,0:T(8,128)(2,1)S(1)}, bf16[128,1152]{1,0:T(8,128)(2,1)S(1)}, u32[]{:S(2)}, u32[]{:S(2)}) %collective-permute-start.13) | collective-permute-done | bytes 294944 | tf_op jit(solution)/shard_map/ppermute | solution.py:193
  69.4 0.2 fusion.2
  69.6 0.0 collective-permute-done.12
  69.6 0.1 broadcast_in_dim.8
  69.7 0.1 maximum_add_fusion
  69.8 0.1 slice_reduce_fusion
  69.9 0.1 fusion
  70.0 1.6 %collective-permute-start.14 = (bf16[128,1024]{1,0:T(8,128)(2,1)S(1)}, bf16[128,1024]{1,0:T(8,128)(2,1)S(1)}, u32[]{:S(2)}, u32[]{:S(2)}) collective-permute-start(bf16[128,1024]{1,0:T(8,128)(2,1)S(1)} %fusion), channel_id=1, source_target_pairs={{0,8},{2,10},{4,12},{6,14},{8,0},{10,2},{12,4},{14,6},{16,24},{18,... | collective-permute-start | bytes 786440 | tf_op jit(solution)/shard_map/ppermute | solution.py:193
  71.6 0.0 collective-permute-start.15
  71.6 0.1 slice_reduce_fusion.1
  71.7 0.9 %slice_divide_fusion.1 = f32[128,1024]{1,0:T(8,128)} fusion(f32[128,1152]{1,0:T(8,128)S(1)} %maximum_add_fusion, f32[128]{0:T(128)S(1)} %slice_reduce_fusion.1), kind=kLoop, calls=%fused_computation.7 | loop fusion | flops 131072 | bytes 1049088 | tf_op jit(solution)/shard_map/div | solution.py:300
  72.6 0.5 collective-permute-done.15
  73.2 1.6 %second_pass.3 = (f32[3,4,192]{2,1,0:T(4,128)S(1)}, f32[3,2,192]{2,1,0:T(2,128)S(1)}, f32[3,2,192]{2,1,0:T(2,128)S(1)}) custom-call(bf16[256,1024]{1,0:T(8,128)(2,1)S(1)} %pad_maximum_fusion.1.cents, f32[1,768]{1,0:T(1,128)S(1)} %get-tuple-element.56.refs_3_.refs_0_, f32[1,384]{1,0:T(1,128)S(1)} %get-tuple-element.57.refs_4_.refs_1_, ...), custom_call_target="tpu_custom_call" | custom-call | flops 805306368 | bytes 3145728 | tf_op jit(solution)/shard_map/second_pass/pallas_call | solution.py:153
  74.8 2.7 %collective-permute-done.14.cents = bf16[128,1024]{1,0:T(8,128)(2,1)S(1)} collective-permute-done((bf16[128,1024]{1,0:T(8,128)(2,1)S(1)}, bf16[128,1024]{1,0:T(8,128)(2,1)S(1)}, u32[]{:S(2)}, u32[]{:S(2)}) %collective-permute-start.14) | collective-permute-done | bytes 262176 | tf_op jit(solution)/shard_map/ppermute | solution.py:193
  77.5 0.0 collective-permute-start.16
  77.5 1.2 %second_pass.4 = (f32[3,4,192]{2,1,0:T(4,128)S(1)}, f32[3,2,192]{2,1,0:T(2,128)S(1)}, f32[3,2,192]{2,1,0:T(2,128)S(1)}) custom-call(bf16[128,1024]{1,0:T(8,128)(2,1)S(1)} %collective-permute-done.14.cents, f32[1,768]{1,0:T(1,128)S(1)} %get-tuple-element.56.refs_3_.refs_0_, f32[1,384]{1,0:T(1,128)S(1)} %get-tuple-element.57.refs_4_.refs_1_, ...), custom_call_target="tpu_custom_call" | custom-call | flops 402653184 | bytes 3145728 | tf_op jit(solution)/shard_map/second_pass/pallas_call | solution.py:153
  78.7 0.3 collective-permute-done.16.cents
  79.0 1.2 %second_pass.5 = (f32[3,4,192]{2,1,0:T(4,128)S(1)}, f32[3,2,192]{2,1,0:T(2,128)S(1)}, f32[3,2,192]{2,1,0:T(2,128)S(1)}) custom-call(bf16[128,1024]{1,0:T(8,128)(2,1)S(1)} %collective-permute-done.16.cents, f32[1,768]{1,0:T(1,128)S(1)} %get-tuple-element.56.refs_3_.refs_0_, f32[1,384]{1,0:T(1,128)S(1)} %get-tuple-element.57.refs_4_.refs_1_, ...), custom_call_target="tpu_custom_call" | custom-call | flops 402653184 | bytes 3145728 | tf_op jit(solution)/shard_map/second_pass/pallas_call | solution.py:153
  80.3 0.1 stack.78
  80.5 9.3 %all_to_all.11 = f32[8,3,192]{2,1,0:T(4,128)S(1)} all-to-all(f32[8,3,192]{2,1,0:T(4,128)S(1)} %copy.74), channel_id=1, replica_groups={{0,2,4,6,16,18,20,22},{8,10,12,14,24,26,28,30},{1,3,5,7,17,19,21,23},{9..., dimensions={0} | all-to-all | bytes 36864 | tf_op jit(solution)/shard_map/all_to_all | solution.py:247
  89.9 0.6 divide_subtract_fusion
  (60 shorter events, 0.9 us)
Async XLA Ops:
  1.8 12.1 %collective-permute-start.2 = (bf16[192,1024]{1,0:T(8,128)(2,1)S(1)}, bf16[192,1024]{1,0:T(8,128)(2,1)S(1)}, u32[]{:S(2)}, u32[]{:S(2)}) collective-permute-start(bf16[192,1024]{1,0:T(8,128)(2,1)S(1)} %convert_element_type.14.refs_0_), channel_id=1, source_target_pairs={{0,2},{2,0},{4,6},{6,4},{8,10},{10,8},{12,14},{14,12},{16,18},{18,... | collective-permute-start | bytes 1179656 | tf_op jit(solution)/shard_map/ppermute | solution.py:193
  5.9 13.3 %collective-permute-start.5 = (bf16[128,1024]{1,0:T(8,128)(2,1)S(1)}, bf16[128,1024]{1,0:T(8,128)(2,1)S(1)}, u32[]{:S(2)}, u32[]{:S(2)}) collective-permute-start(bf16[128,1024]{1,0:T(8,128)(2,1)S(1)} %convert_element_type.13), channel_id=1, source_target_pairs={{0,8},{2,10},{4,12},{6,14},{8,0},{10,2},{12,4},{14,6},{16,24},{18,... | collective-permute-start | bytes 786440 | tf_op jit(solution)/shard_map/ppermute | solution.py:193
  7.5 19.7 %collective-permute-start.1 = (bf16[192,1024]{1,0:T(8,128)(2,1)S(1)}, bf16[192,1024]{1,0:T(8,128)(2,1)S(1)}, u32[]{:S(2)}, u32[]{:S(2)}) collective-permute-start(bf16[192,1024]{1,0:T(8,128)(2,1)S(1)} %convert_element_type.14.refs_0_), channel_id=1, source_target_pairs={{0,16},{2,18},{4,20},{6,22},{8,24},{10,26},{12,28},{14,30},{16,0},... | collective-permute-start | bytes 1179656 | tf_op jit(solution)/shard_map/ppermute | solution.py:193
  10.1 17.1 %collective-permute-start.4 = (bf16[192,1024]{1,0:T(8,128)(2,1)S(1)}, bf16[192,1024]{1,0:T(8,128)(2,1)S(1)}, u32[]{:S(2)}, u32[]{:S(2)}) collective-permute-start(bf16[192,1024]{1,0:T(8,128)(2,1)S(1)} %convert_element_type.14.refs_0_), channel_id=1, source_target_pairs={{0,4},{2,6},{4,0},{6,2},{8,12},{10,14},{12,8},{14,10},{16,20},{18,... | collective-permute-start | bytes 1179656 | tf_op jit(solution)/shard_map/ppermute | solution.py:193
  13.9 14.6 %collective-permute-start.3 = (bf16[192,1024]{1,0:T(8,128)(2,1)S(1)}, bf16[192,1024]{1,0:T(8,128)(2,1)S(1)}, u32[]{:S(2)}, u32[]{:S(2)}) collective-permute-start(bf16[192,1024]{1,0:T(8,128)(2,1)S(1)} %collective-permute-done.2.refs_1_), channel_id=1, source_target_pairs={{0,4},{2,6},{4,0},{6,2},{8,12},{10,14},{12,8},{14,10},{16,20},{18,... | collective-permute-start | bytes 1179656 | tf_op jit(solution)/shard_map/ppermute | solution.py:193
  19.2 8.0 %collective-permute-start.6 = (bf16[128,1024]{1,0:T(8,128)(2,1)S(1)}, bf16[128,1024]{1,0:T(8,128)(2,1)S(1)}, u32[]{:S(2)}, u32[]{:S(2)}) collective-permute-start(bf16[128,1024]{1,0:T(8,128)(2,1)S(1)} %collective-permute-done.5), channel_id=1, source_target_pairs={{0,1},{1,0},{2,3},{3,2},{4,5},{5,4},{6,7},{7,6},{8,9},{9,8},{10,11... | collective-permute-start | bytes 786440 | tf_op jit(solution)/shard_map/ppermute | solution.py:202
  19.2 13.3 %collective-permute-start = (bf16[128,1024]{1,0:T(8,128)(2,1)S(1)}, bf16[128,1024]{1,0:T(8,128)(2,1)S(1)}, u32[]{:S(2)}, u32[]{:S(2)}) collective-permute-start(bf16[128,1024]{1,0:T(8,128)(2,1)S(1)} %convert_element_type.13), channel_id=1, source_target_pairs={{0,1},{1,0},{2,3},{3,2},{4,5},{5,4},{6,7},{7,6},{8,9},{9,8},{10,11... | collective-permute-start | bytes 786440 | tf_op jit(solution)/shard_map/ppermute | solution.py:202
  28.6 11.2 %collective-permute-start.9 = (bf16[192,1024]{1,0:T(8,128)(2,1)S(1)}, bf16[192,1024]{1,0:T(8,128)(2,1)S(1)}, u32[]{:S(2)}, u32[]{:S(2)}) collective-permute-start(bf16[192,1024]{1,0:T(8,128)(2,1)S(1)} %collective-permute-done.1.refs_0_), channel_id=1, source_target_pairs={{0,2},{2,0},{4,6},{6,4},{8,10},{10,8},{12,14},{14,12},{16,18},{18,... | collective-permute-start | bytes 1179656 | tf_op jit(solution)/shard_map/ppermute | solution.py:193
  29.1 13.8 %collective-permute-start.10 = (bf16[192,1024]{1,0:T(8,128)(2,1)S(1)}, bf16[192,1024]{1,0:T(8,128)(2,1)S(1)}, u32[]{:S(2)}, u32[]{:S(2)}) collective-permute-start(bf16[192,1024]{1,0:T(8,128)(2,1)S(1)} %collective-permute-done.1.refs_0_), channel_id=1, source_target_pairs={{0,4},{2,6},{4,0},{6,2},{8,12},{10,14},{12,8},{14,10},{16,20},{18,... | collective-permute-start | bytes 1179656 | tf_op jit(solution)/shard_map/ppermute | solution.py:193
  30.7 10.1 %collective-permute-start.7 = (bf16[96,1024]{1,0:T(8,128)(2,1)S(1)}, bf16[96,1024]{1,0:T(8,128)(2,1)S(1)}, u32[]{:S(2)}, u32[]{:S(2)}) collective-permute-start(bf16[96,1024]{1,0:T(8,128)(2,1)S(1)} %slice.325), channel_id=1, source_target_pairs={{0,16},{2,18},{4,20},{6,22},{8,24},{10,26},{12,28},{14,30},{16,0},... | collective-permute-start | bytes 589832 | tf_op jit(solution)/shard_map/ppermute | solution.py:193
  31.1 11.7 %collective-permute-start.8 = (bf16[96,1024]{1,0:T(8,128)(2,1)S(1)}, bf16[96,1024]{1,0:T(8,128)(2,1)S(1)}, u32[]{:S(2)}, u32[]{:S(2)}) collective-permute-start(bf16[96,1024]{1,0:T(8,128)(2,1)S(1)} %slice.326), channel_id=1, source_target_pairs={{0,6},{2,4},{4,2},{6,0},{8,14},{10,12},{12,10},{14,8},{16,22},{18,... | collective-permute-start | bytes 589832 | tf_op jit(solution)/shard_map/ppermute | solution.py:193
  57.2 2.9 %collective-permute-start.11 = (f32[128,1152]{1,0:T(8,128)S(1)}, f32[128,1152]{1,0:T(8,128)S(1)}, u32[]{:S(2)}, u32[]{:S(2)}) collective-permute-start(f32[128,1152]{1,0:T(8,128)S(1)} %slice.449), channel_id=1, source_target_pairs={{0,1},{1,0},{2,3},{3,2},{4,5},{5,4},{6,7},{7,6},{8,9},{9,8},{10,11... | collective-permute-start | bytes 1769480 | tf_op jit(solution)/shard_map/ppermute | solution.py:202
  59.6 2.3 %copy-start = (f32[128,1024]{1,0:T(8,128)S(1)}, f32[128,1024]{1,0:T(8,128)}, u32[]{:S(2)}) copy-start(f32[128,1024]{1,0:T(8,128)} %refs_9_.1) | copy-start | bytes 1572868
  59.6 10.0 %collective-permute-start.12 = (f32[128,1152]{1,0:T(8,128)S(1)}, f32[128,1152]{1,0:T(8,128)S(1)}, u32[]{:S(2)}, u32[]{:S(2)}) collective-permute-start(f32[128,1152]{1,0:T(8,128)S(1)} %sums_pass.5), channel_id=1, source_target_pairs={{0,1},{1,0},{2,3},{3,2},{4,5},{5,4},{6,7},{7,6},{8,9},{9,8},{10,11... | collective-permute-start | bytes 1769480 | tf_op jit(solution)/shard_map/ppermute | solution.py:202
  60.3 9.0 %collective-permute-start.13 = (bf16[128,1152]{1,0:T(8,128)(2,1)S(1)}, bf16[128,1152]{1,0:T(8,128)(2,1)S(1)}, u32[]{:S(2)}, u32[]{:S(2)}) collective-permute-start(bf16[128,1152]{1,0:T(8,128)(2,1)S(1)} %pad_maximum_fusion.2), channel_id=1, source_target_pairs={{0,8},{2,10},{4,12},{6,14},{8,0},{10,2},{12,4},{14,6},{16,24},{18,... | collective-permute-start | bytes 884744 | tf_op jit(solution)/shard_map/ppermute | solution.py:193
  70.0 7.5 %collective-permute-start.14 = (bf16[128,1024]{1,0:T(8,128)(2,1)S(1)}, bf16[128,1024]{1,0:T(8,128)(2,1)S(1)}, u32[]{:S(2)}, u32[]{:S(2)}) collective-permute-start(bf16[128,1024]{1,0:T(8,128)(2,1)S(1)} %fusion), channel_id=1, source_target_pairs={{0,8},{2,10},{4,12},{6,14},{8,0},{10,2},{12,4},{14,6},{16,24},{18,... | collective-permute-start | bytes 786440 | tf_op jit(solution)/shard_map/ppermute | solution.py:193
  71.6 1.5 %collective-permute-start.15 = (bf16[128,1024]{1,0:T(8,128)(2,1)S(1)}, bf16[128,1024]{1,0:T(8,128)(2,1)S(1)}, u32[]{:S(2)}, u32[]{:S(2)}) collective-permute-start(bf16[128,1024]{1,0:T(8,128)(2,1)S(1)} %fusion), channel_id=1, source_target_pairs={{0,1},{1,0},{2,3},{3,2},{4,5},{5,4},{6,7},{7,6},{8,9},{9,8},{10,11... | collective-permute-start | bytes 786440 | tf_op jit(solution)/shard_map/ppermute | solution.py:202
  77.5 1.5 %collective-permute-start.16 = (bf16[128,1024]{1,0:T(8,128)(2,1)S(1)}, bf16[128,1024]{1,0:T(8,128)(2,1)S(1)}, u32[]{:S(2)}, u32[]{:S(2)}) collective-permute-start(bf16[128,1024]{1,0:T(8,128)(2,1)S(1)} %collective-permute-done.14.cents), channel_id=1, source_target_pairs={{0,1},{1,0},{2,3},{3,2},{4,5},{5,4},{6,7},{7,6},{8,9},{9,8},{10,11... | collective-permute-start | bytes 786440 | tf_op jit(solution)/shard_map/ppermute | solution.py:202
